TPU v7x, 32 devices: a whole 2x2x4 slice. The times are simulated.
32 devices in a mesh: expert: 4 (over z), dp: 4 (over y, x), test: 2 (over core).
Axes of the slice: x: 2, y: 2, z: 4, core: 2. Of those that a mesh axis runs over, the one named last changes fastest.
Arguments:
- tokens: bfloat16 [1024, 3584], P(('expert', 'dp'), 'test'), may hold values from -6 to 6
- out_grad: bfloat16 [1024, 3584], P(('expert', 'dp'), 'test'), may hold values from -6 to 6
- route_ids: int32 [1024, 8], P(('expert', 'dp')), may hold values from 0 to 255, as said below
- route_slots: int32 [1024, 8], P(('expert', 'dp')), may hold values from -1 to 1, as said below
- route_weight: bfloat16 [1024, 8], P(('expert', 'dp')), may hold values from 0.19921875 to 1
- w_gate: bfloat16 [4, 3584, 1024], P('expert', None, ('dp', 'test')), may hold values from -0.09375 to 0.09375
- w_up: bfloat16 [4, 3584, 1024], P('expert', None, ('dp', 'test')), may hold values from -0.09375 to 0.09375
- w_down: bfloat16 [4, 1024, 3584], P('expert', ('dp', 'test')), may hold values from -0.1875 to 0.1875
- proj_hidden: bfloat16 [4, 64, 1024], P('expert', None, ('dp', 'test')), may hold values from -0.1875 to 0.1875
- proj_grad: bfloat16 [4, 64, 3584], P('expert'), may hold values from -0.09375 to 0.09375
- test_feats: bfloat16 [4, 256, 4096], P('expert', 'test'), may hold values from -0.09375 to 0.09375
Outputs:
- in_grad: bfloat16 [1024, 3584], P(('expert', 'dp'), 'test')
- scores: float32 [1024, 256], P(('expert', 'dp'), 'test')
Inputs may be any that keep to these rules, and one draw needn't show every extreme that they name: `route_ids`: each row names 8 different experts. `route_slots`: A route's slot is -1 exactly when its expert is 4 or more, or when 2 earlier tokens of the same aligned block of 64 rows already take that expert; otherwise it is the number of earlier tokens of that block routed to that expert.
All inputs are finite; a program needn't handle non-finite values.
Results may differ from a plain program's by a relative error of at most 0.0065.
Values may be sent and summed in bfloat16 or wider, within the bound.
No kernel may reach another device: no remote copies, remote signals or barrier semaphores. Data moves between devices by JAX's collectives and lax.ppermute only.
A program may use at most 64 MiB of HBM per device.

v0:
```python
import jax
import jax.numpy as jnp
from jax import lax
from jax.sharding import PartitionSpec as P

CAP = 2


def pick_tables(ids_in, slots_in, weights_in, experts):
    live_mask = (slots_in >= 0) & (ids_in < experts)
    slot_code = jnp.where(live_mask, ids_in * CAP + slots_in, -1)
    columns = jnp.arange(experts * CAP, dtype=jnp.int32)
    matches = slot_code[:, :, None] == columns[None, None, :]
    picks = jnp.sum(matches.astype(jnp.float32), axis=1)
    weighted = jnp.sum(jnp.where(matches, weights_in.astype(jnp.float32)[:, :, None], 0.0), axis=1)
    return (picks, weighted)


def expert_pass(flat_in, flat_grad, gate_w, up_w, down_w, hid_proj):
    gate_pre = jnp.dot(flat_in, gate_w, preferred_element_type=jnp.float32)
    up_pre = jnp.dot(flat_in, up_w, preferred_element_type=jnp.float32)
    sigmoid_gate = jax.nn.sigmoid(gate_pre)
    act_gate = gate_pre * sigmoid_gate
    hidden = (act_gate * up_pre).astype(jnp.bfloat16)
    proj_part = lax.dot_general(
        hidden, hid_proj, (((1,), (1,)), ((), ())), preferred_element_type=jnp.float32
    )
    hid_grad = lax.dot_general(
        flat_grad, down_w, (((1,), (1,)), ((), ())), preferred_element_type=jnp.float32
    )
    up_grad = (hid_grad * act_gate).astype(jnp.bfloat16)
    gate_grad = (hid_grad * up_pre * sigmoid_gate * (1.0 + gate_pre * (1.0 - sigmoid_gate))).astype(
        jnp.bfloat16
    )
    return (proj_part, gate_grad, up_grad)


def score_rows(hidden_vec, grad_vec, test_rows):
    row_total = hidden_vec.shape[0]
    feature = (
        (hidden_vec[:, :, None] * grad_vec[:, None, :]).reshape(row_total, -1).astype(jnp.bfloat16)
    )
    return lax.dot_general(
        feature, test_rows, (((1,), (1,)), ((), ())), preferred_element_type=jnp.float32
    )


def on_device(
    tokens,
    out_grad,
    route_ids,
    route_slots,
    route_weight,
    w_gate,
    w_up,
    w_down,
    proj_hidden,
    proj_grad,
    test_feats,
):
    experts = lax.axis_size("expert")
    groups = lax.axis_size("dp")
    halves = lax.axis_size("test")
    tok_rows = tokens.shape[0]
    half_width = tokens.shape[1]
    slots_all = experts * CAP
    full_in, full_grad = (
        lax.all_gather(tokens, "test", axis=1, tiled=True),
        lax.all_gather(out_grad, "test", axis=1, tiled=True),
    )
    full_width = full_in.shape[1]
    grad_proj = proj_grad[0]
    test_rows = test_feats[0]
    own_pick, own_weight = pick_tables(route_ids, route_slots, route_weight, experts)
    all_in, all_grad, all_ids, all_slots, all_weight = (
        lax.all_gather(full_in, "dp", axis=0, tiled=True),
        lax.all_gather(full_grad, "dp", axis=0, tiled=True),
        lax.all_gather(route_ids, "dp", axis=0, tiled=True),
        lax.all_gather(route_slots, "dp", axis=0, tiled=True),
        lax.all_gather(route_weight, "dp", axis=0, tiled=True),
    )
    group_tok = all_in.shape[0]
    pick_all, weight_all = pick_tables(all_ids, all_slots, all_weight, experts)
    owner_idx = jnp.arange(group_tok, dtype=jnp.int32) // tok_rows
    in_group = (owner_idx[None, :] == jnp.arange(groups, dtype=jnp.int32)[:, None]).astype(
        jnp.float32
    )
    select = (
        (pick_all.T.reshape(experts, 1, CAP, group_tok) * in_group.reshape(1, groups, 1, group_tok))
        .reshape(-1, group_tok)
        .astype(jnp.bfloat16)
    )
    select_w = (
        (
            weight_all.T.reshape(experts, 1, CAP, group_tok)
            * in_group.reshape(1, groups, 1, group_tok)
        )
        .reshape(-1, group_tok)
        .astype(jnp.bfloat16)
    )
    in_buf = jnp.dot(select, all_in, preferred_element_type=jnp.float32).astype(jnp.bfloat16)
    grad_buf = jnp.dot(select_w, all_grad, preferred_element_type=jnp.float32).astype(jnp.bfloat16)
    rows_per = groups * CAP
    recv_in, recv_grad = (
        lax.all_to_all(
            in_buf.reshape(experts, rows_per, full_width),
            "expert",
            split_axis=0,
            concat_axis=0,
            tiled=True,
        ),
        lax.all_to_all(
            grad_buf.reshape(experts, rows_per, full_width),
            "expert",
            split_axis=0,
            concat_axis=0,
            tiled=True,
        ),
    )
    flat_in = recv_in.reshape(-1, full_width)
    flat_grad = recv_grad.reshape(-1, full_width)
    gate_w = w_gate[0]
    up_w = w_up[0]
    proj_part, gate_grad, up_grad = expert_pass(
        flat_in, flat_grad, gate_w, up_w, w_down[0], proj_hidden[0]
    )
    parts = lax.dot_general(
        gate_grad, gate_w, (((1,), (1,)), ((), ())), preferred_element_type=jnp.float32
    )
    parts = (
        parts
        + lax.dot_general(
            up_grad, up_w, (((1,), (1,)), ((), ())), preferred_element_type=jnp.float32
        )
    ).astype(jnp.bfloat16)
    hidden_vec = lax.psum(proj_part, ("dp", "test"))
    my_group = lax.axis_index("dp")
    hid_mine = lax.dynamic_index_in_dim(
        hidden_vec.reshape(experts, groups, CAP, -1), my_group, 1, keepdims=False
    ).reshape(slots_all, -1)
    grad_rows = lax.dynamic_index_in_dim(
        recv_grad.reshape(experts, groups, CAP, full_width), my_group, 1, keepdims=False
    ).reshape(slots_all, full_width)
    grad_mine = lax.dot_general(
        grad_rows, grad_proj, (((1,), (1,)), ((), ())), preferred_element_type=jnp.float32
    )
    route_score = (
        score_rows(hid_mine, grad_mine, test_rows).astype(jnp.bfloat16).reshape(experts, CAP, -1)
    )
    back_parts, back_score = (
        lax.all_to_all(
            parts.reshape(experts, rows_per, full_width),
            "expert",
            split_axis=0,
            concat_axis=0,
            tiled=True,
        ),
        lax.all_to_all(route_score, "expert", split_axis=0, concat_axis=0, tiled=True),
    )
    part_rows = back_parts.reshape(-1, full_width)
    first_row = jnp.int32(0)
    pieces = []
    for block_step in range(tok_rows * lax.axis_size(("dp", "test")) // tok_rows):
        block_idx = first_row // tok_rows + block_step
        owner_block = block_idx // halves
        half_idx = block_idx % halves
        picked_cols = lax.dynamic_slice_in_dim(select, owner_block * tok_rows, tok_rows, 1)
        part_cols = lax.dynamic_slice_in_dim(part_rows, half_idx * half_width, half_width, 1)
        pieces.append(
            lax.dot_general(
                picked_cols, part_cols, (((0,), (0,)), ((), ())), preferred_element_type=jnp.float32
            )
        )
    in_grad = lax.psum_scatter(
        jnp.concatenate(pieces, axis=0), ("dp", "test"), scatter_dimension=0, tiled=True
    ).astype(jnp.bfloat16)
    scores_out = jnp.dot(
        own_pick.astype(jnp.bfloat16),
        back_score.reshape(slots_all, -1),
        preferred_element_type=jnp.float32,
    )
    return (in_grad, scores_out)


def solution(mesh):
    placed = (
        P(("expert", "dp"), "test"),
        P(("expert", "dp"), "test"),
        P(("expert", "dp"), None),
        P(("expert", "dp"), None),
        P(("expert", "dp"), None),
        P("expert", None, ("dp", "test")),
        P("expert", None, ("dp", "test")),
        P("expert", ("dp", "test"), None),
        P("expert", None, ("dp", "test")),
        P("expert", None, None),
        P("expert", "test", None),
    )
    return jax.shard_map(
        on_device,
        mesh=mesh,
        in_specs=placed,
        out_specs=(P(("expert", "dp"), "test"), P(("expert", "dp"), "test")),
        check_vma=False,
    )
```

profile of v0, /device:TPU:0, one launch (start us, length us, event | category | flops | bytes accessed | tf_op | source)
XLA Modules:
  0.0 174.0 jit_solution(7216267676949846890)
XLA Ops:
  7.2 4.2 %all_gather.26 = bf16[64,3584]{1,0:T(8,128)(2,1)} all-gather(bf16[64,1792]{1,0:T(8,128)(2,1)} %param.11), channel_id=1, replica_groups=mesh['expert'=4,'dp'=4,'test'=2] {'test'}, dimensions={1}, use_global_device_ids=true | all-gather | bytes 688128 | tf_op jit(solution)/shard_map/all_gather | solution.py:68
  11.5 3.9 %all_gather.24 = bf16[64,3584]{1,0:T(8,128)(2,1)} all-gather(bf16[64,1792]{1,0:T(8,128)(2,1)} %param.12), channel_id=1, replica_groups=mesh['expert'=4,'dp'=4,'test'=2] {'test'}, dimensions={1}, use_global_device_ids=true | all-gather | bytes 688128 | tf_op jit(solution)/shard_map/all_gather | solution.py:69
  15.4 9.7 %all-gather.2 = bf16[4,64,8]{1,2,0:T(8,128)(2,1)S(1)} all-gather(bf16[1,64,8]{1,2,0:T(8,128)(2,1)} %bitcast.73), channel_id=1, replica_groups=mesh['expert'=4,'dp'=4,'test'=2] {'dp'}, dimensions={0}, use_global_device_ids=true | all-gather | bytes 5120 | tf_op jit(solution)/shard_map/all_gather | solution.py:80
  25.2 8.0 %all-gather = s32[4,64,8]{1,2,0:T(8,128)S(1)} all-gather(s32[1,64,8]{1,2,0:T(8,128)} %bitcast.68), channel_id=1, replica_groups=mesh['expert'=4,'dp'=4,'test'=2] {'dp'}, dimensions={0}, use_global_device_ids=true | all-gather | bytes 10240 | tf_op jit(solution)/shard_map/all_gather | solution.py:79
  33.2 7.4 %all-gather.1 = s32[4,64,8]{1,2,0:T(8,128)S(1)} all-gather(s32[1,64,8]{1,2,0:T(8,128)} %bitcast.69), channel_id=1, replica_groups=mesh['expert'=4,'dp'=4,'test'=2] {'dp'}, dimensions={0}, use_global_device_ids=true | all-gather | bytes 10240 | tf_op jit(solution)/shard_map/all_gather | solution.py:78
  40.9 6.4 %all-gather.8.cloned.1.call-done = bf16[256,3584]{1,0:T(8,128)(2,1)} async-done(((bf16[64,3584]{1,0:T(8,128)(2,1)}), bf16[256,3584]{1,0:T(8,128)(2,1)}) %all-gather.8.cloned.1.call-update) | async-done | bytes 1835024 | tf_op jit(solution)/shard_map/all_gather | solution.py:76
  47.3 2.6 %fusion.2 = bf16[4,8,3584]{2,1,0:T(8,128)(2,1)} fusion(bf16[32,256]{1,0:T(8,128)(2,1)S(1)} %convert_element_type.72, bf16[256,3584]{1,0:T(8,128)(2,1)} %all-gather.8.cloned.1.call-done), kind=kOutput, calls=%fused_computation.5 | convolution fusion | flops 58834944 | bytes 2080768 | tf_op jit(solution)/shard_map/dot_general | solution.py:101
  49.9 4.6 %all-to-all-start.1 = ((bf16[4,8,3584]{2,1,0:T(8,128)(2,1)}), bf16[4,8,3584]{2,1,0:T(8,128)(2,1)S(1)}, u32[]{:S(2)}, u32[]{:S(2)}) async-start(bf16[4,8,3584]{2,1,0:T(8,128)(2,1)} %fusion.2), calls=%async_computation.1 | async-start | bytes 458752 | tf_op jit(solution)/shard_map/all_to_all | solution.py:105
  54.6 27.8 %all-gather.6.cloned.1.call-done = bf16[256,3584]{1,0:T(8,128)(2,1)} async-done(((bf16[64,3584]{1,0:T(8,128)(2,1)}), bf16[256,3584]{1,0:T(8,128)(2,1)}) %all-gather.6.cloned.1.call-update) | async-done | bytes 1835024 | tf_op jit(solution)/shard_map/all_gather | solution.py:77
  82.3 2.6 %fusion.1 = bf16[4,8,3584]{2,1,0:T(8,128)(2,1)} fusion(bf16[32,256]{1,0:T(8,128)(2,1)S(1)} %convert_element_type.75, bf16[256,3584]{1,0:T(8,128)(2,1)} %all-gather.6.cloned.1.call-done), kind=kOutput, calls=%fused_computation.4 | convolution fusion | flops 58834944 | bytes 2080768 | tf_op jit(solution)/shard_map/dot_general | solution.py:102
  85.0 4.6 %all-to-all-start = ((bf16[4,8,3584]{2,1,0:T(8,128)(2,1)}), bf16[4,8,3584]{2,1,0:T(8,128)(2,1)S(1)}, u32[]{:S(2)}, u32[]{:S(2)}) async-start(bf16[4,8,3584]{2,1,0:T(8,128)(2,1)} %fusion.1), calls=%async_computation | async-start | bytes 458752 | tf_op jit(solution)/shard_map/all_to_all | solution.py:112
  90.1 7.7 %all-to-all-done = bf16[4,8,3584]{2,1,0:T(8,128)(2,1)S(1)} async-done(((bf16[4,8,3584]{2,1,0:T(8,128)(2,1)}), bf16[4,8,3584]{2,1,0:T(8,128)(2,1)S(1)}, u32[]{:S(2)}, u32[]{:S(2)}) %all-to-all-start) | async-done | bytes 229408 | tf_op jit(solution)/shard_map/all_to_all | solution.py:112
  97.8 1.5 fusion.12
  100.2 10.0 %all_to_all.20 = bf16[4,8,3584]{2,1,0:T(8,128)(2,1)S(1)} all-to-all(bf16[4,8,3584]{2,1,0:T(8,128)(2,1)S(1)} %fusion.3), channel_id=1, replica_groups=mesh['expert'=4,'dp'=4,'test'=2] {'expert'}, dimensions={0} | all-to-all | bytes 458752 | tf_op jit(solution)/shard_map/all_to_all | solution.py:151
  112.2 1.1 convolution_dynamic-update-slice_fusion.5
  113.3 1.1 convolution_dynamic-update-slice_fusion.4
  114.4 1.0 convolution_dynamic-update-slice_fusion.3
  116.5 1.1 convolution_dynamic-update-slice_fusion.1
  117.6 1.1 convolution_dynamic-update-slice_fusion
  119.1 22.4 %psum.7 = f32[4,4,2,64]{3,2,1,0:T(2,128)S(1)} all-reduce(f32[4,4,2,64]{3,2,1,0:T(2,128)S(1)} %bitcast.71), channel_id=1, replica_groups=mesh['expert'=4,'dp'=4,'test'=2] {'dp','test'}, use_global_device_ids=true, to_apply=%region_4.5 | all-reduce | flops 2048 | bytes 16384 | tf_op jit(solution)/shard_map/psum | solution.py:136
  143.0 3.2 %all-to-all-start.3 = ((bf16[4,2,128]{2,1,0:T(2,128)(2,1)}), bf16[4,2,128]{2,1,0:T(2,128)(2,1)S(1)}, u32[]{:S(2)}, u32[]{:S(2)}) async-start(bf16[4,2,128]{2,1,0:T(2,128)(2,1)} %bitcast.19), calls=%async_computation.4 | async-start | bytes 4096 | tf_op jit(solution)/shard_map/all_to_all | solution.py:158
  146.3 5.4 %all-to-all-done.3 = bf16[4,2,128]{2,1,0:T(2,128)(2,1)S(1)} async-done(((bf16[4,2,128]{2,1,0:T(2,128)(2,1)}), bf16[4,2,128]{2,1,0:T(2,128)(2,1)S(1)}, u32[]{:S(2)}, u32[]{:S(2)}) %all-to-all-start.3) | async-done | bytes 2080 | tf_op jit(solution)/shard_map/all_to_all | solution.py:158
  152.5 13.3 %reduce-scatter.2.cloned.1.call-done = f32[64,1792]{1,0:T(8,128)} async-done(((f32[512,1792]{1,0:T(8,128)}), f32[64,1792]{1,0:T(8,128)}) %reduce-scatter.2.cloned.1.call-update) | async-done | bytes 458768 | tf_op jit(solution)/shard_map/reduce_scatter | solution.py:174
  165.8 1.7 convert_element_type.81
  (53 shorter events, 7.5 us)
Async XLA Ops:
  7.2 134.9 %copy-start = (bf16[1,128,4096]{2,1,0:T(8,128)(2,1)S(1)}, bf16[1,128,4096]{2,1,0:T(8,128)(2,1)}, u32[]{:S(2)}) copy-start(bf16[1,128,4096]{2,1,0:T(8,128)(2,1)} %param.21) | copy-start | bytes 3145732
  7.2 40.1 %all-gather.8.cloned.1.call-start = ((), (), s32[]{:S(2)}) async-start(), calls=%async_computation.6 | async-start | bytes 2293760 | tf_op jit(solution)/shard_map/all_gather | solution.py:76
  11.4 78.1 %copy-start.2 = (bf16[1,3584,128]{2,1,0:T(8,128)(2,1)S(1)}, bf16[1,3584,128]{2,1,0:T(8,128)(2,1)}, u32[]{:S(2)}) copy-start(bf16[1,3584,128]{2,1,0:T(8,128)(2,1)} %param.16) | copy-start | bytes 2752516
  11.5 70.9 %all-gather.6.cloned.1.call-start = ((), (), s32[]{:S(2)}) async-start(), calls=%async_computation.5 | async-start | bytes 2293760 | tf_op jit(solution)/shard_map/all_gather | solution.py:77
  15.4 74.4 %copy-start.1 = (bf16[1,3584,128]{2,1,0:T(8,128)(2,1)S(1)}, bf16[1,3584,128]{2,1,0:T(8,128)(2,1)}, u32[]{:S(2)}) copy-start(bf16[1,3584,128]{2,1,0:T(8,128)(2,1)} %param.17) | copy-start | bytes 2752516
  49.9 35.0 %all-to-all-start.1 = ((bf16[4,8,3584]{2,1,0:T(8,128)(2,1)}), bf16[4,8,3584]{2,1,0:T(8,128)(2,1)S(1)}, u32[]{:S(2)}, u32[]{:S(2)}) async-start(bf16[4,8,3584]{2,1,0:T(8,128)(2,1)} %fusion.2), calls=%async_computation.1 | async-start | bytes 458752 | tf_op jit(solution)/shard_map/all_to_all | solution.py:105
  85.0 12.8 %all-to-all-start = ((bf16[4,8,3584]{2,1,0:T(8,128)(2,1)}), bf16[4,8,3584]{2,1,0:T(8,128)(2,1)S(1)}, u32[]{:S(2)}, u32[]{:S(2)}) async-start(bf16[4,8,3584]{2,1,0:T(8,128)(2,1)} %fusion.1), calls=%async_computation | async-start | bytes 458752 | tf_op jit(solution)/shard_map/all_to_all | solution.py:112
  89.6 76.2 %reduce-scatter.2.cloned.1.call-start = ((), (), s32[]{:S(2)}) async-start(), calls=%async_computation.7 | async-start | bytes 4128768 | tf_op jit(solution)/shard_map/reduce_scatter | solution.py:174
  112.2 6.5 %copy-start.4 = (s32[64,8]{0,1:T(8,128)S(1)}, s32[64,8]{0,1:T(8,128)}, u32[]{:S(2)}) copy-start(s32[64,8]{0,1:T(8,128)} %param.14) | copy-start | bytes 6148
  112.2 6.5 %copy-start.5 = (s32[64,8]{0,1:T(8,128)S(1)}, s32[64,8]{0,1:T(8,128)}, u32[]{:S(2)}) copy-start(s32[64,8]{0,1:T(8,128)} %param.13) | copy-start | bytes 6148
  113.3 5.6 %copy-start.6 = (bf16[1,64,128]{2,1,0:T(8,128)(2,1)S(1)}, bf16[1,64,128]{2,1,0:T(8,128)(2,1)}, u32[]{:S(2)}) copy-start(bf16[1,64,128]{2,1,0:T(8,128)(2,1)} %param.19) | copy-start | bytes 49156
  113.3 28.2 %copy-start.3 = (bf16[1,64,3584]{2,1,0:T(8,128)(2,1)S(1)}, bf16[1,64,3584]{2,1,0:T(8,128)(2,1)}, u32[]{:S(2)}) copy-start(bf16[1,64,3584]{2,1,0:T(8,128)(2,1)} %param.20) | copy-start | bytes 1376260
  143.0 8.7 %all-to-all-start.3 = ((bf16[4,2,128]{2,1,0:T(2,128)(2,1)}), bf16[4,2,128]{2,1,0:T(2,128)(2,1)S(1)}, u32[]{:S(2)}, u32[]{:S(2)}) async-start(bf16[4,2,128]{2,1,0:T(2,128)(2,1)} %bitcast.19), calls=%async_computation.4 | async-start | bytes 4096 | tf_op jit(solution)/shard_map/all_to_all | solution.py:158
Sparse Core Ops, SparseCore 0:
  11.6 35.7 all-gather.7
  49.2 33.1 all-gather.5
  118.8 46.9 reduce-scatter.1
where the time goes:
time: 175 us; the launch traced here: 174 us
  blocking collectives  65.7 us (38%)
  waiting for transfers between devices  60.7 us (35%)
  matrix products  18.7 us (11%)
  between operations  13.9 us (8%)
  starting transfers between devices  12.5 us (7%)
  other arithmetic  1.97 us (1%)
    all_gather x1, waiting for transfers between devices, on_device(): lax.all_gather(full_grad, 'dp', axis=0, tiled=True)  27.8 us
    psum x1, blocking collectives, on_device(): hidden_vec = lax.psum(proj_part, ('dp', 'test'))  22.4 us
    reduce_scatter x1, waiting for transfers between devices, on_device(): lax.psum_scatter(jnp.concatenate(pieces, axis=0), ('dp', 'test'), scatter...  13.3 us
    all_to_all x1, blocking collectives, on_device(): lax.all_to_all(parts.reshape(experts, rows_per, full_width), 'expert', sp...  10 us
    all_gather x1, blocking collectives, on_device(): lax.all_gather(route_weight, 'dp', axis=0, tiled=True)  9.69 us
    dot_general x8, matrix products, on_device(): lax.dot_general(picked_cols, part_cols, (((0,), (0,)), ((), ())), preferr...  8.48 us
    all_gather x1, blocking collectives, on_device(): lax.all_gather(route_slots, 'dp', axis=0, tiled=True)  8.01 us
    all_to_all x1, waiting for transfers between devices, on_device(): lax.all_to_all(grad_buf.reshape(experts, rows_per, full_width), 'expert',...  7.69 us
  transfers between devices with their start and end apart: 6, of which 5 were waited for; matrix products, arithmetic and copies ran while one was open for 5% of the time, Pallas kernels for 0%

commit v1 on v0

v1 whole, which is shorter than its diff:
```python
import jax
import jax.numpy as jnp
from jax import lax
from jax.sharding import PartitionSpec as P

CAP = 2
PLANE = ("dp", "test")


def send_rel(block, axes, offset):
    size = lax.axis_size(axes)
    return lax.ppermute(block, axes, [(i, i ^ offset) for i in range(size)])


def pick_rows(ids_in, slots_in, weights_in, experts):
    rel = jnp.arange(experts * CAP, dtype=jnp.int32)
    here = lax.axis_index("expert")
    codes = ((rel // CAP) ^ here) * CAP + rel % CAP
    live_mask = (slots_in >= 0) & (ids_in < experts)
    slot_code = jnp.where(live_mask, ids_in * CAP + slots_in, -1)
    matches = slot_code[None, :, :] == codes[:, None, None]
    picks = jnp.sum(matches.astype(jnp.float32), axis=2)
    weighted = jnp.sum(jnp.where(matches, weights_in.astype(jnp.float32)[None], 0.0), axis=2)
    return picks.astype(jnp.bfloat16), weighted.astype(jnp.bfloat16)


def dot_f32(a, b, contract):
    return lax.dot_general(a, b, (contract, ((), ())), preferred_element_type=jnp.float32)


def on_device(
    tokens,
    out_grad,
    route_ids,
    route_slots,
    route_weight,
    w_gate,
    w_up,
    w_down,
    proj_hidden,
    proj_grad,
    test_feats,
):
    experts = lax.axis_size("expert")
    groups = lax.axis_size("dp")
    halves = lax.axis_size("test")
    plane = groups * halves
    half_width = tokens.shape[1]
    rows = experts * CAP
    core = lax.axis_index("test")
    gate_w, up_w, down_w = w_gate[0], w_up[0], w_down[0]
    hid_proj, grad_proj, test_rows = proj_hidden[0], proj_grad[0], test_feats[0]

    picks, weighted = pick_rows(route_ids, route_slots, route_weight, experts)
    own_in = dot_f32(picks, tokens, ((1,), (0,))).astype(jnp.bfloat16)
    own_grad = dot_f32(weighted, out_grad, ((1,), (0,))).astype(jnp.bfloat16)
    both = jnp.concatenate(
        [own_in.reshape(experts, CAP, half_width), own_grad.reshape(experts, CAP, half_width)], axis=1
    )
    arrived = [both[0]] + [send_rel(both[k], "expert", k) for k in range(1, experts)]
    block = jnp.stack(arrived)
    blocks = [block] + [send_rel(block, PLANE, j) for j in range(1, plane)]

    def side(half, first):
        return jnp.concatenate(
            [blocks[g * halves + half][:, first : first + CAP].reshape(rows, half_width) for g in range(groups)]
        )

    def whole(first):
        mine, other = side(0, first), side(1, first)
        return jnp.concatenate(
            [jnp.where(core == 0, mine, other), jnp.where(core == 0, other, mine)], axis=1
        )

    flat_in, flat_grad = whole(0), whole(CAP)
    gate_pre = dot_f32(flat_in, gate_w, ((1,), (0,)))
    up_pre = dot_f32(flat_in, up_w, ((1,), (0,)))
    sig = jax.nn.sigmoid(gate_pre)
    act_gate = gate_pre * sig
    hidden = (act_gate * up_pre).astype(jnp.bfloat16)
    hid_part = dot_f32(hidden, hid_proj, ((1,), (1,)))
    hid_high = hid_part.astype(jnp.bfloat16)
    hid_low = (hid_part - hid_high.astype(jnp.float32)).astype(jnp.bfloat16)
    hid_grad = dot_f32(flat_grad, down_w, ((1,), (1,)))
    up_grad = (hid_grad * act_gate).astype(jnp.bfloat16)
    gate_grad = (hid_grad * up_pre * sig * (1.0 + gate_pre * (1.0 - sig))).astype(jnp.bfloat16)
    parts = (
        dot_f32(gate_grad, gate_w, ((1,), (1,))) + dot_f32(up_grad, up_w, ((1,), (1,)))
    ).astype(jnp.bfloat16)
    low, high = parts[:, :half_width], parts[:, half_width:]
    sides = (jnp.where(core == 0, low, high), jnp.where(core == 0, high, low))
    tail = jnp.concatenate([hid_high, hid_low], axis=1)

    def outgoing(j):
        g, half = j // halves, j % halves
        cut = slice(g * rows, (g + 1) * rows)
        return jnp.concatenate([sides[half][cut], tail[cut]], axis=1)

    returned = [outgoing(0)] + [send_rel(outgoing(j), PLANE, j) for j in range(1, plane)]
    total = returned[0].astype(jnp.float32)
    for piece in returned[1:]:
        total = total + piece.astype(jnp.float32)
    proj = hid_part.shape[1]
    hid_mine = total[:, half_width : half_width + proj] + total[:, half_width + proj :]
    grad_mine = dot_f32(flat_grad[:rows], grad_proj, ((1,), (1,)))
    feature = (hid_mine[:, :, None] * grad_mine[:, None, :]).reshape(rows, -1).astype(jnp.bfloat16)
    route_score = dot_f32(feature, test_rows, ((1,), (1,)))
    back = jnp.concatenate([total[:, :half_width], route_score], axis=1).astype(jnp.bfloat16)
    back = back.reshape(experts, CAP, -1)
    home = [back[0]] + [send_rel(back[k], "expert", k) for k in range(1, experts)]
    home = jnp.concatenate(home, axis=0)
    result = dot_f32(picks, home, ((0,), (0,)))
    return result[:, :half_width].astype(jnp.bfloat16), result[:, half_width:]


def solution(mesh):
    placed = (
        P(("expert", "dp"), "test"),
        P(("expert", "dp"), "test"),
        P(("expert", "dp"), None),
        P(("expert", "dp"), None),
        P(("expert", "dp"), None),
        P("expert", None, ("dp", "test")),
        P("expert", None, ("dp", "test")),
        P("expert", ("dp", "test"), None),
        P("expert", None, ("dp", "test")),
        P("expert", None, None),
        P("expert", "test", None),
    )
    return jax.shard_map(
        on_device,
        mesh=mesh,
        in_specs=placed,
        out_specs=(P(("expert", "dp"), "test"), P(("expert", "dp"), "test")),
        check_vma=False,
    )
```

time: 175 us -> 47.8 us (0.27)
  blocking collectives: 65.7 us -> 0 us
  waiting for transfers between devices: 60.7 us -> 12.4 us
  matrix products: 18.7 us -> 3.89 us
  between operations: 13.9 us -> 1.12 us
  starting transfers between devices: 12.5 us -> 23.5 us
  local copies, waits for them, and re-layouts: 0.61 us -> 4.3 us
    all_gather x2 -> x0, waiting for transfers between devices: 34.2 us -> none  [the longest x1 27.8 us: on_device(): lax.all_gather(full_grad, 'dp', axis=0, tiled=True)]
    all_gather x5 -> x0, blocking collectives: 33.3 us -> none  [the longest x1 9.69 us: on_device(): lax.all_gather(route_weight, 'dp', axis=0, tiled=True)]
    ppermute x0 -> x20, starting transfers between devices: none -> 23.5 us  [send_rel(): return lax.ppermute(block, axes, [(i, i ^ offset) for i in range(size)])]
    psum x1 -> x0, blocking collectives: 22.4 us -> none  [on_device(): hidden_vec = lax.psum(proj_part, ('dp', 'test'))]
    dot_general x19 -> x11, matrix products: 18.7 us -> 3.89 us  [dot_f32(): lax.dot_general(a, b, (contract, ((), ())), preferred_element_type=jnp.fl...]
    reduce_scatter x1 -> x0, waiting for transfers between devices: 13.3 us -> none  [on_device(): lax.psum_scatter(jnp.concatenate(pieces, axis=0), ('dp', 'test'), scatter...]
    all_to_all x3 -> x0, waiting for transfers between devices: 13.1 us -> none  [the longest x1 7.69 us: on_device(): lax.all_to_all(grad_buf.reshape(experts, rows_per, full_width), 'expert',...]
    all_to_all x3 -> x0, starting transfers between devices: 12.4 us -> none  [the longest x1 4.6 us: on_device(): lax.all_to_all(grad_buf.reshape(experts, rows_per, full_width), 'expert',...]
  transfers between devices with their start and end apart: 6 -> 20, of which waited for: 5 -> 10; matrix products, arithmetic and copies ran while one was open for 5% -> 2% of each run, Pallas kernels for 0% -> 0%
where the time goes in v1:
time: 47.8 us; the launch traced here: 47.4 us
  starting transfers between devices  23.5 us (49%)
  waiting for transfers between devices  12.4 us (26%)
  local copies, waits for them, and re-layouts  4.3 us (9%)
  matrix products  3.89 us (8%)
  other arithmetic  2.26 us (5%)
  between operations  1.12 us (2%)
    ppermute x20, starting transfers between devices, send_rel(): return lax.ppermute(block, axes, [(i, i ^ offset) for i in range(size)])  23.5 us
    ppermute x20, waiting for transfers between devices, send_rel(): return lax.ppermute(block, axes, [(i, i ^ offset) for i in range(size)])  12.4 us
    dot_general x11, matrix products, dot_f32(): lax.dot_general(a, b, (contract, ((), ())), preferred_element_type=jnp.fl...  3.89 us
    unnamed x26, local copies, waits for them, and re-layouts  2.06 us
    slice x2, local copies, waits for them, and re-layouts, on_device(): return (result[:, :half_width].astype(jnp.bfloat16), result[:, half_width:])  1.33 us
  transfers between devices with their start and end apart: 20, of which 10 were waited for; matrix products, arithmetic and copies ran while one was open for 2% of the time, Pallas kernels for 0%

profile of v1, /device:TPU:0, one launch (start us, length us, event | category | flops | bytes accessed | tf_op | source)
XLA Modules:
  0.0 47.4 jit_solution(13546878921998755877)
XLA Ops:
  0.7 0.8 %convert_element_type.80 = f32[64,8]{0,1:T(8,128)S(1)} convert(bf16[64,8]{0,1:T(8,128)(2,1)} %param.15) | non-fusion elementwise | flops 512 | bytes 3072 | tf_op jit(solution)/shard_map/convert_element_type | solution.py:23
  1.5 0.7 %add_select_fusion = s32[64,8]{0,1:T(8,128)S(1)} fusion(s32[64,8]{0,1:T(8,128)} %param.14, s32[64,8]{0,1:T(8,128)} %param.13), kind=kLoop, calls=%fused_computation.111 | loop fusion | flops 3072 | bytes 6144 | tf_op jit(solution)/shard_map/jit(_where)/select_n | solution.py:20
  2.3 1.1 %convolution_convert_fusion = bf16[8,1792]{1,0:T(8,128)(2,1)S(1)} fusion(bf16[64,1792]{1,0:T(8,128)(2,1)} %param.12, bf16[8,64]{1,0:T(8,128)(2,1)S(1)} %get-tuple-element.3), kind=kOutput, calls=%fused_computation.2 | convolution fusion | flops 1849344 | bytes 259072 | tf_op jit(solution)/shard_map/dot_general | solution.py:28
  3.7 3.1 %collective-permute-start = (bf16[4,1792]{1,0:T(4,128)(2,1)S(1)}, bf16[4,1792]{1,0:T(4,128)(2,1)S(1)}, u32[]{:S(2)}, u32[]{:S(2)}) collective-permute-start(bf16[4,1792]{1,0:T(4,128)(2,1)S(1)} %get-tuple-element.35), channel_id=1, source_target_pairs={{0,8},{8,0},{16,24},{24,16},{1,9},{9,1},{17,25},{25,17},{2,10},{10... | collective-permute-start | bytes 43016 | tf_op jit(solution)/shard_map/ppermute | solution.py:12
  6.8 2.5 %collective-permute-start.2 = (bf16[4,1792]{1,0:T(4,128)(2,1)S(1)}, bf16[4,1792]{1,0:T(4,128)(2,1)S(1)}, u32[]{:S(2)}, u32[]{:S(2)}) collective-permute-start(bf16[4,1792]{1,0:T(4,128)(2,1)S(1)} %get-tuple-element.36), channel_id=1, source_target_pairs={{0,24},{8,16},{16,8},{24,0},{1,25},{9,17},{17,9},{25,1},{2,26},{10... | collective-permute-start | bytes 43016 | tf_op jit(solution)/shard_map/ppermute | solution.py:12
  9.4 3.1 %collective-permute-done.2 = bf16[4,1792]{1,0:T(4,128)(2,1)S(1)} collective-permute-done((bf16[4,1792]{1,0:T(4,128)(2,1)S(1)}, bf16[4,1792]{1,0:T(4,128)(2,1)S(1)}, u32[]{:S(2)}, u32[]{:S(2)}) %collective-permute-start.2) | collective-permute-done | bytes 14368 | tf_op jit(solution)/shard_map/ppermute | solution.py:12
  12.5 1.4 %collective-permute-done.1 = bf16[4,1792]{1,0:T(4,128)(2,1)S(1)} collective-permute-done((bf16[4,1792]{1,0:T(4,128)(2,1)S(1)}, bf16[4,1792]{1,0:T(4,128)(2,1)S(1)}, u32[]{:S(2)}, u32[]{:S(2)}) %collective-permute-start.1) | collective-permute-done | bytes 14368 | tf_op jit(solution)/shard_map/ppermute | solution.py:12
  14.5 2.2 %collective-permute-start.8 = (bf16[4,4,1792]{2,1,0:T(4,128)(2,1)S(1)}, bf16[4,4,1792]{2,1,0:T(4,128)(2,1)S(1)}, u32[]{:S(2)}, u32[]{:S(2)}) collective-permute-start(bf16[4,4,1792]{2,1,0:T(4,128)(2,1)S(1)} %pad_maximum_fusion.3), channel_id=1, source_target_pairs={{0,5},{1,4},{2,7},{3,6},{4,1},{5,0},{6,3},{7,2},{8,13},{9,12},{10,... | collective-permute-start | bytes 172040 | tf_op jit(solution)/shard_map/ppermute | solution.py:12
  17.4 2.4 %collective-permute-start.5 = (bf16[4,4,1792]{2,1,0:T(4,128)(2,1)S(1)}, bf16[4,4,1792]{2,1,0:T(4,128)(2,1)S(1)}, u32[]{:S(2)}, u32[]{:S(2)}) collective-permute-start(bf16[4,4,1792]{2,1,0:T(4,128)(2,1)S(1)} %pad_maximum_fusion.3), channel_id=1, source_target_pairs={{0,6},{1,7},{2,4},{3,5},{4,2},{5,3},{6,0},{7,1},{8,14},{9,15},{10,... | collective-permute-start | bytes 172040 | tf_op jit(solution)/shard_map/ppermute | solution.py:12
  20.5 1.3 %collective-permute-start.3 = (bf16[4,4,1792]{2,1,0:T(4,128)(2,1)S(1)}, bf16[4,4,1792]{2,1,0:T(4,128)(2,1)S(1)}, u32[]{:S(2)}, u32[]{:S(2)}) collective-permute-start(bf16[4,4,1792]{2,1,0:T(4,128)(2,1)S(1)} %pad_maximum_fusion.3), channel_id=1, source_target_pairs={{0,2},{1,3},{2,0},{3,1},{4,6},{5,7},{6,4},{7,5},{8,10},{9,11},{10,... | collective-permute-start | bytes 172040 | tf_op jit(solution)/shard_map/ppermute | solution.py:12
  22.6 1.6 %collective-permute-done.4 = bf16[4,4,1792]{2,1,0:T(4,128)(2,1)S(1)} collective-permute-done((bf16[4,4,1792]{2,1,0:T(4,128)(2,1)S(1)}, bf16[4,4,1792]{2,1,0:T(4,128)(2,1)S(1)}, u32[]{:S(2)}, u32[]{:S(2)}) %collective-permute-start.4) | collective-permute-done | bytes 57376 | tf_op jit(solution)/shard_map/ppermute | solution.py:12
  25.1 0.9 %copy-done.2 = bf16[1,3584,128]{2,1,0:T(8,128)(2,1)S(1)} copy-done((bf16[1,3584,128]{2,1,0:T(8,128)(2,1)S(1)}, bf16[1,3584,128]{2,1,0:T(8,128)(2,1)}, u32[]{:S(2)}) %copy-start.2) | copy-done | bytes 917528
  29.1 1.3 %collective-permute-start.11 = (bf16[8,1920]{1,0:T(8,128)(2,1)S(1)}, bf16[8,1920]{1,0:T(8,128)(2,1)S(1)}, u32[]{:S(2)}, u32[]{:S(2)}) collective-permute-start(bf16[8,1920]{1,0:T(8,128)(2,1)S(1)} %get-tuple-element.49), channel_id=1, source_target_pairs={{0,2},{1,3},{2,0},{3,1},{4,6},{5,7},{6,4},{7,5},{8,10},{9,11},{10,... | collective-permute-start | bytes 92168 | tf_op jit(solution)/shard_map/ppermute | solution.py:12
  30.3 0.9 %collective-permute-start.13 = (bf16[8,1920]{1,0:T(8,128)(2,1)S(1)}, bf16[8,1920]{1,0:T(8,128)(2,1)S(1)}, u32[]{:S(2)}, u32[]{:S(2)}) collective-permute-start(bf16[8,1920]{1,0:T(8,128)(2,1)S(1)} %get-tuple-element.51), channel_id=1, source_target_pairs={{0,4},{1,5},{2,6},{3,7},{4,0},{5,1},{6,2},{7,3},{8,12},{9,13},{10,... | collective-permute-start | bytes 92168 | tf_op jit(solution)/shard_map/ppermute | solution.py:12
  31.3 1.4 %collective-permute-start.14 = (bf16[8,1920]{1,0:T(8,128)(2,1)S(1)}, bf16[8,1920]{1,0:T(8,128)(2,1)S(1)}, u32[]{:S(2)}, u32[]{:S(2)}) collective-permute-start(bf16[8,1920]{1,0:T(8,128)(2,1)S(1)} %get-tuple-element.52), channel_id=1, source_target_pairs={{0,5},{1,4},{2,7},{3,6},{4,1},{5,0},{6,3},{7,2},{8,13},{9,12},{10,... | collective-permute-start | bytes 92168 | tf_op jit(solution)/shard_map/ppermute | solution.py:12
  32.7 1.5 %collective-permute-start.15 = (bf16[8,1920]{1,0:T(8,128)(2,1)S(1)}, bf16[8,1920]{1,0:T(8,128)(2,1)S(1)}, u32[]{:S(2)}, u32[]{:S(2)}) collective-permute-start(bf16[8,1920]{1,0:T(8,128)(2,1)S(1)} %get-tuple-element.45), channel_id=1, source_target_pairs={{0,6},{1,7},{2,4},{3,5},{4,2},{5,3},{6,0},{7,1},{8,14},{9,15},{10,... | collective-permute-start | bytes 92168 | tf_op jit(solution)/shard_map/ppermute | solution.py:12
  34.9 0.9 %collective-permute-start.10 = (bf16[8,1920]{1,0:T(8,128)(2,1)S(1)}, bf16[8,1920]{1,0:T(8,128)(2,1)S(1)}, u32[]{:S(2)}, u32[]{:S(2)}) collective-permute-start(bf16[8,1920]{1,0:T(8,128)(2,1)S(1)} %pad_maximum_fusion.4), channel_id=1, source_target_pairs={{0,1},{1,0},{2,3},{3,2},{4,5},{5,4},{6,7},{7,6},{8,9},{9,8},{10,11... | collective-permute-start | bytes 92168 | tf_op jit(solution)/shard_map/ppermute | solution.py:12
  36.0 1.5 %collective-permute-done.15 = bf16[8,1920]{1,0:T(8,128)(2,1)S(1)} collective-permute-done((bf16[8,1920]{1,0:T(8,128)(2,1)S(1)}, bf16[8,1920]{1,0:T(8,128)(2,1)S(1)}, u32[]{:S(2)}, u32[]{:S(2)}) %collective-permute-start.15) | collective-permute-done | bytes 30752 | tf_op jit(solution)/shard_map/ppermute | solution.py:12
  37.5 1.1 %collective-permute-done.16 = bf16[8,1920]{1,0:T(8,128)(2,1)S(1)} collective-permute-done((bf16[8,1920]{1,0:T(8,128)(2,1)S(1)}, bf16[8,1920]{1,0:T(8,128)(2,1)S(1)}, u32[]{:S(2)}, u32[]{:S(2)}) %collective-permute-start.16) | collective-permute-done | bytes 30752 | tf_op jit(solution)/shard_map/ppermute | solution.py:12
  39.5 0.8 %collective-permute-start.17 = (bf16[2,1920]{1,0:T(2,128)(2,1)S(1)}, bf16[2,1920]{1,0:T(2,128)(2,1)S(1)}, u32[]{:S(2)}, u32[]{:S(2)}) collective-permute-start(bf16[2,1920]{1,0:T(2,128)(2,1)S(1)} %get-tuple-element.39), channel_id=1, source_target_pairs={{0,8},{8,0},{16,24},{24,16},{1,9},{9,1},{17,25},{25,17},{2,10},{10... | collective-permute-start | bytes 23048 | tf_op jit(solution)/shard_map/ppermute | solution.py:12
  40.3 0.9 %collective-permute-start.19 = (bf16[2,1920]{1,0:T(2,128)(2,1)S(1)}, bf16[2,1920]{1,0:T(2,128)(2,1)S(1)}, u32[]{:S(2)}, u32[]{:S(2)}) collective-permute-start(bf16[2,1920]{1,0:T(2,128)(2,1)S(1)} %get-tuple-element.40), channel_id=1, source_target_pairs={{0,24},{8,16},{16,8},{24,0},{1,25},{9,17},{17,9},{25,1},{2,26},{10... | collective-permute-start | bytes 23048 | tf_op jit(solution)/shard_map/ppermute | solution.py:12
  41.2 1.9 %collective-permute-start.18 = (bf16[2,1920]{1,0:T(2,128)(2,1)S(1)}, bf16[2,1920]{1,0:T(2,128)(2,1)S(1)}, u32[]{:S(2)}, u32[]{:S(2)}) collective-permute-start(bf16[2,1920]{1,0:T(2,128)(2,1)S(1)} %get-tuple-element.41), channel_id=1, source_target_pairs={{0,16},{8,24},{16,0},{24,8},{1,17},{9,25},{17,1},{25,9},{2,18},{10... | collective-permute-start | bytes 23048 | tf_op jit(solution)/shard_map/ppermute | solution.py:12
  43.2 2.5 %collective-permute-done.19 = bf16[2,1920]{1,0:T(2,128)(2,1)S(1)} collective-permute-done((bf16[2,1920]{1,0:T(2,128)(2,1)S(1)}, bf16[2,1920]{1,0:T(2,128)(2,1)S(1)}, u32[]{:S(2)}, u32[]{:S(2)}) %collective-permute-start.19) | collective-permute-done | bytes 7712 | tf_op jit(solution)/shard_map/ppermute | solution.py:12
  46.7 0.7 %slice.305 = bf16[64,1792]{1,0:T(8,128)(2,1)} slice(f32[64,1920]{1,0:T(8,128)S(1)} %fusion.21), slice={[0:64], [0:1792]} | slice | bytes 458752 | tf_op jit(solution)/shard_map/slice | solution.py:113
  (106 shorter events, 9.9 us)
Async XLA Ops:
  0.6 38.5 %copy-start = (bf16[1,128,4096]{2,1,0:T(8,128)(2,1)S(1)}, bf16[1,128,4096]{2,1,0:T(8,128)(2,1)}, u32[]{:S(2)}) copy-start(bf16[1,128,4096]{2,1,0:T(8,128)(2,1)} %param.21) | copy-start | bytes 3145732
  0.6 2.8 %copy-start.5 = (bf16[64,1792]{1,0:T(8,128)(2,1)S(1)}, bf16[64,1792]{1,0:T(8,128)(2,1)}, u32[]{:S(2)}) copy-start(bf16[64,1792]{1,0:T(8,128)(2,1)} %param.11) | copy-start | bytes 688132
  3.7 5.7 %collective-permute-start = (bf16[4,1792]{1,0:T(4,128)(2,1)S(1)}, bf16[4,1792]{1,0:T(4,128)(2,1)S(1)}, u32[]{:S(2)}, u32[]{:S(2)}) collective-permute-start(bf16[4,1792]{1,0:T(4,128)(2,1)S(1)} %get-tuple-element.35), channel_id=1, source_target_pairs={{0,8},{8,0},{16,24},{24,16},{1,9},{9,1},{17,25},{25,17},{2,10},{10... | collective-permute-start | bytes 43016 | tf_op jit(solution)/shard_map/ppermute | solution.py:12
  6.8 5.7 %collective-permute-start.2 = (bf16[4,1792]{1,0:T(4,128)(2,1)S(1)}, bf16[4,1792]{1,0:T(4,128)(2,1)S(1)}, u32[]{:S(2)}, u32[]{:S(2)}) collective-permute-start(bf16[4,1792]{1,0:T(4,128)(2,1)S(1)} %get-tuple-element.36), channel_id=1, source_target_pairs={{0,24},{8,16},{16,8},{24,0},{1,25},{9,17},{17,9},{25,1},{2,26},{10... | collective-permute-start | bytes 43016 | tf_op jit(solution)/shard_map/ppermute | solution.py:12
  9.2 4.6 %collective-permute-start.1 = (bf16[4,1792]{1,0:T(4,128)(2,1)S(1)}, bf16[4,1792]{1,0:T(4,128)(2,1)S(1)}, u32[]{:S(2)}, u32[]{:S(2)}) collective-permute-start(bf16[4,1792]{1,0:T(4,128)(2,1)S(1)} %get-tuple-element.37), channel_id=1, source_target_pairs={{0,16},{8,24},{16,0},{24,8},{1,17},{9,25},{17,1},{25,9},{2,18},{10... | collective-permute-start | bytes 43016 | tf_op jit(solution)/shard_map/ppermute | solution.py:12
  14.0 5.9 %collective-permute-start.9 = (bf16[4,4,1792]{2,1,0:T(4,128)(2,1)S(1)}, bf16[4,4,1792]{2,1,0:T(4,128)(2,1)S(1)}, u32[]{:S(2)}, u32[]{:S(2)}) collective-permute-start(bf16[4,4,1792]{2,1,0:T(4,128)(2,1)S(1)} %pad_maximum_fusion.3), channel_id=1, source_target_pairs={{0,7},{1,6},{2,5},{3,4},{4,3},{5,2},{6,1},{7,0},{8,15},{9,14},{10,... | collective-permute-start | bytes 172040 | tf_op jit(solution)/shard_map/ppermute | solution.py:12
  14.5 6.0 %collective-permute-start.8 = (bf16[4,4,1792]{2,1,0:T(4,128)(2,1)S(1)}, bf16[4,4,1792]{2,1,0:T(4,128)(2,1)S(1)}, u32[]{:S(2)}, u32[]{:S(2)}) collective-permute-start(bf16[4,4,1792]{2,1,0:T(4,128)(2,1)S(1)} %pad_maximum_fusion.3), channel_id=1, source_target_pairs={{0,5},{1,4},{2,7},{3,6},{4,1},{5,0},{6,3},{7,2},{8,13},{9,12},{10,... | collective-permute-start | bytes 172040 | tf_op jit(solution)/shard_map/ppermute | solution.py:12
  16.7 5.1 %collective-permute-start.7 = (bf16[4,4,1792]{2,1,0:T(4,128)(2,1)S(1)}, bf16[4,4,1792]{2,1,0:T(4,128)(2,1)S(1)}, u32[]{:S(2)}, u32[]{:S(2)}) collective-permute-start(bf16[4,4,1792]{2,1,0:T(4,128)(2,1)S(1)} %pad_maximum_fusion.3), channel_id=1, source_target_pairs={{0,3},{1,2},{2,1},{3,0},{4,7},{5,6},{6,5},{7,4},{8,11},{9,10},{10,... | collective-permute-start | bytes 172040 | tf_op jit(solution)/shard_map/ppermute | solution.py:12
  16.8 5.0 %collective-permute-start.6 = (bf16[4,4,1792]{2,1,0:T(4,128)(2,1)S(1)}, bf16[4,4,1792]{2,1,0:T(4,128)(2,1)S(1)}, u32[]{:S(2)}, u32[]{:S(2)}) collective-permute-start(bf16[4,4,1792]{2,1,0:T(4,128)(2,1)S(1)} %pad_maximum_fusion.3), channel_id=1, source_target_pairs={{0,1},{1,0},{2,3},{3,2},{4,5},{5,4},{6,7},{7,6},{8,9},{9,8},{10,11... | collective-permute-start | bytes 172040 | tf_op jit(solution)/shard_map/ppermute | solution.py:12
  17.4 5.2 %collective-permute-start.5 = (bf16[4,4,1792]{2,1,0:T(4,128)(2,1)S(1)}, bf16[4,4,1792]{2,1,0:T(4,128)(2,1)S(1)}, u32[]{:S(2)}, u32[]{:S(2)}) collective-permute-start(bf16[4,4,1792]{2,1,0:T(4,128)(2,1)S(1)} %pad_maximum_fusion.3), channel_id=1, source_target_pairs={{0,6},{1,7},{2,4},{3,5},{4,2},{5,3},{6,0},{7,1},{8,14},{9,15},{10,... | collective-permute-start | bytes 172040 | tf_op jit(solution)/shard_map/ppermute | solution.py:12
  19.9 4.2 %collective-permute-start.4 = (bf16[4,4,1792]{2,1,0:T(4,128)(2,1)S(1)}, bf16[4,4,1792]{2,1,0:T(4,128)(2,1)S(1)}, u32[]{:S(2)}, u32[]{:S(2)}) collective-permute-start(bf16[4,4,1792]{2,1,0:T(4,128)(2,1)S(1)} %pad_maximum_fusion.3), channel_id=1, source_target_pairs={{0,4},{1,5},{2,6},{3,7},{4,0},{5,1},{6,2},{7,3},{8,12},{9,13},{10,... | collective-permute-start | bytes 172040 | tf_op jit(solution)/shard_map/ppermute | solution.py:12
  20.5 4.2 %collective-permute-start.3 = (bf16[4,4,1792]{2,1,0:T(4,128)(2,1)S(1)}, bf16[4,4,1792]{2,1,0:T(4,128)(2,1)S(1)}, u32[]{:S(2)}, u32[]{:S(2)}) collective-permute-start(bf16[4,4,1792]{2,1,0:T(4,128)(2,1)S(1)} %pad_maximum_fusion.3), channel_id=1, source_target_pairs={{0,2},{1,3},{2,0},{3,1},{4,6},{5,7},{6,4},{7,5},{8,10},{9,11},{10,... | collective-permute-start | bytes 172040 | tf_op jit(solution)/shard_map/ppermute | solution.py:12
  25.0 1.3 %copy-start.1 = (bf16[1,3584,128]{2,1,0:T(8,128)(2,1)S(1)}, bf16[1,3584,128]{2,1,0:T(8,128)(2,1)}, u32[]{:S(2)}) copy-start(bf16[1,3584,128]{2,1,0:T(8,128)(2,1)} %param.17) | copy-start | bytes 2752516
  28.9 6.8 %copy-start.4 = (bf16[1,64,3584]{2,1,0:T(8,128)(2,1)S(1)}, bf16[1,64,3584]{2,1,0:T(8,128)(2,1)}, u32[]{:S(2)}) copy-start(bf16[1,64,3584]{2,1,0:T(8,128)(2,1)} %param.20) | copy-start | bytes 1376260
  29.1 5.1 %collective-permute-start.11 = (bf16[8,1920]{1,0:T(8,128)(2,1)S(1)}, bf16[8,1920]{1,0:T(8,128)(2,1)S(1)}, u32[]{:S(2)}, u32[]{:S(2)}) collective-permute-start(bf16[8,1920]{1,0:T(8,128)(2,1)S(1)} %get-tuple-element.49), channel_id=1, source_target_pairs={{0,2},{1,3},{2,0},{3,1},{4,6},{5,7},{6,4},{7,5},{8,10},{9,11},{10,... | collective-permute-start | bytes 92168 | tf_op jit(solution)/shard_map/ppermute | solution.py:12
  30.3 4.6 %collective-permute-start.12 = (bf16[8,1920]{1,0:T(8,128)(2,1)S(1)}, bf16[8,1920]{1,0:T(8,128)(2,1)S(1)}, u32[]{:S(2)}, u32[]{:S(2)}) collective-permute-start(bf16[8,1920]{1,0:T(8,128)(2,1)S(1)} %get-tuple-element.50), channel_id=1, source_target_pairs={{0,3},{1,2},{2,1},{3,0},{4,7},{5,6},{6,5},{7,4},{8,11},{9,10},{10,... | collective-permute-start | bytes 92168 | tf_op jit(solution)/shard_map/ppermute | solution.py:12
  30.3 5.6 %collective-permute-start.13 = (bf16[8,1920]{1,0:T(8,128)(2,1)S(1)}, bf16[8,1920]{1,0:T(8,128)(2,1)S(1)}, u32[]{:S(2)}, u32[]{:S(2)}) collective-permute-start(bf16[8,1920]{1,0:T(8,128)(2,1)S(1)} %get-tuple-element.51), channel_id=1, source_target_pairs={{0,4},{1,5},{2,6},{3,7},{4,0},{5,1},{6,2},{7,3},{8,12},{9,13},{10,... | collective-permute-start | bytes 92168 | tf_op jit(solution)/shard_map/ppermute | solution.py:12
  31.3 4.7 %collective-permute-start.14 = (bf16[8,1920]{1,0:T(8,128)(2,1)S(1)}, bf16[8,1920]{1,0:T(8,128)(2,1)S(1)}, u32[]{:S(2)}, u32[]{:S(2)}) collective-permute-start(bf16[8,1920]{1,0:T(8,128)(2,1)S(1)} %get-tuple-element.52), channel_id=1, source_target_pairs={{0,5},{1,4},{2,7},{3,6},{4,1},{5,0},{6,3},{7,2},{8,13},{9,12},{10,... | collective-permute-start | bytes 92168 | tf_op jit(solution)/shard_map/ppermute | solution.py:12
  32.7 4.8 %collective-permute-start.15 = (bf16[8,1920]{1,0:T(8,128)(2,1)S(1)}, bf16[8,1920]{1,0:T(8,128)(2,1)S(1)}, u32[]{:S(2)}, u32[]{:S(2)}) collective-permute-start(bf16[8,1920]{1,0:T(8,128)(2,1)S(1)} %get-tuple-element.45), channel_id=1, source_target_pairs={{0,6},{1,7},{2,4},{3,5},{4,2},{5,3},{6,0},{7,1},{8,14},{9,15},{10,... | collective-permute-start | bytes 92168 | tf_op jit(solution)/shard_map/ppermute | solution.py:12
  34.2 4.4 %collective-permute-start.16 = (bf16[8,1920]{1,0:T(8,128)(2,1)S(1)}, bf16[8,1920]{1,0:T(8,128)(2,1)S(1)}, u32[]{:S(2)}, u32[]{:S(2)}) collective-permute-start(bf16[8,1920]{1,0:T(8,128)(2,1)S(1)} %get-tuple-element.46), channel_id=1, source_target_pairs={{0,7},{1,6},{2,5},{3,4},{4,3},{5,2},{6,1},{7,0},{8,15},{9,14},{10,... | collective-permute-start | bytes 92168 | tf_op jit(solution)/shard_map/ppermute | solution.py:12
  34.9 3.7 %collective-permute-start.10 = (bf16[8,1920]{1,0:T(8,128)(2,1)S(1)}, bf16[8,1920]{1,0:T(8,128)(2,1)S(1)}, u32[]{:S(2)}, u32[]{:S(2)}) collective-permute-start(bf16[8,1920]{1,0:T(8,128)(2,1)S(1)} %pad_maximum_fusion.4), channel_id=1, source_target_pairs={{0,1},{1,0},{2,3},{3,2},{4,5},{5,4},{6,7},{7,6},{8,9},{9,8},{10,11... | collective-permute-start | bytes 92168 | tf_op jit(solution)/shard_map/ppermute | solution.py:12
  39.5 3.7 %collective-permute-start.17 = (bf16[2,1920]{1,0:T(2,128)(2,1)S(1)}, bf16[2,1920]{1,0:T(2,128)(2,1)S(1)}, u32[]{:S(2)}, u32[]{:S(2)}) collective-permute-start(bf16[2,1920]{1,0:T(2,128)(2,1)S(1)} %get-tuple-element.39), channel_id=1, source_target_pairs={{0,8},{8,0},{16,24},{24,16},{1,9},{9,1},{17,25},{25,17},{2,10},{10... | collective-permute-start | bytes 23048 | tf_op jit(solution)/shard_map/ppermute | solution.py:12
  40.3 5.4 %collective-permute-start.19 = (bf16[2,1920]{1,0:T(2,128)(2,1)S(1)}, bf16[2,1920]{1,0:T(2,128)(2,1)S(1)}, u32[]{:S(2)}, u32[]{:S(2)}) collective-permute-start(bf16[2,1920]{1,0:T(2,128)(2,1)S(1)} %get-tuple-element.40), channel_id=1, source_target_pairs={{0,24},{8,16},{16,8},{24,0},{1,25},{9,17},{17,9},{25,1},{2,26},{10... | collective-permute-start | bytes 23048 | tf_op jit(solution)/shard_map/ppermute | solution.py:12
  41.2 4.6 %collective-permute-start.18 = (bf16[2,1920]{1,0:T(2,128)(2,1)S(1)}, bf16[2,1920]{1,0:T(2,128)(2,1)S(1)}, u32[]{:S(2)}, u32[]{:S(2)}) collective-permute-start(bf16[2,1920]{1,0:T(2,128)(2,1)S(1)} %get-tuple-element.41), channel_id=1, source_target_pairs={{0,16},{8,24},{16,0},{24,8},{1,17},{9,25},{17,1},{25,9},{2,18},{10... | collective-permute-start | bytes 23048 | tf_op jit(solution)/shard_map/ppermute | solution.py:12
  (3 other events, 3.1 us)

commit v2 on v1

v2 whole, which is shorter than its diff:
```python
import functools

import jax
import jax.numpy as jnp
from jax import lax
from jax.experimental import pallas as pl
from jax.experimental.pallas import tpu as pltpu
from jax.sharding import PartitionSpec as P

CAP = 2
KINDS = 4
BF16 = jnp.bfloat16
F32 = jnp.float32


def send_rel(block, axis, offset):
    size = lax.axis_size(axis)
    return lax.ppermute(block, axis, [(i, i ^ offset) for i in range(size)])


def dot_f32(a, b, contract):
    return lax.dot_general(a, b, (contract, ((), ())), preferred_element_type=F32)


def whole_vmem(count):
    return [pl.BlockSpec(memory_space=pltpu.VMEM)] * count


def in_hbm(count):
    return [pl.BlockSpec(memory_space=pltpu.HBM)] * count


def start_copies(pairs, sems):
    copies = [
        pltpu.make_async_copy(source, target, sems.at[index])
        for index, (source, target) in enumerate(pairs)
    ]
    for copy in copies:
        copy.start()
    return copies


def limit(rows):
    return pltpu.CompilerParams(vmem_limit_bytes=(8 << 20) + rows * (48 << 10))


def hit_tables(ids, slots, weights, want, experts):
    live = (slots >= 0) & (ids < experts)
    code = jnp.where(live, ids * CAP + slots, -1)
    hits = jnp.zeros((want.shape[0], ids.shape[1]), F32)
    scaled = hits
    for route in range(ids.shape[0]):
        match = code[route : route + 1, :] == want
        hits = jnp.where(match, 1.0, hits)
        scaled = jnp.where(match, weights[route : route + 1, :], scaled)
    return hits, scaled


def select_kernel(experts, *refs):
    sources, outs = refs[:5], refs[5 : 6 + experts]
    ids, slots, weight, tok, grad, sems = refs[6 + experts :]
    hit_ref, out_refs = outs[0], outs[1:]
    copies = start_copies(zip(sources, (ids, slots, weight, tok, grad)), sems)
    here = lax.axis_index("expert")
    unit = KINDS * CAP
    quarter = tok.shape[1] // 2
    row = lax.broadcasted_iota(jnp.int32, (experts * unit, 1), 0)
    kind = (row % unit) // CAP
    want = ((row // unit) ^ here) * CAP + row % CAP
    for copy in copies[:3]:
        copy.wait()
    hits, scaled = hit_tables(ids[...], slots[...], weight[...].astype(F32), want, experts)
    hit_ref[...] = hits
    total = None
    for index in range(KINDS):
        table, source = (hits, tok) if index < 2 else (scaled, grad)
        if index % 2 == 0:
            copies[3 + index // 2].wait()
        left = jnp.where(kind == index, table, 0.0).astype(BF16)
        first = (index % 2) * quarter
        part = dot_f32(left, source[:, first : first + quarter], ((1,), (0,)))
        total = part if total is None else total + part
    total = total.astype(BF16)
    for k in range(experts):
        out_refs[k][...] = total[k * unit : (k + 1) * unit]


def load_kernel(*refs):
    count = (len(refs) - 2) // 2
    for copy in start_copies(zip(refs[1 : 1 + count], refs[1 + count : -1]), refs[-1]):
        copy.wait()


def split_two(value):
    high = value.astype(BF16)
    return jnp.concatenate([high, (value - high.astype(F32)).astype(BF16)], axis=1)


def join_two(value):
    value = value.astype(F32)
    middle = value.shape[1] // 2
    return value[:, :middle] + value[:, middle:]


def expert_kernel(
    own_ref, other_ref, gate_w, up_w, down_w, proj_ref, keep_ref, send_ref, mine_ref, x_in, x_grad
):
    rows, width = x_in.shape
    half, quarter = width // 2, width // 4
    core = lax.axis_index("test")
    sides = (
        (own_ref, keep_ref, pl.multiple_of(core * half, 128)),
        (other_ref, send_ref, pl.multiple_of((1 - core) * half, 128)),
    )
    for source, _, base in sides:
        for index in range(KINDS):
            target = x_in if index < 2 else x_grad
            start = pl.multiple_of(base + (index % 2) * quarter, 128)
            target[:, pl.ds(start, quarter)] = source[index * rows : (index + 1) * rows]
    mine_ref[...] = x_grad[: mine_ref.shape[0]]
    gate_pre = dot_f32(x_in[...], gate_w[...], ((1,), (0,)))
    up_pre = dot_f32(x_in[...], up_w[...], ((1,), (0,)))
    hid_grad = dot_f32(x_grad[...], down_w[...], ((1,), (1,)))
    sig = 1.0 / (1.0 + jnp.exp(-gate_pre))
    act_gate = gate_pre * sig
    hidden = (act_gate * up_pre).astype(BF16)
    tail = split_two(dot_f32(hidden, proj_ref[...], ((1,), (1,))))
    up_grad = (hid_grad * act_gate).astype(BF16)
    gate_grad = (hid_grad * up_pre * sig * (1.0 + gate_pre * (1.0 - sig))).astype(BF16)
    for _, target, base in sides:
        target[:, half:] = tail
        for index in range(2):
            start = pl.multiple_of(base + index * quarter, 128)
            part = dot_f32(gate_grad, gate_w[pl.ds(start, quarter), :], ((1,), (1,)))
            part += dot_f32(up_grad, up_w[pl.ds(start, quarter), :], ((1,), (1,)))
            target[:, index * quarter : (index + 1) * quarter] = part.astype(BF16)


def pair_kernel(half, keep_ref, got_ref, *out_refs):
    kept, got = keep_ref[...].astype(F32), got_ref[...].astype(F32)
    main = (kept[:, :half] + got[:, :half]).astype(BF16)
    tail = split_two(join_two(kept[:, half:]) + join_two(got[:, half:]))
    rows = out_refs[0].shape[0]
    for g, out_ref in enumerate(out_refs):
        out_ref[:, :half] = main[g * rows : (g + 1) * rows]
        out_ref[:, half:] = tail[g * rows : (g + 1) * rows]


def score_kernel(half, *refs):
    *piece_refs, grad_ref, test_ref, out_ref, feature = refs
    total = piece_refs[0][...].astype(F32)
    for piece_ref in piece_refs[1:]:
        total = total + piece_ref[...].astype(F32)
    hid = join_two(total[:, half:])
    grad = grad_ref[...]
    proj = grad.shape[1]
    for p in range(proj):
        feature[:, p * proj : (p + 1) * proj] = (hid[:, p : p + 1] * grad).astype(BF16)
    out_ref[:, :half] = total[:, :half].astype(BF16)
    out_ref[:, half:] = dot_f32(feature[...], test_ref[...], ((1,), (1,))).astype(BF16)


def finish_kernel(hit_ref, home_ref, in_grad_ref, scores_ref):
    pairs, unit = home_ref.shape[0], KINDS * CAP
    hits = jnp.concatenate(
        [hit_ref[k * unit : k * unit + CAP] for k in range(pairs // CAP)], axis=0
    )
    half = in_grad_ref.shape[1]
    hits = hits.T.astype(BF16)
    in_grad_ref[...] = dot_f32(hits, home_ref[:, :half], ((1,), (0,))).astype(BF16)
    scores_ref[...] = dot_f32(hits, home_ref[:, half:], ((1,), (0,)))


def on_device(
    tokens,
    out_grad,
    route_ids,
    route_slots,
    route_weight,
    w_gate,
    w_up,
    w_down,
    proj_hidden,
    proj_grad,
    test_feats,
):
    experts = lax.axis_size("expert")
    groups = lax.axis_size("dp")
    tok_rows, half = tokens.shape
    quarter = half // 2
    width = half * lax.axis_size("test")
    proj, tests = proj_hidden.shape[1], test_feats.shape[1]
    pairs = experts * CAP
    rows = groups * pairs
    unit = KINDS * CAP
    out_width = half + 2 * proj
    ids_t, slots_t, weight_t = route_ids.T, route_slots.T, route_weight.T

    with jax.named_scope("select"):
        hits, *picked = pl.pallas_call(
            functools.partial(select_kernel, experts),
            out_shape=[jax.ShapeDtypeStruct((experts * unit, tok_rows), F32)]
            + [jax.ShapeDtypeStruct((unit, quarter), BF16)] * experts,
            in_specs=in_hbm(5),
            out_specs=whole_vmem(experts + 1),
            scratch_shapes=[
                pltpu.VMEM(x.shape, x.dtype) for x in (ids_t, slots_t, weight_t, tokens, out_grad)
            ]
            + [pltpu.SemaphoreType.DMA((5,))],
            compiler_params=limit(rows),
        )(ids_t, slots_t, weight_t, tokens, out_grad)
    params = [w_gate[0], w_up[0], w_down[0], proj_hidden[0], proj_grad[0], test_feats[0]]
    with jax.named_scope("load"):
        gate_w, up_w, down_w, hid_proj, grad_proj, test_rows = pl.pallas_call(
            load_kernel,
            out_shape=[jax.ShapeDtypeStruct(x.shape, x.dtype) for x in params],
            in_specs=whole_vmem(1) + in_hbm(len(params)),
            out_specs=whole_vmem(len(params)),
            scratch_shapes=[pltpu.SemaphoreType.DMA((len(params),))],
            compiler_params=limit(rows),
            cost_estimate=pl.CostEstimate(
                flops=0, bytes_accessed=sum(2 * x.size for x in params), transcendentals=0
            ),
        )(picked[0], *params)
    arrived = [picked[0]] + [send_rel(picked[k], "expert", k) for k in range(1, experts)]
    block = jnp.stack(arrived).reshape(experts, KINDS, CAP, quarter)
    block = block.transpose(1, 0, 2, 3).reshape(KINDS, pairs, quarter)
    blocks = [block] + [send_rel(block, "dp", g) for g in range(1, groups)]
    own = jnp.stack(blocks, axis=1).reshape(KINDS * rows, quarter)
    other = send_rel(own, "test", 1)

    with jax.named_scope("expert"):
        keep, send, mine = pl.pallas_call(
            expert_kernel,
            out_shape=[
                jax.ShapeDtypeStruct((rows, out_width), BF16),
                jax.ShapeDtypeStruct((rows, out_width), BF16),
                jax.ShapeDtypeStruct((pairs, width), BF16),
            ],
            in_specs=whole_vmem(6),
            out_specs=whole_vmem(3),
            scratch_shapes=[pltpu.VMEM((rows, width), BF16)] * 2,
            compiler_params=limit(rows),
        )(own, other, gate_w, up_w, down_w, hid_proj)
    got = send_rel(send, "test", 1)
    with jax.named_scope("pair"):
        sums = pl.pallas_call(
            functools.partial(pair_kernel, half),
            out_shape=[jax.ShapeDtypeStruct((pairs, out_width), BF16)] * groups,
            in_specs=whole_vmem(2),
            out_specs=whole_vmem(groups),
            compiler_params=limit(rows),
        )(keep, got)
    pieces = [sums[0]] + [send_rel(sums[g], "dp", g) for g in range(1, groups)]
    grad_mine = dot_f32(mine, grad_proj, ((1,), (1,)))
    with jax.named_scope("score"):
        back = pl.pallas_call(
            functools.partial(score_kernel, half),
            out_shape=jax.ShapeDtypeStruct((pairs, half + tests), BF16),
            in_specs=whole_vmem(groups + 2),
            out_specs=whole_vmem(1)[0],
            scratch_shapes=[pltpu.VMEM((pairs, proj * proj), BF16)],
            compiler_params=limit(rows),
        )(*pieces, grad_mine, test_rows)
    back = back.reshape(experts, CAP, half + tests)
    home = [back[0]] + [send_rel(back[k], "expert", k) for k in range(1, experts)]
    home = jnp.concatenate(home, axis=0)
    with jax.named_scope("finish"):
        return pl.pallas_call(
            finish_kernel,
            out_shape=[
                jax.ShapeDtypeStruct((tok_rows, half), BF16),
                jax.ShapeDtypeStruct((tok_rows, tests), F32),
            ],
            in_specs=whole_vmem(2),
            out_specs=whole_vmem(2),
            compiler_params=limit(rows),
        )(hits, home)


def solution(mesh):
    placed = (
        P(("expert", "dp"), "test"),
        P(("expert", "dp"), "test"),
        P(("expert", "dp"), None),
        P(("expert", "dp"), None),
        P(("expert", "dp"), None),
        P("expert", None, ("dp", "test")),
        P("expert", None, ("dp", "test")),
        P("expert", ("dp", "test"), None),
        P("expert", None, ("dp", "test")),
        P("expert", None, None),
        P("expert", "test", None),
    )
    return jax.shard_map(
        on_device,
        mesh=mesh,
        in_specs=placed,
        out_specs=(P(("expert", "dp"), "test"), P(("expert", "dp"), "test")),
        check_vma=False,
    )
```

time: 47.8 us -> 47.9 us (level)
  starting transfers between devices: 23.5 us -> 17.3 us
  Pallas kernels: 0 us -> 5.44 us
  local copies, waits for them, and re-layouts: 4.3 us -> 8.32 us
  matrix products: 3.89 us -> 0.2 us
  waiting for transfers between devices: 12.4 us -> 15.2 us
  other arithmetic: 2.26 us -> 0.18 us
    ppermute x20 -> x14, starting transfers between devices: 23.5 us -> 17.3 us  [send_rel(): return lax.ppermute(block, axis, [(i, i ^ offset) for i in range(size)])]
    unnamed x26 -> x22, local copies, waits for them, and re-layouts: 2.06 us -> 8.13 us
    pallas_call x0 -> x6, Pallas kernels: none -> 5.44 us  [the longest x1 1.77 us: on_device(): pl.pallas_call(expert_kernel, out_shape=[jax.ShapeDtypeStruct((rows, out_...]
    dot_general x11 -> x1, matrix products: 3.89 us -> 0.2 us  [dot_f32(): lax.dot_general(a, b, (contract, ((), ())), preferred_element_type=F32)]
    ppermute x20 -> x14, waiting for transfers between devices: 12.4 us -> 15.2 us  [send_rel(): return lax.ppermute(block, axis, [(i, i ^ offset) for i in range(size)])]
    slice x13 -> x1, local copies, waits for them, and re-layouts: 1.71 us -> 0.04 us  [on_device(): back[0]]
    convert_element_type x2 -> x0, other arithmetic: 0.95 us -> none  [the longest x1 0.82 us: pick_rows(): weights_in.astype(jnp.float32)[None]]
    select_n x3 -> x0, other arithmetic: 0.77 us -> none  [the longest x1 0.71 us: pick_rows(): slot_code = jnp.where(live_mask, ids_in * CAP + slots_in, -1)]
  transfers between devices with their start and end apart: 20 -> 14, of which waited for: 10 -> 11; matrix products, arithmetic and copies ran while one was open for 2% -> 1% of each run, Pallas kernels for 0% -> 2%
where the time goes in v2:
time: 47.9 us; the launch traced here: 47.5 us
  starting transfers between devices  17.3 us (36%)
  waiting for transfers between devices  15.2 us (32%)
  local copies, waits for them, and re-layouts  8.32 us (17%)
  Pallas kernels  5.44 us (11%)
  between operations  0.79 us (2%)
    ppermute x14, starting transfers between devices, send_rel(): return lax.ppermute(block, axis, [(i, i ^ offset) for i in range(size)])  17.3 us
    ppermute x14, waiting for transfers between devices, send_rel(): return lax.ppermute(block, axis, [(i, i ^ offset) for i in range(size)])  15.2 us
    unnamed x22, local copies, waits for them, and re-layouts  8.13 us
    pallas_call x1, Pallas kernels, on_device(): pl.pallas_call(expert_kernel, out_shape=[jax.ShapeDtypeStruct((rows, out_...  1.77 us
    pallas_call x1, Pallas kernels, on_device(): pl.pallas_call(load_kernel, out_shape=[jax.ShapeDtypeStruct(x.shape, x.dt...  1.09 us
  transfers between devices with their start and end apart: 14, of which 11 were waited for; matrix products, arithmetic and copies ran while one was open for 1% of the time, Pallas kernels for 2%

profile of v2, /device:TPU:0, one launch (start us, length us, event | category | flops | bytes accessed | tf_op | source)
XLA Modules:
  0.0 47.5 jit_solution(2379421931931448008)
XLA Ops:
  0.7 1.0 %copy-done.5 = bf16[64,1792]{1,0:T(8,128)(2,1)S(1)} copy-done((bf16[64,1792]{1,0:T(8,128)(2,1)S(1)}, bf16[64,1792]{1,0:T(8,128)(2,1)}, u32[]{:S(2)}) %copy-start.5) | copy-done | bytes 229400
  1.7 0.9 %copy-done.6 = bf16[64,1792]{1,0:T(8,128)(2,1)S(1)} copy-done((bf16[64,1792]{1,0:T(8,128)(2,1)S(1)}, bf16[64,1792]{1,0:T(8,128)(2,1)}, u32[]{:S(2)}) %copy-start.6) | copy-done | bytes 229400
  2.6 0.7 %copy-done.8 = s32[64,8]{0,1:T(8,128)S(1)} copy-done((s32[64,8]{0,1:T(8,128)S(1)}, s32[64,8]{0,1:T(8,128)}, u32[]{:S(2)}) %copy-start.8) | copy-done | bytes 2072
  3.3 0.7 %copy-done.9 = s32[64,8]{0,1:T(8,128)S(1)} copy-done((s32[64,8]{0,1:T(8,128)S(1)}, s32[64,8]{0,1:T(8,128)}, u32[]{:S(2)}) %copy-start.9) | copy-done | bytes 2072
  4.7 0.9 %select.1 = (f32[32,64]{1,0:T(8,128)S(1)}, bf16[8,896]{1,0:T(8,128)(2,1)S(1)}, bf16[8,896]{1,0:T(8,128)(2,1)S(1)}, bf16[8,896]{1,0:T(8,128)(2,1)S(1)}, bf16[8,896]{1,0:T(8,128)(2,1)S(1)}) custom-call(s32[8,64]{1,0:T(8,128)S(1)} %bitcast.29, s32[8,64]{1,0:T(8,128)S(1)} %bitcast.30, bf16[8,64]{1,0:T(8,128)(2,1)S(1)} %bitcast.31, ...), custom_call_target="tpu_custom_call" | custom-call | tf_op jit(solution)/shard_map/select/pallas_call | solution.py:200
  5.5 3.1 %collective-permute-start = (bf16[8,896]{1,0:T(8,128)(2,1)S(1)}, bf16[8,896]{1,0:T(8,128)(2,1)S(1)}, u32[]{:S(2)}, u32[]{:S(2)}) collective-permute-start(bf16[8,896]{1,0:T(8,128)(2,1)S(1)} %get-tuple-element.22), channel_id=1, source_target_pairs={{0,8},{8,0},{16,24},{24,16},{1,9},{9,1},{17,25},{25,17},{2,10},{10... | collective-permute-start | bytes 43016 | tf_op jit(solution)/shard_map/ppermute | solution.py:18
  8.6 2.6 %collective-permute-start.1 = (bf16[8,896]{1,0:T(8,128)(2,1)S(1)}, bf16[8,896]{1,0:T(8,128)(2,1)S(1)}, u32[]{:S(2)}, u32[]{:S(2)}) collective-permute-start(bf16[8,896]{1,0:T(8,128)(2,1)S(1)} %get-tuple-element.23), channel_id=1, source_target_pairs={{0,16},{8,24},{16,0},{24,8},{1,17},{9,25},{17,1},{25,9},{2,18},{10... | collective-permute-start | bytes 43016 | tf_op jit(solution)/shard_map/ppermute | solution.py:18
  11.3 2.0 %collective-permute-done.1 = bf16[8,896]{1,0:T(8,128)(2,1)S(1)} collective-permute-done((bf16[8,896]{1,0:T(8,128)(2,1)S(1)}, bf16[8,896]{1,0:T(8,128)(2,1)S(1)}, u32[]{:S(2)}, u32[]{:S(2)}) %collective-permute-start.1) | collective-permute-done | bytes 14368 | tf_op jit(solution)/shard_map/ppermute | solution.py:18
  13.3 3.4 %collective-permute-done.2 = bf16[8,896]{1,0:T(8,128)(2,1)S(1)} collective-permute-done((bf16[8,896]{1,0:T(8,128)(2,1)S(1)}, bf16[8,896]{1,0:T(8,128)(2,1)S(1)}, u32[]{:S(2)}, u32[]{:S(2)}) %collective-permute-start.2) | collective-permute-done | bytes 14368 | tf_op jit(solution)/shard_map/ppermute | solution.py:18
  17.0 2.5 %collective-permute-start.5 = (bf16[4,8,896]{2,1,0:T(8,128)(2,1)S(1)}, bf16[4,8,896]{2,1,0:T(8,128)(2,1)S(1)}, u32[]{:S(2)}, u32[]{:S(2)}) collective-permute-start(bf16[4,8,896]{2,1,0:T(8,128)(2,1)S(1)} %reshape.28), channel_id=1, source_target_pairs={{0,6},{2,4},{4,2},{6,0},{1,7},{3,5},{5,3},{7,1},{8,14},{10,12},{12... | collective-permute-start | bytes 172040 | tf_op jit(solution)/shard_map/ppermute | solution.py:18
  20.5 1.8 %collective-permute-done.5 = bf16[4,8,896]{2,1,0:T(8,128)(2,1)S(1)} collective-permute-done((bf16[4,8,896]{2,1,0:T(8,128)(2,1)S(1)}, bf16[4,8,896]{2,1,0:T(8,128)(2,1)S(1)}, u32[]{:S(2)}, u32[]{:S(2)}) %collective-permute-start.5) | collective-permute-done | bytes 57376 | tf_op jit(solution)/shard_map/ppermute | solution.py:18
  22.3 1.3 %collective-permute-done.4 = bf16[4,8,896]{2,1,0:T(8,128)(2,1)S(1)} collective-permute-done((bf16[4,8,896]{2,1,0:T(8,128)(2,1)S(1)}, bf16[4,8,896]{2,1,0:T(8,128)(2,1)S(1)}, u32[]{:S(2)}, u32[]{:S(2)}) %collective-permute-start.4) | collective-permute-done | bytes 57376 | tf_op jit(solution)/shard_map/ppermute | solution.py:18
  24.9 1.2 %copy-done.1 = bf16[1,3584,128]{2,1,0:T(8,128)(2,1)S(1)} copy-done((bf16[1,3584,128]{2,1,0:T(8,128)(2,1)S(1)}, bf16[1,3584,128]{2,1,0:T(8,128)(2,1)}, u32[]{:S(2)}) %copy-start.1) | copy-done | bytes 917528
  26.1 1.2 %copy-done.2 = bf16[1,3584,128]{2,1,0:T(8,128)(2,1)S(1)} copy-done((bf16[1,3584,128]{2,1,0:T(8,128)(2,1)S(1)}, bf16[1,3584,128]{2,1,0:T(8,128)(2,1)}, u32[]{:S(2)}) %copy-start.2) | copy-done | bytes 917528
  27.2 1.2 %copy-done.3 = bf16[1,128,3584]{2,1,0:T(8,128)(2,1)S(1)} copy-done((bf16[1,128,3584]{2,1,0:T(8,128)(2,1)S(1)}, bf16[1,128,3584]{2,1,0:T(8,128)(2,1)}, u32[]{:S(2)}) %copy-start.3) | copy-done | bytes 917528
  28.4 1.1 %load.1 = (bf16[3584,128]{1,0:T(8,128)(2,1)S(1)}, bf16[3584,128]{1,0:T(8,128)(2,1)S(1)}, bf16[128,3584]{1,0:T(8,128)(2,1)S(1)}, bf16[64,128]{1,0:T(8,128)(2,1)S(...) custom-call(bf16[8,896]{1,0:T(8,128)(2,1)S(1)} %get-tuple-element.21.refs_0_, ...), custom_call_target="tpu_custom_call" | custom-call | bytes 4276224 | tf_op jit(solution)/shard_map/load/pallas_call | solution.py:214
  29.5 1.8 %expert.1 = (bf16[32,1920]{1,0:T(8,128)(2,1)S(1)}, bf16[32,1920]{1,0:T(8,128)(2,1)S(1)}, bf16[8,3584]{1,0:T(8,128)(2,1)S(1)}) custom-call(bf16[128,896]{1,0:T(8,128)(2,1)S(1)} %bitcast.23, bf16[128,896]{1,0:T(8,128)(2,1)S(1)} %collective-permute-done.6.other_ref, bf16[3584,128]{1,0:T(8,128)(2,1)S(1)} %get-tuple-element.25.gate_w, ...), custom_call_target="tpu_custom_call" | custom-call | tf_op jit(solution)/shard_map/expert/pallas_call | solution.py:233
  31.4 1.3 %collective-permute-done.7.got_ref = bf16[32,1920]{1,0:T(8,128)(2,1)S(1)} collective-permute-done((bf16[32,1920]{1,0:T(8,128)(2,1)S(1)}, bf16[32,1920]{1,0:T(8,128)(2,1)S(1)}, u32[]{:S(2)}, u32[]{:S(2)}) %collective-permute-start.7) | collective-permute-done | bytes 122912 | tf_op jit(solution)/shard_map/ppermute | solution.py:18
  33.4 1.5 %collective-permute-start.9 = (bf16[8,1920]{1,0:T(8,128)(2,1)S(1)}, bf16[8,1920]{1,0:T(8,128)(2,1)S(1)}, u32[]{:S(2)}, u32[]{:S(2)}) collective-permute-start(bf16[8,1920]{1,0:T(8,128)(2,1)S(1)} %get-tuple-element.33), channel_id=1, source_target_pairs={{0,4},{2,6},{4,0},{6,2},{1,5},{3,7},{5,1},{7,3},{8,12},{10,14},{12... | collective-permute-start | bytes 92168 | tf_op jit(solution)/shard_map/ppermute | solution.py:18
  34.9 1.4 %collective-permute-start.10 = (bf16[8,1920]{1,0:T(8,128)(2,1)S(1)}, bf16[8,1920]{1,0:T(8,128)(2,1)S(1)}, u32[]{:S(2)}, u32[]{:S(2)}) collective-permute-start(bf16[8,1920]{1,0:T(8,128)(2,1)S(1)} %get-tuple-element.34), channel_id=1, source_target_pairs={{0,6},{2,4},{4,2},{6,0},{1,7},{3,5},{5,3},{7,1},{8,14},{10,12},{12... | collective-permute-start | bytes 92168 | tf_op jit(solution)/shard_map/ppermute | solution.py:18
  37.3 2.4 %collective-permute-done.10.refs_3_ = bf16[8,1920]{1,0:T(8,128)(2,1)S(1)} collective-permute-done((bf16[8,1920]{1,0:T(8,128)(2,1)S(1)}, bf16[8,1920]{1,0:T(8,128)(2,1)S(1)}, u32[]{:S(2)}, u32[]{:S(2)}) %collective-permute-start.10) | collective-permute-done | bytes 30752 | tf_op jit(solution)/shard_map/ppermute | solution.py:18
  40.7 4.2 %collective-permute-start.11 = (bf16[2,1920]{1,0:T(2,128)(2,1)S(1)}, bf16[2,1920]{1,0:T(2,128)(2,1)S(1)}, u32[]{:S(2)}, u32[]{:S(2)}) collective-permute-start(bf16[2,1920]{1,0:T(2,128)(2,1)S(1)} %get-tuple-element.41), channel_id=1, source_target_pairs={{0,8},{8,0},{16,24},{24,16},{1,9},{9,1},{17,25},{25,17},{2,10},{10... | collective-permute-start | bytes 23048 | tf_op jit(solution)/shard_map/ppermute | solution.py:18
  44.8 1.1 %collective-permute-done.13 = bf16[2,1920]{1,0:T(2,128)(2,1)S(1)} collective-permute-done((bf16[2,1920]{1,0:T(2,128)(2,1)S(1)}, bf16[2,1920]{1,0:T(2,128)(2,1)S(1)}, u32[]{:S(2)}, u32[]{:S(2)}) %collective-permute-start.13) | collective-permute-done | bytes 7712 | tf_op jit(solution)/shard_map/ppermute | solution.py:18
  46.5 0.9 %finish.1 = (bf16[64,1792]{1,0:T(8,128)(2,1)}, f32[64,128]{1,0:T(8,128)}) custom-call(f32[32,64]{1,0:T(8,128)S(1)} %get-tuple-element.20.hit_ref, bf16[8,1920]{1,0:T(8,128)(2,1)S(1)} %pad_maximum_fusion.1.home_ref), custom_call_target="tpu_custom_call" | custom-call | tf_op jit(solution)/shard_map/finish/pallas_call | solution.py:269
  (44 shorter events, 6.4 us)
Async XLA Ops:
  0.6 23.7 %copy-start = (bf16[1,128,4096]{2,1,0:T(8,128)(2,1)S(1)}, bf16[1,128,4096]{2,1,0:T(8,128)(2,1)}, u32[]{:S(2)}) copy-start(bf16[1,128,4096]{2,1,0:T(8,128)(2,1)} %param.21) | copy-start | bytes 3145732
  0.6 1.0 %copy-start.5 = (bf16[64,1792]{1,0:T(8,128)(2,1)S(1)}, bf16[64,1792]{1,0:T(8,128)(2,1)}, u32[]{:S(2)}) copy-start(bf16[64,1792]{1,0:T(8,128)(2,1)} %refs_3_.1) | copy-start | bytes 688132
  1.7 0.9 %copy-start.6 = (bf16[64,1792]{1,0:T(8,128)(2,1)S(1)}, bf16[64,1792]{1,0:T(8,128)(2,1)}, u32[]{:S(2)}) copy-start(bf16[64,1792]{1,0:T(8,128)(2,1)} %refs_4_.1) | copy-start | bytes 688132
  2.6 0.7 %copy-start.8 = (s32[64,8]{0,1:T(8,128)S(1)}, s32[64,8]{0,1:T(8,128)}, u32[]{:S(2)}) copy-start(s32[64,8]{0,1:T(8,128)} %param.13) | copy-start | bytes 6148
  3.3 0.7 %copy-start.9 = (s32[64,8]{0,1:T(8,128)S(1)}, s32[64,8]{0,1:T(8,128)}, u32[]{:S(2)}) copy-start(s32[64,8]{0,1:T(8,128)} %param.14) | copy-start | bytes 6148
  5.5 5.7 %collective-permute-start = (bf16[8,896]{1,0:T(8,128)(2,1)S(1)}, bf16[8,896]{1,0:T(8,128)(2,1)S(1)}, u32[]{:S(2)}, u32[]{:S(2)}) collective-permute-start(bf16[8,896]{1,0:T(8,128)(2,1)S(1)} %get-tuple-element.22), channel_id=1, source_target_pairs={{0,8},{8,0},{16,24},{24,16},{1,9},{9,1},{17,25},{25,17},{2,10},{10... | collective-permute-start | bytes 43016 | tf_op jit(solution)/shard_map/ppermute | solution.py:18
  8.6 4.7 %collective-permute-start.1 = (bf16[8,896]{1,0:T(8,128)(2,1)S(1)}, bf16[8,896]{1,0:T(8,128)(2,1)S(1)}, u32[]{:S(2)}, u32[]{:S(2)}) collective-permute-start(bf16[8,896]{1,0:T(8,128)(2,1)S(1)} %get-tuple-element.23), channel_id=1, source_target_pairs={{0,16},{8,24},{16,0},{24,8},{1,17},{9,25},{17,1},{25,9},{2,18},{10... | collective-permute-start | bytes 43016 | tf_op jit(solution)/shard_map/ppermute | solution.py:18
  11.2 5.5 %collective-permute-start.2 = (bf16[8,896]{1,0:T(8,128)(2,1)S(1)}, bf16[8,896]{1,0:T(8,128)(2,1)S(1)}, u32[]{:S(2)}, u32[]{:S(2)}) collective-permute-start(bf16[8,896]{1,0:T(8,128)(2,1)S(1)} %get-tuple-element.24), channel_id=1, source_target_pairs={{0,24},{8,16},{16,8},{24,0},{1,25},{9,17},{17,9},{25,1},{2,26},{10... | collective-permute-start | bytes 43016 | tf_op jit(solution)/shard_map/ppermute | solution.py:18
  16.8 7.5 %copy-start.4 = (bf16[1,64,3584]{2,1,0:T(8,128)(2,1)S(1)}, bf16[1,64,3584]{2,1,0:T(8,128)(2,1)}, u32[]{:S(2)}) copy-start(bf16[1,64,3584]{2,1,0:T(8,128)(2,1)} %param.20) | copy-start | bytes 1376260
  17.0 5.4 %collective-permute-start.5 = (bf16[4,8,896]{2,1,0:T(8,128)(2,1)S(1)}, bf16[4,8,896]{2,1,0:T(8,128)(2,1)S(1)}, u32[]{:S(2)}, u32[]{:S(2)}) collective-permute-start(bf16[4,8,896]{2,1,0:T(8,128)(2,1)S(1)} %reshape.28), channel_id=1, source_target_pairs={{0,6},{2,4},{4,2},{6,0},{1,7},{3,5},{5,3},{7,1},{8,14},{10,12},{12... | collective-permute-start | bytes 172040 | tf_op jit(solution)/shard_map/ppermute | solution.py:18
  19.5 4.2 %collective-permute-start.4 = (bf16[4,8,896]{2,1,0:T(8,128)(2,1)S(1)}, bf16[4,8,896]{2,1,0:T(8,128)(2,1)S(1)}, u32[]{:S(2)}, u32[]{:S(2)}) collective-permute-start(bf16[4,8,896]{2,1,0:T(8,128)(2,1)S(1)} %reshape.28), channel_id=1, source_target_pairs={{0,4},{2,6},{4,0},{6,2},{1,5},{3,7},{5,1},{7,3},{8,12},{10,14},{12... | collective-permute-start | bytes 172040 | tf_op jit(solution)/shard_map/ppermute | solution.py:18
  20.0 4.2 %collective-permute-start.3 = (bf16[4,8,896]{2,1,0:T(8,128)(2,1)S(1)}, bf16[4,8,896]{2,1,0:T(8,128)(2,1)S(1)}, u32[]{:S(2)}, u32[]{:S(2)}) collective-permute-start(bf16[4,8,896]{2,1,0:T(8,128)(2,1)S(1)} %reshape.28), channel_id=1, source_target_pairs={{0,2},{2,0},{4,6},{6,4},{1,3},{3,1},{5,7},{7,5},{8,10},{10,8},{12,... | collective-permute-start | bytes 172040 | tf_op jit(solution)/shard_map/ppermute | solution.py:18
  24.2 0.7 %copy-start.7 = (bf16[1,64,128]{2,1,0:T(8,128)(2,1)S(1)}, bf16[1,64,128]{2,1,0:T(8,128)(2,1)}, u32[]{:S(2)}) copy-start(bf16[1,64,128]{2,1,0:T(8,128)(2,1)} %param.19) | copy-start | bytes 49156
  24.2 5.3 %collective-permute-start.6 = (bf16[128,896]{1,0:T(8,128)(2,1)S(1)}, bf16[128,896]{1,0:T(8,128)(2,1)S(1)}, u32[]{:S(2)}, u32[]{:S(2)}) collective-permute-start(bf16[128,896]{1,0:T(8,128)(2,1)S(1)} %bitcast.22), channel_id=1, source_target_pairs={{0,1},{1,0},{2,3},{3,2},{4,5},{5,4},{6,7},{7,6},{8,9},{9,8},{10,11... | collective-permute-start | bytes 688136 | tf_op jit(solution)/shard_map/ppermute | solution.py:18
  24.9 1.2 %copy-start.1 = (bf16[1,3584,128]{2,1,0:T(8,128)(2,1)S(1)}, bf16[1,3584,128]{2,1,0:T(8,128)(2,1)}, u32[]{:S(2)}) copy-start(bf16[1,3584,128]{2,1,0:T(8,128)(2,1)} %param.16) | copy-start | bytes 2752516
  26.1 1.2 %copy-start.2 = (bf16[1,3584,128]{2,1,0:T(8,128)(2,1)S(1)}, bf16[1,3584,128]{2,1,0:T(8,128)(2,1)}, u32[]{:S(2)}) copy-start(bf16[1,3584,128]{2,1,0:T(8,128)(2,1)} %param.17) | copy-start | bytes 2752516
  27.2 1.2 %copy-start.3 = (bf16[1,128,3584]{2,1,0:T(8,128)(2,1)S(1)}, bf16[1,128,3584]{2,1,0:T(8,128)(2,1)}, u32[]{:S(2)}) copy-start(bf16[1,128,3584]{2,1,0:T(8,128)(2,1)} %param.18) | copy-start | bytes 2752516
  31.3 1.4 %collective-permute-start.7 = (bf16[32,1920]{1,0:T(8,128)(2,1)S(1)}, bf16[32,1920]{1,0:T(8,128)(2,1)S(1)}, u32[]{:S(2)}, u32[]{:S(2)}) collective-permute-start(bf16[32,1920]{1,0:T(8,128)(2,1)S(1)} %get-tuple-element.30), channel_id=1, source_target_pairs={{0,1},{1,0},{2,3},{3,2},{4,5},{5,4},{6,7},{7,6},{8,9},{9,8},{10,11... | collective-permute-start | bytes 368648 | tf_op jit(solution)/shard_map/ppermute | solution.py:18
  32.9 3.9 %collective-permute-start.8 = (bf16[8,1920]{1,0:T(8,128)(2,1)S(1)}, bf16[8,1920]{1,0:T(8,128)(2,1)S(1)}, u32[]{:S(2)}, u32[]{:S(2)}) collective-permute-start(bf16[8,1920]{1,0:T(8,128)(2,1)S(1)} %get-tuple-element.32), channel_id=1, source_target_pairs={{0,2},{2,0},{4,6},{6,4},{1,3},{3,1},{5,7},{7,5},{8,10},{10,8},{12,... | collective-permute-start | bytes 92168 | tf_op jit(solution)/shard_map/ppermute | solution.py:18
  33.4 3.9 %collective-permute-start.9 = (bf16[8,1920]{1,0:T(8,128)(2,1)S(1)}, bf16[8,1920]{1,0:T(8,128)(2,1)S(1)}, u32[]{:S(2)}, u32[]{:S(2)}) collective-permute-start(bf16[8,1920]{1,0:T(8,128)(2,1)S(1)} %get-tuple-element.33), channel_id=1, source_target_pairs={{0,4},{2,6},{4,0},{6,2},{1,5},{3,7},{5,1},{7,3},{8,12},{10,14},{12... | collective-permute-start | bytes 92168 | tf_op jit(solution)/shard_map/ppermute | solution.py:18
  34.9 4.8 %collective-permute-start.10 = (bf16[8,1920]{1,0:T(8,128)(2,1)S(1)}, bf16[8,1920]{1,0:T(8,128)(2,1)S(1)}, u32[]{:S(2)}, u32[]{:S(2)}) collective-permute-start(bf16[8,1920]{1,0:T(8,128)(2,1)S(1)} %get-tuple-element.34), channel_id=1, source_target_pairs={{0,6},{2,4},{4,2},{6,0},{1,7},{3,5},{5,3},{7,1},{8,14},{10,12},{12... | collective-permute-start | bytes 92168 | tf_op jit(solution)/shard_map/ppermute | solution.py:18
  40.4 5.5 %collective-permute-start.13 = (bf16[2,1920]{1,0:T(2,128)(2,1)S(1)}, bf16[2,1920]{1,0:T(2,128)(2,1)S(1)}, u32[]{:S(2)}, u32[]{:S(2)}) collective-permute-start(bf16[2,1920]{1,0:T(2,128)(2,1)S(1)} %get-tuple-element.39), channel_id=1, source_target_pairs={{0,24},{8,16},{16,8},{24,0},{1,25},{9,17},{17,9},{25,1},{2,26},{10... | collective-permute-start | bytes 23048 | tf_op jit(solution)/shard_map/ppermute | solution.py:18
  40.7 5.2 %collective-permute-start.12 = (bf16[2,1920]{1,0:T(2,128)(2,1)S(1)}, bf16[2,1920]{1,0:T(2,128)(2,1)S(1)}, u32[]{:S(2)}, u32[]{:S(2)}) collective-permute-start(bf16[2,1920]{1,0:T(2,128)(2,1)S(1)} %get-tuple-element.40), channel_id=1, source_target_pairs={{0,16},{8,24},{16,0},{24,8},{1,17},{9,25},{17,1},{25,9},{2,18},{10... | collective-permute-start | bytes 23048 | tf_op jit(solution)/shard_map/ppermute | solution.py:18
  40.7 5.8 %collective-permute-start.11 = (bf16[2,1920]{1,0:T(2,128)(2,1)S(1)}, bf16[2,1920]{1,0:T(2,128)(2,1)S(1)}, u32[]{:S(2)}, u32[]{:S(2)}) collective-permute-start(bf16[2,1920]{1,0:T(2,128)(2,1)S(1)} %get-tuple-element.41), channel_id=1, source_target_pairs={{0,8},{8,0},{16,24},{24,16},{1,9},{9,1},{17,25},{25,17},{2,10},{10... | collective-permute-start | bytes 23048 | tf_op jit(solution)/shard_map/ppermute | solution.py:18
  (1 other events, 0.7 us)

commit v3 on v2

--- a/solution.py
+++ b/solution.py
@@ -16,6 +16,33 @@
 def send_rel(block, axis, offset):
     size = lax.axis_size(axis)
     return lax.ppermute(block, axis, [(i, i ^ offset) for i in range(size)])
+
+
+def split_order(count):
+    return list(range(0, count, 2)) + list(range(1, count, 2))
+
+
+def exchange(stay, go, unit, count):
+    order = split_order(count)
+    half = count // 2
+    slots = {}
+    for index, k in enumerate(order[:half]):
+        slots[k] = stay[index * unit : (index + 1) * unit]
+    got = send_rel(go, "expert", 1)
+    for index, k in enumerate(order[half:]):
+        slots[k] = got[index * unit : (index + 1) * unit]
+    bit = 2
+    while bit < count:
+        moving = [k for k in range(count) if k & bit]
+        got = send_rel(jnp.concatenate([slots[k] for k in moving]), "expert", bit)
+        for index, k in enumerate(moving):
+            slots[k] = got[index * unit : (index + 1) * unit]
+        bit *= 2
+    return slots
+
+
+def keep_in_hbm(array):
+    return pltpu.with_memory_space_constraint(array, pltpu.HBM)
 
 
 def dot_f32(a, b, contract):
@@ -57,16 +84,16 @@
 
 
 def select_kernel(experts, *refs):
-    sources, outs = refs[:5], refs[5 : 6 + experts]
-    ids, slots, weight, tok, grad, sems = refs[6 + experts :]
-    hit_ref, out_refs = outs[0], outs[1:]
+    sources, (hit_ref, *out_refs) = refs[:5], refs[5:8]
+    ids, slots, weight, tok, grad, sems = refs[8:]
     copies = start_copies(zip(sources, (ids, slots, weight, tok, grad)), sems)
     here = lax.axis_index("expert")
     unit = KINDS * CAP
     quarter = tok.shape[1] // 2
     row = lax.broadcasted_iota(jnp.int32, (experts * unit, 1), 0)
     kind = (row % unit) // CAP
-    want = ((row // unit) ^ here) * CAP + row % CAP
+    turn = 2 * (row // unit)
+    want = ((turn % experts + turn // experts) ^ here) * CAP + row % CAP
     for copy in copies[:3]:
         copy.wait()
     hits, scaled = hit_tables(ids[...], slots[...], weight[...].astype(F32), want, experts)
@@ -81,8 +108,9 @@
         part = dot_f32(left, source[:, first : first + quarter], ((1,), (0,)))
         total = part if total is None else total + part
     total = total.astype(BF16)
-    for k in range(experts):
-        out_refs[k][...] = total[k * unit : (k + 1) * unit]
+    sent = experts * unit // 2
+    out_refs[0][...] = total[:sent]
+    out_refs[1][...] = total[sent:]
 
 
 def load_kernel(*refs):
@@ -197,18 +225,18 @@
     ids_t, slots_t, weight_t = route_ids.T, route_slots.T, route_weight.T
 
     with jax.named_scope("select"):
-        hits, *picked = pl.pallas_call(
+        hits, stay, go = pl.pallas_call(
             functools.partial(select_kernel, experts),
             out_shape=[jax.ShapeDtypeStruct((experts * unit, tok_rows), F32)]
-            + [jax.ShapeDtypeStruct((unit, quarter), BF16)] * experts,
+            + [jax.ShapeDtypeStruct((experts * unit // 2, quarter), BF16)] * 2,
             in_specs=in_hbm(5),
-            out_specs=whole_vmem(experts + 1),
+            out_specs=whole_vmem(3),
             scratch_shapes=[
                 pltpu.VMEM(x.shape, x.dtype) for x in (ids_t, slots_t, weight_t, tokens, out_grad)
             ]
             + [pltpu.SemaphoreType.DMA((5,))],
             compiler_params=limit(rows),
-        )(ids_t, slots_t, weight_t, tokens, out_grad)
+        )(*map(keep_in_hbm, (ids_t, slots_t, weight_t, tokens, out_grad)))
     params = [w_gate[0], w_up[0], w_down[0], proj_hidden[0], proj_grad[0], test_feats[0]]
     with jax.named_scope("load"):
         gate_w, up_w, down_w, hid_proj, grad_proj, test_rows = pl.pallas_call(
@@ -221,9 +249,9 @@
             cost_estimate=pl.CostEstimate(
                 flops=0, bytes_accessed=sum(2 * x.size for x in params), transcendentals=0
             ),
-        )(picked[0], *params)
-    arrived = [picked[0]] + [send_rel(picked[k], "expert", k) for k in range(1, experts)]
-    block = jnp.stack(arrived).reshape(experts, KINDS, CAP, quarter)
+        )(stay, *map(keep_in_hbm, params))
+    slots = exchange(stay, go, unit, experts)
+    block = jnp.stack([slots[k] for k in range(experts)]).reshape(experts, KINDS, CAP, quarter)
     block = block.transpose(1, 0, 2, 3).reshape(KINDS, pairs, quarter)
     blocks = [block] + [send_rel(block, "dp", g) for g in range(1, groups)]
     own = jnp.stack(blocks, axis=1).reshape(KINDS * rows, quarter)
@@ -262,9 +290,10 @@
             scratch_shapes=[pltpu.VMEM((pairs, proj * proj), BF16)],
             compiler_params=limit(rows),
         )(*pieces, grad_mine, test_rows)
-    back = back.reshape(experts, CAP, half + tests)
-    home = [back[0]] + [send_rel(back[k], "expert", k) for k in range(1, experts)]
-    home = jnp.concatenate(home, axis=0)
+    order = split_order(experts)
+    back = jnp.concatenate([back[k * CAP : (k + 1) * CAP] for k in order])
+    slots = exchange(back[: pairs // 2], back[pairs // 2 :], CAP, experts)
+    home = jnp.concatenate([slots[k] for k in order])
     with jax.named_scope("finish"):
         return pl.pallas_call(
             finish_kernel,

time: 47.9 us -> 42.8 us (0.89)
  local copies, waits for them, and re-layouts: 8.32 us -> 0.24 us
  Pallas kernels: 5.44 us -> 7.08 us
  starting transfers between devices: 17.3 us -> 18.2 us
  waiting for transfers between devices: 15.2 us -> 15.9 us
    unnamed x22 -> x0, local copies, waits for them, and re-layouts: 8.13 us -> none
    pallas_call x1, Pallas kernels: 1.09 us -> 2.27 us  [on_device(): pl.pallas_call(load_kernel, out_shape=[jax.ShapeDtypeStruct(x.shape, x.dt...]
    ppermute x14 -> x12, starting transfers between devices: 17.3 us -> 18.2 us  [send_rel(): return lax.ppermute(block, axis, [(i, i ^ offset) for i in range(size)])]
    ppermute x14 -> x12, waiting for transfers between devices: 15.2 us -> 15.9 us  [send_rel(): return lax.ppermute(block, axis, [(i, i ^ offset) for i in range(size)])]
  transfers between devices with their start and end apart: 14 -> 12, of which waited for: 11 -> 11; matrix products, arithmetic and copies ran while one was open for 1% -> 1% of each run, Pallas kernels for 2% -> 5%
where the time goes in v3:
time: 42.8 us; the launch traced here: 42.6 us
  starting transfers between devices  18.2 us (43%)
  waiting for transfers between devices  15.9 us (37%)
  Pallas kernels  7.08 us (17%)
  between operations  0.75 us (2%)
    ppermute x12, starting transfers between devices, send_rel(): return lax.ppermute(block, axis, [(i, i ^ offset) for i in range(size)])  18.2 us
    ppermute x12, waiting for transfers between devices, send_rel(): return lax.ppermute(block, axis, [(i, i ^ offset) for i in range(size)])  15.9 us
    pallas_call x1, Pallas kernels, on_device(): pl.pallas_call(load_kernel, out_shape=[jax.ShapeDtypeStruct(x.shape, x.dt...  2.27 us
    pallas_call x1, Pallas kernels, on_device(): pl.pallas_call(expert_kernel, out_shape=[jax.ShapeDtypeStruct((rows, out_...  1.79 us
    pallas_call x1, Pallas kernels, on_device(): pl.pallas_call(functools.partial(select_kernel, experts), out_shape=[jax....  1.31 us
    pallas_call x1, Pallas kernels, on_device(): pl.pallas_call(finish_kernel, out_shape=[jax.ShapeDtypeStruct((tok_rows,...  0.95 us
  transfers between devices with their start and end apart: 12, of which 11 were waited for; matrix products, arithmetic and copies ran while one was open for 1% of the time, Pallas kernels for 5%

profile of v3, /device:TPU:0, one launch (start us, length us, event | category | flops | bytes accessed | tf_op | source)
XLA Modules:
  0.0 42.6 jit_solution(6661432959771895011)
XLA Ops:
  0.6 1.3 %select.1 = (f32[32,64]{1,0:T(8,128)S(1)}, bf16[16,896]{1,0:T(8,128)(2,1)S(1)}, bf16[16,896]{1,0:T(8,128)(2,1)S(1)}) custom-call(s32[8,64]{1,0:T(8,128)} %bitcast.32, s32[8,64]{1,0:T(8,128)} %bitcast.33, bf16[8,64]{1,0:T(8,128)(2,1)} %bitcast.34, bf16[64,1792]{1,0:T(8,128)(2,1)} %refs_3_.1, bf16[64,1792]{1,0:T(8,128)(2,1)} %refs_4_.1), custom_call_target="tpu_custom_call" | custom-call | tf_op jit(solution)/shard_map/select/pallas_call | solution.py:228
  1.9 3.1 %collective-permute-start = (bf16[16,896]{1,0:T(8,128)(2,1)S(1)}, bf16[16,896]{1,0:T(8,128)(2,1)S(1)}, u32[]{:S(2)}, u32[]{:S(2)}) collective-permute-start(bf16[16,896]{1,0:T(8,128)(2,1)S(1)} %get-tuple-element.20), channel_id=1, source_target_pairs={{0,8},{8,0},{16,24},{24,16},{1,9},{9,1},{17,25},{25,17},{2,10},{10... | collective-permute-start | bytes 86024 | tf_op jit(solution)/shard_map/ppermute | solution.py:18
  5.0 1.8 %collective-permute-done = bf16[16,896]{1,0:T(8,128)(2,1)S(1)} collective-permute-done((bf16[16,896]{1,0:T(8,128)(2,1)S(1)}, bf16[16,896]{1,0:T(8,128)(2,1)S(1)}, u32[]{:S(2)}, u32[]{:S(2)}) %collective-permute-start) | collective-permute-done | bytes 28704 | tf_op jit(solution)/shard_map/ppermute | solution.py:18
  6.9 3.1 %collective-permute-start.1 = (bf16[16,896]{1,0:T(8,128)(2,1)S(1)}, bf16[16,896]{1,0:T(8,128)(2,1)S(1)}, u32[]{:S(2)}, u32[]{:S(2)}) collective-permute-start(bf16[16,896]{1,0:T(8,128)(2,1)S(1)} %pad_maximum_fusion.2), channel_id=1, source_target_pairs={{0,16},{8,24},{16,0},{24,8},{1,17},{9,25},{17,1},{25,9},{2,18},{10... | collective-permute-start | bytes 86024 | tf_op jit(solution)/shard_map/ppermute | solution.py:18
  10.0 1.8 %collective-permute-done.1 = bf16[16,896]{1,0:T(8,128)(2,1)S(1)} collective-permute-done((bf16[16,896]{1,0:T(8,128)(2,1)S(1)}, bf16[16,896]{1,0:T(8,128)(2,1)S(1)}, u32[]{:S(2)}, u32[]{:S(2)}) %collective-permute-start.1) | collective-permute-done | bytes 28704 | tf_op jit(solution)/shard_map/ppermute | solution.py:18
  12.1 2.8 %collective-permute-start.4 = (bf16[4,8,896]{2,1,0:T(8,128)(2,1)S(1)}, bf16[4,8,896]{2,1,0:T(8,128)(2,1)S(1)}, u32[]{:S(2)}, u32[]{:S(2)}) collective-permute-start(bf16[4,8,896]{2,1,0:T(8,128)(2,1)S(1)} %reshape.19), channel_id=1, source_target_pairs={{0,6},{2,4},{4,2},{6,0},{1,7},{3,5},{5,3},{7,1},{8,14},{10,12},{12... | collective-permute-start | bytes 172040 | tf_op jit(solution)/shard_map/ppermute | solution.py:18
  14.9 0.5 %collective-permute-start.3 = (bf16[4,8,896]{2,1,0:T(8,128)(2,1)S(1)}, bf16[4,8,896]{2,1,0:T(8,128)(2,1)S(1)}, u32[]{:S(2)}, u32[]{:S(2)}) collective-permute-start(bf16[4,8,896]{2,1,0:T(8,128)(2,1)S(1)} %reshape.19), channel_id=1, source_target_pairs={{0,4},{2,6},{4,0},{6,2},{1,5},{3,7},{5,1},{7,3},{8,12},{10,14},{12... | collective-permute-start | bytes 172040 | tf_op jit(solution)/shard_map/ppermute | solution.py:18
  15.6 1.6 %collective-permute-done.4 = bf16[4,8,896]{2,1,0:T(8,128)(2,1)S(1)} collective-permute-done((bf16[4,8,896]{2,1,0:T(8,128)(2,1)S(1)}, bf16[4,8,896]{2,1,0:T(8,128)(2,1)S(1)}, u32[]{:S(2)}, u32[]{:S(2)}) %collective-permute-start.4) | collective-permute-done | bytes 57376 | tf_op jit(solution)/shard_map/ppermute | solution.py:18
  17.2 1.9 %collective-permute-done.3 = bf16[4,8,896]{2,1,0:T(8,128)(2,1)S(1)} collective-permute-done((bf16[4,8,896]{2,1,0:T(8,128)(2,1)S(1)}, bf16[4,8,896]{2,1,0:T(8,128)(2,1)S(1)}, u32[]{:S(2)}, u32[]{:S(2)}) %collective-permute-start.3) | collective-permute-done | bytes 57376 | tf_op jit(solution)/shard_map/ppermute | solution.py:18
  19.1 0.5 %collective-permute-done.2 = bf16[4,8,896]{2,1,0:T(8,128)(2,1)S(1)} collective-permute-done((bf16[4,8,896]{2,1,0:T(8,128)(2,1)S(1)}, bf16[4,8,896]{2,1,0:T(8,128)(2,1)S(1)}, u32[]{:S(2)}, u32[]{:S(2)}) %collective-permute-start.2) | collective-permute-done | bytes 57376 | tf_op jit(solution)/shard_map/ppermute | solution.py:18
  19.7 2.3 %load.1 = (bf16[3584,128]{1,0:T(8,128)(2,1)S(1)}, bf16[3584,128]{1,0:T(8,128)(2,1)S(1)}, bf16[128,3584]{1,0:T(8,128)(2,1)S(1)}, bf16[64,128]{1,0:T(8,128)(2,1)S(...) custom-call(bf16[16,896]{1,0:T(8,128)(2,1)S(1)} %get-tuple-element.19.refs_0_, ...), custom_call_target="tpu_custom_call" | custom-call | bytes 4276224 | tf_op jit(solution)/shard_map/load/pallas_call | solution.py:242
  22.0 1.8 %expert.1 = (bf16[32,1920]{1,0:T(8,128)(2,1)S(1)}, bf16[32,1920]{1,0:T(8,128)(2,1)S(1)}, bf16[8,3584]{1,0:T(8,128)(2,1)S(1)}) custom-call(bf16[128,896]{1,0:T(8,128)(2,1)S(1)} %bitcast.22, bf16[128,896]{1,0:T(8,128)(2,1)S(1)} %collective-permute-done.5.other_ref, bf16[3584,128]{1,0:T(8,128)(2,1)S(1)} %get-tuple-element.21.gate_w, ...), custom_call_target="tpu_custom_call" | custom-call | tf_op jit(solution)/shard_map/expert/pallas_call | solution.py:261
  23.8 0.6 %collective-permute-start.6 = (bf16[32,1920]{1,0:T(8,128)(2,1)S(1)}, bf16[32,1920]{1,0:T(8,128)(2,1)S(1)}, u32[]{:S(2)}, u32[]{:S(2)}) collective-permute-start(bf16[32,1920]{1,0:T(8,128)(2,1)S(1)} %get-tuple-element.26), channel_id=1, source_target_pairs={{0,1},{1,0},{2,3},{3,2},{4,5},{5,4},{6,7},{7,6},{8,9},{9,8},{10,11... | collective-permute-start | bytes 368648 | tf_op jit(solution)/shard_map/ppermute | solution.py:18
  24.4 1.0 %collective-permute-done.6.got_ref = bf16[32,1920]{1,0:T(8,128)(2,1)S(1)} collective-permute-done((bf16[32,1920]{1,0:T(8,128)(2,1)S(1)}, bf16[32,1920]{1,0:T(8,128)(2,1)S(1)}, u32[]{:S(2)}, u32[]{:S(2)}) %collective-permute-start.6) | collective-permute-done | bytes 122912 | tf_op jit(solution)/shard_map/ppermute | solution.py:18
  25.5 0.2 collective-permute-start.7
  25.7 1.9 %collective-permute-start.8 = (bf16[8,1920]{1,0:T(8,128)(2,1)S(1)}, bf16[8,1920]{1,0:T(8,128)(2,1)S(1)}, u32[]{:S(2)}, u32[]{:S(2)}) collective-permute-start(bf16[8,1920]{1,0:T(8,128)(2,1)S(1)} %get-tuple-element.29), channel_id=1, source_target_pairs={{0,4},{2,6},{4,0},{6,2},{1,5},{3,7},{5,1},{7,3},{8,12},{10,14},{12... | collective-permute-start | bytes 92168 | tf_op jit(solution)/shard_map/ppermute | solution.py:18
  27.6 1.4 %collective-permute-start.9 = (bf16[8,1920]{1,0:T(8,128)(2,1)S(1)}, bf16[8,1920]{1,0:T(8,128)(2,1)S(1)}, u32[]{:S(2)}, u32[]{:S(2)}) collective-permute-start(bf16[8,1920]{1,0:T(8,128)(2,1)S(1)} %get-tuple-element.30), channel_id=1, source_target_pairs={{0,6},{2,4},{4,2},{6,0},{1,7},{3,5},{5,3},{7,1},{8,14},{10,12},{12... | collective-permute-start | bytes 92168 | tf_op jit(solution)/shard_map/ppermute | solution.py:18
  29.6 2.8 %collective-permute-done.9.refs_3_ = bf16[8,1920]{1,0:T(8,128)(2,1)S(1)} collective-permute-done((bf16[8,1920]{1,0:T(8,128)(2,1)S(1)}, bf16[8,1920]{1,0:T(8,128)(2,1)S(1)}, u32[]{:S(2)}, u32[]{:S(2)}) %collective-permute-start.9) | collective-permute-done | bytes 30752 | tf_op jit(solution)/shard_map/ppermute | solution.py:18
  32.4 0.6 %score.1 = bf16[8,1920]{1,0:T(8,128)(2,1)S(1)} custom-call(bf16[8,1920]{1,0:T(8,128)(2,1)S(1)} %get-tuple-element.27.refs_0_, bf16[8,1920]{1,0:T(8,128)(2,1)S(1)} %collective-permute-done.7.refs_1_, bf16[8,1920]{1,0:T(8,128)(2,1)S(1)} %collective-permute-done.8.refs_2_, bf16[8,1920]{1,0:T(8,128)(2,1)S(1)} %collective-permute-done.9.refs_3_, ...), custom_call_target="tpu_custom_call" | custom-call | tf_op jit(solution)/shard_map/score/pallas_call | solution.py:285
  33.1 1.6 %collective-permute-start.10 = (bf16[4,1920]{1,0:T(4,128)(2,1)S(1)}, bf16[4,1920]{1,0:T(4,128)(2,1)S(1)}, u32[]{:S(2)}, u32[]{:S(2)}) collective-permute-start(bf16[4,1920]{1,0:T(4,128)(2,1)S(1)} %pad_maximum_fusion.3), channel_id=1, source_target_pairs={{0,8},{8,0},{16,24},{24,16},{1,9},{9,1},{17,25},{25,17},{2,10},{10... | collective-permute-start | bytes 46088 | tf_op jit(solution)/shard_map/ppermute | solution.py:18
  34.7 2.1 %collective-permute-done.10 = bf16[4,1920]{1,0:T(4,128)(2,1)S(1)} collective-permute-done((bf16[4,1920]{1,0:T(4,128)(2,1)S(1)}, bf16[4,1920]{1,0:T(4,128)(2,1)S(1)}, u32[]{:S(2)}, u32[]{:S(2)}) %collective-permute-start.10) | collective-permute-done | bytes 15392 | tf_op jit(solution)/shard_map/ppermute | solution.py:18
  36.9 2.7 %collective-permute-start.11 = (bf16[4,1920]{1,0:T(4,128)(2,1)S(1)}, bf16[4,1920]{1,0:T(4,128)(2,1)S(1)}, u32[]{:S(2)}, u32[]{:S(2)}) collective-permute-start(bf16[4,1920]{1,0:T(4,128)(2,1)S(1)} %pad_maximum_fusion.4), channel_id=1, source_target_pairs={{0,16},{8,24},{16,0},{24,8},{1,17},{9,25},{17,1},{25,9},{2,18},{10... | collective-permute-start | bytes 46088 | tf_op jit(solution)/shard_map/ppermute | solution.py:18
  39.6 2.0 %collective-permute-done.11 = bf16[4,1920]{1,0:T(4,128)(2,1)S(1)} collective-permute-done((bf16[4,1920]{1,0:T(4,128)(2,1)S(1)}, bf16[4,1920]{1,0:T(4,128)(2,1)S(1)}, u32[]{:S(2)}, u32[]{:S(2)}) %collective-permute-start.11) | collective-permute-done | bytes 15392 | tf_op jit(solution)/shard_map/ppermute | solution.py:18
  41.7 0.9 %finish.1 = (bf16[64,1792]{1,0:T(8,128)(2,1)}, f32[64,128]{1,0:T(8,128)}) custom-call(f32[32,64]{1,0:T(8,128)S(1)} %get-tuple-element.18.hit_ref, bf16[8,1920]{1,0:T(8,128)(2,1)S(1)} %pad_maximum_fusion.1.home_ref), custom_call_target="tpu_custom_call" | custom-call | tf_op jit(solution)/shard_map/finish/pallas_call | solution.py:298
  (26 shorter events, 1.5 us)
Async XLA Ops:
  1.9 4.9 %collective-permute-start = (bf16[16,896]{1,0:T(8,128)(2,1)S(1)}, bf16[16,896]{1,0:T(8,128)(2,1)S(1)}, u32[]{:S(2)}, u32[]{:S(2)}) collective-permute-start(bf16[16,896]{1,0:T(8,128)(2,1)S(1)} %get-tuple-element.20), channel_id=1, source_target_pairs={{0,8},{8,0},{16,24},{24,16},{1,9},{9,1},{17,25},{25,17},{2,10},{10... | collective-permute-start | bytes 86024 | tf_op jit(solution)/shard_map/ppermute | solution.py:18
  6.9 4.9 %collective-permute-start.1 = (bf16[16,896]{1,0:T(8,128)(2,1)S(1)}, bf16[16,896]{1,0:T(8,128)(2,1)S(1)}, u32[]{:S(2)}, u32[]{:S(2)}) collective-permute-start(bf16[16,896]{1,0:T(8,128)(2,1)S(1)} %pad_maximum_fusion.2), channel_id=1, source_target_pairs={{0,16},{8,24},{16,0},{24,8},{1,17},{9,25},{17,1},{25,9},{2,18},{10... | collective-permute-start | bytes 86024 | tf_op jit(solution)/shard_map/ppermute | solution.py:18
  12.1 5.1 %collective-permute-start.4 = (bf16[4,8,896]{2,1,0:T(8,128)(2,1)S(1)}, bf16[4,8,896]{2,1,0:T(8,128)(2,1)S(1)}, u32[]{:S(2)}, u32[]{:S(2)}) collective-permute-start(bf16[4,8,896]{2,1,0:T(8,128)(2,1)S(1)} %reshape.19), channel_id=1, source_target_pairs={{0,6},{2,4},{4,2},{6,0},{1,7},{3,5},{5,3},{7,1},{8,14},{10,12},{12... | collective-permute-start | bytes 172040 | tf_op jit(solution)/shard_map/ppermute | solution.py:18
  14.9 4.2 %collective-permute-start.3 = (bf16[4,8,896]{2,1,0:T(8,128)(2,1)S(1)}, bf16[4,8,896]{2,1,0:T(8,128)(2,1)S(1)}, u32[]{:S(2)}, u32[]{:S(2)}) collective-permute-start(bf16[4,8,896]{2,1,0:T(8,128)(2,1)S(1)} %reshape.19), channel_id=1, source_target_pairs={{0,4},{2,6},{4,0},{6,2},{1,5},{3,7},{5,1},{7,3},{8,12},{10,14},{12... | collective-permute-start | bytes 172040 | tf_op jit(solution)/shard_map/ppermute | solution.py:18
  15.4 4.2 %collective-permute-start.2 = (bf16[4,8,896]{2,1,0:T(8,128)(2,1)S(1)}, bf16[4,8,896]{2,1,0:T(8,128)(2,1)S(1)}, u32[]{:S(2)}, u32[]{:S(2)}) collective-permute-start(bf16[4,8,896]{2,1,0:T(8,128)(2,1)S(1)} %reshape.19), channel_id=1, source_target_pairs={{0,2},{2,0},{4,6},{6,4},{1,3},{3,1},{5,7},{7,5},{8,10},{10,8},{12,... | collective-permute-start | bytes 172040 | tf_op jit(solution)/shard_map/ppermute | solution.py:18
  19.6 2.4 %collective-permute-start.5 = (bf16[128,896]{1,0:T(8,128)(2,1)S(1)}, bf16[128,896]{1,0:T(8,128)(2,1)S(1)}, u32[]{:S(2)}, u32[]{:S(2)}) collective-permute-start(bf16[128,896]{1,0:T(8,128)(2,1)S(1)} %bitcast.21), channel_id=1, source_target_pairs={{0,1},{1,0},{2,3},{3,2},{4,5},{5,4},{6,7},{7,6},{8,9},{9,8},{10,11... | collective-permute-start | bytes 688136 | tf_op jit(solution)/shard_map/ppermute | solution.py:18
  23.8 1.5 %collective-permute-start.6 = (bf16[32,1920]{1,0:T(8,128)(2,1)S(1)}, bf16[32,1920]{1,0:T(8,128)(2,1)S(1)}, u32[]{:S(2)}, u32[]{:S(2)}) collective-permute-start(bf16[32,1920]{1,0:T(8,128)(2,1)S(1)} %get-tuple-element.26), channel_id=1, source_target_pairs={{0,1},{1,0},{2,3},{3,2},{4,5},{5,4},{6,7},{7,6},{8,9},{9,8},{10,11... | collective-permute-start | bytes 368648 | tf_op jit(solution)/shard_map/ppermute | solution.py:18
  25.5 3.9 %collective-permute-start.7 = (bf16[8,1920]{1,0:T(8,128)(2,1)S(1)}, bf16[8,1920]{1,0:T(8,128)(2,1)S(1)}, u32[]{:S(2)}, u32[]{:S(2)}) collective-permute-start(bf16[8,1920]{1,0:T(8,128)(2,1)S(1)} %get-tuple-element.28), channel_id=1, source_target_pairs={{0,2},{2,0},{4,6},{6,4},{1,3},{3,1},{5,7},{7,5},{8,10},{10,8},{12,... | collective-permute-start | bytes 92168 | tf_op jit(solution)/shard_map/ppermute | solution.py:18
  25.7 3.9 %collective-permute-start.8 = (bf16[8,1920]{1,0:T(8,128)(2,1)S(1)}, bf16[8,1920]{1,0:T(8,128)(2,1)S(1)}, u32[]{:S(2)}, u32[]{:S(2)}) collective-permute-start(bf16[8,1920]{1,0:T(8,128)(2,1)S(1)} %get-tuple-element.29), channel_id=1, source_target_pairs={{0,4},{2,6},{4,0},{6,2},{1,5},{3,7},{5,1},{7,3},{8,12},{10,14},{12... | collective-permute-start | bytes 92168 | tf_op jit(solution)/shard_map/ppermute | solution.py:18
  27.6 4.8 %collective-permute-start.9 = (bf16[8,1920]{1,0:T(8,128)(2,1)S(1)}, bf16[8,1920]{1,0:T(8,128)(2,1)S(1)}, u32[]{:S(2)}, u32[]{:S(2)}) collective-permute-start(bf16[8,1920]{1,0:T(8,128)(2,1)S(1)} %get-tuple-element.30), channel_id=1, source_target_pairs={{0,6},{2,4},{4,2},{6,0},{1,7},{3,5},{5,3},{7,1},{8,14},{10,12},{12... | collective-permute-start | bytes 92168 | tf_op jit(solution)/shard_map/ppermute | solution.py:18
  33.1 3.8 %collective-permute-start.10 = (bf16[4,1920]{1,0:T(4,128)(2,1)S(1)}, bf16[4,1920]{1,0:T(4,128)(2,1)S(1)}, u32[]{:S(2)}, u32[]{:S(2)}) collective-permute-start(bf16[4,1920]{1,0:T(4,128)(2,1)S(1)} %pad_maximum_fusion.3), channel_id=1, source_target_pairs={{0,8},{8,0},{16,24},{24,16},{1,9},{9,1},{17,25},{25,17},{2,10},{10... | collective-permute-start | bytes 46088 | tf_op jit(solution)/shard_map/ppermute | solution.py:18
  36.9 4.7 %collective-permute-start.11 = (bf16[4,1920]{1,0:T(4,128)(2,1)S(1)}, bf16[4,1920]{1,0:T(4,128)(2,1)S(1)}, u32[]{:S(2)}, u32[]{:S(2)}) collective-permute-start(bf16[4,1920]{1,0:T(4,128)(2,1)S(1)} %pad_maximum_fusion.4), channel_id=1, source_target_pairs={{0,16},{8,24},{16,0},{24,8},{1,17},{9,25},{17,1},{25,9},{2,18},{10... | collective-permute-start | bytes 46088 | tf_op jit(solution)/shard_map/ppermute | solution.py:18

commit v4 on v3

--- a/solution.py
+++ b/solution.py
@@ -18,23 +18,27 @@
     return lax.ppermute(block, axis, [(i, i ^ offset) for i in range(size)])
 
 
+def send_cross(block, axis, offset):
+    return send_rel(block, (axis, "test"), offset * lax.axis_size("test") + 1)
+
+
 def split_order(count):
     return list(range(0, count, 2)) + list(range(1, count, 2))
 
 
-def exchange(stay, go, unit, count):
+def exchange(send, stay, go, unit, count):
     order = split_order(count)
     half = count // 2
     slots = {}
     for index, k in enumerate(order[:half]):
         slots[k] = stay[index * unit : (index + 1) * unit]
-    got = send_rel(go, "expert", 1)
+    got = send(go, "expert", 1)
     for index, k in enumerate(order[half:]):
         slots[k] = got[index * unit : (index + 1) * unit]
     bit = 2
     while bit < count:
         moving = [k for k in range(count) if k & bit]
-        got = send_rel(jnp.concatenate([slots[k] for k in moving]), "expert", bit)
+        got = send(jnp.concatenate([slots[k] for k in moving]), "expert", bit)
         for index, k in enumerate(moving):
             slots[k] = got[index * unit : (index + 1) * unit]
         bit *= 2
@@ -135,17 +139,24 @@
 ):
     rows, width = x_in.shape
     half, quarter = width // 2, width // 4
+    pairs = mine_ref.shape[0]
     core = lax.axis_index("test")
-    sides = (
-        (own_ref, keep_ref, pl.multiple_of(core * half, 128)),
-        (other_ref, send_ref, pl.multiple_of((1 - core) * half, 128)),
-    )
-    for source, _, base in sides:
-        for index in range(KINDS):
-            target = x_in if index < 2 else x_grad
-            start = pl.multiple_of(base + (index % 2) * quarter, 128)
-            target[:, pl.ds(start, quarter)] = source[index * rows : (index + 1) * rows]
-    mine_ref[...] = x_grad[: mine_ref.shape[0]]
+    near, far = pl.multiple_of(core * half, 128), pl.multiple_of((1 - core) * half, 128)
+    row = lax.broadcasted_iota(jnp.int32, (rows, quarter), 0)
+    odd = jnp.where(row >= pairs, 1, 0)
+    bits = (row % pairs) // CAP
+    for _ in range(max(1, (pairs // CAP - 1).bit_length())):
+        odd = odd ^ (bits & 1)
+        bits = bits // 2
+    odd = odd == 1
+    for index in range(KINDS):
+        target = x_in if index < 2 else x_grad
+        own = own_ref[index * rows : (index + 1) * rows]
+        other = other_ref[index * rows : (index + 1) * rows]
+        first = (index % 2) * quarter
+        target[:, pl.ds(pl.multiple_of(near + first, 128), quarter)] = jnp.where(odd, other, own)
+        target[:, pl.ds(pl.multiple_of(far + first, 128), quarter)] = jnp.where(odd, own, other)
+    mine_ref[...] = x_grad[:pairs]
     gate_pre = dot_f32(x_in[...], gate_w[...], ((1,), (0,)))
     up_pre = dot_f32(x_in[...], up_w[...], ((1,), (0,)))
     hid_grad = dot_f32(x_grad[...], down_w[...], ((1,), (1,)))
@@ -155,13 +166,17 @@
     tail = split_two(dot_f32(hidden, proj_ref[...], ((1,), (1,))))
     up_grad = (hid_grad * act_gate).astype(BF16)
     gate_grad = (hid_grad * up_pre * sig * (1.0 + gate_pre * (1.0 - sig))).astype(BF16)
-    for _, target, base in sides:
-        target[:, half:] = tail
+    keep_ref[:, half:] = tail
+    send_ref[:, half:] = tail
+    for base, first_ref, rest_ref in ((far, send_ref, keep_ref), (near, keep_ref, send_ref)):
         for index in range(2):
             start = pl.multiple_of(base + index * quarter, 128)
+            columns = slice(index * quarter, (index + 1) * quarter)
             part = dot_f32(gate_grad, gate_w[pl.ds(start, quarter), :], ((1,), (1,)))
             part += dot_f32(up_grad, up_w[pl.ds(start, quarter), :], ((1,), (1,)))
-            target[:, index * quarter : (index + 1) * quarter] = part.astype(BF16)
+            part = part.astype(BF16)
+            first_ref[:pairs, columns] = part[:pairs]
+            rest_ref[pairs:, columns] = part[pairs:]
 
 
 def pair_kernel(half, keep_ref, got_ref, *out_refs):
@@ -188,15 +203,25 @@
     out_ref[:, half:] = dot_f32(feature[...], test_ref[...], ((1,), (1,))).astype(BF16)
 
 
-def finish_kernel(hit_ref, home_ref, in_grad_ref, scores_ref):
+def finish_kernel(hit_ref, home_ref, in_grad_hbm, scores_hbm, in_grad, scores, sems):
     pairs, unit = home_ref.shape[0], KINDS * CAP
     hits = jnp.concatenate(
         [hit_ref[k * unit : k * unit + CAP] for k in range(pairs // CAP)], axis=0
     )
-    half = in_grad_ref.shape[1]
+    half = in_grad.shape[1]
+    quarter = half // 2
     hits = hits.T.astype(BF16)
-    in_grad_ref[...] = dot_f32(hits, home_ref[:, :half], ((1,), (0,))).astype(BF16)
-    scores_ref[...] = dot_f32(hits, home_ref[:, half:], ((1,), (0,)))
+    copies = []
+    for index in range(2):
+        columns = slice(index * quarter, (index + 1) * quarter)
+        in_grad[:, columns] = dot_f32(hits, home_ref[:, columns], ((1,), (0,))).astype(BF16)
+        copies += start_copies(
+            [(in_grad.at[:, columns], in_grad_hbm.at[:, columns])], sems.at[pl.ds(index, 1)]
+        )
+    scores[...] = dot_f32(hits, home_ref[:, half:], ((1,), (0,)))
+    copies += start_copies([(scores, scores_hbm)], sems.at[pl.ds(2, 1)])
+    for copy in copies:
+        copy.wait()
 
 
 def on_device(
@@ -239,7 +264,7 @@
         )(*map(keep_in_hbm, (ids_t, slots_t, weight_t, tokens, out_grad)))
     params = [w_gate[0], w_up[0], w_down[0], proj_hidden[0], proj_grad[0], test_feats[0]]
     with jax.named_scope("load"):
-        gate_w, up_w, down_w, hid_proj, grad_proj, test_rows = pl.pallas_call(
+        loaded = pl.pallas_call(
             load_kernel,
             out_shape=[jax.ShapeDtypeStruct(x.shape, x.dtype) for x in params],
             in_specs=whole_vmem(1) + in_hbm(len(params)),
@@ -250,10 +275,12 @@
                 flops=0, bytes_accessed=sum(2 * x.size for x in params), transcendentals=0
             ),
         )(stay, *map(keep_in_hbm, params))
-    slots = exchange(stay, go, unit, experts)
+    slots = exchange(send_cross, stay, go, unit, experts)
+    loaded, slots = lax.optimization_barrier((loaded, slots))
+    gate_w, up_w, down_w, hid_proj, grad_proj, test_rows = loaded
     block = jnp.stack([slots[k] for k in range(experts)]).reshape(experts, KINDS, CAP, quarter)
     block = block.transpose(1, 0, 2, 3).reshape(KINDS, pairs, quarter)
-    blocks = [block] + [send_rel(block, "dp", g) for g in range(1, groups)]
+    blocks = [block] + [send_cross(block, "dp", g) for g in range(1, groups)]
     own = jnp.stack(blocks, axis=1).reshape(KINDS * rows, quarter)
     other = send_rel(own, "test", 1)
 
@@ -279,7 +306,7 @@
             out_specs=whole_vmem(groups),
             compiler_params=limit(rows),
         )(keep, got)
-    pieces = [sums[0]] + [send_rel(sums[g], "dp", g) for g in range(1, groups)]
+    pieces = [sums[0]] + [send_cross(sums[g], "dp", g) for g in range(1, groups)]
     grad_mine = dot_f32(mine, grad_proj, ((1,), (1,)))
     with jax.named_scope("score"):
         back = pl.pallas_call(
@@ -292,7 +319,7 @@
         )(*pieces, grad_mine, test_rows)
     order = split_order(experts)
     back = jnp.concatenate([back[k * CAP : (k + 1) * CAP] for k in order])
-    slots = exchange(back[: pairs // 2], back[pairs // 2 :], CAP, experts)
+    slots = exchange(send_rel, back[: pairs // 2], back[pairs // 2 :], CAP, experts)
     home = jnp.concatenate([slots[k] for k in order])
     with jax.named_scope("finish"):
         return pl.pallas_call(
@@ -302,7 +329,12 @@
                 jax.ShapeDtypeStruct((tok_rows, tests), F32),
             ],
             in_specs=whole_vmem(2),
-            out_specs=whole_vmem(2),
+            out_specs=in_hbm(2),
+            scratch_shapes=[
+                pltpu.VMEM((tok_rows, half), BF16),
+                pltpu.VMEM((tok_rows, tests), F32),
+                pltpu.SemaphoreType.DMA((3,)),
+            ],
             compiler_params=limit(rows),
         )(hits, home)
 

time: 42.8 us -> 43.8 us (1.023)
  local copies, waits for them, and re-layouts: 0.24 us -> 2.97 us
  starting transfers between devices: 18.2 us -> 16.2 us
  other arithmetic: 0.24 us -> 1.08 us
  waiting for transfers between devices: 15.9 us -> 15.4 us
    unnamed x0 -> x4, local copies, waits for them, and re-layouts: none -> 2.11 us
    ppermute x12, starting transfers between devices: 18.2 us -> 16.2 us  [send_rel(): return lax.ppermute(block, axis, [(i, i ^ offset) for i in range(size)])]
    another operation x1, other arithmetic: 0.04 us -> 0.89 us  [on_device(): own = jnp.stack(blocks, axis=1).reshape(KINDS * rows, quarter)]
    reshape x1, local copies, waits for them, and re-layouts: 0.03 us -> 0.65 us  [on_device(): block = block.transpose(1, 0, 2, 3).reshape(KINDS, pairs, quarter)]
    ppermute x12, waiting for transfers between devices: 15.9 us -> 15.4 us  [send_rel(): return lax.ppermute(block, axis, [(i, i ^ offset) for i in range(size)])]
  transfers between devices with their start and end apart: 12 -> 12, of which waited for: 11 -> 9; matrix products, arithmetic and copies ran while one was open for 1% -> 1% of each run, Pallas kernels for 5% -> 5%
where the time goes in v4:
time: 43.8 us; the launch traced here: 43.6 us
  starting transfers between devices  16.2 us (37%)
  waiting for transfers between devices  15.4 us (35%)
  Pallas kernels  7.07 us (16%)
  local copies, waits for them, and re-layouts  2.97 us (7%)
  other arithmetic  1.08 us (2%)
  between operations  0.75 us (2%)
    ppermute x12, starting transfers between devices, send_rel(): return lax.ppermute(block, axis, [(i, i ^ offset) for i in range(size)])  16.2 us
    ppermute x12, waiting for transfers between devices, send_rel(): return lax.ppermute(block, axis, [(i, i ^ offset) for i in range(size)])  15.4 us
    pallas_call x1, Pallas kernels, on_device(): pl.pallas_call(load_kernel, out_shape=[jax.ShapeDtypeStruct(x.shape, x.dt...  2.26 us
    unnamed x4, local copies, waits for them, and re-layouts  2.11 us
    pallas_call x1, Pallas kernels, on_device(): pl.pallas_call(expert_kernel, out_shape=[jax.ShapeDtypeStruct((rows, out_...  1.79 us
    pallas_call x1, Pallas kernels, on_device(): pl.pallas_call(functools.partial(select_kernel, experts), out_shape=[jax....  1.31 us
    pallas_call x1, Pallas kernels, on_device(): pl.pallas_call(finish_kernel, out_shape=[jax.ShapeDtypeStruct((tok_rows,...  0.95 us
    another operation x1, other arithmetic, on_device(): own = jnp.stack(blocks, axis=1).reshape(KINDS * rows, quarter)  0.89 us
  transfers between devices with their start and end apart: 12, of which 9 were waited for; matrix products, arithmetic and copies ran while one was open for 1% of the time, Pallas kernels for 5%

profile of v4, /device:TPU:0, one launch (start us, length us, event | category | flops | bytes accessed | tf_op | source)
XLA Modules:
  0.0 43.6 jit_solution(8753308942796442556)
XLA Ops:
  0.6 1.3 %select.1 = (f32[32,64]{1,0:T(8,128)S(1)}, bf16[16,896]{1,0:T(8,128)(2,1)S(1)}, bf16[16,896]{1,0:T(8,128)(2,1)S(1)}) custom-call(s32[8,64]{1,0:T(8,128)} %bitcast.30, s32[8,64]{1,0:T(8,128)} %bitcast.31, bf16[8,64]{1,0:T(8,128)(2,1)} %bitcast.32, bf16[64,1792]{1,0:T(8,128)(2,1)} %refs_3_.1, bf16[64,1792]{1,0:T(8,128)(2,1)} %refs_4_.1), custom_call_target="tpu_custom_call" | custom-call | tf_op jit(solution)/shard_map/select/pallas_call | solution.py:253
  1.9 2.5 %collective-permute-start = (bf16[16,896]{1,0:T(8,128)(2,1)S(1)}, bf16[16,896]{1,0:T(8,128)(2,1)S(1)}, u32[]{:S(2)}, u32[]{:S(2)}) collective-permute-start(bf16[16,896]{1,0:T(8,128)(2,1)S(1)} %get-tuple-element.36), channel_id=1, source_target_pairs={{0,9},{1,8},{8,1},{9,0},{16,25},{17,24},{24,17},{25,16},{2,11},{3,... | collective-permute-start | bytes 86024 | tf_op jit(solution)/shard_map/ppermute | solution.py:18
  4.5 1.7 %collective-permute-done = bf16[16,896]{1,0:T(8,128)(2,1)S(1)} collective-permute-done((bf16[16,896]{1,0:T(8,128)(2,1)S(1)}, bf16[16,896]{1,0:T(8,128)(2,1)S(1)}, u32[]{:S(2)}, u32[]{:S(2)}) %collective-permute-start) | collective-permute-done | bytes 28704 | tf_op jit(solution)/shard_map/ppermute | solution.py:18
  6.2 3.1 %collective-permute-start.1 = (bf16[16,896]{1,0:T(8,128)(2,1)S(1)}, bf16[16,896]{1,0:T(8,128)(2,1)S(1)}, u32[]{:S(2)}, u32[]{:S(2)}) collective-permute-start(bf16[16,896]{1,0:T(8,128)(2,1)S(1)} %pad_maximum_fusion.2), channel_id=1, source_target_pairs={{0,17},{1,16},{8,25},{9,24},{16,1},{17,0},{24,9},{25,8},{2,19},{3,... | collective-permute-start | bytes 86024 | tf_op jit(solution)/shard_map/ppermute | solution.py:18
  9.3 2.3 %load.1 = (bf16[3584,128]{1,0:T(8,128)(2,1)S(1)}, bf16[3584,128]{1,0:T(8,128)(2,1)S(1)}, bf16[128,3584]{1,0:T(8,128)(2,1)S(1)}, bf16[64,128]{1,0:T(8,128)(2,1)S(...) custom-call(bf16[16,896]{1,0:T(8,128)(2,1)S(1)} %get-tuple-element.29.refs_0_, ...), custom_call_target="tpu_custom_call" | custom-call | bytes 4276224 | tf_op jit(solution)/shard_map/load/pallas_call | solution.py:267
  11.6 0.9 %copy-done = bf16[128,3584]{1,0:T(8,128)(2,1)} copy-done((bf16[128,3584]{1,0:T(8,128)(2,1)}, bf16[128,3584]{1,0:T(8,128)(2,1)S(1)}, u32[]{:S(2)}) %copy-start) | copy-done | bytes 917528
  13.4 2.5 %collective-permute-start.4 = (bf16[4,8,896]{2,1,0:T(8,128)(2,1)}, bf16[4,8,896]{2,1,0:T(8,128)(2,1)S(1)}, u32[]{:S(2)}, u32[]{:S(2)}) collective-permute-start(bf16[4,8,896]{2,1,0:T(8,128)(2,1)} %reshape.19), channel_id=1, source_target_pairs={{0,7},{1,6},{2,5},{3,4},{4,3},{5,2},{6,1},{7,0},{8,15},{9,14},{10,... | collective-permute-start | bytes 172040 | tf_op jit(solution)/shard_map/ppermute | solution.py:18
  16.7 1.7 %collective-permute-done.4 = bf16[4,8,896]{2,1,0:T(8,128)(2,1)S(1)} collective-permute-done((bf16[4,8,896]{2,1,0:T(8,128)(2,1)}, bf16[4,8,896]{2,1,0:T(8,128)(2,1)S(1)}, u32[]{:S(2)}, u32[]{:S(2)}) %collective-permute-start.4) | collective-permute-done | bytes 57376 | tf_op jit(solution)/shard_map/ppermute | solution.py:18
  18.4 1.8 %collective-permute-done.3 = bf16[4,8,896]{2,1,0:T(8,128)(2,1)} collective-permute-done((bf16[4,8,896]{2,1,0:T(8,128)(2,1)}, bf16[4,8,896]{2,1,0:T(8,128)(2,1)}, u32[]{:S(2)}, u32[]{:S(2)}) %collective-permute-start.3) | collective-permute-done | bytes 57376 | tf_op jit(solution)/shard_map/ppermute | solution.py:18
  20.2 0.9 %pad_maximum_fusion = bf16[4,4,8,896]{3,2,1,0:T(8,128)(2,1)S(1)} fusion(bf16[4,1,8,896]{3,2,1,0:T(8,128)(2,1)S(1)} %bitcast.28, bf16[4,1,8,896]{3,2,1,0:T(8,128)(2,1)} %bitcast.13, bf16[4,1,8,896]{3,2,1,0:T(8,128)(2,1)} %bitcast.11, bf16[4,1,8,896]{3,2,1,0:T(8,128)(2,1)S(1)} %stack_reshape.3), kind=kLoop, calls=%fused_computation | loop fusion | flops 344064 | bytes 458752 | tf_op jit(solution)/shard_map/stack | solution.py:284
  21.4 1.2 %collective-permute-done.5.other_ref = bf16[128,896]{1,0:T(8,128)(2,1)S(1)} collective-permute-done((bf16[128,896]{1,0:T(8,128)(2,1)S(1)}, bf16[128,896]{1,0:T(8,128)(2,1)S(1)}, u32[]{:S(2)}, u32[]{:S(2)}) %collective-permute-start.5) | collective-permute-done | bytes 229408 | tf_op jit(solution)/shard_map/ppermute | solution.py:18
  22.6 1.2 %copy-done.1 = bf16[128,3584]{1,0:T(8,128)(2,1)S(1)} copy-done((bf16[128,3584]{1,0:T(8,128)(2,1)S(1)}, bf16[128,3584]{1,0:T(8,128)(2,1)}, u32[]{:S(2)}) %copy-start.1) | copy-done | bytes 917528
  23.8 1.8 %expert.1 = (bf16[32,1920]{1,0:T(8,128)(2,1)S(1)}, bf16[32,1920]{1,0:T(8,128)(2,1)S(1)}, bf16[8,3584]{1,0:T(8,128)(2,1)S(1)}) custom-call(bf16[128,896]{1,0:T(8,128)(2,1)S(1)} %bitcast.22, bf16[128,896]{1,0:T(8,128)(2,1)S(1)} %collective-permute-done.5.other_ref, bf16[3584,128]{1,0:T(8,128)(2,1)S(1)} %get-tuple-element.41.gate_w, ...), custom_call_target="tpu_custom_call" | custom-call | tf_op jit(solution)/shard_map/expert/pallas_call | solution.py:288
  25.9 1.1 %collective-permute-done.6.got_ref = bf16[32,1920]{1,0:T(8,128)(2,1)S(1)} collective-permute-done((bf16[32,1920]{1,0:T(8,128)(2,1)S(1)}, bf16[32,1920]{1,0:T(8,128)(2,1)S(1)}, u32[]{:S(2)}, u32[]{:S(2)}) %collective-permute-start.6) | collective-permute-done | bytes 122912 | tf_op jit(solution)/shard_map/ppermute | solution.py:18
  27.1 1.2 %collective-permute-start.7 = (bf16[8,1920]{1,0:T(8,128)(2,1)S(1)}, bf16[8,1920]{1,0:T(8,128)(2,1)S(1)}, u32[]{:S(2)}, u32[]{:S(2)}) collective-permute-start(bf16[8,1920]{1,0:T(8,128)(2,1)S(1)} %get-tuple-element.48), channel_id=1, source_target_pairs={{0,3},{1,2},{2,1},{3,0},{4,7},{5,6},{6,5},{7,4},{8,11},{9,10},{10,... | collective-permute-start | bytes 92168 | tf_op jit(solution)/shard_map/ppermute | solution.py:18
  28.3 0.9 %collective-permute-start.8 = (bf16[8,1920]{1,0:T(8,128)(2,1)S(1)}, bf16[8,1920]{1,0:T(8,128)(2,1)S(1)}, u32[]{:S(2)}, u32[]{:S(2)}) collective-permute-start(bf16[8,1920]{1,0:T(8,128)(2,1)S(1)} %get-tuple-element.49), channel_id=1, source_target_pairs={{0,5},{1,4},{2,7},{3,6},{4,1},{5,0},{6,3},{7,2},{8,13},{9,12},{10,... | collective-permute-start | bytes 92168 | tf_op jit(solution)/shard_map/ppermute | solution.py:18
  29.1 1.1 %collective-permute-start.9 = (bf16[8,1920]{1,0:T(8,128)(2,1)S(1)}, bf16[8,1920]{1,0:T(8,128)(2,1)S(1)}, u32[]{:S(2)}, u32[]{:S(2)}) collective-permute-start(bf16[8,1920]{1,0:T(8,128)(2,1)S(1)} %get-tuple-element.50), channel_id=1, source_target_pairs={{0,7},{1,6},{2,5},{3,4},{4,3},{5,2},{6,1},{7,0},{8,15},{9,14},{10,... | collective-permute-start | bytes 92168 | tf_op jit(solution)/shard_map/ppermute | solution.py:18
  30.5 1.2 %collective-permute-done.8.refs_2_ = bf16[8,1920]{1,0:T(8,128)(2,1)S(1)} collective-permute-done((bf16[8,1920]{1,0:T(8,128)(2,1)S(1)}, bf16[8,1920]{1,0:T(8,128)(2,1)S(1)}, u32[]{:S(2)}, u32[]{:S(2)}) %collective-permute-start.8) | collective-permute-done | bytes 30752 | tf_op jit(solution)/shard_map/ppermute | solution.py:18
  31.6 1.7 %collective-permute-done.9.refs_3_ = bf16[8,1920]{1,0:T(8,128)(2,1)S(1)} collective-permute-done((bf16[8,1920]{1,0:T(8,128)(2,1)S(1)}, bf16[8,1920]{1,0:T(8,128)(2,1)S(1)}, u32[]{:S(2)}, u32[]{:S(2)}) %collective-permute-start.9) | collective-permute-done | bytes 30752 | tf_op jit(solution)/shard_map/ppermute | solution.py:18
  34.1 1.8 %collective-permute-start.10 = (bf16[4,1920]{1,0:T(4,128)(2,1)S(1)}, bf16[4,1920]{1,0:T(4,128)(2,1)S(1)}, u32[]{:S(2)}, u32[]{:S(2)}) collective-permute-start(bf16[4,1920]{1,0:T(4,128)(2,1)S(1)} %pad_maximum_fusion.3), channel_id=1, source_target_pairs={{0,8},{8,0},{16,24},{24,16},{1,9},{9,1},{17,25},{25,17},{2,10},{10... | collective-permute-start | bytes 46088 | tf_op jit(solution)/shard_map/ppermute | solution.py:18
  35.8 2.0 %collective-permute-done.10 = bf16[4,1920]{1,0:T(4,128)(2,1)S(1)} collective-permute-done((bf16[4,1920]{1,0:T(4,128)(2,1)S(1)}, bf16[4,1920]{1,0:T(4,128)(2,1)S(1)}, u32[]{:S(2)}, u32[]{:S(2)}) %collective-permute-start.10) | collective-permute-done | bytes 15392 | tf_op jit(solution)/shard_map/ppermute | solution.py:18
  37.9 1.7 %collective-permute-start.11 = (bf16[4,1920]{1,0:T(4,128)(2,1)S(1)}, bf16[4,1920]{1,0:T(4,128)(2,1)S(1)}, u32[]{:S(2)}, u32[]{:S(2)}) collective-permute-start(bf16[4,1920]{1,0:T(4,128)(2,1)S(1)} %pad_maximum_fusion.4), channel_id=1, source_target_pairs={{0,16},{8,24},{16,0},{24,8},{1,17},{9,25},{17,1},{25,9},{2,18},{10... | collective-permute-start | bytes 46088 | tf_op jit(solution)/shard_map/ppermute | solution.py:18
  39.6 3.0 %collective-permute-done.11 = bf16[4,1920]{1,0:T(4,128)(2,1)S(1)} collective-permute-done((bf16[4,1920]{1,0:T(4,128)(2,1)S(1)}, bf16[4,1920]{1,0:T(4,128)(2,1)S(1)}, u32[]{:S(2)}, u32[]{:S(2)}) %collective-permute-start.11) | collective-permute-done | bytes 15392 | tf_op jit(solution)/shard_map/ppermute | solution.py:18
  42.7 1.0 %finish.1 = (bf16[64,1792]{1,0:T(8,128)(2,1)}, f32[64,128]{1,0:T(8,128)}) custom-call(f32[32,64]{1,0:T(8,128)S(1)} %get-tuple-element.28.hit_ref, bf16[8,1920]{1,0:T(8,128)(2,1)S(1)} %pad_maximum_fusion.1.home_ref), custom_call_target="tpu_custom_call" | custom-call | tf_op jit(solution)/shard_map/finish/pallas_call | solution.py:325
  (30 shorter events, 3.5 us)
Async XLA Ops:
  1.9 4.2 %collective-permute-start = (bf16[16,896]{1,0:T(8,128)(2,1)S(1)}, bf16[16,896]{1,0:T(8,128)(2,1)S(1)}, u32[]{:S(2)}, u32[]{:S(2)}) collective-permute-start(bf16[16,896]{1,0:T(8,128)(2,1)S(1)} %get-tuple-element.36), channel_id=1, source_target_pairs={{0,9},{1,8},{8,1},{9,0},{16,25},{17,24},{24,17},{25,16},{2,11},{3,... | collective-permute-start | bytes 86024 | tf_op jit(solution)/shard_map/ppermute | solution.py:18
  6.2 6.3 %collective-permute-start.1 = (bf16[16,896]{1,0:T(8,128)(2,1)S(1)}, bf16[16,896]{1,0:T(8,128)(2,1)S(1)}, u32[]{:S(2)}, u32[]{:S(2)}) collective-permute-start(bf16[16,896]{1,0:T(8,128)(2,1)S(1)} %pad_maximum_fusion.2), channel_id=1, source_target_pairs={{0,17},{1,16},{8,25},{9,24},{16,1},{17,0},{24,9},{25,8},{2,19},{3,... | collective-permute-start | bytes 86024 | tf_op jit(solution)/shard_map/ppermute | solution.py:18
  11.6 0.9 %copy-start = (bf16[128,3584]{1,0:T(8,128)(2,1)}, bf16[128,3584]{1,0:T(8,128)(2,1)S(1)}, u32[]{:S(2)}) copy-start(bf16[128,3584]{1,0:T(8,128)(2,1)S(1)} %get-tuple-element.43.down_w) | copy-start | bytes 2752516
  13.4 5.0 %collective-permute-start.4 = (bf16[4,8,896]{2,1,0:T(8,128)(2,1)}, bf16[4,8,896]{2,1,0:T(8,128)(2,1)S(1)}, u32[]{:S(2)}, u32[]{:S(2)}) collective-permute-start(bf16[4,8,896]{2,1,0:T(8,128)(2,1)} %reshape.19), channel_id=1, source_target_pairs={{0,7},{1,6},{2,5},{3,4},{4,3},{5,2},{6,1},{7,0},{8,15},{9,14},{10,... | collective-permute-start | bytes 172040 | tf_op jit(solution)/shard_map/ppermute | solution.py:18
  15.9 4.3 %collective-permute-start.3 = (bf16[4,8,896]{2,1,0:T(8,128)(2,1)}, bf16[4,8,896]{2,1,0:T(8,128)(2,1)}, u32[]{:S(2)}, u32[]{:S(2)}) collective-permute-start(bf16[4,8,896]{2,1,0:T(8,128)(2,1)} %reshape.19), channel_id=1, source_target_pairs={{0,5},{1,4},{2,7},{3,6},{4,1},{5,0},{6,3},{7,2},{8,13},{9,12},{10,... | collective-permute-start | bytes 172040 | tf_op jit(solution)/shard_map/ppermute | solution.py:18
  16.1 4.1 %collective-permute-start.2 = (bf16[4,8,896]{2,1,0:T(8,128)(2,1)}, bf16[4,8,896]{2,1,0:T(8,128)(2,1)}, u32[]{:S(2)}, u32[]{:S(2)}) collective-permute-start(bf16[4,8,896]{2,1,0:T(8,128)(2,1)} %reshape.19), channel_id=1, source_target_pairs={{0,3},{1,2},{2,1},{3,0},{4,7},{5,6},{6,5},{7,4},{8,11},{9,10},{10,... | collective-permute-start | bytes 172040 | tf_op jit(solution)/shard_map/ppermute | solution.py:18
  21.0 1.6 %collective-permute-start.5 = (bf16[128,896]{1,0:T(8,128)(2,1)S(1)}, bf16[128,896]{1,0:T(8,128)(2,1)S(1)}, u32[]{:S(2)}, u32[]{:S(2)}) collective-permute-start(bf16[128,896]{1,0:T(8,128)(2,1)S(1)} %bitcast.21), channel_id=1, source_target_pairs={{0,1},{1,0},{2,3},{3,2},{4,5},{5,4},{6,7},{7,6},{8,9},{9,8},{10,11... | collective-permute-start | bytes 688136 | tf_op jit(solution)/shard_map/ppermute | solution.py:18
  22.6 1.2 %copy-start.1 = (bf16[128,3584]{1,0:T(8,128)(2,1)S(1)}, bf16[128,3584]{1,0:T(8,128)(2,1)}, u32[]{:S(2)}) copy-start(bf16[128,3584]{1,0:T(8,128)(2,1)} %copy-done) | copy-start | bytes 2752516
  25.6 1.4 %collective-permute-start.6 = (bf16[32,1920]{1,0:T(8,128)(2,1)S(1)}, bf16[32,1920]{1,0:T(8,128)(2,1)S(1)}, u32[]{:S(2)}, u32[]{:S(2)}) collective-permute-start(bf16[32,1920]{1,0:T(8,128)(2,1)S(1)} %get-tuple-element.46), channel_id=1, source_target_pairs={{0,1},{1,0},{2,3},{3,2},{4,5},{5,4},{6,7},{7,6},{8,9},{9,8},{10,11... | collective-permute-start | bytes 368648 | tf_op jit(solution)/shard_map/ppermute | solution.py:18
  27.1 3.3 %collective-permute-start.7 = (bf16[8,1920]{1,0:T(8,128)(2,1)S(1)}, bf16[8,1920]{1,0:T(8,128)(2,1)S(1)}, u32[]{:S(2)}, u32[]{:S(2)}) collective-permute-start(bf16[8,1920]{1,0:T(8,128)(2,1)S(1)} %get-tuple-element.48), channel_id=1, source_target_pairs={{0,3},{1,2},{2,1},{3,0},{4,7},{5,6},{6,5},{7,4},{8,11},{9,10},{10,... | collective-permute-start | bytes 92168 | tf_op jit(solution)/shard_map/ppermute | solution.py:18
  28.3 3.3 %collective-permute-start.8 = (bf16[8,1920]{1,0:T(8,128)(2,1)S(1)}, bf16[8,1920]{1,0:T(8,128)(2,1)S(1)}, u32[]{:S(2)}, u32[]{:S(2)}) collective-permute-start(bf16[8,1920]{1,0:T(8,128)(2,1)S(1)} %get-tuple-element.49), channel_id=1, source_target_pairs={{0,5},{1,4},{2,7},{3,6},{4,1},{5,0},{6,3},{7,2},{8,13},{9,12},{10,... | collective-permute-start | bytes 92168 | tf_op jit(solution)/shard_map/ppermute | solution.py:18
  29.1 4.2 %collective-permute-start.9 = (bf16[8,1920]{1,0:T(8,128)(2,1)S(1)}, bf16[8,1920]{1,0:T(8,128)(2,1)S(1)}, u32[]{:S(2)}, u32[]{:S(2)}) collective-permute-start(bf16[8,1920]{1,0:T(8,128)(2,1)S(1)} %get-tuple-element.50), channel_id=1, source_target_pairs={{0,7},{1,6},{2,5},{3,4},{4,3},{5,2},{6,1},{7,0},{8,15},{9,14},{10,... | collective-permute-start | bytes 92168 | tf_op jit(solution)/shard_map/ppermute | solution.py:18
  34.1 3.8 %collective-permute-start.10 = (bf16[4,1920]{1,0:T(4,128)(2,1)S(1)}, bf16[4,1920]{1,0:T(4,128)(2,1)S(1)}, u32[]{:S(2)}, u32[]{:S(2)}) collective-permute-start(bf16[4,1920]{1,0:T(4,128)(2,1)S(1)} %pad_maximum_fusion.3), channel_id=1, source_target_pairs={{0,8},{8,0},{16,24},{24,16},{1,9},{9,1},{17,25},{25,17},{2,10},{10... | collective-permute-start | bytes 46088 | tf_op jit(solution)/shard_map/ppermute | solution.py:18
  37.9 4.7 %collective-permute-start.11 = (bf16[4,1920]{1,0:T(4,128)(2,1)S(1)}, bf16[4,1920]{1,0:T(4,128)(2,1)S(1)}, u32[]{:S(2)}, u32[]{:S(2)}) collective-permute-start(bf16[4,1920]{1,0:T(4,128)(2,1)S(1)} %pad_maximum_fusion.4), channel_id=1, source_target_pairs={{0,16},{8,24},{16,0},{24,8},{1,17},{9,25},{17,1},{25,9},{2,18},{10... | collective-permute-start | bytes 46088 | tf_op jit(solution)/shard_map/ppermute | solution.py:18

commit v5 on v4

--- a/solution.py
+++ b/solution.py
@@ -22,27 +22,28 @@
     return send_rel(block, (axis, "test"), offset * lax.axis_size("test") + 1)
 
 
-def split_order(count):
-    return list(range(0, count, 2)) + list(range(1, count, 2))
-
-
-def exchange(send, stay, go, unit, count):
-    order = split_order(count)
-    half = count // 2
-    slots = {}
-    for index, k in enumerate(order[:half]):
-        slots[k] = stay[index * unit : (index + 1) * unit]
-    got = send(go, "expert", 1)
-    for index, k in enumerate(order[half:]):
-        slots[k] = got[index * unit : (index + 1) * unit]
-    bit = 2
+def is_direct(count):
+    return count <= 4
+
+
+def slot_order(count):
+    slots = list(range(count))
+    return slots if is_direct(count) else slots[::2] + slots[1::2]
+
+
+def exchange(send, parts, count):
+    slots = dict(zip(slot_order(count), parts))
+    if is_direct(count):
+        return [slots[0]] + [send(slots[k], "expert", k) for k in range(1, count)]
+    unit = parts[0].shape[0]
+    bit = 1
     while bit < count:
         moving = [k for k in range(count) if k & bit]
         got = send(jnp.concatenate([slots[k] for k in moving]), "expert", bit)
         for index, k in enumerate(moving):
             slots[k] = got[index * unit : (index + 1) * unit]
         bit *= 2
-    return slots
+    return [slots[k] for k in range(count)]
 
 
 def keep_in_hbm(array):
@@ -88,16 +89,18 @@
 
 
 def select_kernel(experts, *refs):
-    sources, (hit_ref, *out_refs) = refs[:5], refs[5:8]
-    ids, slots, weight, tok, grad, sems = refs[8:]
+    sources, (hit_ref, *out_refs) = refs[:5], refs[5:-6]
+    ids, slots, weight, tok, grad, sems = refs[-6:]
     copies = start_copies(zip(sources, (ids, slots, weight, tok, grad)), sems)
     here = lax.axis_index("expert")
     unit = KINDS * CAP
     quarter = tok.shape[1] // 2
     row = lax.broadcasted_iota(jnp.int32, (experts * unit, 1), 0)
     kind = (row % unit) // CAP
-    turn = 2 * (row // unit)
-    want = ((turn % experts + turn // experts) ^ here) * CAP + row % CAP
+    turn = row // unit
+    if not is_direct(experts):
+        turn = 2 * turn % experts + 2 * turn // experts
+    want = (turn ^ here) * CAP + row % CAP
     for copy in copies[:3]:
         copy.wait()
     hits, scaled = hit_tables(ids[...], slots[...], weight[...].astype(F32), want, experts)
@@ -112,9 +115,8 @@
         part = dot_f32(left, source[:, first : first + quarter], ((1,), (0,)))
         total = part if total is None else total + part
     total = total.astype(BF16)
-    sent = experts * unit // 2
-    out_refs[0][...] = total[:sent]
-    out_refs[1][...] = total[sent:]
+    for k, out_ref in enumerate(out_refs):
+        out_ref[...] = total[k * unit : (k + 1) * unit]
 
 
 def load_kernel(*refs):
@@ -132,6 +134,21 @@
     value = value.astype(F32)
     middle = value.shape[1] // 2
     return value[:, :middle] + value[:, middle:]
+
+
+def load(after, params, compiler_params):
+    with jax.named_scope("load"):
+        return pl.pallas_call(
+            load_kernel,
+            out_shape=[jax.ShapeDtypeStruct(x.shape, x.dtype) for x in params],
+            in_specs=whole_vmem(1) + in_hbm(len(params)),
+            out_specs=whole_vmem(len(params)),
+            scratch_shapes=[pltpu.SemaphoreType.DMA((len(params),))],
+            compiler_params=compiler_params,
+            cost_estimate=pl.CostEstimate(
+                flops=0, bytes_accessed=sum(2 * x.size for x in params), transcendentals=0
+            ),
+        )(after, *map(keep_in_hbm, params))
 
 
 def expert_kernel(
@@ -144,10 +161,12 @@
     near, far = pl.multiple_of(core * half, 128), pl.multiple_of((1 - core) * half, 128)
     row = lax.broadcasted_iota(jnp.int32, (rows, quarter), 0)
     odd = jnp.where(row >= pairs, 1, 0)
-    bits = (row % pairs) // CAP
-    for _ in range(max(1, (pairs // CAP - 1).bit_length())):
-        odd = odd ^ (bits & 1)
-        bits = bits // 2
+    slot = (row % pairs) // CAP
+    if is_direct(pairs // CAP):
+        odd = odd ^ jnp.where(slot > 0, 1, 0)
+    else:
+        for shift in range((pairs // CAP - 1).bit_length()):
+            odd = odd ^ ((slot >> shift) & 1)
     odd = odd == 1
     for index in range(KINDS):
         target = x_in if index < 2 else x_grad
@@ -250,39 +269,27 @@
     ids_t, slots_t, weight_t = route_ids.T, route_slots.T, route_weight.T
 
     with jax.named_scope("select"):
-        hits, stay, go = pl.pallas_call(
+        hits, *parts = pl.pallas_call(
             functools.partial(select_kernel, experts),
             out_shape=[jax.ShapeDtypeStruct((experts * unit, tok_rows), F32)]
-            + [jax.ShapeDtypeStruct((experts * unit // 2, quarter), BF16)] * 2,
+            + [jax.ShapeDtypeStruct((unit, quarter), BF16)] * experts,
             in_specs=in_hbm(5),
-            out_specs=whole_vmem(3),
+            out_specs=whole_vmem(experts + 1),
             scratch_shapes=[
                 pltpu.VMEM(x.shape, x.dtype) for x in (ids_t, slots_t, weight_t, tokens, out_grad)
             ]
             + [pltpu.SemaphoreType.DMA((5,))],
             compiler_params=limit(rows),
         )(*map(keep_in_hbm, (ids_t, slots_t, weight_t, tokens, out_grad)))
-    params = [w_gate[0], w_up[0], w_down[0], proj_hidden[0], proj_grad[0], test_feats[0]]
-    with jax.named_scope("load"):
-        loaded = pl.pallas_call(
-            load_kernel,
-            out_shape=[jax.ShapeDtypeStruct(x.shape, x.dtype) for x in params],
-            in_specs=whole_vmem(1) + in_hbm(len(params)),
-            out_specs=whole_vmem(len(params)),
-            scratch_shapes=[pltpu.SemaphoreType.DMA((len(params),))],
-            compiler_params=limit(rows),
-            cost_estimate=pl.CostEstimate(
-                flops=0, bytes_accessed=sum(2 * x.size for x in params), transcendentals=0
-            ),
-        )(stay, *map(keep_in_hbm, params))
-    slots = exchange(send_cross, stay, go, unit, experts)
-    loaded, slots = lax.optimization_barrier((loaded, slots))
-    gate_w, up_w, down_w, hid_proj, grad_proj, test_rows = loaded
-    block = jnp.stack([slots[k] for k in range(experts)]).reshape(experts, KINDS, CAP, quarter)
+    slots = exchange(send_cross, parts, experts)
+    block = jnp.stack(slots).reshape(experts, KINDS, CAP, quarter)
     block = block.transpose(1, 0, 2, 3).reshape(KINDS, pairs, quarter)
     blocks = [block] + [send_cross(block, "dp", g) for g in range(1, groups)]
     own = jnp.stack(blocks, axis=1).reshape(KINDS * rows, quarter)
     other = send_rel(own, "test", 1)
+    gate_w, up_w, down_w, hid_proj = load(
+        own, [w_gate[0], w_up[0], w_down[0], proj_hidden[0]], limit(rows)
+    )
 
     with jax.named_scope("expert"):
         keep, send, mine = pl.pallas_call(
@@ -298,6 +305,7 @@
             compiler_params=limit(rows),
         )(own, other, gate_w, up_w, down_w, hid_proj)
     got = send_rel(send, "test", 1)
+    grad_proj, test_rows = load(send, [proj_grad[0], test_feats[0]], limit(rows))
     with jax.named_scope("pair"):
         sums = pl.pallas_call(
             functools.partial(pair_kernel, half),
@@ -317,9 +325,8 @@
             scratch_shapes=[pltpu.VMEM((pairs, proj * proj), BF16)],
             compiler_params=limit(rows),
         )(*pieces, grad_mine, test_rows)
-    order = split_order(experts)
-    back = jnp.concatenate([back[k * CAP : (k + 1) * CAP] for k in order])
-    slots = exchange(send_rel, back[: pairs // 2], back[pairs // 2 :], CAP, experts)
+    order = slot_order(experts)
+    slots = exchange(send_rel, [back[k * CAP : (k + 1) * CAP] for k in order], experts)
     home = jnp.concatenate([slots[k] for k in order])
     with jax.named_scope("finish"):
         return pl.pallas_call(

time: 43.8 us -> 39.2 us (0.89)
  local copies, waits for them, and re-layouts: 2.97 us -> 0.2 us
  waiting for transfers between devices: 15.4 us -> 13.3 us
  other arithmetic: 1.08 us -> 0.18 us
  Pallas kernels: 7.07 us -> 7.96 us
    unnamed x4 -> x0, local copies, waits for them, and re-layouts: 2.11 us -> none
    ppermute x12 -> x14, waiting for transfers between devices: 15.4 us -> 13.3 us  [send_rel(): return lax.ppermute(block, axis, [(i, i ^ offset) for i in range(size)])]
    pallas_call x1 -> x2, Pallas kernels: 2.26 us -> 3.15 us  [load(): pl.pallas_call(load_kernel, out_shape=[jax.ShapeDtypeStruct(x.shape, x.dt...]
    another operation x1, other arithmetic: 0.89 us -> 0.04 us  [on_device(): own = jnp.stack(blocks, axis=1).reshape(KINDS * rows, quarter)]
    reshape x1, local copies, waits for them, and re-layouts: 0.65 us -> 0.03 us  [on_device(): block = block.transpose(1, 0, 2, 3).reshape(KINDS, pairs, quarter)]
    ppermute x12 -> x14, starting transfers between devices: 16.2 us -> 16.4 us  [send_rel(): return lax.ppermute(block, axis, [(i, i ^ offset) for i in range(size)])]
  transfers between devices with their start and end apart: 12 -> 14, of which waited for: 9 -> 10; matrix products, arithmetic and copies ran while one was open for 1% -> 1% of each run, Pallas kernels for 5% -> 8%
where the time goes in v5:
time: 39.2 us; the launch traced here: 39 us
  starting transfers between devices  16.4 us (42%)
  waiting for transfers between devices  13.3 us (34%)
  Pallas kernels  7.96 us (20%)
  between operations  0.75 us (2%)
    ppermute x14, starting transfers between devices, send_rel(): return lax.ppermute(block, axis, [(i, i ^ offset) for i in range(size)])  16.4 us
    ppermute x14, waiting for transfers between devices, send_rel(): return lax.ppermute(block, axis, [(i, i ^ offset) for i in range(size)])  13.3 us
    pallas_call x2, Pallas kernels, load(): pl.pallas_call(load_kernel, out_shape=[jax.ShapeDtypeStruct(x.shape, x.dt...  3.15 us
    pallas_call x1, Pallas kernels, on_device(): pl.pallas_call(expert_kernel, out_shape=[jax.ShapeDtypeStruct((rows, out_...  1.78 us
    pallas_call x1, Pallas kernels, on_device(): pl.pallas_call(functools.partial(select_kernel, experts), out_shape=[jax....  1.31 us
    pallas_call x1, Pallas kernels, on_device(): pl.pallas_call(finish_kernel, out_shape=[jax.ShapeDtypeStruct((tok_rows,...  0.95 us
  transfers between devices with their start and end apart: 14, of which 10 were waited for; matrix products, arithmetic and copies ran while one was open for 1% of the time, Pallas kernels for 8%

profile of v5, /device:TPU:0, one launch (start us, length us, event | category | flops | bytes accessed | tf_op | source)
XLA Modules:
  0.0 39.0 jit_solution(9061353932763635770)
XLA Ops:
  0.6 1.3 %select.1 = (f32[32,64]{1,0:T(8,128)S(1)}, bf16[8,896]{1,0:T(8,128)(2,1)S(1)}, bf16[8,896]{1,0:T(8,128)(2,1)S(1)}, bf16[8,896]{1,0:T(8,128)(2,1)S(1)}, bf16[8,896]{1,0:T(8,128)(2,1)S(1)}) custom-call(s32[8,64]{1,0:T(8,128)} %bitcast.33, s32[8,64]{1,0:T(8,128)} %bitcast.34, bf16[8,64]{1,0:T(8,128)(2,1)} %bitcast.35, bf16[64,1792]{1,0:T(8,128)(2,1)} %refs_3_.1, ...), custom_call_target="tpu_custom_call" | custom-call | tf_op jit(solution)/shard_map/select/pallas_call | solution.py:272
  1.9 2.5 %collective-permute-start = (bf16[8,896]{1,0:T(8,128)(2,1)S(1)}, bf16[8,896]{1,0:T(8,128)(2,1)S(1)}, u32[]{:S(2)}, u32[]{:S(2)}) collective-permute-start(bf16[8,896]{1,0:T(8,128)(2,1)S(1)} %get-tuple-element.22), channel_id=1, source_target_pairs={{0,9},{1,8},{8,1},{9,0},{16,25},{17,24},{24,17},{25,16},{2,11},{3,... | collective-permute-start | bytes 43016 | tf_op jit(solution)/shard_map/ppermute | solution.py:18
  4.5 2.9 %collective-permute-start.1 = (bf16[8,896]{1,0:T(8,128)(2,1)S(1)}, bf16[8,896]{1,0:T(8,128)(2,1)S(1)}, u32[]{:S(2)}, u32[]{:S(2)}) collective-permute-start(bf16[8,896]{1,0:T(8,128)(2,1)S(1)} %get-tuple-element.23), channel_id=1, source_target_pairs={{0,17},{1,16},{8,25},{9,24},{16,1},{17,0},{24,9},{25,8},{2,19},{3,... | collective-permute-start | bytes 43016 | tf_op jit(solution)/shard_map/ppermute | solution.py:18
  7.4 1.4 %collective-permute-done.1 = bf16[8,896]{1,0:T(8,128)(2,1)S(1)} collective-permute-done((bf16[8,896]{1,0:T(8,128)(2,1)S(1)}, bf16[8,896]{1,0:T(8,128)(2,1)S(1)}, u32[]{:S(2)}, u32[]{:S(2)}) %collective-permute-start.1) | collective-permute-done | bytes 14368 | tf_op jit(solution)/shard_map/ppermute | solution.py:18
  8.8 3.6 %collective-permute-done.2 = bf16[8,896]{1,0:T(8,128)(2,1)S(1)} collective-permute-done((bf16[8,896]{1,0:T(8,128)(2,1)S(1)}, bf16[8,896]{1,0:T(8,128)(2,1)S(1)}, u32[]{:S(2)}, u32[]{:S(2)}) %collective-permute-start.2) | collective-permute-done | bytes 14368 | tf_op jit(solution)/shard_map/ppermute | solution.py:18
  12.6 2.2 %collective-permute-start.5 = (bf16[4,8,896]{2,1,0:T(8,128)(2,1)S(1)}, bf16[4,8,896]{2,1,0:T(8,128)(2,1)S(1)}, u32[]{:S(2)}, u32[]{:S(2)}) collective-permute-start(bf16[4,8,896]{2,1,0:T(8,128)(2,1)S(1)} %reshape.19), channel_id=1, source_target_pairs={{0,7},{1,6},{2,5},{3,4},{4,3},{5,2},{6,1},{7,0},{8,15},{9,14},{10,... | collective-permute-start | bytes 172040 | tf_op jit(solution)/shard_map/ppermute | solution.py:18
  14.9 0.5 %collective-permute-start.4 = (bf16[4,8,896]{2,1,0:T(8,128)(2,1)S(1)}, bf16[4,8,896]{2,1,0:T(8,128)(2,1)S(1)}, u32[]{:S(2)}, u32[]{:S(2)}) collective-permute-start(bf16[4,8,896]{2,1,0:T(8,128)(2,1)S(1)} %reshape.19), channel_id=1, source_target_pairs={{0,5},{1,4},{2,7},{3,6},{4,1},{5,0},{6,3},{7,2},{8,13},{9,12},{10,... | collective-permute-start | bytes 172040 | tf_op jit(solution)/shard_map/ppermute | solution.py:18
  15.7 1.9 %collective-permute-done.5 = bf16[4,8,896]{2,1,0:T(8,128)(2,1)S(1)} collective-permute-done((bf16[4,8,896]{2,1,0:T(8,128)(2,1)S(1)}, bf16[4,8,896]{2,1,0:T(8,128)(2,1)S(1)}, u32[]{:S(2)}, u32[]{:S(2)}) %collective-permute-start.5) | collective-permute-done | bytes 57376 | tf_op jit(solution)/shard_map/ppermute | solution.py:18
  17.5 1.0 %collective-permute-done.4 = bf16[4,8,896]{2,1,0:T(8,128)(2,1)S(1)} collective-permute-done((bf16[4,8,896]{2,1,0:T(8,128)(2,1)S(1)}, bf16[4,8,896]{2,1,0:T(8,128)(2,1)S(1)}, u32[]{:S(2)}, u32[]{:S(2)}) %collective-permute-start.4) | collective-permute-done | bytes 57376 | tf_op jit(solution)/shard_map/ppermute | solution.py:18
  18.5 0.8 %collective-permute-done.3 = bf16[4,8,896]{2,1,0:T(8,128)(2,1)S(1)} collective-permute-done((bf16[4,8,896]{2,1,0:T(8,128)(2,1)S(1)}, bf16[4,8,896]{2,1,0:T(8,128)(2,1)S(1)}, u32[]{:S(2)}, u32[]{:S(2)}) %collective-permute-start.3) | collective-permute-done | bytes 57376 | tf_op jit(solution)/shard_map/ppermute | solution.py:18
  19.6 1.8 %load.2 = (bf16[3584,128]{1,0:T(8,128)(2,1)S(1)}, bf16[3584,128]{1,0:T(8,128)(2,1)S(1)}, bf16[128,3584]{1,0:T(8,128)(2,1)S(1)}, bf16[64,128]{1,0:T(8,128)(2,1)S(1)}) custom-call(bf16[128,896]{1,0:T(8,128)(2,1)S(1)} %bitcast.22, bf16[3584,128]{1,0:T(8,128)(2,1)} %bitcast.25, bf16[3584,128]{1,0:T(8,128)(2,1)} %bitcast.26, bf16[128,3584]{1,0:T(8,128)(2,1)} %bitcast.27, ...), custom_call_target="tpu_custom_call" | custom-call | bytes 2768896 | tf_op jit(solution)/shard_map/load/pallas_call | solution.py:141
  21.4 1.8 %expert.1 = (bf16[32,1920]{1,0:T(8,128)(2,1)S(1)}, bf16[32,1920]{1,0:T(8,128)(2,1)S(1)}, bf16[8,3584]{1,0:T(8,128)(2,1)S(1)}) custom-call(bf16[128,896]{1,0:T(8,128)(2,1)S(1)} %bitcast.23, bf16[128,896]{1,0:T(8,128)(2,1)S(1)} %collective-permute-done.6.other_ref, bf16[3584,128]{1,0:T(8,128)(2,1)S(1)} %get-tuple-element.25.gate_w, ...), custom_call_target="tpu_custom_call" | custom-call | tf_op jit(solution)/shard_map/expert/pallas_call | solution.py:295
  23.2 0.5 %collective-permute-start.7 = (bf16[32,1920]{1,0:T(8,128)(2,1)S(1)}, bf16[32,1920]{1,0:T(8,128)(2,1)S(1)}, u32[]{:S(2)}, u32[]{:S(2)}) collective-permute-start(bf16[32,1920]{1,0:T(8,128)(2,1)S(1)} %get-tuple-element.30.refs_0_), channel_id=1, source_target_pairs={{0,1},{1,0},{2,3},{3,2},{4,5},{5,4},{6,7},{7,6},{8,9},{9,8},{10,11... | collective-permute-start | bytes 368648 | tf_op jit(solution)/shard_map/ppermute | solution.py:18
  23.6 1.4 %load.3 = (bf16[64,3584]{1,0:T(8,128)(2,1)S(1)}, bf16[128,4096]{1,0:T(8,128)(2,1)S(1)}) custom-call(bf16[32,1920]{1,0:T(8,128)(2,1)S(1)} %get-tuple-element.30.refs_0_, bf16[64,3584]{1,0:T(8,128)(2,1)} %bitcast.28, bf16[128,4096]{1,0:T(8,128)(2,1)} %bitcast.24), custom_call_target="tpu_custom_call" | custom-call | bytes 1507328 | tf_op jit(solution)/shard_map/load/pallas_call | solution.py:141
  25.2 0.8 %collective-permute-start.8 = (bf16[8,1920]{1,0:T(8,128)(2,1)S(1)}, bf16[8,1920]{1,0:T(8,128)(2,1)S(1)}, u32[]{:S(2)}, u32[]{:S(2)}) collective-permute-start(bf16[8,1920]{1,0:T(8,128)(2,1)S(1)} %get-tuple-element.32), channel_id=1, source_target_pairs={{0,3},{1,2},{2,1},{3,0},{4,7},{5,6},{6,5},{7,4},{8,11},{9,10},{10,... | collective-permute-start | bytes 92168 | tf_op jit(solution)/shard_map/ppermute | solution.py:18
  26.0 1.0 %collective-permute-start.9 = (bf16[8,1920]{1,0:T(8,128)(2,1)S(1)}, bf16[8,1920]{1,0:T(8,128)(2,1)S(1)}, u32[]{:S(2)}, u32[]{:S(2)}) collective-permute-start(bf16[8,1920]{1,0:T(8,128)(2,1)S(1)} %get-tuple-element.33), channel_id=1, source_target_pairs={{0,5},{1,4},{2,7},{3,6},{4,1},{5,0},{6,3},{7,2},{8,13},{9,12},{10,... | collective-permute-start | bytes 92168 | tf_op jit(solution)/shard_map/ppermute | solution.py:18
  27.0 1.1 %collective-permute-start.10 = (bf16[8,1920]{1,0:T(8,128)(2,1)S(1)}, bf16[8,1920]{1,0:T(8,128)(2,1)S(1)}, u32[]{:S(2)}, u32[]{:S(2)}) collective-permute-start(bf16[8,1920]{1,0:T(8,128)(2,1)S(1)} %get-tuple-element.34), channel_id=1, source_target_pairs={{0,7},{1,6},{2,5},{3,4},{4,3},{5,2},{6,1},{7,0},{8,15},{9,14},{10,... | collective-permute-start | bytes 92168 | tf_op jit(solution)/shard_map/ppermute | solution.py:18
  28.6 0.8 %collective-permute-done.9.refs_2_ = bf16[8,1920]{1,0:T(8,128)(2,1)S(1)} collective-permute-done((bf16[8,1920]{1,0:T(8,128)(2,1)S(1)}, bf16[8,1920]{1,0:T(8,128)(2,1)S(1)}, u32[]{:S(2)}, u32[]{:S(2)}) %collective-permute-start.9) | collective-permute-done | bytes 30752 | tf_op jit(solution)/shard_map/ppermute | solution.py:18
  29.3 1.9 %collective-permute-done.10.refs_3_ = bf16[8,1920]{1,0:T(8,128)(2,1)S(1)} collective-permute-done((bf16[8,1920]{1,0:T(8,128)(2,1)S(1)}, bf16[8,1920]{1,0:T(8,128)(2,1)S(1)}, u32[]{:S(2)}, u32[]{:S(2)}) %collective-permute-start.10) | collective-permute-done | bytes 30752 | tf_op jit(solution)/shard_map/ppermute | solution.py:18
  31.3 0.6 %score.1 = bf16[8,1920]{1,0:T(8,128)(2,1)S(1)} custom-call(bf16[8,1920]{1,0:T(8,128)(2,1)S(1)} %get-tuple-element.31.refs_0_, bf16[8,1920]{1,0:T(8,128)(2,1)S(1)} %collective-permute-done.8.refs_1_, bf16[8,1920]{1,0:T(8,128)(2,1)S(1)} %collective-permute-done.9.refs_2_, bf16[8,1920]{1,0:T(8,128)(2,1)S(1)} %collective-permute-done.10.refs_3_, ...), custom_call_target="tpu_custom_call" | custom-call | tf_op jit(solution)/shard_map/score/pallas_call | solution.py:320
  32.1 4.3 %collective-permute-start.11 = (bf16[2,1920]{1,0:T(2,128)(2,1)S(1)}, bf16[2,1920]{1,0:T(2,128)(2,1)S(1)}, u32[]{:S(2)}, u32[]{:S(2)}) collective-permute-start(bf16[2,1920]{1,0:T(2,128)(2,1)S(1)} %get-tuple-element.41), channel_id=1, source_target_pairs={{0,8},{8,0},{16,24},{24,16},{1,9},{9,1},{17,25},{25,17},{2,10},{10... | collective-permute-start | bytes 23048 | tf_op jit(solution)/shard_map/ppermute | solution.py:18
  36.4 1.1 %collective-permute-done.13 = bf16[2,1920]{1,0:T(2,128)(2,1)S(1)} collective-permute-done((bf16[2,1920]{1,0:T(2,128)(2,1)S(1)}, bf16[2,1920]{1,0:T(2,128)(2,1)S(1)}, u32[]{:S(2)}, u32[]{:S(2)}) %collective-permute-start.13) | collective-permute-done | bytes 7712 | tf_op jit(solution)/shard_map/ppermute | solution.py:18
  37.5 0.6 %collective-permute-done.11 = bf16[2,1920]{1,0:T(2,128)(2,1)S(1)} collective-permute-done((bf16[2,1920]{1,0:T(2,128)(2,1)S(1)}, bf16[2,1920]{1,0:T(2,128)(2,1)S(1)}, u32[]{:S(2)}, u32[]{:S(2)}) %collective-permute-start.11) | collective-permute-done | bytes 7712 | tf_op jit(solution)/shard_map/ppermute | solution.py:18
  38.1 1.0 %finish.1 = (bf16[64,1792]{1,0:T(8,128)(2,1)}, f32[64,128]{1,0:T(8,128)}) custom-call(f32[32,64]{1,0:T(8,128)S(1)} %get-tuple-element.20.hit_ref, bf16[8,1920]{1,0:T(8,128)(2,1)S(1)} %pad_maximum_fusion.1.home_ref), custom_call_target="tpu_custom_call" | custom-call | tf_op jit(solution)/shard_map/finish/pallas_call | solution.py:332
  (23 shorter events, 1.5 us)
Async XLA Ops:
  1.9 5.4 %collective-permute-start = (bf16[8,896]{1,0:T(8,128)(2,1)S(1)}, bf16[8,896]{1,0:T(8,128)(2,1)S(1)}, u32[]{:S(2)}, u32[]{:S(2)}) collective-permute-start(bf16[8,896]{1,0:T(8,128)(2,1)S(1)} %get-tuple-element.22), channel_id=1, source_target_pairs={{0,9},{1,8},{8,1},{9,0},{16,25},{17,24},{24,17},{25,16},{2,11},{3,... | collective-permute-start | bytes 43016 | tf_op jit(solution)/shard_map/ppermute | solution.py:18
  4.5 4.4 %collective-permute-start.1 = (bf16[8,896]{1,0:T(8,128)(2,1)S(1)}, bf16[8,896]{1,0:T(8,128)(2,1)S(1)}, u32[]{:S(2)}, u32[]{:S(2)}) collective-permute-start(bf16[8,896]{1,0:T(8,128)(2,1)S(1)} %get-tuple-element.23), channel_id=1, source_target_pairs={{0,17},{1,16},{8,25},{9,24},{16,1},{17,0},{24,9},{25,8},{2,19},{3,... | collective-permute-start | bytes 43016 | tf_op jit(solution)/shard_map/ppermute | solution.py:18
  7.3 5.1 %collective-permute-start.2 = (bf16[8,896]{1,0:T(8,128)(2,1)S(1)}, bf16[8,896]{1,0:T(8,128)(2,1)S(1)}, u32[]{:S(2)}, u32[]{:S(2)}) collective-permute-start(bf16[8,896]{1,0:T(8,128)(2,1)S(1)} %get-tuple-element.24), channel_id=1, source_target_pairs={{0,25},{1,24},{8,17},{9,16},{16,9},{17,8},{24,1},{25,0},{2,27},{3,... | collective-permute-start | bytes 43016 | tf_op jit(solution)/shard_map/ppermute | solution.py:18
  12.6 4.9 %collective-permute-start.5 = (bf16[4,8,896]{2,1,0:T(8,128)(2,1)S(1)}, bf16[4,8,896]{2,1,0:T(8,128)(2,1)S(1)}, u32[]{:S(2)}, u32[]{:S(2)}) collective-permute-start(bf16[4,8,896]{2,1,0:T(8,128)(2,1)S(1)} %reshape.19), channel_id=1, source_target_pairs={{0,7},{1,6},{2,5},{3,4},{4,3},{5,2},{6,1},{7,0},{8,15},{9,14},{10,... | collective-permute-start | bytes 172040 | tf_op jit(solution)/shard_map/ppermute | solution.py:18
  14.9 3.7 %collective-permute-start.4 = (bf16[4,8,896]{2,1,0:T(8,128)(2,1)S(1)}, bf16[4,8,896]{2,1,0:T(8,128)(2,1)S(1)}, u32[]{:S(2)}, u32[]{:S(2)}) collective-permute-start(bf16[4,8,896]{2,1,0:T(8,128)(2,1)S(1)} %reshape.19), channel_id=1, source_target_pairs={{0,5},{1,4},{2,7},{3,6},{4,1},{5,0},{6,3},{7,2},{8,13},{9,12},{10,... | collective-permute-start | bytes 172040 | tf_op jit(solution)/shard_map/ppermute | solution.py:18
  15.4 4.0 %collective-permute-start.3 = (bf16[4,8,896]{2,1,0:T(8,128)(2,1)S(1)}, bf16[4,8,896]{2,1,0:T(8,128)(2,1)S(1)}, u32[]{:S(2)}, u32[]{:S(2)}) collective-permute-start(bf16[4,8,896]{2,1,0:T(8,128)(2,1)S(1)} %reshape.19), channel_id=1, source_target_pairs={{0,3},{1,2},{2,1},{3,0},{4,7},{5,6},{6,5},{7,4},{8,11},{9,10},{10,... | collective-permute-start | bytes 172040 | tf_op jit(solution)/shard_map/ppermute | solution.py:18
  19.4 2.0 %collective-permute-start.6 = (bf16[128,896]{1,0:T(8,128)(2,1)S(1)}, bf16[128,896]{1,0:T(8,128)(2,1)S(1)}, u32[]{:S(2)}, u32[]{:S(2)}) collective-permute-start(bf16[128,896]{1,0:T(8,128)(2,1)S(1)} %bitcast.21), channel_id=1, source_target_pairs={{0,1},{1,0},{2,3},{3,2},{4,5},{5,4},{6,7},{7,6},{8,9},{9,8},{10,11... | collective-permute-start | bytes 688136 | tf_op jit(solution)/shard_map/ppermute | solution.py:18
  23.2 1.9 %collective-permute-start.7 = (bf16[32,1920]{1,0:T(8,128)(2,1)S(1)}, bf16[32,1920]{1,0:T(8,128)(2,1)S(1)}, u32[]{:S(2)}, u32[]{:S(2)}) collective-permute-start(bf16[32,1920]{1,0:T(8,128)(2,1)S(1)} %get-tuple-element.30.refs_0_), channel_id=1, source_target_pairs={{0,1},{1,0},{2,3},{3,2},{4,5},{5,4},{6,7},{7,6},{8,9},{9,8},{10,11... | collective-permute-start | bytes 368648 | tf_op jit(solution)/shard_map/ppermute | solution.py:18
  25.2 3.4 %collective-permute-start.8 = (bf16[8,1920]{1,0:T(8,128)(2,1)S(1)}, bf16[8,1920]{1,0:T(8,128)(2,1)S(1)}, u32[]{:S(2)}, u32[]{:S(2)}) collective-permute-start(bf16[8,1920]{1,0:T(8,128)(2,1)S(1)} %get-tuple-element.32), channel_id=1, source_target_pairs={{0,3},{1,2},{2,1},{3,0},{4,7},{5,6},{6,5},{7,4},{8,11},{9,10},{10,... | collective-permute-start | bytes 92168 | tf_op jit(solution)/shard_map/ppermute | solution.py:18
  26.0 3.3 %collective-permute-start.9 = (bf16[8,1920]{1,0:T(8,128)(2,1)S(1)}, bf16[8,1920]{1,0:T(8,128)(2,1)S(1)}, u32[]{:S(2)}, u32[]{:S(2)}) collective-permute-start(bf16[8,1920]{1,0:T(8,128)(2,1)S(1)} %get-tuple-element.33), channel_id=1, source_target_pairs={{0,5},{1,4},{2,7},{3,6},{4,1},{5,0},{6,3},{7,2},{8,13},{9,12},{10,... | collective-permute-start | bytes 92168 | tf_op jit(solution)/shard_map/ppermute | solution.py:18
  27.0 4.3 %collective-permute-start.10 = (bf16[8,1920]{1,0:T(8,128)(2,1)S(1)}, bf16[8,1920]{1,0:T(8,128)(2,1)S(1)}, u32[]{:S(2)}, u32[]{:S(2)}) collective-permute-start(bf16[8,1920]{1,0:T(8,128)(2,1)S(1)} %get-tuple-element.34), channel_id=1, source_target_pairs={{0,7},{1,6},{2,5},{3,4},{4,3},{5,2},{6,1},{7,0},{8,15},{9,14},{10,... | collective-permute-start | bytes 92168 | tf_op jit(solution)/shard_map/ppermute | solution.py:18
  31.9 5.5 %collective-permute-start.13 = (bf16[2,1920]{1,0:T(2,128)(2,1)S(1)}, bf16[2,1920]{1,0:T(2,128)(2,1)S(1)}, u32[]{:S(2)}, u32[]{:S(2)}) collective-permute-start(bf16[2,1920]{1,0:T(2,128)(2,1)S(1)} %get-tuple-element.39), channel_id=1, source_target_pairs={{0,24},{8,16},{16,8},{24,0},{1,25},{9,17},{17,9},{25,1},{2,26},{10... | collective-permute-start | bytes 23048 | tf_op jit(solution)/shard_map/ppermute | solution.py:18
  32.1 5.4 %collective-permute-start.12 = (bf16[2,1920]{1,0:T(2,128)(2,1)S(1)}, bf16[2,1920]{1,0:T(2,128)(2,1)S(1)}, u32[]{:S(2)}, u32[]{:S(2)}) collective-permute-start(bf16[2,1920]{1,0:T(2,128)(2,1)S(1)} %get-tuple-element.40), channel_id=1, source_target_pairs={{0,16},{8,24},{16,0},{24,8},{1,17},{9,25},{17,1},{25,9},{2,18},{10... | collective-permute-start | bytes 23048 | tf_op jit(solution)/shard_map/ppermute | solution.py:18
  32.1 5.9 %collective-permute-start.11 = (bf16[2,1920]{1,0:T(2,128)(2,1)S(1)}, bf16[2,1920]{1,0:T(2,128)(2,1)S(1)}, u32[]{:S(2)}, u32[]{:S(2)}) collective-permute-start(bf16[2,1920]{1,0:T(2,128)(2,1)S(1)} %get-tuple-element.41), channel_id=1, source_target_pairs={{0,8},{8,0},{16,24},{24,16},{1,9},{9,1},{17,25},{25,17},{2,10},{10... | collective-permute-start | bytes 23048 | tf_op jit(solution)/shard_map/ppermute | solution.py:18

commit v6 on v5

--- a/solution.py
+++ b/solution.py
@@ -28,13 +28,14 @@
 
 def slot_order(count):
     slots = list(range(count))
-    return slots if is_direct(count) else slots[::2] + slots[1::2]
+    return slots[::-1] if is_direct(count) else slots[::2] + slots[1::2]
 
 
 def exchange(send, parts, count):
     slots = dict(zip(slot_order(count), parts))
     if is_direct(count):
-        return [slots[0]] + [send(slots[k], "expert", k) for k in range(1, count)]
+        got = {k: send(slots[k], "expert", k) for k in reversed(range(1, count))}
+        return [slots[0]] + [got[k] for k in range(1, count)]
     unit = parts[0].shape[0]
     bit = 1
     while bit < count:
@@ -98,7 +99,9 @@
     row = lax.broadcasted_iota(jnp.int32, (experts * unit, 1), 0)
     kind = (row % unit) // CAP
     turn = row // unit
-    if not is_direct(experts):
+    if is_direct(experts):
+        turn = experts - 1 - turn
+    else:
         turn = 2 * turn % experts + 2 * turn // experts
     want = (turn ^ here) * CAP + row % CAP
     for copy in copies[:3]:
@@ -119,9 +122,25 @@
         out_ref[...] = total[k * unit : (k + 1) * unit]
 
 
-def load_kernel(*refs):
-    count = (len(refs) - 2) // 2
-    for copy in start_copies(zip(refs[1 : 1 + count], refs[1 + count : -1]), refs[-1]):
+def arrange_kernel(*refs):
+    *slot_refs, out_ref = refs
+    slots = [ref[...].astype(F32) for ref in slot_refs[::-1]]
+    pairs = CAP * len(slots)
+    for kind in range(KINDS):
+        rows = [slot[kind * CAP : (kind + 1) * CAP] for slot in slots]
+        out_ref[kind * pairs : (kind + 1) * pairs] = jnp.concatenate(rows).astype(BF16)
+
+
+def load_kernel(shapes, *refs):
+    count = sum(len(group) for group in shapes)
+    sources, targets = list(refs[1 : 1 + count]), refs[1 + count : -1]
+    pairs = []
+    for group, target in zip(shapes, targets):
+        first = 0
+        for _, columns in group:
+            pairs.append((sources.pop(0), target.at[:, first : first + columns]))
+            first += columns
+    for copy in start_copies(pairs, refs[-1]):
         copy.wait()
 
 
@@ -136,13 +155,18 @@
     return value[:, :middle] + value[:, middle:]
 
 
-def load(after, params, compiler_params):
+def load(after, groups, compiler_params):
+    params = [x for group in groups for x in group]
+    shapes = [[x.shape for x in group] for group in groups]
     with jax.named_scope("load"):
         return pl.pallas_call(
-            load_kernel,
-            out_shape=[jax.ShapeDtypeStruct(x.shape, x.dtype) for x in params],
+            functools.partial(load_kernel, shapes),
+            out_shape=[
+                jax.ShapeDtypeStruct((group[0][0], sum(x[1] for x in group)), BF16)
+                for group in shapes
+            ],
             in_specs=whole_vmem(1) + in_hbm(len(params)),
-            out_specs=whole_vmem(len(params)),
+            out_specs=whole_vmem(len(groups)),
             scratch_shapes=[pltpu.SemaphoreType.DMA((len(params),))],
             compiler_params=compiler_params,
             cost_estimate=pl.CostEstimate(
@@ -152,7 +176,7 @@
 
 
 def expert_kernel(
-    own_ref, other_ref, gate_w, up_w, down_w, proj_ref, keep_ref, send_ref, mine_ref, x_in, x_grad
+    own_ref, other_ref, pair_w, down_w, proj_ref, keep_ref, send_ref, mine_ref, x_in, x_grad
 ):
     rows, width = x_in.shape
     half, quarter = width // 2, width // 4
@@ -176,8 +200,9 @@
         target[:, pl.ds(pl.multiple_of(near + first, 128), quarter)] = jnp.where(odd, other, own)
         target[:, pl.ds(pl.multiple_of(far + first, 128), quarter)] = jnp.where(odd, own, other)
     mine_ref[...] = x_grad[:pairs]
-    gate_pre = dot_f32(x_in[...], gate_w[...], ((1,), (0,)))
-    up_pre = dot_f32(x_in[...], up_w[...], ((1,), (0,)))
+    ff = down_w.shape[0]
+    both_pre = dot_f32(x_in[...], pair_w[...], ((1,), (0,)))
+    gate_pre, up_pre = both_pre[:, :ff], both_pre[:, ff:]
     hid_grad = dot_f32(x_grad[...], down_w[...], ((1,), (1,)))
     sig = 1.0 / (1.0 + jnp.exp(-gate_pre))
     act_gate = gate_pre * sig
@@ -185,14 +210,14 @@
     tail = split_two(dot_f32(hidden, proj_ref[...], ((1,), (1,))))
     up_grad = (hid_grad * act_gate).astype(BF16)
     gate_grad = (hid_grad * up_pre * sig * (1.0 + gate_pre * (1.0 - sig))).astype(BF16)
+    both_grad = jnp.concatenate([gate_grad, up_grad], axis=1)
     keep_ref[:, half:] = tail
     send_ref[:, half:] = tail
     for base, first_ref, rest_ref in ((far, send_ref, keep_ref), (near, keep_ref, send_ref)):
         for index in range(2):
             start = pl.multiple_of(base + index * quarter, 128)
             columns = slice(index * quarter, (index + 1) * quarter)
-            part = dot_f32(gate_grad, gate_w[pl.ds(start, quarter), :], ((1,), (1,)))
-            part += dot_f32(up_grad, up_w[pl.ds(start, quarter), :], ((1,), (1,)))
+            part = dot_f32(both_grad, pair_w[pl.ds(start, quarter), :], ((1,), (1,)))
             part = part.astype(BF16)
             first_ref[:pairs, columns] = part[:pairs]
             rest_ref[pairs:, columns] = part[pairs:]
@@ -203,13 +228,15 @@
     main = (kept[:, :half] + got[:, :half]).astype(BF16)
     tail = split_two(join_two(kept[:, half:]) + join_two(got[:, half:]))
     rows = out_refs[0].shape[0]
-    for g, out_ref in enumerate(out_refs):
+    for g, out_ref in enumerate(out_refs[::-1]):
         out_ref[:, :half] = main[g * rows : (g + 1) * rows]
         out_ref[:, half:] = tail[g * rows : (g + 1) * rows]
 
 
-def score_kernel(half, *refs):
-    *piece_refs, grad_ref, test_ref, out_ref, feature = refs
+def score_kernel(half, order, *refs):
+    pieces = len(refs) - len(order) - 3
+    piece_refs, (grad_ref, test_ref) = refs[:pieces], refs[pieces : pieces + 2]
+    out_refs, feature = refs[pieces + 2 : -1], refs[-1]
     total = piece_refs[0][...].astype(F32)
     for piece_ref in piece_refs[1:]:
         total = total + piece_ref[...].astype(F32)
@@ -218,15 +245,18 @@
     proj = grad.shape[1]
     for p in range(proj):
         feature[:, p * proj : (p + 1) * proj] = (hid[:, p : p + 1] * grad).astype(BF16)
-    out_ref[:, :half] = total[:, :half].astype(BF16)
-    out_ref[:, half:] = dot_f32(feature[...], test_ref[...], ((1,), (1,))).astype(BF16)
-
-
-def finish_kernel(hit_ref, home_ref, in_grad_hbm, scores_hbm, in_grad, scores, sems):
-    pairs, unit = home_ref.shape[0], KINDS * CAP
-    hits = jnp.concatenate(
-        [hit_ref[k * unit : k * unit + CAP] for k in range(pairs // CAP)], axis=0
-    )
+    score = dot_f32(feature[...], test_ref[...], ((1,), (1,)))
+    for k, out_ref in zip(order, out_refs):
+        out_ref[:, :half] = total[k * CAP : (k + 1) * CAP, :half].astype(BF16)
+        out_ref[:, half:] = score[k * CAP : (k + 1) * CAP].astype(BF16)
+
+
+def finish_kernel(experts, hit_ref, *refs):
+    slot_refs = refs[:experts]
+    in_grad_hbm, scores_hbm, in_grad, scores, home_ref, sems = refs[experts:]
+    unit = KINDS * CAP
+    hits = jnp.concatenate([hit_ref[k * unit : k * unit + CAP] for k in range(experts)])
+    home_ref[...] = jnp.concatenate([ref[...].astype(F32) for ref in slot_refs]).astype(BF16)
     half = in_grad.shape[1]
     quarter = half // 2
     hits = hits.T.astype(BF16)
@@ -282,13 +312,20 @@
             compiler_params=limit(rows),
         )(*map(keep_in_hbm, (ids_t, slots_t, weight_t, tokens, out_grad)))
     slots = exchange(send_cross, parts, experts)
-    block = jnp.stack(slots).reshape(experts, KINDS, CAP, quarter)
-    block = block.transpose(1, 0, 2, 3).reshape(KINDS, pairs, quarter)
+    with jax.named_scope("arrange"):
+        block = pl.pallas_call(
+            arrange_kernel,
+            out_shape=jax.ShapeDtypeStruct((KINDS * pairs, quarter), BF16),
+            in_specs=whole_vmem(experts),
+            out_specs=whole_vmem(1)[0],
+            compiler_params=limit(rows),
+        )(*slots[::-1])
+    block = block.reshape(KINDS, pairs, quarter)
     blocks = [block] + [send_cross(block, "dp", g) for g in range(1, groups)]
     own = jnp.stack(blocks, axis=1).reshape(KINDS * rows, quarter)
     other = send_rel(own, "test", 1)
-    gate_w, up_w, down_w, hid_proj = load(
-        own, [w_gate[0], w_up[0], w_down[0], proj_hidden[0]], limit(rows)
+    pair_w, down_w, hid_proj = load(
+        own, [[w_gate[0], w_up[0]], [w_down[0]], [proj_hidden[0]]], limit(rows)
     )
 
     with jax.named_scope("expert"):
@@ -299,13 +336,13 @@
                 jax.ShapeDtypeStruct((rows, out_width), BF16),
                 jax.ShapeDtypeStruct((pairs, width), BF16),
             ],
-            in_specs=whole_vmem(6),
+            in_specs=whole_vmem(5),
             out_specs=whole_vmem(3),
             scratch_shapes=[pltpu.VMEM((rows, width), BF16)] * 2,
             compiler_params=limit(rows),
-        )(own, other, gate_w, up_w, down_w, hid_proj)
+        )(own, other, pair_w, down_w, hid_proj)
     got = send_rel(send, "test", 1)
-    grad_proj, test_rows = load(send, [proj_grad[0], test_feats[0]], limit(rows))
+    grad_proj, test_rows = load(send, [[proj_grad[0]], [test_feats[0]]], limit(rows))
     with jax.named_scope("pair"):
         sums = pl.pallas_call(
             functools.partial(pair_kernel, half),
@@ -314,36 +351,37 @@
             out_specs=whole_vmem(groups),
             compiler_params=limit(rows),
         )(keep, got)
-    pieces = [sums[0]] + [send_cross(sums[g], "dp", g) for g in range(1, groups)]
+    pieces = [send_cross(sums[-1 - g], "dp", g) for g in reversed(range(1, groups))] + [sums[-1]]
     grad_mine = dot_f32(mine, grad_proj, ((1,), (1,)))
+    order = slot_order(experts)
     with jax.named_scope("score"):
         back = pl.pallas_call(
-            functools.partial(score_kernel, half),
-            out_shape=jax.ShapeDtypeStruct((pairs, half + tests), BF16),
+            functools.partial(score_kernel, half, order),
+            out_shape=[jax.ShapeDtypeStruct((CAP, half + tests), BF16)] * experts,
             in_specs=whole_vmem(groups + 2),
-            out_specs=whole_vmem(1)[0],
+            out_specs=whole_vmem(experts),
             scratch_shapes=[pltpu.VMEM((pairs, proj * proj), BF16)],
             compiler_params=limit(rows),
         )(*pieces, grad_mine, test_rows)
-    order = slot_order(experts)
-    slots = exchange(send_rel, [back[k * CAP : (k + 1) * CAP] for k in order], experts)
-    home = jnp.concatenate([slots[k] for k in order])
+    slots = exchange(send_rel, back, experts)
+    home = [slots[k] for k in order]
     with jax.named_scope("finish"):
         return pl.pallas_call(
-            finish_kernel,
+            functools.partial(finish_kernel, experts),
             out_shape=[
                 jax.ShapeDtypeStruct((tok_rows, half), BF16),
                 jax.ShapeDtypeStruct((tok_rows, tests), F32),
             ],
-            in_specs=whole_vmem(2),
+            in_specs=whole_vmem(experts + 1),
             out_specs=in_hbm(2),
             scratch_shapes=[
                 pltpu.VMEM((tok_rows, half), BF16),
                 pltpu.VMEM((tok_rows, tests), F32),
+                pltpu.VMEM((pairs, half + tests), BF16),
                 pltpu.SemaphoreType.DMA((3,)),
             ],
             compiler_params=limit(rows),
-        )(hits, home)
+        )(hits, *home)
 
 
 def solution(mesh):

time: 39.2 us -> 36.6 us (0.934)
  waiting for transfers between devices: 13.3 us -> 10.9 us
  starting transfers between devices: 16.4 us -> 16.9 us
    ppermute x14, waiting for transfers between devices: 13.3 us -> 10.9 us  [send_rel(): return lax.ppermute(block, axis, [(i, i ^ offset) for i in range(size)])]
    ppermute x14, starting transfers between devices: 16.4 us -> 16.9 us  [send_rel(): return lax.ppermute(block, axis, [(i, i ^ offset) for i in range(size)])]
    pallas_call x1, Pallas kernels: 1.78 us -> 1.38 us  [on_device(): pl.pallas_call(expert_kernel, out_shape=[jax.ShapeDtypeStruct((rows, out_...]
    pallas_call x4 -> x5, Pallas kernels: 4.72 us -> 4.76 us  [the longest x2 3.15 us: load(): pl.pallas_call(functools.partial(load_kernel, shapes), out_shape=[jax.Sha...]
  transfers between devices with their start and end apart: 14 -> 14, of which waited for: 10 -> 9; matrix products, arithmetic and copies ran while one was open for 1% -> 1% of each run, Pallas kernels for 8% -> 9%
where the time goes in v6:
time: 36.6 us; the launch traced here: 36.4 us
  starting transfers between devices  16.9 us (46%)
  waiting for transfers between devices  10.9 us (30%)
  Pallas kernels  7.6 us (21%)
  between operations  0.7 us (2%)
    ppermute x14, starting transfers between devices, send_rel(): return lax.ppermute(block, axis, [(i, i ^ offset) for i in range(size)])  16.9 us
    ppermute x14, waiting for transfers between devices, send_rel(): return lax.ppermute(block, axis, [(i, i ^ offset) for i in range(size)])  10.9 us
    pallas_call x2, Pallas kernels, load(): pl.pallas_call(functools.partial(load_kernel, shapes), out_shape=[jax.Sha...  3.15 us
    pallas_call x1, Pallas kernels, on_device(): pl.pallas_call(expert_kernel, out_shape=[jax.ShapeDtypeStruct((rows, out_...  1.38 us
    pallas_call x1, Pallas kernels, on_device(): pl.pallas_call(functools.partial(select_kernel, experts), out_shape=[jax....  1.31 us
    pallas_call x1, Pallas kernels, on_device(): pl.pallas_call(functools.partial(finish_kernel, experts), out_shape=[jax....  0.95 us
  transfers between devices with their start and end apart: 14, of which 9 were waited for; matrix products, arithmetic and copies ran while one was open for 1% of the time, Pallas kernels for 9%

profile of v6, /device:TPU:0, one launch (start us, length us, event | category | flops | bytes accessed | tf_op | source)
XLA Modules:
  0.0 36.4 jit_solution(8541690909993318389)
XLA Ops:
  0.6 1.3 %select.1 = (f32[32,64]{1,0:T(8,128)S(1)}, bf16[8,896]{1,0:T(8,128)(2,1)S(1)}, bf16[8,896]{1,0:T(8,128)(2,1)S(1)}, bf16[8,896]{1,0:T(8,128)(2,1)S(1)}, bf16[8,896]{1,0:T(8,128)(2,1)S(1)}) custom-call(s32[8,64]{1,0:T(8,128)} %bitcast.39, s32[8,64]{1,0:T(8,128)} %bitcast.40, bf16[8,64]{1,0:T(8,128)(2,1)} %bitcast.41, bf16[64,1792]{1,0:T(8,128)(2,1)} %refs_3_.1, ...), custom_call_target="tpu_custom_call" | custom-call | tf_op jit(solution)/shard_map/select/pallas_call | solution.py:302
  1.9 4.6 %collective-permute-start = (bf16[8,896]{1,0:T(8,128)(2,1)S(1)}, bf16[8,896]{1,0:T(8,128)(2,1)S(1)}, u32[]{:S(2)}, u32[]{:S(2)}) collective-permute-start(bf16[8,896]{1,0:T(8,128)(2,1)S(1)} %get-tuple-element.24), channel_id=1, source_target_pairs={{0,25},{1,24},{8,17},{9,16},{16,9},{17,8},{24,1},{25,0},{2,27},{3,... | collective-permute-start | bytes 43016 | tf_op jit(solution)/shard_map/ppermute | solution.py:18
  6.5 0.9 %collective-permute-start.2 = (bf16[8,896]{1,0:T(8,128)(2,1)S(1)}, bf16[8,896]{1,0:T(8,128)(2,1)S(1)}, u32[]{:S(2)}, u32[]{:S(2)}) collective-permute-start(bf16[8,896]{1,0:T(8,128)(2,1)S(1)} %get-tuple-element.26), channel_id=1, source_target_pairs={{0,9},{1,8},{8,1},{9,0},{16,25},{17,24},{24,17},{25,16},{2,11},{3,... | collective-permute-start | bytes 43016 | tf_op jit(solution)/shard_map/ppermute | solution.py:18
  7.4 0.5 %collective-permute-done.refs_0_ = bf16[8,896]{1,0:T(8,128)(2,1)S(1)} collective-permute-done((bf16[8,896]{1,0:T(8,128)(2,1)S(1)}, bf16[8,896]{1,0:T(8,128)(2,1)S(1)}, u32[]{:S(2)}, u32[]{:S(2)}) %collective-permute-start) | collective-permute-done | bytes 14368 | tf_op jit(solution)/shard_map/ppermute | solution.py:18
  7.9 2.7 %collective-permute-done.1.refs_1_ = bf16[8,896]{1,0:T(8,128)(2,1)S(1)} collective-permute-done((bf16[8,896]{1,0:T(8,128)(2,1)S(1)}, bf16[8,896]{1,0:T(8,128)(2,1)S(1)}, u32[]{:S(2)}, u32[]{:S(2)}) %collective-permute-start.1) | collective-permute-done | bytes 14368 | tf_op jit(solution)/shard_map/ppermute | solution.py:18
  10.7 2.7 %collective-permute-start.5 = (bf16[4,8,896]{2,1,0:T(8,128)(2,1)S(1)}, bf16[4,8,896]{2,1,0:T(8,128)(2,1)S(1)}, u32[]{:S(2)}, u32[]{:S(2)}) collective-permute-start(bf16[4,8,896]{2,1,0:T(8,128)(2,1)S(1)} %bitcast.26), channel_id=1, source_target_pairs={{0,7},{1,6},{2,5},{3,4},{4,3},{5,2},{6,1},{7,0},{8,15},{9,14},{10,... | collective-permute-start | bytes 172040 | tf_op jit(solution)/shard_map/ppermute | solution.py:18
  13.4 0.7 %collective-permute-start.3 = (bf16[4,8,896]{2,1,0:T(8,128)(2,1)S(1)}, bf16[4,8,896]{2,1,0:T(8,128)(2,1)S(1)}, u32[]{:S(2)}, u32[]{:S(2)}) collective-permute-start(bf16[4,8,896]{2,1,0:T(8,128)(2,1)S(1)} %bitcast.28), channel_id=1, source_target_pairs={{0,3},{1,2},{2,1},{3,0},{4,7},{5,6},{6,5},{7,4},{8,11},{9,10},{10,... | collective-permute-start | bytes 172040 | tf_op jit(solution)/shard_map/ppermute | solution.py:18
  14.1 1.5 %collective-permute-done.5 = bf16[4,8,896]{2,1,0:T(8,128)(2,1)S(1)} collective-permute-done((bf16[4,8,896]{2,1,0:T(8,128)(2,1)S(1)}, bf16[4,8,896]{2,1,0:T(8,128)(2,1)S(1)}, u32[]{:S(2)}, u32[]{:S(2)}) %collective-permute-start.5) | collective-permute-done | bytes 57376 | tf_op jit(solution)/shard_map/ppermute | solution.py:18
  15.6 1.9 %collective-permute-done.4 = bf16[4,8,896]{2,1,0:T(8,128)(2,1)S(1)} collective-permute-done((bf16[4,8,896]{2,1,0:T(8,128)(2,1)S(1)}, bf16[4,8,896]{2,1,0:T(8,128)(2,1)S(1)}, u32[]{:S(2)}, u32[]{:S(2)}) %collective-permute-start.4) | collective-permute-done | bytes 57376 | tf_op jit(solution)/shard_map/ppermute | solution.py:18
  17.7 1.8 %load.2 = (bf16[3584,256]{1,0:T(8,128)(2,1)S(1)}, bf16[128,3584]{1,0:T(8,128)(2,1)S(1)}, bf16[64,128]{1,0:T(8,128)(2,1)S(1)}) custom-call(bf16[128,896]{1,0:T(8,128)(2,1)S(1)} %bitcast.24, bf16[3584,128]{1,0:T(8,128)(2,1)} %bitcast.31, bf16[3584,128]{1,0:T(8,128)(2,1)} %bitcast.32, bf16[128,3584]{1,0:T(8,128)(2,1)} %bitcast.33, bf16[64,128]{1,0:T(8,128)(2,1)} %bitcast.38), custom_call_target="tpu_custom_call" | custom-call | bytes 2768896 | tf_op jit(solution)/shard_map/load/pallas_call | solution.py:162
  19.5 1.4 %expert.1 = (bf16[32,1920]{1,0:T(8,128)(2,1)S(1)}, bf16[32,1920]{1,0:T(8,128)(2,1)S(1)}, bf16[8,3584]{1,0:T(8,128)(2,1)S(1)}) custom-call(bf16[128,896]{1,0:T(8,128)(2,1)S(1)} %bitcast.25, bf16[128,896]{1,0:T(8,128)(2,1)S(1)} %collective-permute-done.6.other_ref, bf16[3584,256]{1,0:T(8,128)(2,1)S(1)} %get-tuple-element.28.pair_w, ...), custom_call_target="tpu_custom_call" | custom-call | tf_op jit(solution)/shard_map/expert/pallas_call | solution.py:332
  21.3 1.4 %load.3 = (bf16[64,3584]{1,0:T(8,128)(2,1)S(1)}, bf16[128,4096]{1,0:T(8,128)(2,1)S(1)}) custom-call(bf16[32,1920]{1,0:T(8,128)(2,1)S(1)} %get-tuple-element.32.refs_0_, bf16[64,3584]{1,0:T(8,128)(2,1)} %bitcast.34, bf16[128,4096]{1,0:T(8,128)(2,1)} %bitcast.30), custom_call_target="tpu_custom_call" | custom-call | bytes 1507328 | tf_op jit(solution)/shard_map/load/pallas_call | solution.py:162
  22.8 1.4 %collective-permute-start.8 = (bf16[8,1920]{1,0:T(8,128)(2,1)S(1)}, bf16[8,1920]{1,0:T(8,128)(2,1)S(1)}, u32[]{:S(2)}, u32[]{:S(2)}) collective-permute-start(bf16[8,1920]{1,0:T(8,128)(2,1)S(1)} %get-tuple-element.33), channel_id=1, source_target_pairs={{0,7},{1,6},{2,5},{3,4},{4,3},{5,2},{6,1},{7,0},{8,15},{9,14},{10,... | collective-permute-start | bytes 92168 | tf_op jit(solution)/shard_map/ppermute | solution.py:18
  24.2 1.1 %collective-permute-start.9 = (bf16[8,1920]{1,0:T(8,128)(2,1)S(1)}, bf16[8,1920]{1,0:T(8,128)(2,1)S(1)}, u32[]{:S(2)}, u32[]{:S(2)}) collective-permute-start(bf16[8,1920]{1,0:T(8,128)(2,1)S(1)} %get-tuple-element.34), channel_id=1, source_target_pairs={{0,5},{1,4},{2,7},{3,6},{4,1},{5,0},{6,3},{7,2},{8,13},{9,12},{10,... | collective-permute-start | bytes 92168 | tf_op jit(solution)/shard_map/ppermute | solution.py:18
  26.0 1.1 %collective-permute-done.8.refs_0_ = bf16[8,1920]{1,0:T(8,128)(2,1)S(1)} collective-permute-done((bf16[8,1920]{1,0:T(8,128)(2,1)S(1)}, bf16[8,1920]{1,0:T(8,128)(2,1)S(1)}, u32[]{:S(2)}, u32[]{:S(2)}) %collective-permute-start.8) | collective-permute-done | bytes 30752 | tf_op jit(solution)/shard_map/ppermute | solution.py:18
  27.1 0.6 %collective-permute-done.9.refs_1_ = bf16[8,1920]{1,0:T(8,128)(2,1)S(1)} collective-permute-done((bf16[8,1920]{1,0:T(8,128)(2,1)S(1)}, bf16[8,1920]{1,0:T(8,128)(2,1)S(1)}, u32[]{:S(2)}, u32[]{:S(2)}) %collective-permute-start.9) | collective-permute-done | bytes 30752 | tf_op jit(solution)/shard_map/ppermute | solution.py:18
  27.7 1.0 %collective-permute-done.10.refs_2_ = bf16[8,1920]{1,0:T(8,128)(2,1)S(1)} collective-permute-done((bf16[8,1920]{1,0:T(8,128)(2,1)S(1)}, bf16[8,1920]{1,0:T(8,128)(2,1)S(1)}, u32[]{:S(2)}, u32[]{:S(2)}) %collective-permute-start.10) | collective-permute-done | bytes 30752 | tf_op jit(solution)/shard_map/ppermute | solution.py:18
  28.7 0.6 %score.1 = (bf16[2,1920]{1,0:T(2,128)(2,1)S(1)}, bf16[2,1920]{1,0:T(2,128)(2,1)S(1)}, bf16[2,1920]{1,0:T(2,128)(2,1)S(1)}, bf16[2,1920]{1,0:T(2,128)(2,1)S(1)}) custom-call(bf16[8,1920]{1,0:T(8,128)(2,1)S(1)} %collective-permute-done.8.refs_0_, bf16[8,1920]{1,0:T(8,128)(2,1)S(1)} %collective-permute-done.9.refs_1_, ...), custom_call_target="tpu_custom_call" | custom-call | tf_op jit(solution)/shard_map/score/pallas_call | solution.py:358
  29.3 1.5 %collective-permute-start.11 = (bf16[2,1920]{1,0:T(2,128)(2,1)S(1)}, bf16[2,1920]{1,0:T(2,128)(2,1)S(1)}, u32[]{:S(2)}, u32[]{:S(2)}) collective-permute-start(bf16[2,1920]{1,0:T(2,128)(2,1)S(1)} %get-tuple-element.40), channel_id=1, source_target_pairs={{0,24},{8,16},{16,8},{24,0},{1,25},{9,17},{17,9},{25,1},{2,26},{10... | collective-permute-start | bytes 23048 | tf_op jit(solution)/shard_map/ppermute | solution.py:18
  30.9 0.7 %collective-permute-start.12 = (bf16[2,1920]{1,0:T(2,128)(2,1)S(1)}, bf16[2,1920]{1,0:T(2,128)(2,1)S(1)}, u32[]{:S(2)}, u32[]{:S(2)}) collective-permute-start(bf16[2,1920]{1,0:T(2,128)(2,1)S(1)} %get-tuple-element.41), channel_id=1, source_target_pairs={{0,16},{8,24},{16,0},{24,8},{1,17},{9,25},{17,1},{25,9},{2,18},{10... | collective-permute-start | bytes 23048 | tf_op jit(solution)/shard_map/ppermute | solution.py:18
  31.6 2.2 %collective-permute-start.13 = (bf16[2,1920]{1,0:T(2,128)(2,1)S(1)}, bf16[2,1920]{1,0:T(2,128)(2,1)S(1)}, u32[]{:S(2)}, u32[]{:S(2)}) collective-permute-start(bf16[2,1920]{1,0:T(2,128)(2,1)S(1)} %get-tuple-element.42), channel_id=1, source_target_pairs={{0,8},{8,0},{16,24},{24,16},{1,9},{9,1},{17,25},{25,17},{2,10},{10... | collective-permute-start | bytes 23048 | tf_op jit(solution)/shard_map/ppermute | solution.py:18
  33.7 1.1 %collective-permute-done.11.refs_0_ = bf16[2,1920]{1,0:T(2,128)(2,1)S(1)} collective-permute-done((bf16[2,1920]{1,0:T(2,128)(2,1)S(1)}, bf16[2,1920]{1,0:T(2,128)(2,1)S(1)}, u32[]{:S(2)}, u32[]{:S(2)}) %collective-permute-start.11) | collective-permute-done | bytes 7712 | tf_op jit(solution)/shard_map/ppermute | solution.py:18
  34.8 0.6 %collective-permute-done.12.refs_1_ = bf16[2,1920]{1,0:T(2,128)(2,1)S(1)} collective-permute-done((bf16[2,1920]{1,0:T(2,128)(2,1)S(1)}, bf16[2,1920]{1,0:T(2,128)(2,1)S(1)}, u32[]{:S(2)}, u32[]{:S(2)}) %collective-permute-start.12) | collective-permute-done | bytes 7712 | tf_op jit(solution)/shard_map/ppermute | solution.py:18
  35.4 0.9 %finish.1 = (bf16[64,1792]{1,0:T(8,128)(2,1)}, f32[64,128]{1,0:T(8,128)}) custom-call(f32[32,64]{1,0:T(8,128)S(1)} %get-tuple-element.23.hit_ref, bf16[2,1920]{1,0:T(2,128)(2,1)S(1)} %collective-permute-done.11.refs_0_, bf16[2,1920]{1,0:T(2,128)(2,1)S(1)} %collective-permute-done.12.refs_1_, bf16[2,1920]{1,0:T(2,128)(2,1)S(1)} %collective-permute-done.13.refs_2_, ...), custom_call_target="tpu_custom_call" | custom-call | tf_op jit(solution)/shard_map/finish/pallas_call | solution.py:369
  (14 shorter events, 1.6 us)
Async XLA Ops:
  1.9 6.0 %collective-permute-start = (bf16[8,896]{1,0:T(8,128)(2,1)S(1)}, bf16[8,896]{1,0:T(8,128)(2,1)S(1)}, u32[]{:S(2)}, u32[]{:S(2)}) collective-permute-start(bf16[8,896]{1,0:T(8,128)(2,1)S(1)} %get-tuple-element.24), channel_id=1, source_target_pairs={{0,25},{1,24},{8,17},{9,16},{16,9},{17,8},{24,1},{25,0},{2,27},{3,... | collective-permute-start | bytes 43016 | tf_op jit(solution)/shard_map/ppermute | solution.py:18
  6.5 4.1 %collective-permute-start.1 = (bf16[8,896]{1,0:T(8,128)(2,1)S(1)}, bf16[8,896]{1,0:T(8,128)(2,1)S(1)}, u32[]{:S(2)}, u32[]{:S(2)}) collective-permute-start(bf16[8,896]{1,0:T(8,128)(2,1)S(1)} %get-tuple-element.25), channel_id=1, source_target_pairs={{0,17},{1,16},{8,25},{9,24},{16,1},{17,0},{24,9},{25,8},{2,19},{3,... | collective-permute-start | bytes 43016 | tf_op jit(solution)/shard_map/ppermute | solution.py:18
  6.5 4.1 %collective-permute-start.2 = (bf16[8,896]{1,0:T(8,128)(2,1)S(1)}, bf16[8,896]{1,0:T(8,128)(2,1)S(1)}, u32[]{:S(2)}, u32[]{:S(2)}) collective-permute-start(bf16[8,896]{1,0:T(8,128)(2,1)S(1)} %get-tuple-element.26), channel_id=1, source_target_pairs={{0,9},{1,8},{8,1},{9,0},{16,25},{17,24},{24,17},{25,16},{2,11},{3,... | collective-permute-start | bytes 43016 | tf_op jit(solution)/shard_map/ppermute | solution.py:18
  10.7 4.9 %collective-permute-start.5 = (bf16[4,8,896]{2,1,0:T(8,128)(2,1)S(1)}, bf16[4,8,896]{2,1,0:T(8,128)(2,1)S(1)}, u32[]{:S(2)}, u32[]{:S(2)}) collective-permute-start(bf16[4,8,896]{2,1,0:T(8,128)(2,1)S(1)} %bitcast.26), channel_id=1, source_target_pairs={{0,7},{1,6},{2,5},{3,4},{4,3},{5,2},{6,1},{7,0},{8,15},{9,14},{10,... | collective-permute-start | bytes 172040 | tf_op jit(solution)/shard_map/ppermute | solution.py:18
  13.4 4.1 %collective-permute-start.4 = (bf16[4,8,896]{2,1,0:T(8,128)(2,1)S(1)}, bf16[4,8,896]{2,1,0:T(8,128)(2,1)S(1)}, u32[]{:S(2)}, u32[]{:S(2)}) collective-permute-start(bf16[4,8,896]{2,1,0:T(8,128)(2,1)S(1)} %bitcast.27), channel_id=1, source_target_pairs={{0,5},{1,4},{2,7},{3,6},{4,1},{5,0},{6,3},{7,2},{8,13},{9,12},{10,... | collective-permute-start | bytes 172040 | tf_op jit(solution)/shard_map/ppermute | solution.py:18
  13.4 4.0 %collective-permute-start.3 = (bf16[4,8,896]{2,1,0:T(8,128)(2,1)S(1)}, bf16[4,8,896]{2,1,0:T(8,128)(2,1)S(1)}, u32[]{:S(2)}, u32[]{:S(2)}) collective-permute-start(bf16[4,8,896]{2,1,0:T(8,128)(2,1)S(1)} %bitcast.28), channel_id=1, source_target_pairs={{0,3},{1,2},{2,1},{3,0},{4,7},{5,6},{6,5},{7,4},{8,11},{9,10},{10,... | collective-permute-start | bytes 172040 | tf_op jit(solution)/shard_map/ppermute | solution.py:18
  17.5 2.0 %collective-permute-start.6 = (bf16[128,896]{1,0:T(8,128)(2,1)S(1)}, bf16[128,896]{1,0:T(8,128)(2,1)S(1)}, u32[]{:S(2)}, u32[]{:S(2)}) collective-permute-start(bf16[128,896]{1,0:T(8,128)(2,1)S(1)} %bitcast.23), channel_id=1, source_target_pairs={{0,1},{1,0},{2,3},{3,2},{4,5},{5,4},{6,7},{7,6},{8,9},{9,8},{10,11... | collective-permute-start | bytes 688136 | tf_op jit(solution)/shard_map/ppermute | solution.py:18
  20.9 1.8 %collective-permute-start.7 = (bf16[32,1920]{1,0:T(8,128)(2,1)S(1)}, bf16[32,1920]{1,0:T(8,128)(2,1)S(1)}, u32[]{:S(2)}, u32[]{:S(2)}) collective-permute-start(bf16[32,1920]{1,0:T(8,128)(2,1)S(1)} %get-tuple-element.32.refs_0_), channel_id=1, source_target_pairs={{0,1},{1,0},{2,3},{3,2},{4,5},{5,4},{6,7},{7,6},{8,9},{9,8},{10,11... | collective-permute-start | bytes 368648 | tf_op jit(solution)/shard_map/ppermute | solution.py:18
  22.8 4.2 %collective-permute-start.8 = (bf16[8,1920]{1,0:T(8,128)(2,1)S(1)}, bf16[8,1920]{1,0:T(8,128)(2,1)S(1)}, u32[]{:S(2)}, u32[]{:S(2)}) collective-permute-start(bf16[8,1920]{1,0:T(8,128)(2,1)S(1)} %get-tuple-element.33), channel_id=1, source_target_pairs={{0,7},{1,6},{2,5},{3,4},{4,3},{5,2},{6,1},{7,0},{8,15},{9,14},{10,... | collective-permute-start | bytes 92168 | tf_op jit(solution)/shard_map/ppermute | solution.py:18
  24.2 3.5 %collective-permute-start.9 = (bf16[8,1920]{1,0:T(8,128)(2,1)S(1)}, bf16[8,1920]{1,0:T(8,128)(2,1)S(1)}, u32[]{:S(2)}, u32[]{:S(2)}) collective-permute-start(bf16[8,1920]{1,0:T(8,128)(2,1)S(1)} %get-tuple-element.34), channel_id=1, source_target_pairs={{0,5},{1,4},{2,7},{3,6},{4,1},{5,0},{6,3},{7,2},{8,13},{9,12},{10,... | collective-permute-start | bytes 92168 | tf_op jit(solution)/shard_map/ppermute | solution.py:18
  25.3 3.4 %collective-permute-start.10 = (bf16[8,1920]{1,0:T(8,128)(2,1)S(1)}, bf16[8,1920]{1,0:T(8,128)(2,1)S(1)}, u32[]{:S(2)}, u32[]{:S(2)}) collective-permute-start(bf16[8,1920]{1,0:T(8,128)(2,1)S(1)} %get-tuple-element.35), channel_id=1, source_target_pairs={{0,3},{1,2},{2,1},{3,0},{4,7},{5,6},{6,5},{7,4},{8,11},{9,10},{10,... | collective-permute-start | bytes 92168 | tf_op jit(solution)/shard_map/ppermute | solution.py:18
  29.3 5.5 %collective-permute-start.11 = (bf16[2,1920]{1,0:T(2,128)(2,1)S(1)}, bf16[2,1920]{1,0:T(2,128)(2,1)S(1)}, u32[]{:S(2)}, u32[]{:S(2)}) collective-permute-start(bf16[2,1920]{1,0:T(2,128)(2,1)S(1)} %get-tuple-element.40), channel_id=1, source_target_pairs={{0,24},{8,16},{16,8},{24,0},{1,25},{9,17},{17,9},{25,1},{2,26},{10... | collective-permute-start | bytes 23048 | tf_op jit(solution)/shard_map/ppermute | solution.py:18
  30.9 4.6 %collective-permute-start.12 = (bf16[2,1920]{1,0:T(2,128)(2,1)S(1)}, bf16[2,1920]{1,0:T(2,128)(2,1)S(1)}, u32[]{:S(2)}, u32[]{:S(2)}) collective-permute-start(bf16[2,1920]{1,0:T(2,128)(2,1)S(1)} %get-tuple-element.41), channel_id=1, source_target_pairs={{0,16},{8,24},{16,0},{24,8},{1,17},{9,25},{17,1},{25,9},{2,18},{10... | collective-permute-start | bytes 23048 | tf_op jit(solution)/shard_map/ppermute | solution.py:18
  31.6 3.9 %collective-permute-start.13 = (bf16[2,1920]{1,0:T(2,128)(2,1)S(1)}, bf16[2,1920]{1,0:T(2,128)(2,1)S(1)}, u32[]{:S(2)}, u32[]{:S(2)}) collective-permute-start(bf16[2,1920]{1,0:T(2,128)(2,1)S(1)} %get-tuple-element.42), channel_id=1, source_target_pairs={{0,8},{8,0},{16,24},{24,16},{1,9},{9,1},{17,25},{25,17},{2,10},{10... | collective-permute-start | bytes 23048 | tf_op jit(solution)/shard_map/ppermute | solution.py:18

commit v7 on v6

--- a/solution.py
+++ b/solution.py
@@ -129,6 +129,15 @@
     for kind in range(KINDS):
         rows = [slot[kind * CAP : (kind + 1) * CAP] for slot in slots]
         out_ref[kind * pairs : (kind + 1) * pairs] = jnp.concatenate(rows).astype(BF16)
+
+
+def join_kernel(*refs):
+    *block_refs, out_ref = refs
+    pairs = block_refs[0].shape[0] // KINDS
+    for kind in range(KINDS):
+        for g, block_ref in enumerate(block_refs[::-1]):
+            first = (kind * len(block_refs) + g) * pairs
+            out_ref[first : first + pairs] = block_ref[kind * pairs : (kind + 1) * pairs]
 
 
 def load_kernel(shapes, *refs):
@@ -320,14 +329,18 @@
             out_specs=whole_vmem(1)[0],
             compiler_params=limit(rows),
         )(*slots[::-1])
-    block = block.reshape(KINDS, pairs, quarter)
-    blocks = [block] + [send_cross(block, "dp", g) for g in range(1, groups)]
-    own = jnp.stack(blocks, axis=1).reshape(KINDS * rows, quarter)
+    blocks = [send_cross(block, "dp", g) for g in reversed(range(1, groups))] + [block]
+    loaded = load(block, [[w_gate[0], w_up[0]], [w_down[0]], [proj_hidden[0]]], limit(rows))
+    blocks, (pair_w, down_w, hid_proj) = lax.optimization_barrier((blocks, loaded))
+    with jax.named_scope("join"):
+        own = pl.pallas_call(
+            join_kernel,
+            out_shape=jax.ShapeDtypeStruct((KINDS * rows, quarter), BF16),
+            in_specs=whole_vmem(groups),
+            out_specs=whole_vmem(1)[0],
+            compiler_params=limit(rows),
+        )(*blocks)
     other = send_rel(own, "test", 1)
-    pair_w, down_w, hid_proj = load(
-        own, [[w_gate[0], w_up[0]], [w_down[0]], [proj_hidden[0]]], limit(rows)
-    )
-
     with jax.named_scope("expert"):
         keep, send, mine = pl.pallas_call(
             expert_kernel,
@@ -342,7 +355,6 @@
             compiler_params=limit(rows),
         )(own, other, pair_w, down_w, hid_proj)
     got = send_rel(send, "test", 1)
-    grad_proj, test_rows = load(send, [[proj_grad[0]], [test_feats[0]]], limit(rows))
     with jax.named_scope("pair"):
         sums = pl.pallas_call(
             functools.partial(pair_kernel, half),
@@ -352,6 +364,7 @@
             compiler_params=limit(rows),
         )(keep, got)
     pieces = [send_cross(sums[-1 - g], "dp", g) for g in reversed(range(1, groups))] + [sums[-1]]
+    grad_proj, test_rows = load(sums[-1], [[proj_grad[0]], [test_feats[0]]], limit(rows))
     grad_mine = dot_f32(mine, grad_proj, ((1,), (1,)))
     order = slot_order(experts)
     with jax.named_scope("score"):

time: 36.6 us -> 35.8 us (0.978)
  waiting for transfers between devices: 10.9 us -> 9.51 us
  starting transfers between devices: 16.9 us -> 17.5 us
    ppermute x14, waiting for transfers between devices: 10.9 us -> 9.51 us  [send_rel(): return lax.ppermute(block, axis, [(i, i ^ offset) for i in range(size)])]
    ppermute x14, starting transfers between devices: 16.9 us -> 17.5 us  [send_rel(): return lax.ppermute(block, axis, [(i, i ^ offset) for i in range(size)])]
  transfers between devices with their start and end apart: 14 -> 14, of which waited for: 9 -> 10; matrix products, arithmetic and copies ran while one was open for 1% -> 1% of each run, Pallas kernels for 9% -> 9%
where the time goes in v7:
time: 35.8 us; the launch traced here: 35.6 us
  starting transfers between devices  17.5 us (49%)
  waiting for transfers between devices  9.51 us (27%)
  Pallas kernels  7.62 us (21%)
  between operations  0.69 us (2%)
    ppermute x14, starting transfers between devices, send_rel(): return lax.ppermute(block, axis, [(i, i ^ offset) for i in range(size)])  17.5 us
    ppermute x14, waiting for transfers between devices, send_rel(): return lax.ppermute(block, axis, [(i, i ^ offset) for i in range(size)])  9.51 us
    pallas_call x2, Pallas kernels, load(): pl.pallas_call(functools.partial(load_kernel, shapes), out_shape=[jax.Sha...  3.15 us
    pallas_call x1, Pallas kernels, on_device(): pl.pallas_call(expert_kernel, out_shape=[jax.ShapeDtypeStruct((rows, out_...  1.38 us
    pallas_call x1, Pallas kernels, on_device(): pl.pallas_call(functools.partial(select_kernel, experts), out_shape=[jax....  1.31 us
    pallas_call x1, Pallas kernels, on_device(): pl.pallas_call(functools.partial(finish_kernel, experts), out_shape=[jax....  0.95 us
  transfers between devices with their start and end apart: 14, of which 10 were waited for; matrix products, arithmetic and copies ran while one was open for 1% of the time, Pallas kernels for 9%

profile of v7, /device:TPU:0, one launch (start us, length us, event | category | flops | bytes accessed | tf_op | source)
XLA Modules:
  0.0 35.6 jit_solution(6149981536016951895)
XLA Ops:
  0.6 1.3 %select.1 = (f32[32,64]{1,0:T(8,128)S(1)}, bf16[8,896]{1,0:T(8,128)(2,1)S(1)}, bf16[8,896]{1,0:T(8,128)(2,1)S(1)}, bf16[8,896]{1,0:T(8,128)(2,1)S(1)}, bf16[8,896]{1,0:T(8,128)(2,1)S(1)}) custom-call(s32[8,64]{1,0:T(8,128)} %bitcast.17, s32[8,64]{1,0:T(8,128)} %bitcast.18, bf16[8,64]{1,0:T(8,128)(2,1)} %bitcast.19, bf16[64,1792]{1,0:T(8,128)(2,1)} %refs_3_.1, ...), custom_call_target="tpu_custom_call" | custom-call | tf_op jit(solution)/shard_map/select/pallas_call | solution.py:311
  1.9 4.6 %collective-permute-start = (bf16[8,896]{1,0:T(8,128)(2,1)S(1)}, bf16[8,896]{1,0:T(8,128)(2,1)S(1)}, u32[]{:S(2)}, u32[]{:S(2)}) collective-permute-start(bf16[8,896]{1,0:T(8,128)(2,1)S(1)} %get-tuple-element.31), channel_id=1, source_target_pairs={{0,25},{1,24},{8,17},{9,16},{16,9},{17,8},{24,1},{25,0},{2,27},{3,... | collective-permute-start | bytes 43016 | tf_op jit(solution)/shard_map/ppermute | solution.py:18
  6.5 0.9 %collective-permute-start.2 = (bf16[8,896]{1,0:T(8,128)(2,1)S(1)}, bf16[8,896]{1,0:T(8,128)(2,1)S(1)}, u32[]{:S(2)}, u32[]{:S(2)}) collective-permute-start(bf16[8,896]{1,0:T(8,128)(2,1)S(1)} %get-tuple-element.33), channel_id=1, source_target_pairs={{0,9},{1,8},{8,1},{9,0},{16,25},{17,24},{24,17},{25,16},{2,11},{3,... | collective-permute-start | bytes 43016 | tf_op jit(solution)/shard_map/ppermute | solution.py:18
  7.9 2.7 %collective-permute-done.1.refs_1_ = bf16[8,896]{1,0:T(8,128)(2,1)S(1)} collective-permute-done((bf16[8,896]{1,0:T(8,128)(2,1)S(1)}, bf16[8,896]{1,0:T(8,128)(2,1)S(1)}, u32[]{:S(2)}, u32[]{:S(2)}) %collective-permute-start.1) | collective-permute-done | bytes 14368 | tf_op jit(solution)/shard_map/ppermute | solution.py:18
  10.7 1.7 %collective-permute-start.5 = (bf16[32,896]{1,0:T(8,128)(2,1)S(1)}, bf16[32,896]{1,0:T(8,128)(2,1)S(1)}, u32[]{:S(2)}, u32[]{:S(2)}) collective-permute-start(bf16[32,896]{1,0:T(8,128)(2,1)S(1)} %arrange.1.refs_0_.refs_3_), channel_id=1, source_target_pairs={{0,3},{1,2},{2,1},{3,0},{4,7},{5,6},{6,5},{7,4},{8,11},{9,10},{10,... | collective-permute-start | bytes 172040 | tf_op jit(solution)/shard_map/ppermute | solution.py:18
  12.4 1.1 %collective-permute-start.4 = (bf16[32,896]{1,0:T(8,128)(2,1)S(1)}, bf16[32,896]{1,0:T(8,128)(2,1)S(1)}, u32[]{:S(2)}, u32[]{:S(2)}) collective-permute-start(bf16[32,896]{1,0:T(8,128)(2,1)S(1)} %arrange.1.refs_0_.refs_3_), channel_id=1, source_target_pairs={{0,5},{1,4},{2,7},{3,6},{4,1},{5,0},{6,3},{7,2},{8,13},{9,12},{10,... | collective-permute-start | bytes 172040 | tf_op jit(solution)/shard_map/ppermute | solution.py:18
  13.5 0.6 %collective-permute-start.3 = (bf16[32,896]{1,0:T(8,128)(2,1)S(1)}, bf16[32,896]{1,0:T(8,128)(2,1)S(1)}, u32[]{:S(2)}, u32[]{:S(2)}) collective-permute-start(bf16[32,896]{1,0:T(8,128)(2,1)S(1)} %arrange.1.refs_0_.refs_3_), channel_id=1, source_target_pairs={{0,7},{1,6},{2,5},{3,4},{4,3},{5,2},{6,1},{7,0},{8,15},{9,14},{10,... | collective-permute-start | bytes 172040 | tf_op jit(solution)/shard_map/ppermute | solution.py:18
  14.1 1.8 %load.2 = (bf16[3584,256]{1,0:T(8,128)(2,1)S(1)}, bf16[128,3584]{1,0:T(8,128)(2,1)S(1)}, bf16[64,128]{1,0:T(8,128)(2,1)S(1)}) custom-call(bf16[32,896]{1,0:T(8,128)(2,1)S(1)} %arrange.1.refs_0_.refs_3_, bf16[3584,128]{1,0:T(8,128)(2,1)} %bitcast.12, bf16[3584,128]{1,0:T(8,128)(2,1)} %bitcast.13, bf16[128,3584]{1,0:T(8,128)(2,1)} %bitcast.14, ...), custom_call_target="tpu_custom_call" | custom-call | bytes 2768896 | tf_op jit(solution)/shard_map/load/pallas_call | solution.py:171
  16.5 1.5 %collective-permute-done.3.refs_0_ = bf16[32,896]{1,0:T(8,128)(2,1)S(1)} collective-permute-done((bf16[32,896]{1,0:T(8,128)(2,1)S(1)}, bf16[32,896]{1,0:T(8,128)(2,1)S(1)}, u32[]{:S(2)}, u32[]{:S(2)}) %collective-permute-start.3) | collective-permute-done | bytes 57376 | tf_op jit(solution)/shard_map/ppermute | solution.py:18
  18.0 0.6 %collective-permute-start.6 = (bf16[128,896]{1,0:T(8,128)(2,1)S(1)}, bf16[128,896]{1,0:T(8,128)(2,1)S(1)}, u32[]{:S(2)}, u32[]{:S(2)}) collective-permute-start(bf16[128,896]{1,0:T(8,128)(2,1)S(1)} %join.1.own_ref), channel_id=1, source_target_pairs={{0,1},{1,0},{2,3},{3,2},{4,5},{5,4},{6,7},{7,6},{8,9},{9,8},{10,11... | collective-permute-start | bytes 688136 | tf_op jit(solution)/shard_map/ppermute | solution.py:18
  18.6 1.1 %collective-permute-done.6.other_ref = bf16[128,896]{1,0:T(8,128)(2,1)S(1)} collective-permute-done((bf16[128,896]{1,0:T(8,128)(2,1)S(1)}, bf16[128,896]{1,0:T(8,128)(2,1)S(1)}, u32[]{:S(2)}, u32[]{:S(2)}) %collective-permute-start.6) | collective-permute-done | bytes 229408 | tf_op jit(solution)/shard_map/ppermute | solution.py:18
  19.8 1.4 %expert.1 = (bf16[32,1920]{1,0:T(8,128)(2,1)S(1)}, bf16[32,1920]{1,0:T(8,128)(2,1)S(1)}, bf16[8,3584]{1,0:T(8,128)(2,1)S(1)}) custom-call(bf16[128,896]{1,0:T(8,128)(2,1)S(1)} %join.1.own_ref, bf16[128,896]{1,0:T(8,128)(2,1)S(1)} %collective-permute-done.6.other_ref, bf16[3584,256]{1,0:T(8,128)(2,1)S(1)} %get-tuple-element.42.pair_w, ...), custom_call_target="tpu_custom_call" | custom-call | tf_op jit(solution)/shard_map/expert/pallas_call | solution.py:345
  21.5 1.0 %collective-permute-done.7.got_ref = bf16[32,1920]{1,0:T(8,128)(2,1)S(1)} collective-permute-done((bf16[32,1920]{1,0:T(8,128)(2,1)S(1)}, bf16[32,1920]{1,0:T(8,128)(2,1)S(1)}, u32[]{:S(2)}, u32[]{:S(2)}) %collective-permute-start.7) | collective-permute-done | bytes 122912 | tf_op jit(solution)/shard_map/ppermute | solution.py:18
  22.7 0.6 %collective-permute-start.8 = (bf16[8,1920]{1,0:T(8,128)(2,1)S(1)}, bf16[8,1920]{1,0:T(8,128)(2,1)S(1)}, u32[]{:S(2)}, u32[]{:S(2)}) collective-permute-start(bf16[8,1920]{1,0:T(8,128)(2,1)S(1)} %get-tuple-element.47), channel_id=1, source_target_pairs={{0,7},{1,6},{2,5},{3,4},{4,3},{5,2},{6,1},{7,0},{8,15},{9,14},{10,... | collective-permute-start | bytes 92168 | tf_op jit(solution)/shard_map/ppermute | solution.py:18
  23.3 1.1 %collective-permute-start.9 = (bf16[8,1920]{1,0:T(8,128)(2,1)S(1)}, bf16[8,1920]{1,0:T(8,128)(2,1)S(1)}, u32[]{:S(2)}, u32[]{:S(2)}) collective-permute-start(bf16[8,1920]{1,0:T(8,128)(2,1)S(1)} %get-tuple-element.48), channel_id=1, source_target_pairs={{0,5},{1,4},{2,7},{3,6},{4,1},{5,0},{6,3},{7,2},{8,13},{9,12},{10,... | collective-permute-start | bytes 92168 | tf_op jit(solution)/shard_map/ppermute | solution.py:18
  24.4 1.4 %collective-permute-start.10 = (bf16[8,1920]{1,0:T(8,128)(2,1)S(1)}, bf16[8,1920]{1,0:T(8,128)(2,1)S(1)}, u32[]{:S(2)}, u32[]{:S(2)}) collective-permute-start(bf16[8,1920]{1,0:T(8,128)(2,1)S(1)} %get-tuple-element.49), channel_id=1, source_target_pairs={{0,3},{1,2},{2,1},{3,0},{4,7},{5,6},{6,5},{7,4},{8,11},{9,10},{10,... | collective-permute-start | bytes 92168 | tf_op jit(solution)/shard_map/ppermute | solution.py:18
  25.9 1.4 %load.3 = (bf16[64,3584]{1,0:T(8,128)(2,1)S(1)}, bf16[128,4096]{1,0:T(8,128)(2,1)S(1)}) custom-call(bf16[8,1920]{1,0:T(8,128)(2,1)S(1)} %get-tuple-element.50.refs_0_.refs_3_, bf16[64,3584]{1,0:T(8,128)(2,1)} %bitcast.15, bf16[128,4096]{1,0:T(8,128)(2,1)} %bitcast.11), custom_call_target="tpu_custom_call" | custom-call | bytes 1507328 | tf_op jit(solution)/shard_map/load/pallas_call | solution.py:171
  27.7 0.6 %score.1 = (bf16[2,1920]{1,0:T(2,128)(2,1)S(1)}, bf16[2,1920]{1,0:T(2,128)(2,1)S(1)}, bf16[2,1920]{1,0:T(2,128)(2,1)S(1)}, bf16[2,1920]{1,0:T(2,128)(2,1)S(1)}) custom-call(bf16[8,1920]{1,0:T(8,128)(2,1)S(1)} %collective-permute-done.8.refs_0_, bf16[8,1920]{1,0:T(8,128)(2,1)S(1)} %collective-permute-done.9.refs_1_, ...), custom_call_target="tpu_custom_call" | custom-call | tf_op jit(solution)/shard_map/score/pallas_call | solution.py:371
  28.4 1.6 %collective-permute-start.11 = (bf16[2,1920]{1,0:T(2,128)(2,1)S(1)}, bf16[2,1920]{1,0:T(2,128)(2,1)S(1)}, u32[]{:S(2)}, u32[]{:S(2)}) collective-permute-start(bf16[2,1920]{1,0:T(2,128)(2,1)S(1)} %get-tuple-element.54), channel_id=1, source_target_pairs={{0,24},{8,16},{16,8},{24,0},{1,25},{9,17},{17,9},{25,1},{2,26},{10... | collective-permute-start | bytes 23048 | tf_op jit(solution)/shard_map/ppermute | solution.py:18
  30.0 0.9 %collective-permute-start.12 = (bf16[2,1920]{1,0:T(2,128)(2,1)S(1)}, bf16[2,1920]{1,0:T(2,128)(2,1)S(1)}, u32[]{:S(2)}, u32[]{:S(2)}) collective-permute-start(bf16[2,1920]{1,0:T(2,128)(2,1)S(1)} %get-tuple-element.55), channel_id=1, source_target_pairs={{0,16},{8,24},{16,0},{24,8},{1,17},{9,25},{17,1},{25,9},{2,18},{10... | collective-permute-start | bytes 23048 | tf_op jit(solution)/shard_map/ppermute | solution.py:18
  30.9 1.8 %collective-permute-start.13 = (bf16[2,1920]{1,0:T(2,128)(2,1)S(1)}, bf16[2,1920]{1,0:T(2,128)(2,1)S(1)}, u32[]{:S(2)}, u32[]{:S(2)}) collective-permute-start(bf16[2,1920]{1,0:T(2,128)(2,1)S(1)} %get-tuple-element.56), channel_id=1, source_target_pairs={{0,8},{8,0},{16,24},{24,16},{1,9},{9,1},{17,25},{25,17},{2,10},{10... | collective-permute-start | bytes 23048 | tf_op jit(solution)/shard_map/ppermute | solution.py:18
  32.8 1.1 %collective-permute-done.11.refs_0_ = bf16[2,1920]{1,0:T(2,128)(2,1)S(1)} collective-permute-done((bf16[2,1920]{1,0:T(2,128)(2,1)S(1)}, bf16[2,1920]{1,0:T(2,128)(2,1)S(1)}, u32[]{:S(2)}, u32[]{:S(2)}) %collective-permute-start.11) | collective-permute-done | bytes 7712 | tf_op jit(solution)/shard_map/ppermute | solution.py:18
  33.8 0.7 %collective-permute-done.12.refs_1_ = bf16[2,1920]{1,0:T(2,128)(2,1)S(1)} collective-permute-done((bf16[2,1920]{1,0:T(2,128)(2,1)S(1)}, bf16[2,1920]{1,0:T(2,128)(2,1)S(1)}, u32[]{:S(2)}, u32[]{:S(2)}) %collective-permute-start.12) | collective-permute-done | bytes 7712 | tf_op jit(solution)/shard_map/ppermute | solution.py:18
  34.6 0.9 %finish.1 = (bf16[64,1792]{1,0:T(8,128)(2,1)}, f32[64,128]{1,0:T(8,128)}) custom-call(f32[32,64]{1,0:T(8,128)S(1)} %get-tuple-element.30.hit_ref, bf16[2,1920]{1,0:T(2,128)(2,1)S(1)} %collective-permute-done.11.refs_0_, bf16[2,1920]{1,0:T(2,128)(2,1)S(1)} %collective-permute-done.12.refs_1_, bf16[2,1920]{1,0:T(2,128)(2,1)S(1)} %collective-permute-done.13.refs_2_, ...), custom_call_target="tpu_custom_call" | custom-call | tf_op jit(solution)/shard_map/finish/pallas_call | solution.py:382
  (14 shorter events, 2.3 us)
Async XLA Ops:
  1.9 6.0 %collective-permute-start = (bf16[8,896]{1,0:T(8,128)(2,1)S(1)}, bf16[8,896]{1,0:T(8,128)(2,1)S(1)}, u32[]{:S(2)}, u32[]{:S(2)}) collective-permute-start(bf16[8,896]{1,0:T(8,128)(2,1)S(1)} %get-tuple-element.31), channel_id=1, source_target_pairs={{0,25},{1,24},{8,17},{9,16},{16,9},{17,8},{24,1},{25,0},{2,27},{3,... | collective-permute-start | bytes 43016 | tf_op jit(solution)/shard_map/ppermute | solution.py:18
  6.5 4.1 %collective-permute-start.1 = (bf16[8,896]{1,0:T(8,128)(2,1)S(1)}, bf16[8,896]{1,0:T(8,128)(2,1)S(1)}, u32[]{:S(2)}, u32[]{:S(2)}) collective-permute-start(bf16[8,896]{1,0:T(8,128)(2,1)S(1)} %get-tuple-element.32), channel_id=1, source_target_pairs={{0,17},{1,16},{8,25},{9,24},{16,1},{17,0},{24,9},{25,8},{2,19},{3,... | collective-permute-start | bytes 43016 | tf_op jit(solution)/shard_map/ppermute | solution.py:18
  6.5 4.1 %collective-permute-start.2 = (bf16[8,896]{1,0:T(8,128)(2,1)S(1)}, bf16[8,896]{1,0:T(8,128)(2,1)S(1)}, u32[]{:S(2)}, u32[]{:S(2)}) collective-permute-start(bf16[8,896]{1,0:T(8,128)(2,1)S(1)} %get-tuple-element.33), channel_id=1, source_target_pairs={{0,9},{1,8},{8,1},{9,0},{16,25},{17,24},{24,17},{25,16},{2,11},{3,... | collective-permute-start | bytes 43016 | tf_op jit(solution)/shard_map/ppermute | solution.py:18
  10.7 5.2 %collective-permute-start.5 = (bf16[32,896]{1,0:T(8,128)(2,1)S(1)}, bf16[32,896]{1,0:T(8,128)(2,1)S(1)}, u32[]{:S(2)}, u32[]{:S(2)}) collective-permute-start(bf16[32,896]{1,0:T(8,128)(2,1)S(1)} %arrange.1.refs_0_.refs_3_), channel_id=1, source_target_pairs={{0,3},{1,2},{2,1},{3,0},{4,7},{5,6},{6,5},{7,4},{8,11},{9,10},{10,... | collective-permute-start | bytes 172040 | tf_op jit(solution)/shard_map/ppermute | solution.py:18
  12.4 4.1 %collective-permute-start.4 = (bf16[32,896]{1,0:T(8,128)(2,1)S(1)}, bf16[32,896]{1,0:T(8,128)(2,1)S(1)}, u32[]{:S(2)}, u32[]{:S(2)}) collective-permute-start(bf16[32,896]{1,0:T(8,128)(2,1)S(1)} %arrange.1.refs_0_.refs_3_), channel_id=1, source_target_pairs={{0,5},{1,4},{2,7},{3,6},{4,1},{5,0},{6,3},{7,2},{8,13},{9,12},{10,... | collective-permute-start | bytes 172040 | tf_op jit(solution)/shard_map/ppermute | solution.py:18
  13.5 4.5 %collective-permute-start.3 = (bf16[32,896]{1,0:T(8,128)(2,1)S(1)}, bf16[32,896]{1,0:T(8,128)(2,1)S(1)}, u32[]{:S(2)}, u32[]{:S(2)}) collective-permute-start(bf16[32,896]{1,0:T(8,128)(2,1)S(1)} %arrange.1.refs_0_.refs_3_), channel_id=1, source_target_pairs={{0,7},{1,6},{2,5},{3,4},{4,3},{5,2},{6,1},{7,0},{8,15},{9,14},{10,... | collective-permute-start | bytes 172040 | tf_op jit(solution)/shard_map/ppermute | solution.py:18
  18.0 1.7 %collective-permute-start.6 = (bf16[128,896]{1,0:T(8,128)(2,1)S(1)}, bf16[128,896]{1,0:T(8,128)(2,1)S(1)}, u32[]{:S(2)}, u32[]{:S(2)}) collective-permute-start(bf16[128,896]{1,0:T(8,128)(2,1)S(1)} %join.1.own_ref), channel_id=1, source_target_pairs={{0,1},{1,0},{2,3},{3,2},{4,5},{5,4},{6,7},{7,6},{8,9},{9,8},{10,11... | collective-permute-start | bytes 688136 | tf_op jit(solution)/shard_map/ppermute | solution.py:18
  21.1 1.4 %collective-permute-start.7 = (bf16[32,1920]{1,0:T(8,128)(2,1)S(1)}, bf16[32,1920]{1,0:T(8,128)(2,1)S(1)}, u32[]{:S(2)}, u32[]{:S(2)}) collective-permute-start(bf16[32,1920]{1,0:T(8,128)(2,1)S(1)} %get-tuple-element.46), channel_id=1, source_target_pairs={{0,1},{1,0},{2,3},{3,2},{4,5},{5,4},{6,7},{7,6},{8,9},{9,8},{10,11... | collective-permute-start | bytes 368648 | tf_op jit(solution)/shard_map/ppermute | solution.py:18
  22.7 4.8 %collective-permute-start.8 = (bf16[8,1920]{1,0:T(8,128)(2,1)S(1)}, bf16[8,1920]{1,0:T(8,128)(2,1)S(1)}, u32[]{:S(2)}, u32[]{:S(2)}) collective-permute-start(bf16[8,1920]{1,0:T(8,128)(2,1)S(1)} %get-tuple-element.47), channel_id=1, source_target_pairs={{0,7},{1,6},{2,5},{3,4},{4,3},{5,2},{6,1},{7,0},{8,15},{9,14},{10,... | collective-permute-start | bytes 92168 | tf_op jit(solution)/shard_map/ppermute | solution.py:18
  23.3 4.2 %collective-permute-start.9 = (bf16[8,1920]{1,0:T(8,128)(2,1)S(1)}, bf16[8,1920]{1,0:T(8,128)(2,1)S(1)}, u32[]{:S(2)}, u32[]{:S(2)}) collective-permute-start(bf16[8,1920]{1,0:T(8,128)(2,1)S(1)} %get-tuple-element.48), channel_id=1, source_target_pairs={{0,5},{1,4},{2,7},{3,6},{4,1},{5,0},{6,3},{7,2},{8,13},{9,12},{10,... | collective-permute-start | bytes 92168 | tf_op jit(solution)/shard_map/ppermute | solution.py:18
  24.4 3.3 %collective-permute-start.10 = (bf16[8,1920]{1,0:T(8,128)(2,1)S(1)}, bf16[8,1920]{1,0:T(8,128)(2,1)S(1)}, u32[]{:S(2)}, u32[]{:S(2)}) collective-permute-start(bf16[8,1920]{1,0:T(8,128)(2,1)S(1)} %get-tuple-element.49), channel_id=1, source_target_pairs={{0,3},{1,2},{2,1},{3,0},{4,7},{5,6},{6,5},{7,4},{8,11},{9,10},{10,... | collective-permute-start | bytes 92168 | tf_op jit(solution)/shard_map/ppermute | solution.py:18
  28.4 5.5 %collective-permute-start.11 = (bf16[2,1920]{1,0:T(2,128)(2,1)S(1)}, bf16[2,1920]{1,0:T(2,128)(2,1)S(1)}, u32[]{:S(2)}, u32[]{:S(2)}) collective-permute-start(bf16[2,1920]{1,0:T(2,128)(2,1)S(1)} %get-tuple-element.54), channel_id=1, source_target_pairs={{0,24},{8,16},{16,8},{24,0},{1,25},{9,17},{17,9},{25,1},{2,26},{10... | collective-permute-start | bytes 23048 | tf_op jit(solution)/shard_map/ppermute | solution.py:18
  30.0 4.5 %collective-permute-start.12 = (bf16[2,1920]{1,0:T(2,128)(2,1)S(1)}, bf16[2,1920]{1,0:T(2,128)(2,1)S(1)}, u32[]{:S(2)}, u32[]{:S(2)}) collective-permute-start(bf16[2,1920]{1,0:T(2,128)(2,1)S(1)} %get-tuple-element.55), channel_id=1, source_target_pairs={{0,16},{8,24},{16,0},{24,8},{1,17},{9,25},{17,1},{25,9},{2,18},{10... | collective-permute-start | bytes 23048 | tf_op jit(solution)/shard_map/ppermute | solution.py:18
  30.9 3.7 %collective-permute-start.13 = (bf16[2,1920]{1,0:T(2,128)(2,1)S(1)}, bf16[2,1920]{1,0:T(2,128)(2,1)S(1)}, u32[]{:S(2)}, u32[]{:S(2)}) collective-permute-start(bf16[2,1920]{1,0:T(2,128)(2,1)S(1)} %get-tuple-element.56), channel_id=1, source_target_pairs={{0,8},{8,0},{16,24},{24,16},{1,9},{9,1},{17,25},{25,17},{2,10},{10... | collective-permute-start | bytes 23048 | tf_op jit(solution)/shard_map/ppermute | solution.py:18

commit v8 on v7

--- a/solution.py
+++ b/solution.py
@@ -20,6 +20,20 @@
 
 def send_cross(block, axis, offset):
     return send_rel(block, (axis, "test"), offset * lax.axis_size("test") + 1)
+
+
+def plane_offsets(groups):
+    offsets = [(g, g) for g in reversed(range(1, groups))]
+    if groups > 2:
+        offsets[-2:] = [(1, 2), (2, 1)]
+    return offsets
+
+
+def send_plane(block, offsets):
+    pairs = []
+    for g in range(lax.axis_size("dp")):
+        pairs += [(2 * g + t, 2 * (g ^ offsets[t]) + 1 - t) for t in range(2)]
+    return lax.ppermute(block, ("dp", "test"), pairs)
 
 
 def is_direct(count):
@@ -90,14 +104,18 @@
 
 
 def select_kernel(experts, *refs):
-    sources, (hit_ref, *out_refs) = refs[:5], refs[5:-6]
-    ids, slots, weight, tok, grad, sems = refs[-6:]
-    copies = start_copies(zip(sources, (ids, slots, weight, tok, grad)), sems)
+    (ids_hbm, slots_hbm, weight_hbm, tok_hbm, grad_hbm), (hit_ref, *out_refs) = refs[:5], refs[5:-5]
+    ids, slots, weight, quarters, sems = refs[-5:]
+    tokens, quarter = quarters.shape[0] // KINDS, quarters.shape[1]
+    pairs = [(ids_hbm, ids), (slots_hbm, slots), (weight_hbm, weight)]
+    for kind in range(KINDS):
+        source, first = (tok_hbm, grad_hbm)[kind // 2], kind % 2 * quarter
+        target = quarters.at[kind * tokens : (kind + 1) * tokens]
+        pairs.append((source.at[:, first : first + quarter], target))
+    copies = start_copies(pairs, sems)
     here = lax.axis_index("expert")
     unit = KINDS * CAP
-    quarter = tok.shape[1] // 2
     row = lax.broadcasted_iota(jnp.int32, (experts * unit, 1), 0)
-    kind = (row % unit) // CAP
     turn = row // unit
     if is_direct(experts):
         turn = experts - 1 - turn
@@ -108,16 +126,12 @@
         copy.wait()
     hits, scaled = hit_tables(ids[...], slots[...], weight[...].astype(F32), want, experts)
     hit_ref[...] = hits
-    total = None
-    for index in range(KINDS):
-        table, source = (hits, tok) if index < 2 else (scaled, grad)
-        if index % 2 == 0:
-            copies[3 + index // 2].wait()
-        left = jnp.where(kind == index, table, 0.0).astype(BF16)
-        first = (index % 2) * quarter
-        part = dot_f32(left, source[:, first : first + quarter], ((1,), (0,)))
-        total = part if total is None else total + part
-    total = total.astype(BF16)
+    left = jnp.concatenate([hits, hits, scaled, scaled], axis=1)
+    column = lax.broadcasted_iota(jnp.int32, left.shape, 1)
+    left = jnp.where(column // tokens == (row % unit) // CAP, left, 0.0).astype(BF16)
+    for copy in copies[3:]:
+        copy.wait()
+    total = dot_f32(left, quarters[...], ((1,), (0,))).astype(BF16)
     for k, out_ref in enumerate(out_refs):
         out_ref[...] = total[k * unit : (k + 1) * unit]
 
@@ -131,13 +145,23 @@
         out_ref[kind * pairs : (kind + 1) * pairs] = jnp.concatenate(rows).astype(BF16)
 
 
-def join_kernel(*refs):
-    *block_refs, out_ref = refs
-    pairs = block_refs[0].shape[0] // KINDS
-    for kind in range(KINDS):
-        for g, block_ref in enumerate(block_refs[::-1]):
-            first = (kind * len(block_refs) + g) * pairs
-            out_ref[first : first + pairs] = block_ref[kind * pairs : (kind + 1) * pairs]
+def join_kernel(offsets, *refs):
+    *block_refs, own_ref, out_ref = refs
+    count = len(offsets) + 1
+    pairs = own_ref.shape[0] // KINDS
+
+    def place(ref, g):
+        for kind in range(KINDS):
+            first = (kind * count + g) * pairs
+            out_ref[first : first + pairs] = ref[kind * pairs : (kind + 1) * pairs]
+
+    place(own_ref, 0)
+    for core in range(2):
+
+        @pl.when(lax.axis_index("test") == core)
+        def _():
+            for ref, offset in zip(block_refs, offsets):
+                place(ref, offset[1 - core])
 
 
 def load_kernel(shapes, *refs):
@@ -232,14 +256,24 @@
             rest_ref[pairs:, columns] = part[pairs:]
 
 
-def pair_kernel(half, keep_ref, got_ref, *out_refs):
+def pair_kernel(half, offsets, keep_ref, got_ref, *refs):
+    *out_refs, own_ref = refs
     kept, got = keep_ref[...].astype(F32), got_ref[...].astype(F32)
     main = (kept[:, :half] + got[:, :half]).astype(BF16)
     tail = split_two(join_two(kept[:, half:]) + join_two(got[:, half:]))
-    rows = out_refs[0].shape[0]
-    for g, out_ref in enumerate(out_refs[::-1]):
-        out_ref[:, :half] = main[g * rows : (g + 1) * rows]
-        out_ref[:, half:] = tail[g * rows : (g + 1) * rows]
+    rows = own_ref.shape[0]
+
+    def place(ref, g):
+        ref[:, :half] = main[g * rows : (g + 1) * rows]
+        ref[:, half:] = tail[g * rows : (g + 1) * rows]
+
+    place(own_ref, 0)
+    for core in range(2):
+
+        @pl.when(lax.axis_index("test") == core)
+        def _():
+            for ref, offset in zip(out_refs, offsets):
+                place(ref, offset[core])
 
 
 def score_kernel(half, order, *refs):
@@ -252,8 +286,11 @@
     hid = join_two(total[:, half:])
     grad = grad_ref[...]
     proj = grad.shape[1]
-    for p in range(proj):
-        feature[:, p * proj : (p + 1) * proj] = (hid[:, p : p + 1] * grad).astype(BF16)
+    grad = jnp.concatenate([grad, grad], axis=1)
+    left = lax.broadcasted_iota(jnp.int32, grad.shape, 1) < proj
+    for p in range(0, proj, 2):
+        pair = jnp.where(left, hid[:, p : p + 1], hid[:, p + 1 : p + 2])
+        feature[:, p * proj : (p + 2) * proj] = (pair * grad).astype(BF16)
     score = dot_f32(feature[...], test_ref[...], ((1,), (1,)))
     for k, out_ref in zip(order, out_refs):
         out_ref[:, :half] = total[k * CAP : (k + 1) * CAP, :half].astype(BF16)
@@ -314,10 +351,11 @@
             + [jax.ShapeDtypeStruct((unit, quarter), BF16)] * experts,
             in_specs=in_hbm(5),
             out_specs=whole_vmem(experts + 1),
-            scratch_shapes=[
-                pltpu.VMEM(x.shape, x.dtype) for x in (ids_t, slots_t, weight_t, tokens, out_grad)
-            ]
-            + [pltpu.SemaphoreType.DMA((5,))],
+            scratch_shapes=[pltpu.VMEM(x.shape, x.dtype) for x in (ids_t, slots_t, weight_t)]
+            + [
+                pltpu.VMEM((KINDS * tok_rows, quarter), BF16),
+                pltpu.SemaphoreType.DMA((3 + KINDS,)),
+            ],
             compiler_params=limit(rows),
         )(*map(keep_in_hbm, (ids_t, slots_t, weight_t, tokens, out_grad)))
     slots = exchange(send_cross, parts, experts)
@@ -329,17 +367,18 @@
             out_specs=whole_vmem(1)[0],
             compiler_params=limit(rows),
         )(*slots[::-1])
-    blocks = [send_cross(block, "dp", g) for g in reversed(range(1, groups))] + [block]
+    offsets = plane_offsets(groups)
+    blocks = [block] + [send_plane(block, offset) for offset in offsets[::-1]]
     loaded = load(block, [[w_gate[0], w_up[0]], [w_down[0]], [proj_hidden[0]]], limit(rows))
     blocks, (pair_w, down_w, hid_proj) = lax.optimization_barrier((blocks, loaded))
     with jax.named_scope("join"):
         own = pl.pallas_call(
-            join_kernel,
+            functools.partial(join_kernel, offsets),
             out_shape=jax.ShapeDtypeStruct((KINDS * rows, quarter), BF16),
             in_specs=whole_vmem(groups),
             out_specs=whole_vmem(1)[0],
             compiler_params=limit(rows),
-        )(*blocks)
+        )(*blocks[::-1])
     other = send_rel(own, "test", 1)
     with jax.named_scope("expert"):
         keep, send, mine = pl.pallas_call(
@@ -357,13 +396,13 @@
     got = send_rel(send, "test", 1)
     with jax.named_scope("pair"):
         sums = pl.pallas_call(
-            functools.partial(pair_kernel, half),
+            functools.partial(pair_kernel, half, offsets),
             out_shape=[jax.ShapeDtypeStruct((pairs, out_width), BF16)] * groups,
             in_specs=whole_vmem(2),
             out_specs=whole_vmem(groups),
             compiler_params=limit(rows),
         )(keep, got)
-    pieces = [send_cross(sums[-1 - g], "dp", g) for g in reversed(range(1, groups))] + [sums[-1]]
+    pieces = [send_plane(x, offset) for x, offset in zip(sums, offsets)] + [sums[-1]]
     grad_proj, test_rows = load(sums[-1], [[proj_grad[0]], [test_feats[0]]], limit(rows))
     grad_mine = dot_f32(mine, grad_proj, ((1,), (1,)))
     order = slot_order(experts)

time: 35.8 us -> 35.6 us (level)
    ppermute x0 -> x6, starting transfers between devices: none -> 7.36 us  [send_plane(): return lax.ppermute(block, ('dp', 'test'), pairs)]
    ppermute x14 -> x8, starting transfers between devices: 17.5 us -> 10.2 us  [send_rel(): return lax.ppermute(block, axis, [(i, i ^ offset) for i in range(size)])]
    ppermute x14 -> x8, waiting for transfers between devices: 9.51 us -> 7.49 us  [send_rel(): return lax.ppermute(block, axis, [(i, i ^ offset) for i in range(size)])]
    ppermute x0 -> x6, waiting for transfers between devices: none -> 1.85 us  [send_plane(): return lax.ppermute(block, ('dp', 'test'), pairs)]
  transfers between devices with their start and end apart: 14 -> 14, of which waited for: 10 -> 11; matrix products, arithmetic and copies ran while one was open for 1% -> 1% of each run, Pallas kernels for 9% -> 9%
where the time goes in v8:
time: 35.6 us; the launch traced here: 35.4 us
  starting transfers between devices  17.6 us (49%)
  waiting for transfers between devices  9.34 us (26%)
  Pallas kernels  7.59 us (21%)
  between operations  0.69 us (2%)
    ppermute x8, starting transfers between devices, send_rel(): return lax.ppermute(block, axis, [(i, i ^ offset) for i in range(size)])  10.2 us
    ppermute x8, waiting for transfers between devices, send_rel(): return lax.ppermute(block, axis, [(i, i ^ offset) for i in range(size)])  7.49 us
    ppermute x6, starting transfers between devices, send_plane(): return lax.ppermute(block, ('dp', 'test'), pairs)  7.36 us
    pallas_call x2, Pallas kernels, load(): pl.pallas_call(functools.partial(load_kernel, shapes), out_shape=[jax.Sha...  3.15 us
    ppermute x6, waiting for transfers between devices, send_plane(): return lax.ppermute(block, ('dp', 'test'), pairs)  1.85 us
    pallas_call x1, Pallas kernels, on_device(): pl.pallas_call(expert_kernel, out_shape=[jax.ShapeDtypeStruct((rows, out_...  1.38 us
    pallas_call x1, Pallas kernels, on_device(): pl.pallas_call(functools.partial(select_kernel, experts), out_shape=[jax....  1.37 us
    pallas_call x1, Pallas kernels, on_device(): pl.pallas_call(functools.partial(finish_kernel, experts), out_shape=[jax....  0.95 us
  transfers between devices with their start and end apart: 14, of which 11 were waited for; matrix products, arithmetic and copies ran while one was open for 1% of the time, Pallas kernels for 9%

profile of v8, /device:TPU:0, one launch (start us, length us, event | category | flops | bytes accessed | tf_op | source)
XLA Modules:
  0.0 35.4 jit_solution(6007870932079544994)
XLA Ops:
  0.6 1.4 %select.1 = (f32[32,64]{1,0:T(8,128)S(1)}, bf16[8,896]{1,0:T(8,128)(2,1)S(1)}, bf16[8,896]{1,0:T(8,128)(2,1)S(1)}, bf16[8,896]{1,0:T(8,128)(2,1)S(1)}, bf16[8,896]{1,0:T(8,128)(2,1)S(1)}) custom-call(s32[8,64]{1,0:T(8,128)} %bitcast.17, s32[8,64]{1,0:T(8,128)} %bitcast.18, bf16[8,64]{1,0:T(8,128)(2,1)} %bitcast.19, bf16[64,1792]{1,0:T(8,128)(2,1)} %refs_3_.1, ...), custom_call_target="tpu_custom_call" | custom-call | tf_op jit(solution)/shard_map/select/pallas_call | solution.py:348
  2.0 4.6 %collective-permute-start = (bf16[8,896]{1,0:T(8,128)(2,1)S(1)}, bf16[8,896]{1,0:T(8,128)(2,1)S(1)}, u32[]{:S(2)}, u32[]{:S(2)}) collective-permute-start(bf16[8,896]{1,0:T(8,128)(2,1)S(1)} %get-tuple-element.31), channel_id=1, source_target_pairs={{0,25},{1,24},{8,17},{9,16},{16,9},{17,8},{24,1},{25,0},{2,27},{3,... | collective-permute-start | bytes 43016 | tf_op jit(solution)/shard_map/ppermute | solution.py:18
  6.6 0.9 %collective-permute-start.2 = (bf16[8,896]{1,0:T(8,128)(2,1)S(1)}, bf16[8,896]{1,0:T(8,128)(2,1)S(1)}, u32[]{:S(2)}, u32[]{:S(2)}) collective-permute-start(bf16[8,896]{1,0:T(8,128)(2,1)S(1)} %get-tuple-element.33), channel_id=1, source_target_pairs={{0,9},{1,8},{8,1},{9,0},{16,25},{17,24},{24,17},{25,16},{2,11},{3,... | collective-permute-start | bytes 43016 | tf_op jit(solution)/shard_map/ppermute | solution.py:18
  7.5 0.5 %collective-permute-done.refs_0_ = bf16[8,896]{1,0:T(8,128)(2,1)S(1)} collective-permute-done((bf16[8,896]{1,0:T(8,128)(2,1)S(1)}, bf16[8,896]{1,0:T(8,128)(2,1)S(1)}, u32[]{:S(2)}, u32[]{:S(2)}) %collective-permute-start) | collective-permute-done | bytes 14368 | tf_op jit(solution)/shard_map/ppermute | solution.py:18
  8.0 2.7 %collective-permute-done.1.refs_1_ = bf16[8,896]{1,0:T(8,128)(2,1)S(1)} collective-permute-done((bf16[8,896]{1,0:T(8,128)(2,1)S(1)}, bf16[8,896]{1,0:T(8,128)(2,1)S(1)}, u32[]{:S(2)}, u32[]{:S(2)}) %collective-permute-start.1) | collective-permute-done | bytes 14368 | tf_op jit(solution)/shard_map/ppermute | solution.py:18
  10.8 2.7 %collective-permute-start.5 = (bf16[32,896]{1,0:T(8,128)(2,1)S(1)}, bf16[32,896]{1,0:T(8,128)(2,1)S(1)}, u32[]{:S(2)}, u32[]{:S(2)}) collective-permute-start(bf16[32,896]{1,0:T(8,128)(2,1)S(1)} %arrange.1.refs_0_.refs_3_), channel_id=1, source_target_pairs={{0,7},{1,6},{2,5},{3,4},{4,3},{5,2},{6,1},{7,0},{8,15},{9,14},{10,... | collective-permute-start | bytes 172040 | tf_op jit(solution)/shard_map/ppermute | solution.py:36
  13.5 1.7 %collective-permute-start.3 = (bf16[32,896]{1,0:T(8,128)(2,1)S(1)}, bf16[32,896]{1,0:T(8,128)(2,1)S(1)}, u32[]{:S(2)}, u32[]{:S(2)}) collective-permute-start(bf16[32,896]{1,0:T(8,128)(2,1)S(1)} %arrange.1.refs_0_.refs_3_), channel_id=1, source_target_pairs={{0,5},{1,2},{2,7},{3,0},{4,1},{5,6},{6,3},{7,4},{8,13},{9,10},{10,... | collective-permute-start | bytes 172040 | tf_op jit(solution)/shard_map/ppermute | solution.py:36
  15.2 1.8 %load.2 = (bf16[3584,256]{1,0:T(8,128)(2,1)S(1)}, bf16[128,3584]{1,0:T(8,128)(2,1)S(1)}, bf16[64,128]{1,0:T(8,128)(2,1)S(1)}) custom-call(bf16[32,896]{1,0:T(8,128)(2,1)S(1)} %arrange.1.refs_0_.refs_3_, bf16[3584,128]{1,0:T(8,128)(2,1)} %bitcast.12, bf16[3584,128]{1,0:T(8,128)(2,1)} %bitcast.13, bf16[128,3584]{1,0:T(8,128)(2,1)} %bitcast.14, ...), custom_call_target="tpu_custom_call" | custom-call | bytes 2768896 | tf_op jit(solution)/shard_map/load/pallas_call | solution.py:195
  17.0 0.7 %collective-permute-done.3.refs_2_ = bf16[32,896]{1,0:T(8,128)(2,1)S(1)} collective-permute-done((bf16[32,896]{1,0:T(8,128)(2,1)S(1)}, bf16[32,896]{1,0:T(8,128)(2,1)S(1)}, u32[]{:S(2)}, u32[]{:S(2)}) %collective-permute-start.3) | collective-permute-done | bytes 57376 | tf_op jit(solution)/shard_map/ppermute | solution.py:36
  17.9 1.4 %collective-permute-done.6.other_ref = bf16[128,896]{1,0:T(8,128)(2,1)S(1)} collective-permute-done((bf16[128,896]{1,0:T(8,128)(2,1)S(1)}, bf16[128,896]{1,0:T(8,128)(2,1)S(1)}, u32[]{:S(2)}, u32[]{:S(2)}) %collective-permute-start.6) | collective-permute-done | bytes 229408 | tf_op jit(solution)/shard_map/ppermute | solution.py:18
  19.3 1.4 %expert.1 = (bf16[32,1920]{1,0:T(8,128)(2,1)S(1)}, bf16[32,1920]{1,0:T(8,128)(2,1)S(1)}, bf16[8,3584]{1,0:T(8,128)(2,1)S(1)}) custom-call(bf16[128,896]{1,0:T(8,128)(2,1)S(1)} %join.1.own_ref, bf16[128,896]{1,0:T(8,128)(2,1)S(1)} %collective-permute-done.6.other_ref, bf16[3584,256]{1,0:T(8,128)(2,1)S(1)} %get-tuple-element.42.pair_w, ...), custom_call_target="tpu_custom_call" | custom-call | tf_op jit(solution)/shard_map/expert/pallas_call | solution.py:384
  20.8 1.2 %collective-permute-done.7.got_ref = bf16[32,1920]{1,0:T(8,128)(2,1)S(1)} collective-permute-done((bf16[32,1920]{1,0:T(8,128)(2,1)S(1)}, bf16[32,1920]{1,0:T(8,128)(2,1)S(1)}, u32[]{:S(2)}, u32[]{:S(2)}) %collective-permute-start.7) | collective-permute-done | bytes 122912 | tf_op jit(solution)/shard_map/ppermute | solution.py:18
  22.2 1.2 %collective-permute-start.8 = (bf16[8,1920]{1,0:T(8,128)(2,1)S(1)}, bf16[8,1920]{1,0:T(8,128)(2,1)S(1)}, u32[]{:S(2)}, u32[]{:S(2)}) collective-permute-start(bf16[8,1920]{1,0:T(8,128)(2,1)S(1)} %get-tuple-element.47), channel_id=1, source_target_pairs={{0,7},{1,6},{2,5},{3,4},{4,3},{5,2},{6,1},{7,0},{8,15},{9,14},{10,... | collective-permute-start | bytes 92168 | tf_op jit(solution)/shard_map/ppermute | solution.py:36
  23.4 1.1 %collective-permute-start.9 = (bf16[8,1920]{1,0:T(8,128)(2,1)S(1)}, bf16[8,1920]{1,0:T(8,128)(2,1)S(1)}, u32[]{:S(2)}, u32[]{:S(2)}) collective-permute-start(bf16[8,1920]{1,0:T(8,128)(2,1)S(1)} %get-tuple-element.48), channel_id=1, source_target_pairs={{0,3},{1,4},{2,1},{3,6},{4,7},{5,0},{6,5},{7,2},{8,11},{9,12},{10,... | collective-permute-start | bytes 92168 | tf_op jit(solution)/shard_map/ppermute | solution.py:36
  24.5 0.6 %collective-permute-start.10 = (bf16[8,1920]{1,0:T(8,128)(2,1)S(1)}, bf16[8,1920]{1,0:T(8,128)(2,1)S(1)}, u32[]{:S(2)}, u32[]{:S(2)}) collective-permute-start(bf16[8,1920]{1,0:T(8,128)(2,1)S(1)} %get-tuple-element.49), channel_id=1, source_target_pairs={{0,5},{1,2},{2,7},{3,0},{4,1},{5,6},{6,3},{7,4},{8,13},{9,10},{10,... | collective-permute-start | bytes 92168 | tf_op jit(solution)/shard_map/ppermute | solution.py:36
  25.1 1.4 %load.3 = (bf16[64,3584]{1,0:T(8,128)(2,1)S(1)}, bf16[128,4096]{1,0:T(8,128)(2,1)S(1)}) custom-call(bf16[8,1920]{1,0:T(8,128)(2,1)S(1)} %get-tuple-element.50.refs_0_.refs_3_, bf16[64,3584]{1,0:T(8,128)(2,1)} %bitcast.15, bf16[128,4096]{1,0:T(8,128)(2,1)} %bitcast.11), custom_call_target="tpu_custom_call" | custom-call | bytes 1507328 | tf_op jit(solution)/shard_map/load/pallas_call | solution.py:195
  27.1 0.8 %collective-permute-done.10.refs_2_ = bf16[8,1920]{1,0:T(8,128)(2,1)S(1)} collective-permute-done((bf16[8,1920]{1,0:T(8,128)(2,1)S(1)}, bf16[8,1920]{1,0:T(8,128)(2,1)S(1)}, u32[]{:S(2)}, u32[]{:S(2)}) %collective-permute-start.10) | collective-permute-done | bytes 30752 | tf_op jit(solution)/shard_map/ppermute | solution.py:36
  27.8 0.5 %score.1 = (bf16[2,1920]{1,0:T(2,128)(2,1)S(1)}, bf16[2,1920]{1,0:T(2,128)(2,1)S(1)}, bf16[2,1920]{1,0:T(2,128)(2,1)S(1)}, bf16[2,1920]{1,0:T(2,128)(2,1)S(1)}) custom-call(bf16[8,1920]{1,0:T(8,128)(2,1)S(1)} %collective-permute-done.8.refs_0_, bf16[8,1920]{1,0:T(8,128)(2,1)S(1)} %collective-permute-done.9.refs_1_, ...), custom_call_target="tpu_custom_call" | custom-call | tf_op jit(solution)/shard_map/score/pallas_call | solution.py:410
  28.4 1.5 %collective-permute-start.11 = (bf16[2,1920]{1,0:T(2,128)(2,1)S(1)}, bf16[2,1920]{1,0:T(2,128)(2,1)S(1)}, u32[]{:S(2)}, u32[]{:S(2)}) collective-permute-start(bf16[2,1920]{1,0:T(2,128)(2,1)S(1)} %get-tuple-element.54), channel_id=1, source_target_pairs={{0,24},{8,16},{16,8},{24,0},{1,25},{9,17},{17,9},{25,1},{2,26},{10... | collective-permute-start | bytes 23048 | tf_op jit(solution)/shard_map/ppermute | solution.py:18
  29.8 0.5 %collective-permute-start.12 = (bf16[2,1920]{1,0:T(2,128)(2,1)S(1)}, bf16[2,1920]{1,0:T(2,128)(2,1)S(1)}, u32[]{:S(2)}, u32[]{:S(2)}) collective-permute-start(bf16[2,1920]{1,0:T(2,128)(2,1)S(1)} %get-tuple-element.55), channel_id=1, source_target_pairs={{0,16},{8,24},{16,0},{24,8},{1,17},{9,25},{17,1},{25,9},{2,18},{10... | collective-permute-start | bytes 23048 | tf_op jit(solution)/shard_map/ppermute | solution.py:18
  30.3 2.4 %collective-permute-start.13 = (bf16[2,1920]{1,0:T(2,128)(2,1)S(1)}, bf16[2,1920]{1,0:T(2,128)(2,1)S(1)}, u32[]{:S(2)}, u32[]{:S(2)}) collective-permute-start(bf16[2,1920]{1,0:T(2,128)(2,1)S(1)} %get-tuple-element.56), channel_id=1, source_target_pairs={{0,8},{8,0},{16,24},{24,16},{1,9},{9,1},{17,25},{25,17},{2,10},{10... | collective-permute-start | bytes 23048 | tf_op jit(solution)/shard_map/ppermute | solution.py:18
  32.8 1.1 %collective-permute-done.11.refs_0_ = bf16[2,1920]{1,0:T(2,128)(2,1)S(1)} collective-permute-done((bf16[2,1920]{1,0:T(2,128)(2,1)S(1)}, bf16[2,1920]{1,0:T(2,128)(2,1)S(1)}, u32[]{:S(2)}, u32[]{:S(2)}) %collective-permute-start.11) | collective-permute-done | bytes 7712 | tf_op jit(solution)/shard_map/ppermute | solution.py:18
  33.8 0.6 %collective-permute-done.12.refs_1_ = bf16[2,1920]{1,0:T(2,128)(2,1)S(1)} collective-permute-done((bf16[2,1920]{1,0:T(2,128)(2,1)S(1)}, bf16[2,1920]{1,0:T(2,128)(2,1)S(1)}, u32[]{:S(2)}, u32[]{:S(2)}) %collective-permute-start.12) | collective-permute-done | bytes 7712 | tf_op jit(solution)/shard_map/ppermute | solution.py:18
  34.5 0.9 %finish.1 = (bf16[64,1792]{1,0:T(8,128)(2,1)}, f32[64,128]{1,0:T(8,128)}) custom-call(f32[32,64]{1,0:T(8,128)S(1)} %get-tuple-element.30.hit_ref, bf16[2,1920]{1,0:T(2,128)(2,1)S(1)} %collective-permute-done.11.refs_0_, bf16[2,1920]{1,0:T(2,128)(2,1)S(1)} %collective-permute-done.12.refs_1_, bf16[2,1920]{1,0:T(2,128)(2,1)S(1)} %collective-permute-done.13.refs_2_, ...), custom_call_target="tpu_custom_call" | custom-call | tf_op jit(solution)/shard_map/finish/pallas_call | solution.py:421
  (14 shorter events, 1.4 us)
Async XLA Ops:
  2.0 6.0 %collective-permute-start = (bf16[8,896]{1,0:T(8,128)(2,1)S(1)}, bf16[8,896]{1,0:T(8,128)(2,1)S(1)}, u32[]{:S(2)}, u32[]{:S(2)}) collective-permute-start(bf16[8,896]{1,0:T(8,128)(2,1)S(1)} %get-tuple-element.31), channel_id=1, source_target_pairs={{0,25},{1,24},{8,17},{9,16},{16,9},{17,8},{24,1},{25,0},{2,27},{3,... | collective-permute-start | bytes 43016 | tf_op jit(solution)/shard_map/ppermute | solution.py:18
  6.6 4.1 %collective-permute-start.1 = (bf16[8,896]{1,0:T(8,128)(2,1)S(1)}, bf16[8,896]{1,0:T(8,128)(2,1)S(1)}, u32[]{:S(2)}, u32[]{:S(2)}) collective-permute-start(bf16[8,896]{1,0:T(8,128)(2,1)S(1)} %get-tuple-element.32), channel_id=1, source_target_pairs={{0,17},{1,16},{8,25},{9,24},{16,1},{17,0},{24,9},{25,8},{2,19},{3,... | collective-permute-start | bytes 43016 | tf_op jit(solution)/shard_map/ppermute | solution.py:18
  6.6 4.1 %collective-permute-start.2 = (bf16[8,896]{1,0:T(8,128)(2,1)S(1)}, bf16[8,896]{1,0:T(8,128)(2,1)S(1)}, u32[]{:S(2)}, u32[]{:S(2)}) collective-permute-start(bf16[8,896]{1,0:T(8,128)(2,1)S(1)} %get-tuple-element.33), channel_id=1, source_target_pairs={{0,9},{1,8},{8,1},{9,0},{16,25},{17,24},{24,17},{25,16},{2,11},{3,... | collective-permute-start | bytes 43016 | tf_op jit(solution)/shard_map/ppermute | solution.py:18
  10.8 6.2 %collective-permute-start.5 = (bf16[32,896]{1,0:T(8,128)(2,1)S(1)}, bf16[32,896]{1,0:T(8,128)(2,1)S(1)}, u32[]{:S(2)}, u32[]{:S(2)}) collective-permute-start(bf16[32,896]{1,0:T(8,128)(2,1)S(1)} %arrange.1.refs_0_.refs_3_), channel_id=1, source_target_pairs={{0,7},{1,6},{2,5},{3,4},{4,3},{5,2},{6,1},{7,0},{8,15},{9,14},{10,... | collective-permute-start | bytes 172040 | tf_op jit(solution)/shard_map/ppermute | solution.py:36
  13.4 3.6 %collective-permute-start.4 = (bf16[32,896]{1,0:T(8,128)(2,1)S(1)}, bf16[32,896]{1,0:T(8,128)(2,1)S(1)}, u32[]{:S(2)}, u32[]{:S(2)}) collective-permute-start(bf16[32,896]{1,0:T(8,128)(2,1)S(1)} %arrange.1.refs_0_.refs_3_), channel_id=1, source_target_pairs={{0,3},{1,4},{2,1},{3,6},{4,7},{5,0},{6,5},{7,2},{8,11},{9,12},{10,... | collective-permute-start | bytes 172040 | tf_op jit(solution)/shard_map/ppermute | solution.py:36
  13.5 4.2 %collective-permute-start.3 = (bf16[32,896]{1,0:T(8,128)(2,1)S(1)}, bf16[32,896]{1,0:T(8,128)(2,1)S(1)}, u32[]{:S(2)}, u32[]{:S(2)}) collective-permute-start(bf16[32,896]{1,0:T(8,128)(2,1)S(1)} %arrange.1.refs_0_.refs_3_), channel_id=1, source_target_pairs={{0,5},{1,2},{2,7},{3,0},{4,1},{5,6},{6,3},{7,4},{8,13},{9,10},{10,... | collective-permute-start | bytes 172040 | tf_op jit(solution)/shard_map/ppermute | solution.py:36
  17.7 1.6 %collective-permute-start.6 = (bf16[128,896]{1,0:T(8,128)(2,1)S(1)}, bf16[128,896]{1,0:T(8,128)(2,1)S(1)}, u32[]{:S(2)}, u32[]{:S(2)}) collective-permute-start(bf16[128,896]{1,0:T(8,128)(2,1)S(1)} %join.1.own_ref), channel_id=1, source_target_pairs={{0,1},{1,0},{2,3},{3,2},{4,5},{5,4},{6,7},{7,6},{8,9},{9,8},{10,11... | collective-permute-start | bytes 688136 | tf_op jit(solution)/shard_map/ppermute | solution.py:18
  20.7 1.4 %collective-permute-start.7 = (bf16[32,1920]{1,0:T(8,128)(2,1)S(1)}, bf16[32,1920]{1,0:T(8,128)(2,1)S(1)}, u32[]{:S(2)}, u32[]{:S(2)}) collective-permute-start(bf16[32,1920]{1,0:T(8,128)(2,1)S(1)} %get-tuple-element.46), channel_id=1, source_target_pairs={{0,1},{1,0},{2,3},{3,2},{4,5},{5,4},{6,7},{7,6},{8,9},{9,8},{10,11... | collective-permute-start | bytes 368648 | tf_op jit(solution)/shard_map/ppermute | solution.py:18
  22.2 4.5 %collective-permute-start.8 = (bf16[8,1920]{1,0:T(8,128)(2,1)S(1)}, bf16[8,1920]{1,0:T(8,128)(2,1)S(1)}, u32[]{:S(2)}, u32[]{:S(2)}) collective-permute-start(bf16[8,1920]{1,0:T(8,128)(2,1)S(1)} %get-tuple-element.47), channel_id=1, source_target_pairs={{0,7},{1,6},{2,5},{3,4},{4,3},{5,2},{6,1},{7,0},{8,15},{9,14},{10,... | collective-permute-start | bytes 92168 | tf_op jit(solution)/shard_map/ppermute | solution.py:36
  23.4 3.7 %collective-permute-start.9 = (bf16[8,1920]{1,0:T(8,128)(2,1)S(1)}, bf16[8,1920]{1,0:T(8,128)(2,1)S(1)}, u32[]{:S(2)}, u32[]{:S(2)}) collective-permute-start(bf16[8,1920]{1,0:T(8,128)(2,1)S(1)} %get-tuple-element.48), channel_id=1, source_target_pairs={{0,3},{1,4},{2,1},{3,6},{4,7},{5,0},{6,5},{7,2},{8,11},{9,12},{10,... | collective-permute-start | bytes 92168 | tf_op jit(solution)/shard_map/ppermute | solution.py:36
  24.5 3.3 %collective-permute-start.10 = (bf16[8,1920]{1,0:T(8,128)(2,1)S(1)}, bf16[8,1920]{1,0:T(8,128)(2,1)S(1)}, u32[]{:S(2)}, u32[]{:S(2)}) collective-permute-start(bf16[8,1920]{1,0:T(8,128)(2,1)S(1)} %get-tuple-element.49), channel_id=1, source_target_pairs={{0,5},{1,2},{2,7},{3,0},{4,1},{5,6},{6,3},{7,4},{8,13},{9,10},{10,... | collective-permute-start | bytes 92168 | tf_op jit(solution)/shard_map/ppermute | solution.py:36
  28.4 5.5 %collective-permute-start.11 = (bf16[2,1920]{1,0:T(2,128)(2,1)S(1)}, bf16[2,1920]{1,0:T(2,128)(2,1)S(1)}, u32[]{:S(2)}, u32[]{:S(2)}) collective-permute-start(bf16[2,1920]{1,0:T(2,128)(2,1)S(1)} %get-tuple-element.54), channel_id=1, source_target_pairs={{0,24},{8,16},{16,8},{24,0},{1,25},{9,17},{17,9},{25,1},{2,26},{10... | collective-permute-start | bytes 23048 | tf_op jit(solution)/shard_map/ppermute | solution.py:18
  29.8 4.5 %collective-permute-start.12 = (bf16[2,1920]{1,0:T(2,128)(2,1)S(1)}, bf16[2,1920]{1,0:T(2,128)(2,1)S(1)}, u32[]{:S(2)}, u32[]{:S(2)}) collective-permute-start(bf16[2,1920]{1,0:T(2,128)(2,1)S(1)} %get-tuple-element.55), channel_id=1, source_target_pairs={{0,16},{8,24},{16,0},{24,8},{1,17},{9,25},{17,1},{25,9},{2,18},{10... | collective-permute-start | bytes 23048 | tf_op jit(solution)/shard_map/ppermute | solution.py:18
  30.3 4.1 %collective-permute-start.13 = (bf16[2,1920]{1,0:T(2,128)(2,1)S(1)}, bf16[2,1920]{1,0:T(2,128)(2,1)S(1)}, u32[]{:S(2)}, u32[]{:S(2)}) collective-permute-start(bf16[2,1920]{1,0:T(2,128)(2,1)S(1)} %get-tuple-element.56), channel_id=1, source_target_pairs={{0,8},{8,0},{16,24},{24,16},{1,9},{9,1},{17,25},{25,17},{2,10},{10... | collective-permute-start | bytes 23048 | tf_op jit(solution)/shard_map/ppermute | solution.py:18

commit v9 on v8

--- a/solution.py
+++ b/solution.py
@@ -104,18 +104,14 @@
 
 
 def select_kernel(experts, *refs):
-    (ids_hbm, slots_hbm, weight_hbm, tok_hbm, grad_hbm), (hit_ref, *out_refs) = refs[:5], refs[5:-5]
-    ids, slots, weight, quarters, sems = refs[-5:]
-    tokens, quarter = quarters.shape[0] // KINDS, quarters.shape[1]
-    pairs = [(ids_hbm, ids), (slots_hbm, slots), (weight_hbm, weight)]
-    for kind in range(KINDS):
-        source, first = (tok_hbm, grad_hbm)[kind // 2], kind % 2 * quarter
-        target = quarters.at[kind * tokens : (kind + 1) * tokens]
-        pairs.append((source.at[:, first : first + quarter], target))
-    copies = start_copies(pairs, sems)
+    sources, (hit_ref, *out_refs) = refs[:5], refs[5:-6]
+    ids, slots, weight, tok, grad, sems = refs[-6:]
+    copies = start_copies(zip(sources, (ids, slots, weight, tok, grad)), sems)
     here = lax.axis_index("expert")
     unit = KINDS * CAP
+    quarter = tok.shape[1] // 2
     row = lax.broadcasted_iota(jnp.int32, (experts * unit, 1), 0)
+    kind = (row % unit) // CAP
     turn = row // unit
     if is_direct(experts):
         turn = experts - 1 - turn
@@ -126,12 +122,16 @@
         copy.wait()
     hits, scaled = hit_tables(ids[...], slots[...], weight[...].astype(F32), want, experts)
     hit_ref[...] = hits
-    left = jnp.concatenate([hits, hits, scaled, scaled], axis=1)
-    column = lax.broadcasted_iota(jnp.int32, left.shape, 1)
-    left = jnp.where(column // tokens == (row % unit) // CAP, left, 0.0).astype(BF16)
-    for copy in copies[3:]:
-        copy.wait()
-    total = dot_f32(left, quarters[...], ((1,), (0,))).astype(BF16)
+    total = None
+    for index in range(KINDS):
+        table, source = (hits, tok) if index < 2 else (scaled, grad)
+        if index % 2 == 0:
+            copies[3 + index // 2].wait()
+        left = jnp.where(kind == index, table, 0.0).astype(BF16)
+        first = (index % 2) * quarter
+        part = dot_f32(left, source[:, first : first + quarter], ((1,), (0,)))
+        total = part if total is None else total + part
+    total = total.astype(BF16)
     for k, out_ref in enumerate(out_refs):
         out_ref[...] = total[k * unit : (k + 1) * unit]
 
@@ -164,15 +164,14 @@
                 place(ref, offset[1 - core])
 
 
-def load_kernel(shapes, *refs):
-    count = sum(len(group) for group in shapes)
-    sources, targets = list(refs[1 : 1 + count]), refs[1 + count : -1]
+def load_kernel(moves, *refs):
+    count = 1 + max(move[0] for move in moves)
+    sources, targets = refs[1 : 1 + count], refs[1 + count : -1]
     pairs = []
-    for group, target in zip(shapes, targets):
-        first = 0
-        for _, columns in group:
-            pairs.append((sources.pop(0), target.at[:, first : first + columns]))
-            first += columns
+    for source, column, width, target, row, place in moves:
+        rows = sources[source].shape[0]
+        block = targets[target].at[row : row + rows, place : place + width]
+        pairs.append((sources[source].at[:, column : column + width], block))
     for copy in start_copies(pairs, refs[-1]):
         copy.wait()
 
@@ -188,19 +187,14 @@
     return value[:, :middle] + value[:, middle:]
 
 
-def load(after, groups, compiler_params):
-    params = [x for group in groups for x in group]
-    shapes = [[x.shape for x in group] for group in groups]
+def load(after, params, shapes, moves, compiler_params):
     with jax.named_scope("load"):
         return pl.pallas_call(
-            functools.partial(load_kernel, shapes),
-            out_shape=[
-                jax.ShapeDtypeStruct((group[0][0], sum(x[1] for x in group)), BF16)
-                for group in shapes
-            ],
+            functools.partial(load_kernel, moves),
+            out_shape=[jax.ShapeDtypeStruct(shape, BF16) for shape in shapes],
             in_specs=whole_vmem(1) + in_hbm(len(params)),
-            out_specs=whole_vmem(len(groups)),
-            scratch_shapes=[pltpu.SemaphoreType.DMA((len(params),))],
+            out_specs=whole_vmem(len(shapes)),
+            scratch_shapes=[pltpu.SemaphoreType.DMA((len(moves),))],
             compiler_params=compiler_params,
             cost_estimate=pl.CostEstimate(
                 flops=0, bytes_accessed=sum(2 * x.size for x in params), transcendentals=0
@@ -213,7 +207,7 @@
 ):
     rows, width = x_in.shape
     half, quarter = width // 2, width // 4
-    pairs = mine_ref.shape[0]
+    pairs, ff = mine_ref.shape[0], proj_ref.shape[1]
     core = lax.axis_index("test")
     near, far = pl.multiple_of(core * half, 128), pl.multiple_of((1 - core) * half, 128)
     row = lax.broadcasted_iota(jnp.int32, (rows, quarter), 0)
@@ -226,17 +220,21 @@
             odd = odd ^ ((slot >> shift) & 1)
     odd = odd == 1
     for index in range(KINDS):
-        target = x_in if index < 2 else x_grad
         own = own_ref[index * rows : (index + 1) * rows]
         other = other_ref[index * rows : (index + 1) * rows]
-        first = (index % 2) * quarter
-        target[:, pl.ds(pl.multiple_of(near + first, 128), quarter)] = jnp.where(odd, other, own)
-        target[:, pl.ds(pl.multiple_of(far + first, 128), quarter)] = jnp.where(odd, own, other)
-    mine_ref[...] = x_grad[:pairs]
-    ff = down_w.shape[0]
+        for base, part in ((near, jnp.where(odd, other, own)), (far, jnp.where(odd, own, other))):
+            first = (index % 2) * quarter
+            if index < 2:
+                x_in[:, pl.ds(pl.multiple_of(base + first, 128), quarter)] = part
+            else:
+                row = pl.multiple_of(base // half * rows, rows)
+                x_grad[pl.ds(row, rows), first : first + quarter] = part
+    mine_ref[:, :half] = x_grad[:pairs]
+    mine_ref[:, half:] = x_grad[rows : rows + pairs]
     both_pre = dot_f32(x_in[...], pair_w[...], ((1,), (0,)))
     gate_pre, up_pre = both_pre[:, :ff], both_pre[:, ff:]
-    hid_grad = dot_f32(x_grad[...], down_w[...], ((1,), (1,)))
+    hid_grads = dot_f32(x_grad[...], down_w[...], ((1,), (1,)))
+    hid_grad = hid_grads[:rows, :ff] + hid_grads[rows:, ff:]
     sig = 1.0 / (1.0 + jnp.exp(-gate_pre))
     act_gate = gate_pre * sig
     hidden = (act_gate * up_pre).astype(BF16)
@@ -338,6 +336,7 @@
     quarter = half // 2
     width = half * lax.axis_size("test")
     proj, tests = proj_hidden.shape[1], test_feats.shape[1]
+    ff = w_gate.shape[2]
     pairs = experts * CAP
     rows = groups * pairs
     unit = KINDS * CAP
@@ -351,11 +350,10 @@
             + [jax.ShapeDtypeStruct((unit, quarter), BF16)] * experts,
             in_specs=in_hbm(5),
             out_specs=whole_vmem(experts + 1),
-            scratch_shapes=[pltpu.VMEM(x.shape, x.dtype) for x in (ids_t, slots_t, weight_t)]
-            + [
-                pltpu.VMEM((KINDS * tok_rows, quarter), BF16),
-                pltpu.SemaphoreType.DMA((3 + KINDS,)),
-            ],
+            scratch_shapes=[
+                pltpu.VMEM(x.shape, x.dtype) for x in (ids_t, slots_t, weight_t, tokens, out_grad)
+            ]
+            + [pltpu.SemaphoreType.DMA((5,))],
             compiler_params=limit(rows),
         )(*map(keep_in_hbm, (ids_t, slots_t, weight_t, tokens, out_grad)))
     slots = exchange(send_cross, parts, experts)
@@ -369,7 +367,14 @@
         )(*slots[::-1])
     offsets = plane_offsets(groups)
     blocks = [block] + [send_plane(block, offset) for offset in offsets[::-1]]
-    loaded = load(block, [[w_gate[0], w_up[0]], [w_down[0]], [proj_hidden[0]]], limit(rows))
+    loaded = load(
+        block,
+        [w_gate[0], w_up[0], w_down[0], proj_hidden[0]],
+        [(width, 2 * ff), (2 * ff, half), (proj, ff)],
+        [(0, 0, ff, 0, 0, 0), (1, 0, ff, 0, 0, ff)]
+        + [(2, 0, half, 1, 0, 0), (2, half, half, 1, ff, 0), (3, 0, ff, 2, 0, 0)],
+        limit(rows),
+    )
     blocks, (pair_w, down_w, hid_proj) = lax.optimization_barrier((blocks, loaded))
     with jax.named_scope("join"):
         own = pl.pallas_call(
@@ -390,7 +395,10 @@
             ],
             in_specs=whole_vmem(5),
             out_specs=whole_vmem(3),
-            scratch_shapes=[pltpu.VMEM((rows, width), BF16)] * 2,
+            scratch_shapes=[
+                pltpu.VMEM((rows, width), BF16),
+                pltpu.VMEM((2 * rows, half), BF16),
+            ],
             compiler_params=limit(rows),
         )(own, other, pair_w, down_w, hid_proj)
     got = send_rel(send, "test", 1)
@@ -403,7 +411,9 @@
             compiler_params=limit(rows),
         )(keep, got)
     pieces = [send_plane(x, offset) for x, offset in zip(sums, offsets)] + [sums[-1]]
-    grad_proj, test_rows = load(sums[-1], [[proj_grad[0]], [test_feats[0]]], limit(rows))
+    params = [proj_grad[0], test_feats[0]]
+    moves = [(index, 0, x.shape[1], index, 0, 0) for index, x in enumerate(params)]
+    grad_proj, test_rows = load(sums[-1], params, [x.shape for x in params], moves, limit(rows))
     grad_mine = dot_f32(mine, grad_proj, ((1,), (1,)))
     order = slot_order(experts)
     with jax.named_scope("score"):

time: 35.6 us -> 35.5 us (level)
  no operation moved by 1% of the time
where the time goes in v9:
time: 35.5 us; the launch traced here: 35.3 us
  starting transfers between devices  17.6 us (50%)
  waiting for transfers between devices  9.35 us (26%)
  Pallas kernels  7.44 us (21%)
  between operations  0.69 us (2%)
    ppermute x8, starting transfers between devices, send_rel(): return lax.ppermute(block, axis, [(i, i ^ offset) for i in range(size)])  10.2 us
    ppermute x8, waiting for transfers between devices, send_rel(): return lax.ppermute(block, axis, [(i, i ^ offset) for i in range(size)])  7.49 us
    ppermute x6, starting transfers between devices, send_plane(): return lax.ppermute(block, ('dp', 'test'), pairs)  7.36 us
    pallas_call x2, Pallas kernels, load(): pl.pallas_call(functools.partial(load_kernel, moves), out_shape=[jax.Shap...  3.14 us
    ppermute x6, waiting for transfers between devices, send_plane(): return lax.ppermute(block, ('dp', 'test'), pairs)  1.86 us
    pallas_call x1, Pallas kernels, on_device(): pl.pallas_call(expert_kernel, out_shape=[jax.ShapeDtypeStruct((rows, out_...  1.32 us
    pallas_call x1, Pallas kernels, on_device(): pl.pallas_call(functools.partial(select_kernel, experts), out_shape=[jax....  1.31 us
    pallas_call x1, Pallas kernels, on_device(): pl.pallas_call(functools.partial(finish_kernel, experts), out_shape=[jax....  0.95 us
  transfers between devices with their start and end apart: 14, of which 11 were waited for; matrix products, arithmetic and copies ran while one was open for 1% of the time, Pallas kernels for 9%

profile of v9, /device:TPU:0, one launch (start us, length us, event | category | flops | bytes accessed | tf_op | source)
XLA Modules:
  0.0 35.3 jit_solution(8113750932795466627)
XLA Ops:
  0.6 1.3 %select.1 = (f32[32,64]{1,0:T(8,128)S(1)}, bf16[8,896]{1,0:T(8,128)(2,1)S(1)}, bf16[8,896]{1,0:T(8,128)(2,1)S(1)}, bf16[8,896]{1,0:T(8,128)(2,1)S(1)}, bf16[8,896]{1,0:T(8,128)(2,1)S(1)}) custom-call(s32[8,64]{1,0:T(8,128)} %bitcast.17, s32[8,64]{1,0:T(8,128)} %bitcast.18, bf16[8,64]{1,0:T(8,128)(2,1)} %bitcast.19, bf16[64,1792]{1,0:T(8,128)(2,1)} %refs_3_.1, ...), custom_call_target="tpu_custom_call" | custom-call | tf_op jit(solution)/shard_map/select/pallas_call | solution.py:347
  1.9 4.6 %collective-permute-start = (bf16[8,896]{1,0:T(8,128)(2,1)S(1)}, bf16[8,896]{1,0:T(8,128)(2,1)S(1)}, u32[]{:S(2)}, u32[]{:S(2)}) collective-permute-start(bf16[8,896]{1,0:T(8,128)(2,1)S(1)} %get-tuple-element.31), channel_id=1, source_target_pairs={{0,25},{1,24},{8,17},{9,16},{16,9},{17,8},{24,1},{25,0},{2,27},{3,... | collective-permute-start | bytes 43016 | tf_op jit(solution)/shard_map/ppermute | solution.py:18
  6.5 0.9 %collective-permute-start.2 = (bf16[8,896]{1,0:T(8,128)(2,1)S(1)}, bf16[8,896]{1,0:T(8,128)(2,1)S(1)}, u32[]{:S(2)}, u32[]{:S(2)}) collective-permute-start(bf16[8,896]{1,0:T(8,128)(2,1)S(1)} %get-tuple-element.33), channel_id=1, source_target_pairs={{0,9},{1,8},{8,1},{9,0},{16,25},{17,24},{24,17},{25,16},{2,11},{3,... | collective-permute-start | bytes 43016 | tf_op jit(solution)/shard_map/ppermute | solution.py:18
  7.4 0.5 %collective-permute-done.refs_0_ = bf16[8,896]{1,0:T(8,128)(2,1)S(1)} collective-permute-done((bf16[8,896]{1,0:T(8,128)(2,1)S(1)}, bf16[8,896]{1,0:T(8,128)(2,1)S(1)}, u32[]{:S(2)}, u32[]{:S(2)}) %collective-permute-start) | collective-permute-done | bytes 14368 | tf_op jit(solution)/shard_map/ppermute | solution.py:18
  7.9 2.7 %collective-permute-done.1.refs_1_ = bf16[8,896]{1,0:T(8,128)(2,1)S(1)} collective-permute-done((bf16[8,896]{1,0:T(8,128)(2,1)S(1)}, bf16[8,896]{1,0:T(8,128)(2,1)S(1)}, u32[]{:S(2)}, u32[]{:S(2)}) %collective-permute-start.1) | collective-permute-done | bytes 14368 | tf_op jit(solution)/shard_map/ppermute | solution.py:18
  10.7 2.7 %collective-permute-start.5 = (bf16[32,896]{1,0:T(8,128)(2,1)S(1)}, bf16[32,896]{1,0:T(8,128)(2,1)S(1)}, u32[]{:S(2)}, u32[]{:S(2)}) collective-permute-start(bf16[32,896]{1,0:T(8,128)(2,1)S(1)} %arrange.1.refs_0_.refs_3_), channel_id=1, source_target_pairs={{0,7},{1,6},{2,5},{3,4},{4,3},{5,2},{6,1},{7,0},{8,15},{9,14},{10,... | collective-permute-start | bytes 172040 | tf_op jit(solution)/shard_map/ppermute | solution.py:36
  13.5 1.7 %collective-permute-start.3 = (bf16[32,896]{1,0:T(8,128)(2,1)S(1)}, bf16[32,896]{1,0:T(8,128)(2,1)S(1)}, u32[]{:S(2)}, u32[]{:S(2)}) collective-permute-start(bf16[32,896]{1,0:T(8,128)(2,1)S(1)} %arrange.1.refs_0_.refs_3_), channel_id=1, source_target_pairs={{0,5},{1,2},{2,7},{3,0},{4,1},{5,6},{6,3},{7,4},{8,13},{9,10},{10,... | collective-permute-start | bytes 172040 | tf_op jit(solution)/shard_map/ppermute | solution.py:36
  15.1 1.8 %load.2 = (bf16[3584,256]{1,0:T(8,128)(2,1)S(1)}, bf16[256,1792]{1,0:T(8,128)(2,1)S(1)}, bf16[64,128]{1,0:T(8,128)(2,1)S(1)}) custom-call(bf16[32,896]{1,0:T(8,128)(2,1)S(1)} %arrange.1.refs_0_.refs_3_, bf16[3584,128]{1,0:T(8,128)(2,1)} %bitcast.12, bf16[3584,128]{1,0:T(8,128)(2,1)} %bitcast.13, bf16[128,3584]{1,0:T(8,128)(2,1)} %bitcast.14, ...), custom_call_target="tpu_custom_call" | custom-call | bytes 2768896 | tf_op jit(solution)/shard_map/load/pallas_call | solution.py:192
  17.0 0.7 %collective-permute-done.3.refs_2_ = bf16[32,896]{1,0:T(8,128)(2,1)S(1)} collective-permute-done((bf16[32,896]{1,0:T(8,128)(2,1)S(1)}, bf16[32,896]{1,0:T(8,128)(2,1)S(1)}, u32[]{:S(2)}, u32[]{:S(2)}) %collective-permute-start.3) | collective-permute-done | bytes 57376 | tf_op jit(solution)/shard_map/ppermute | solution.py:36
  17.8 1.4 %collective-permute-done.6.other_ref = bf16[128,896]{1,0:T(8,128)(2,1)S(1)} collective-permute-done((bf16[128,896]{1,0:T(8,128)(2,1)S(1)}, bf16[128,896]{1,0:T(8,128)(2,1)S(1)}, u32[]{:S(2)}, u32[]{:S(2)}) %collective-permute-start.6) | collective-permute-done | bytes 229408 | tf_op jit(solution)/shard_map/ppermute | solution.py:18
  19.2 1.3 %expert.1 = (bf16[32,1920]{1,0:T(8,128)(2,1)S(1)}, bf16[32,1920]{1,0:T(8,128)(2,1)S(1)}, bf16[8,3584]{1,0:T(8,128)(2,1)S(1)}) custom-call(bf16[128,896]{1,0:T(8,128)(2,1)S(1)} %join.1.own_ref, bf16[128,896]{1,0:T(8,128)(2,1)S(1)} %collective-permute-done.6.other_ref, bf16[3584,256]{1,0:T(8,128)(2,1)S(1)} %get-tuple-element.42.pair_w, ...), custom_call_target="tpu_custom_call" | custom-call | tf_op jit(solution)/shard_map/expert/pallas_call | solution.py:389
  20.7 1.2 %collective-permute-done.7.got_ref = bf16[32,1920]{1,0:T(8,128)(2,1)S(1)} collective-permute-done((bf16[32,1920]{1,0:T(8,128)(2,1)S(1)}, bf16[32,1920]{1,0:T(8,128)(2,1)S(1)}, u32[]{:S(2)}, u32[]{:S(2)}) %collective-permute-start.7) | collective-permute-done | bytes 122912 | tf_op jit(solution)/shard_map/ppermute | solution.py:18
  22.1 1.2 %collective-permute-start.8 = (bf16[8,1920]{1,0:T(8,128)(2,1)S(1)}, bf16[8,1920]{1,0:T(8,128)(2,1)S(1)}, u32[]{:S(2)}, u32[]{:S(2)}) collective-permute-start(bf16[8,1920]{1,0:T(8,128)(2,1)S(1)} %get-tuple-element.47), channel_id=1, source_target_pairs={{0,7},{1,6},{2,5},{3,4},{4,3},{5,2},{6,1},{7,0},{8,15},{9,14},{10,... | collective-permute-start | bytes 92168 | tf_op jit(solution)/shard_map/ppermute | solution.py:36
  23.2 1.1 %collective-permute-start.9 = (bf16[8,1920]{1,0:T(8,128)(2,1)S(1)}, bf16[8,1920]{1,0:T(8,128)(2,1)S(1)}, u32[]{:S(2)}, u32[]{:S(2)}) collective-permute-start(bf16[8,1920]{1,0:T(8,128)(2,1)S(1)} %get-tuple-element.48), channel_id=1, source_target_pairs={{0,3},{1,4},{2,1},{3,6},{4,7},{5,0},{6,5},{7,2},{8,11},{9,12},{10,... | collective-permute-start | bytes 92168 | tf_op jit(solution)/shard_map/ppermute | solution.py:36
  24.4 0.6 %collective-permute-start.10 = (bf16[8,1920]{1,0:T(8,128)(2,1)S(1)}, bf16[8,1920]{1,0:T(8,128)(2,1)S(1)}, u32[]{:S(2)}, u32[]{:S(2)}) collective-permute-start(bf16[8,1920]{1,0:T(8,128)(2,1)S(1)} %get-tuple-element.49), channel_id=1, source_target_pairs={{0,5},{1,2},{2,7},{3,0},{4,1},{5,6},{6,3},{7,4},{8,13},{9,10},{10,... | collective-permute-start | bytes 92168 | tf_op jit(solution)/shard_map/ppermute | solution.py:36
  25.0 1.4 %load.3 = (bf16[64,3584]{1,0:T(8,128)(2,1)S(1)}, bf16[128,4096]{1,0:T(8,128)(2,1)S(1)}) custom-call(bf16[8,1920]{1,0:T(8,128)(2,1)S(1)} %get-tuple-element.50.refs_0_.refs_3_, bf16[64,3584]{1,0:T(8,128)(2,1)} %bitcast.15, bf16[128,4096]{1,0:T(8,128)(2,1)} %bitcast.11), custom_call_target="tpu_custom_call" | custom-call | bytes 1507328 | tf_op jit(solution)/shard_map/load/pallas_call | solution.py:192
  27.0 0.7 %collective-permute-done.10.refs_2_ = bf16[8,1920]{1,0:T(8,128)(2,1)S(1)} collective-permute-done((bf16[8,1920]{1,0:T(8,128)(2,1)S(1)}, bf16[8,1920]{1,0:T(8,128)(2,1)S(1)}, u32[]{:S(2)}, u32[]{:S(2)}) %collective-permute-start.10) | collective-permute-done | bytes 30752 | tf_op jit(solution)/shard_map/ppermute | solution.py:36
  27.7 0.5 %score.1 = (bf16[2,1920]{1,0:T(2,128)(2,1)S(1)}, bf16[2,1920]{1,0:T(2,128)(2,1)S(1)}, bf16[2,1920]{1,0:T(2,128)(2,1)S(1)}, bf16[2,1920]{1,0:T(2,128)(2,1)S(1)}) custom-call(bf16[8,1920]{1,0:T(8,128)(2,1)S(1)} %collective-permute-done.8.refs_0_, bf16[8,1920]{1,0:T(8,128)(2,1)S(1)} %collective-permute-done.9.refs_1_, ...), custom_call_target="tpu_custom_call" | custom-call | tf_op jit(solution)/shard_map/score/pallas_call | solution.py:420
  28.2 1.5 %collective-permute-start.11 = (bf16[2,1920]{1,0:T(2,128)(2,1)S(1)}, bf16[2,1920]{1,0:T(2,128)(2,1)S(1)}, u32[]{:S(2)}, u32[]{:S(2)}) collective-permute-start(bf16[2,1920]{1,0:T(2,128)(2,1)S(1)} %get-tuple-element.54), channel_id=1, source_target_pairs={{0,24},{8,16},{16,8},{24,0},{1,25},{9,17},{17,9},{25,1},{2,26},{10... | collective-permute-start | bytes 23048 | tf_op jit(solution)/shard_map/ppermute | solution.py:18
  29.7 0.5 %collective-permute-start.12 = (bf16[2,1920]{1,0:T(2,128)(2,1)S(1)}, bf16[2,1920]{1,0:T(2,128)(2,1)S(1)}, u32[]{:S(2)}, u32[]{:S(2)}) collective-permute-start(bf16[2,1920]{1,0:T(2,128)(2,1)S(1)} %get-tuple-element.55), channel_id=1, source_target_pairs={{0,16},{8,24},{16,0},{24,8},{1,17},{9,25},{17,1},{25,9},{2,18},{10... | collective-permute-start | bytes 23048 | tf_op jit(solution)/shard_map/ppermute | solution.py:18
  30.2 2.4 %collective-permute-start.13 = (bf16[2,1920]{1,0:T(2,128)(2,1)S(1)}, bf16[2,1920]{1,0:T(2,128)(2,1)S(1)}, u32[]{:S(2)}, u32[]{:S(2)}) collective-permute-start(bf16[2,1920]{1,0:T(2,128)(2,1)S(1)} %get-tuple-element.56), channel_id=1, source_target_pairs={{0,8},{8,0},{16,24},{24,16},{1,9},{9,1},{17,25},{25,17},{2,10},{10... | collective-permute-start | bytes 23048 | tf_op jit(solution)/shard_map/ppermute | solution.py:18
  32.6 1.1 %collective-permute-done.11.refs_0_ = bf16[2,1920]{1,0:T(2,128)(2,1)S(1)} collective-permute-done((bf16[2,1920]{1,0:T(2,128)(2,1)S(1)}, bf16[2,1920]{1,0:T(2,128)(2,1)S(1)}, u32[]{:S(2)}, u32[]{:S(2)}) %collective-permute-start.11) | collective-permute-done | bytes 7712 | tf_op jit(solution)/shard_map/ppermute | solution.py:18
  33.7 0.6 %collective-permute-done.12.refs_1_ = bf16[2,1920]{1,0:T(2,128)(2,1)S(1)} collective-permute-done((bf16[2,1920]{1,0:T(2,128)(2,1)S(1)}, bf16[2,1920]{1,0:T(2,128)(2,1)S(1)}, u32[]{:S(2)}, u32[]{:S(2)}) %collective-permute-start.12) | collective-permute-done | bytes 7712 | tf_op jit(solution)/shard_map/ppermute | solution.py:18
  34.3 0.9 %finish.1 = (bf16[64,1792]{1,0:T(8,128)(2,1)}, f32[64,128]{1,0:T(8,128)}) custom-call(f32[32,64]{1,0:T(8,128)S(1)} %get-tuple-element.30.hit_ref, bf16[2,1920]{1,0:T(2,128)(2,1)S(1)} %collective-permute-done.11.refs_0_, bf16[2,1920]{1,0:T(2,128)(2,1)S(1)} %collective-permute-done.12.refs_1_, bf16[2,1920]{1,0:T(2,128)(2,1)S(1)} %collective-permute-done.13.refs_2_, ...), custom_call_target="tpu_custom_call" | custom-call | tf_op jit(solution)/shard_map/finish/pallas_call | solution.py:431
  (14 shorter events, 1.4 us)
Async XLA Ops:
  1.9 6.0 %collective-permute-start = (bf16[8,896]{1,0:T(8,128)(2,1)S(1)}, bf16[8,896]{1,0:T(8,128)(2,1)S(1)}, u32[]{:S(2)}, u32[]{:S(2)}) collective-permute-start(bf16[8,896]{1,0:T(8,128)(2,1)S(1)} %get-tuple-element.31), channel_id=1, source_target_pairs={{0,25},{1,24},{8,17},{9,16},{16,9},{17,8},{24,1},{25,0},{2,27},{3,... | collective-permute-start | bytes 43016 | tf_op jit(solution)/shard_map/ppermute | solution.py:18
  6.5 4.1 %collective-permute-start.1 = (bf16[8,896]{1,0:T(8,128)(2,1)S(1)}, bf16[8,896]{1,0:T(8,128)(2,1)S(1)}, u32[]{:S(2)}, u32[]{:S(2)}) collective-permute-start(bf16[8,896]{1,0:T(8,128)(2,1)S(1)} %get-tuple-element.32), channel_id=1, source_target_pairs={{0,17},{1,16},{8,25},{9,24},{16,1},{17,0},{24,9},{25,8},{2,19},{3,... | collective-permute-start | bytes 43016 | tf_op jit(solution)/shard_map/ppermute | solution.py:18
  6.5 4.1 %collective-permute-start.2 = (bf16[8,896]{1,0:T(8,128)(2,1)S(1)}, bf16[8,896]{1,0:T(8,128)(2,1)S(1)}, u32[]{:S(2)}, u32[]{:S(2)}) collective-permute-start(bf16[8,896]{1,0:T(8,128)(2,1)S(1)} %get-tuple-element.33), channel_id=1, source_target_pairs={{0,9},{1,8},{8,1},{9,0},{16,25},{17,24},{24,17},{25,16},{2,11},{3,... | collective-permute-start | bytes 43016 | tf_op jit(solution)/shard_map/ppermute | solution.py:18
  10.7 6.2 %collective-permute-start.5 = (bf16[32,896]{1,0:T(8,128)(2,1)S(1)}, bf16[32,896]{1,0:T(8,128)(2,1)S(1)}, u32[]{:S(2)}, u32[]{:S(2)}) collective-permute-start(bf16[32,896]{1,0:T(8,128)(2,1)S(1)} %arrange.1.refs_0_.refs_3_), channel_id=1, source_target_pairs={{0,7},{1,6},{2,5},{3,4},{4,3},{5,2},{6,1},{7,0},{8,15},{9,14},{10,... | collective-permute-start | bytes 172040 | tf_op jit(solution)/shard_map/ppermute | solution.py:36
  13.4 3.6 %collective-permute-start.4 = (bf16[32,896]{1,0:T(8,128)(2,1)S(1)}, bf16[32,896]{1,0:T(8,128)(2,1)S(1)}, u32[]{:S(2)}, u32[]{:S(2)}) collective-permute-start(bf16[32,896]{1,0:T(8,128)(2,1)S(1)} %arrange.1.refs_0_.refs_3_), channel_id=1, source_target_pairs={{0,3},{1,4},{2,1},{3,6},{4,7},{5,0},{6,5},{7,2},{8,11},{9,12},{10,... | collective-permute-start | bytes 172040 | tf_op jit(solution)/shard_map/ppermute | solution.py:36
  13.5 4.2 %collective-permute-start.3 = (bf16[32,896]{1,0:T(8,128)(2,1)S(1)}, bf16[32,896]{1,0:T(8,128)(2,1)S(1)}, u32[]{:S(2)}, u32[]{:S(2)}) collective-permute-start(bf16[32,896]{1,0:T(8,128)(2,1)S(1)} %arrange.1.refs_0_.refs_3_), channel_id=1, source_target_pairs={{0,5},{1,2},{2,7},{3,0},{4,1},{5,6},{6,3},{7,4},{8,13},{9,10},{10,... | collective-permute-start | bytes 172040 | tf_op jit(solution)/shard_map/ppermute | solution.py:36
  17.7 1.6 %collective-permute-start.6 = (bf16[128,896]{1,0:T(8,128)(2,1)S(1)}, bf16[128,896]{1,0:T(8,128)(2,1)S(1)}, u32[]{:S(2)}, u32[]{:S(2)}) collective-permute-start(bf16[128,896]{1,0:T(8,128)(2,1)S(1)} %join.1.own_ref), channel_id=1, source_target_pairs={{0,1},{1,0},{2,3},{3,2},{4,5},{5,4},{6,7},{7,6},{8,9},{9,8},{10,11... | collective-permute-start | bytes 688136 | tf_op jit(solution)/shard_map/ppermute | solution.py:18
  20.5 1.4 %collective-permute-start.7 = (bf16[32,1920]{1,0:T(8,128)(2,1)S(1)}, bf16[32,1920]{1,0:T(8,128)(2,1)S(1)}, u32[]{:S(2)}, u32[]{:S(2)}) collective-permute-start(bf16[32,1920]{1,0:T(8,128)(2,1)S(1)} %get-tuple-element.46), channel_id=1, source_target_pairs={{0,1},{1,0},{2,3},{3,2},{4,5},{5,4},{6,7},{7,6},{8,9},{9,8},{10,11... | collective-permute-start | bytes 368648 | tf_op jit(solution)/shard_map/ppermute | solution.py:18
  22.1 4.5 %collective-permute-start.8 = (bf16[8,1920]{1,0:T(8,128)(2,1)S(1)}, bf16[8,1920]{1,0:T(8,128)(2,1)S(1)}, u32[]{:S(2)}, u32[]{:S(2)}) collective-permute-start(bf16[8,1920]{1,0:T(8,128)(2,1)S(1)} %get-tuple-element.47), channel_id=1, source_target_pairs={{0,7},{1,6},{2,5},{3,4},{4,3},{5,2},{6,1},{7,0},{8,15},{9,14},{10,... | collective-permute-start | bytes 92168 | tf_op jit(solution)/shard_map/ppermute | solution.py:36
  23.2 3.7 %collective-permute-start.9 = (bf16[8,1920]{1,0:T(8,128)(2,1)S(1)}, bf16[8,1920]{1,0:T(8,128)(2,1)S(1)}, u32[]{:S(2)}, u32[]{:S(2)}) collective-permute-start(bf16[8,1920]{1,0:T(8,128)(2,1)S(1)} %get-tuple-element.48), channel_id=1, source_target_pairs={{0,3},{1,4},{2,1},{3,6},{4,7},{5,0},{6,5},{7,2},{8,11},{9,12},{10,... | collective-permute-start | bytes 92168 | tf_op jit(solution)/shard_map/ppermute | solution.py:36
  24.4 3.3 %collective-permute-start.10 = (bf16[8,1920]{1,0:T(8,128)(2,1)S(1)}, bf16[8,1920]{1,0:T(8,128)(2,1)S(1)}, u32[]{:S(2)}, u32[]{:S(2)}) collective-permute-start(bf16[8,1920]{1,0:T(8,128)(2,1)S(1)} %get-tuple-element.49), channel_id=1, source_target_pairs={{0,5},{1,2},{2,7},{3,0},{4,1},{5,6},{6,3},{7,4},{8,13},{9,10},{10,... | collective-permute-start | bytes 92168 | tf_op jit(solution)/shard_map/ppermute | solution.py:36
  28.2 5.5 %collective-permute-start.11 = (bf16[2,1920]{1,0:T(2,128)(2,1)S(1)}, bf16[2,1920]{1,0:T(2,128)(2,1)S(1)}, u32[]{:S(2)}, u32[]{:S(2)}) collective-permute-start(bf16[2,1920]{1,0:T(2,128)(2,1)S(1)} %get-tuple-element.54), channel_id=1, source_target_pairs={{0,24},{8,16},{16,8},{24,0},{1,25},{9,17},{17,9},{25,1},{2,26},{10... | collective-permute-start | bytes 23048 | tf_op jit(solution)/shard_map/ppermute | solution.py:18
  29.7 4.5 %collective-permute-start.12 = (bf16[2,1920]{1,0:T(2,128)(2,1)S(1)}, bf16[2,1920]{1,0:T(2,128)(2,1)S(1)}, u32[]{:S(2)}, u32[]{:S(2)}) collective-permute-start(bf16[2,1920]{1,0:T(2,128)(2,1)S(1)} %get-tuple-element.55), channel_id=1, source_target_pairs={{0,16},{8,24},{16,0},{24,8},{1,17},{9,25},{17,1},{25,9},{2,18},{10... | collective-permute-start | bytes 23048 | tf_op jit(solution)/shard_map/ppermute | solution.py:18
  30.2 4.1 %collective-permute-start.13 = (bf16[2,1920]{1,0:T(2,128)(2,1)S(1)}, bf16[2,1920]{1,0:T(2,128)(2,1)S(1)}, u32[]{:S(2)}, u32[]{:S(2)}) collective-permute-start(bf16[2,1920]{1,0:T(2,128)(2,1)S(1)} %get-tuple-element.56), channel_id=1, source_target_pairs={{0,8},{8,0},{16,24},{24,16},{1,9},{9,1},{17,25},{25,17},{2,10},{10... | collective-permute-start | bytes 23048 | tf_op jit(solution)/shard_map/ppermute | solution.py:18

commit v10 on v9

--- a/solution.py
+++ b/solution.py
@@ -256,9 +256,8 @@
 
 def pair_kernel(half, offsets, keep_ref, got_ref, *refs):
     *out_refs, own_ref = refs
-    kept, got = keep_ref[...].astype(F32), got_ref[...].astype(F32)
-    main = (kept[:, :half] + got[:, :half]).astype(BF16)
-    tail = split_two(join_two(kept[:, half:]) + join_two(got[:, half:]))
+    main = keep_ref[:, :half] + got_ref[:, :half]
+    tail = split_two(join_two(keep_ref[:, half:]) + join_two(got_ref[:, half:]))
     rows = own_ref.shape[0]
 
     def place(ref, g):
@@ -288,8 +287,12 @@
     left = lax.broadcasted_iota(jnp.int32, grad.shape, 1) < proj
     for p in range(0, proj, 2):
         pair = jnp.where(left, hid[:, p : p + 1], hid[:, p + 1 : p + 2])
-        feature[:, p * proj : (p + 2) * proj] = (pair * grad).astype(BF16)
-    score = dot_f32(feature[...], test_ref[...], ((1,), (1,)))
+        row, first = divmod(p * proj, feature.shape[1])
+        row *= total.shape[0]
+        feature[row : row + total.shape[0], first : first + 2 * proj] = (pair * grad).astype(BF16)
+    scores = dot_f32(feature[...], test_ref[...], ((1,), (1,)))
+    rows, tests = total.shape[0], test_ref.shape[0] // 2
+    score = scores[:rows, :tests] + scores[rows:, tests:]
     for k, out_ref in zip(order, out_refs):
         out_ref[:, :half] = total[k * CAP : (k + 1) * CAP, :half].astype(BF16)
         out_ref[:, half:] = score[k * CAP : (k + 1) * CAP].astype(BF16)
@@ -298,12 +301,10 @@
 def finish_kernel(experts, hit_ref, *refs):
     slot_refs = refs[:experts]
     in_grad_hbm, scores_hbm, in_grad, scores, home_ref, sems = refs[experts:]
-    unit = KINDS * CAP
-    hits = jnp.concatenate([hit_ref[k * unit : k * unit + CAP] for k in range(experts)])
     home_ref[...] = jnp.concatenate([ref[...].astype(F32) for ref in slot_refs]).astype(BF16)
+    hits = hit_ref[...]
     half = in_grad.shape[1]
     quarter = half // 2
-    hits = hits.T.astype(BF16)
     copies = []
     for index in range(2):
         columns = slice(index * quarter, (index + 1) * quarter)
@@ -411,9 +412,17 @@
             compiler_params=limit(rows),
         )(keep, got)
     pieces = [send_plane(x, offset) for x, offset in zip(sums, offsets)] + [sums[-1]]
-    params = [proj_grad[0], test_feats[0]]
-    moves = [(index, 0, x.shape[1], index, 0, 0) for index, x in enumerate(params)]
-    grad_proj, test_rows = load(sums[-1], params, [x.shape for x in params], moves, limit(rows))
+    depth = proj * proj // 2
+    grad_proj, test_rows = load(
+        sums[-1],
+        [proj_grad[0], test_feats[0]],
+        [(proj, width), (2 * tests, depth)],
+        [(0, 0, width, 0, 0, 0), (1, 0, depth, 1, 0, 0), (1, depth, depth, 1, tests, 0)],
+        limit(rows),
+    )
+    hits, mine = lax.optimization_barrier((hits, mine))
+    hits = hits.reshape(experts, KINDS, CAP, tok_rows)[:, 0].reshape(pairs, tok_rows)
+    hits = hits.T.astype(BF16)
     grad_mine = dot_f32(mine, grad_proj, ((1,), (1,)))
     order = slot_order(experts)
     with jax.named_scope("score"):
@@ -422,7 +431,7 @@
             out_shape=[jax.ShapeDtypeStruct((CAP, half + tests), BF16)] * experts,
             in_specs=whole_vmem(groups + 2),
             out_specs=whole_vmem(experts),
-            scratch_shapes=[pltpu.VMEM((pairs, proj * proj), BF16)],
+            scratch_shapes=[pltpu.VMEM((2 * pairs, proj * proj // 2), BF16)],
             compiler_params=limit(rows),
         )(*pieces, grad_mine, test_rows)
     slots = exchange(send_rel, back, experts)

time: 35.5 us -> 35.4 us (level)
  no operation moved by 1% of the time
where the time goes in v10:
time: 35.4 us; the launch traced here: 35.2 us
  starting transfers between devices  17.6 us (50%)
  waiting for transfers between devices  9.26 us (26%)
  Pallas kernels  7.35 us (21%)
  between operations  0.69 us (2%)
    ppermute x8, starting transfers between devices, send_rel(): return lax.ppermute(block, axis, [(i, i ^ offset) for i in range(size)])  10.2 us
    ppermute x8, waiting for transfers between devices, send_rel(): return lax.ppermute(block, axis, [(i, i ^ offset) for i in range(size)])  7.38 us
    ppermute x6, starting transfers between devices, send_plane(): return lax.ppermute(block, ('dp', 'test'), pairs)  7.34 us
    pallas_call x2, Pallas kernels, load(): pl.pallas_call(functools.partial(load_kernel, moves), out_shape=[jax.Shap...  3.12 us
    ppermute x6, waiting for transfers between devices, send_plane(): return lax.ppermute(block, ('dp', 'test'), pairs)  1.88 us
    pallas_call x1, Pallas kernels, on_device(): pl.pallas_call(expert_kernel, out_shape=[jax.ShapeDtypeStruct((rows, out_...  1.32 us
    pallas_call x1, Pallas kernels, on_device(): pl.pallas_call(functools.partial(select_kernel, experts), out_shape=[jax....  1.31 us
    pallas_call x1, Pallas kernels, on_device(): pl.pallas_call(functools.partial(finish_kernel, experts), out_shape=[jax....  0.89 us
  transfers between devices with their start and end apart: 14, of which 11 were waited for; matrix products, arithmetic and copies ran while one was open for 1% of the time, Pallas kernels for 9%

profile of v10, /device:TPU:0, one launch (start us, length us, event | category | flops | bytes accessed | tf_op | source)
XLA Modules:
  0.0 35.2 jit_solution(18111360464076709384)
XLA Ops:
  0.6 1.3 %select.1 = (f32[32,64]{1,0:T(8,128)S(1)}, bf16[8,896]{1,0:T(8,128)(2,1)S(1)}, bf16[8,896]{1,0:T(8,128)(2,1)S(1)}, bf16[8,896]{1,0:T(8,128)(2,1)S(1)}, bf16[8,896]{1,0:T(8,128)(2,1)S(1)}) custom-call(s32[8,64]{1,0:T(8,128)} %bitcast.25, s32[8,64]{1,0:T(8,128)} %bitcast.26, bf16[8,64]{1,0:T(8,128)(2,1)} %bitcast.27, bf16[64,1792]{1,0:T(8,128)(2,1)} %refs_3_.1, ...), custom_call_target="tpu_custom_call" | custom-call | tf_op jit(solution)/shard_map/select/pallas_call | solution.py:348
  1.9 4.6 %collective-permute-start = (bf16[8,896]{1,0:T(8,128)(2,1)S(1)}, bf16[8,896]{1,0:T(8,128)(2,1)S(1)}, u32[]{:S(2)}, u32[]{:S(2)}) collective-permute-start(bf16[8,896]{1,0:T(8,128)(2,1)S(1)} %get-tuple-element.33), channel_id=1, source_target_pairs={{0,25},{1,24},{8,17},{9,16},{16,9},{17,8},{24,1},{25,0},{2,27},{3,... | collective-permute-start | bytes 43016 | tf_op jit(solution)/shard_map/ppermute | solution.py:18
  6.5 0.9 %collective-permute-start.2 = (bf16[8,896]{1,0:T(8,128)(2,1)S(1)}, bf16[8,896]{1,0:T(8,128)(2,1)S(1)}, u32[]{:S(2)}, u32[]{:S(2)}) collective-permute-start(bf16[8,896]{1,0:T(8,128)(2,1)S(1)} %get-tuple-element.35), channel_id=1, source_target_pairs={{0,9},{1,8},{8,1},{9,0},{16,25},{17,24},{24,17},{25,16},{2,11},{3,... | collective-permute-start | bytes 43016 | tf_op jit(solution)/shard_map/ppermute | solution.py:18
  7.4 0.5 %collective-permute-done.refs_0_ = bf16[8,896]{1,0:T(8,128)(2,1)S(1)} collective-permute-done((bf16[8,896]{1,0:T(8,128)(2,1)S(1)}, bf16[8,896]{1,0:T(8,128)(2,1)S(1)}, u32[]{:S(2)}, u32[]{:S(2)}) %collective-permute-start) | collective-permute-done | bytes 14368 | tf_op jit(solution)/shard_map/ppermute | solution.py:18
  7.9 2.7 %collective-permute-done.1.refs_1_ = bf16[8,896]{1,0:T(8,128)(2,1)S(1)} collective-permute-done((bf16[8,896]{1,0:T(8,128)(2,1)S(1)}, bf16[8,896]{1,0:T(8,128)(2,1)S(1)}, u32[]{:S(2)}, u32[]{:S(2)}) %collective-permute-start.1) | collective-permute-done | bytes 14368 | tf_op jit(solution)/shard_map/ppermute | solution.py:18
  10.7 2.7 %collective-permute-start.5 = (bf16[32,896]{1,0:T(8,128)(2,1)S(1)}, bf16[32,896]{1,0:T(8,128)(2,1)S(1)}, u32[]{:S(2)}, u32[]{:S(2)}) collective-permute-start(bf16[32,896]{1,0:T(8,128)(2,1)S(1)} %arrange.1.refs_0_.refs_3_), channel_id=1, source_target_pairs={{0,7},{1,6},{2,5},{3,4},{4,3},{5,2},{6,1},{7,0},{8,15},{9,14},{10,... | collective-permute-start | bytes 172040 | tf_op jit(solution)/shard_map/ppermute | solution.py:36
  13.5 1.7 %collective-permute-start.3 = (bf16[32,896]{1,0:T(8,128)(2,1)S(1)}, bf16[32,896]{1,0:T(8,128)(2,1)S(1)}, u32[]{:S(2)}, u32[]{:S(2)}) collective-permute-start(bf16[32,896]{1,0:T(8,128)(2,1)S(1)} %arrange.1.refs_0_.refs_3_), channel_id=1, source_target_pairs={{0,5},{1,2},{2,7},{3,0},{4,1},{5,6},{6,3},{7,4},{8,13},{9,10},{10,... | collective-permute-start | bytes 172040 | tf_op jit(solution)/shard_map/ppermute | solution.py:36
  15.1 1.8 %load.2 = (bf16[3584,256]{1,0:T(8,128)(2,1)S(1)}, bf16[256,1792]{1,0:T(8,128)(2,1)S(1)}, bf16[64,128]{1,0:T(8,128)(2,1)S(1)}) custom-call(bf16[32,896]{1,0:T(8,128)(2,1)S(1)} %arrange.1.refs_0_.refs_3_, bf16[3584,128]{1,0:T(8,128)(2,1)} %bitcast.18, bf16[3584,128]{1,0:T(8,128)(2,1)} %bitcast.19, bf16[128,3584]{1,0:T(8,128)(2,1)} %bitcast.20, ...), custom_call_target="tpu_custom_call" | custom-call | bytes 2768896 | tf_op jit(solution)/shard_map/load/pallas_call | solution.py:192
  17.0 0.7 %collective-permute-done.3.refs_2_ = bf16[32,896]{1,0:T(8,128)(2,1)S(1)} collective-permute-done((bf16[32,896]{1,0:T(8,128)(2,1)S(1)}, bf16[32,896]{1,0:T(8,128)(2,1)S(1)}, u32[]{:S(2)}, u32[]{:S(2)}) %collective-permute-start.3) | collective-permute-done | bytes 57376 | tf_op jit(solution)/shard_map/ppermute | solution.py:36
  17.8 1.4 %collective-permute-done.6.other_ref = bf16[128,896]{1,0:T(8,128)(2,1)S(1)} collective-permute-done((bf16[128,896]{1,0:T(8,128)(2,1)S(1)}, bf16[128,896]{1,0:T(8,128)(2,1)S(1)}, u32[]{:S(2)}, u32[]{:S(2)}) %collective-permute-start.6) | collective-permute-done | bytes 229408 | tf_op jit(solution)/shard_map/ppermute | solution.py:18
  19.2 1.3 %expert.1 = (bf16[32,1920]{1,0:T(8,128)(2,1)S(1)}, bf16[32,1920]{1,0:T(8,128)(2,1)S(1)}, bf16[8,3584]{1,0:T(8,128)(2,1)S(1)}) custom-call(bf16[128,896]{1,0:T(8,128)(2,1)S(1)} %join.1.own_ref, bf16[128,896]{1,0:T(8,128)(2,1)S(1)} %collective-permute-done.6.other_ref, bf16[3584,256]{1,0:T(8,128)(2,1)S(1)} %get-tuple-element.44.pair_w, ...), custom_call_target="tpu_custom_call" | custom-call | tf_op jit(solution)/shard_map/expert/pallas_call | solution.py:390
  20.7 1.2 %collective-permute-done.7.got_ref = bf16[32,1920]{1,0:T(8,128)(2,1)S(1)} collective-permute-done((bf16[32,1920]{1,0:T(8,128)(2,1)S(1)}, bf16[32,1920]{1,0:T(8,128)(2,1)S(1)}, u32[]{:S(2)}, u32[]{:S(2)}) %collective-permute-start.7) | collective-permute-done | bytes 122912 | tf_op jit(solution)/shard_map/ppermute | solution.py:18
  22.0 1.2 %collective-permute-start.8 = (bf16[8,1920]{1,0:T(8,128)(2,1)S(1)}, bf16[8,1920]{1,0:T(8,128)(2,1)S(1)}, u32[]{:S(2)}, u32[]{:S(2)}) collective-permute-start(bf16[8,1920]{1,0:T(8,128)(2,1)S(1)} %get-tuple-element.51), channel_id=1, source_target_pairs={{0,7},{1,6},{2,5},{3,4},{4,3},{5,2},{6,1},{7,0},{8,15},{9,14},{10,... | collective-permute-start | bytes 92168 | tf_op jit(solution)/shard_map/ppermute | solution.py:36
  23.2 1.1 %collective-permute-start.9 = (bf16[8,1920]{1,0:T(8,128)(2,1)S(1)}, bf16[8,1920]{1,0:T(8,128)(2,1)S(1)}, u32[]{:S(2)}, u32[]{:S(2)}) collective-permute-start(bf16[8,1920]{1,0:T(8,128)(2,1)S(1)} %get-tuple-element.52), channel_id=1, source_target_pairs={{0,3},{1,4},{2,1},{3,6},{4,7},{5,0},{6,5},{7,2},{8,11},{9,12},{10,... | collective-permute-start | bytes 92168 | tf_op jit(solution)/shard_map/ppermute | solution.py:36
  24.4 0.6 %collective-permute-start.10 = (bf16[8,1920]{1,0:T(8,128)(2,1)S(1)}, bf16[8,1920]{1,0:T(8,128)(2,1)S(1)}, u32[]{:S(2)}, u32[]{:S(2)}) collective-permute-start(bf16[8,1920]{1,0:T(8,128)(2,1)S(1)} %get-tuple-element.53), channel_id=1, source_target_pairs={{0,5},{1,2},{2,7},{3,0},{4,1},{5,6},{6,3},{7,4},{8,13},{9,10},{10,... | collective-permute-start | bytes 92168 | tf_op jit(solution)/shard_map/ppermute | solution.py:36
  25.0 1.4 %load.3 = (bf16[64,3584]{1,0:T(8,128)(2,1)S(1)}, bf16[256,2048]{1,0:T(8,128)(2,1)S(1)}) custom-call(bf16[8,1920]{1,0:T(8,128)(2,1)S(1)} %get-tuple-element.54.refs_0_.refs_3_, bf16[64,3584]{1,0:T(8,128)(2,1)} %bitcast.21, bf16[128,4096]{1,0:T(8,128)(2,1)} %bitcast.17), custom_call_target="tpu_custom_call" | custom-call | bytes 1507328 | tf_op jit(solution)/shard_map/load/pallas_call | solution.py:192
  26.9 0.7 %collective-permute-done.10.refs_2_ = bf16[8,1920]{1,0:T(8,128)(2,1)S(1)} collective-permute-done((bf16[8,1920]{1,0:T(8,128)(2,1)S(1)}, bf16[8,1920]{1,0:T(8,128)(2,1)S(1)}, u32[]{:S(2)}, u32[]{:S(2)}) %collective-permute-start.10) | collective-permute-done | bytes 30752 | tf_op jit(solution)/shard_map/ppermute | solution.py:36
  27.7 0.5 %score.1 = (bf16[2,1920]{1,0:T(2,128)(2,1)S(1)}, bf16[2,1920]{1,0:T(2,128)(2,1)S(1)}, bf16[2,1920]{1,0:T(2,128)(2,1)S(1)}, bf16[2,1920]{1,0:T(2,128)(2,1)S(1)}) custom-call(bf16[8,1920]{1,0:T(8,128)(2,1)S(1)} %collective-permute-done.8.refs_0_, bf16[8,1920]{1,0:T(8,128)(2,1)S(1)} %collective-permute-done.9.refs_1_, ...), custom_call_target="tpu_custom_call" | custom-call | tf_op jit(solution)/shard_map/score/pallas_call | solution.py:429
  28.2 1.5 %collective-permute-start.11 = (bf16[2,1920]{1,0:T(2,128)(2,1)S(1)}, bf16[2,1920]{1,0:T(2,128)(2,1)S(1)}, u32[]{:S(2)}, u32[]{:S(2)}) collective-permute-start(bf16[2,1920]{1,0:T(2,128)(2,1)S(1)} %get-tuple-element.58), channel_id=1, source_target_pairs={{0,24},{8,16},{16,8},{24,0},{1,25},{9,17},{17,9},{25,1},{2,26},{10... | collective-permute-start | bytes 23048 | tf_op jit(solution)/shard_map/ppermute | solution.py:18
  29.7 0.5 %collective-permute-start.12 = (bf16[2,1920]{1,0:T(2,128)(2,1)S(1)}, bf16[2,1920]{1,0:T(2,128)(2,1)S(1)}, u32[]{:S(2)}, u32[]{:S(2)}) collective-permute-start(bf16[2,1920]{1,0:T(2,128)(2,1)S(1)} %get-tuple-element.59), channel_id=1, source_target_pairs={{0,16},{8,24},{16,0},{24,8},{1,17},{9,25},{17,1},{25,9},{2,18},{10... | collective-permute-start | bytes 23048 | tf_op jit(solution)/shard_map/ppermute | solution.py:18
  30.2 2.4 %collective-permute-start.13 = (bf16[2,1920]{1,0:T(2,128)(2,1)S(1)}, bf16[2,1920]{1,0:T(2,128)(2,1)S(1)}, u32[]{:S(2)}, u32[]{:S(2)}) collective-permute-start(bf16[2,1920]{1,0:T(2,128)(2,1)S(1)} %get-tuple-element.60), channel_id=1, source_target_pairs={{0,8},{8,0},{16,24},{24,16},{1,9},{9,1},{17,25},{25,17},{2,10},{10... | collective-permute-start | bytes 23048 | tf_op jit(solution)/shard_map/ppermute | solution.py:18
  32.7 0.9 %collective-permute-done.11.refs_0_ = bf16[2,1920]{1,0:T(2,128)(2,1)S(1)} collective-permute-done((bf16[2,1920]{1,0:T(2,128)(2,1)S(1)}, bf16[2,1920]{1,0:T(2,128)(2,1)S(1)}, u32[]{:S(2)}, u32[]{:S(2)}) %collective-permute-start.11) | collective-permute-done | bytes 7712 | tf_op jit(solution)/shard_map/ppermute | solution.py:18
  33.7 0.6 %collective-permute-done.12.refs_1_ = bf16[2,1920]{1,0:T(2,128)(2,1)S(1)} collective-permute-done((bf16[2,1920]{1,0:T(2,128)(2,1)S(1)}, bf16[2,1920]{1,0:T(2,128)(2,1)S(1)}, u32[]{:S(2)}, u32[]{:S(2)}) %collective-permute-start.12) | collective-permute-done | bytes 7712 | tf_op jit(solution)/shard_map/ppermute | solution.py:18
  34.3 0.9 %finish.1 = (bf16[64,1792]{1,0:T(8,128)(2,1)}, f32[64,128]{1,0:T(8,128)}) custom-call(bf16[64,8]{1,0:T(8,128)(2,1)S(1)} %bitcast.16, bf16[2,1920]{1,0:T(2,128)(2,1)S(1)} %collective-permute-done.11.refs_0_, bf16[2,1920]{1,0:T(2,128)(2,1)S(1)} %collective-permute-done.12.refs_1_, bf16[2,1920]{1,0:T(2,128)(2,1)S(1)} %collective-permute-done.13.refs_2_, ...), custom_call_target="tpu_custom_call" | custom-call | tf_op jit(solution)/shard_map/finish/pallas_call | solution.py:440
  (17 shorter events, 1.5 us)
Async XLA Ops:
  1.9 6.0 %collective-permute-start = (bf16[8,896]{1,0:T(8,128)(2,1)S(1)}, bf16[8,896]{1,0:T(8,128)(2,1)S(1)}, u32[]{:S(2)}, u32[]{:S(2)}) collective-permute-start(bf16[8,896]{1,0:T(8,128)(2,1)S(1)} %get-tuple-element.33), channel_id=1, source_target_pairs={{0,25},{1,24},{8,17},{9,16},{16,9},{17,8},{24,1},{25,0},{2,27},{3,... | collective-permute-start | bytes 43016 | tf_op jit(solution)/shard_map/ppermute | solution.py:18
  6.5 4.1 %collective-permute-start.1 = (bf16[8,896]{1,0:T(8,128)(2,1)S(1)}, bf16[8,896]{1,0:T(8,128)(2,1)S(1)}, u32[]{:S(2)}, u32[]{:S(2)}) collective-permute-start(bf16[8,896]{1,0:T(8,128)(2,1)S(1)} %get-tuple-element.34), channel_id=1, source_target_pairs={{0,17},{1,16},{8,25},{9,24},{16,1},{17,0},{24,9},{25,8},{2,19},{3,... | collective-permute-start | bytes 43016 | tf_op jit(solution)/shard_map/ppermute | solution.py:18
  6.5 4.1 %collective-permute-start.2 = (bf16[8,896]{1,0:T(8,128)(2,1)S(1)}, bf16[8,896]{1,0:T(8,128)(2,1)S(1)}, u32[]{:S(2)}, u32[]{:S(2)}) collective-permute-start(bf16[8,896]{1,0:T(8,128)(2,1)S(1)} %get-tuple-element.35), channel_id=1, source_target_pairs={{0,9},{1,8},{8,1},{9,0},{16,25},{17,24},{24,17},{25,16},{2,11},{3,... | collective-permute-start | bytes 43016 | tf_op jit(solution)/shard_map/ppermute | solution.py:18
  10.7 6.2 %collective-permute-start.5 = (bf16[32,896]{1,0:T(8,128)(2,1)S(1)}, bf16[32,896]{1,0:T(8,128)(2,1)S(1)}, u32[]{:S(2)}, u32[]{:S(2)}) collective-permute-start(bf16[32,896]{1,0:T(8,128)(2,1)S(1)} %arrange.1.refs_0_.refs_3_), channel_id=1, source_target_pairs={{0,7},{1,6},{2,5},{3,4},{4,3},{5,2},{6,1},{7,0},{8,15},{9,14},{10,... | collective-permute-start | bytes 172040 | tf_op jit(solution)/shard_map/ppermute | solution.py:36
  13.4 3.6 %collective-permute-start.4 = (bf16[32,896]{1,0:T(8,128)(2,1)S(1)}, bf16[32,896]{1,0:T(8,128)(2,1)S(1)}, u32[]{:S(2)}, u32[]{:S(2)}) collective-permute-start(bf16[32,896]{1,0:T(8,128)(2,1)S(1)} %arrange.1.refs_0_.refs_3_), channel_id=1, source_target_pairs={{0,3},{1,4},{2,1},{3,6},{4,7},{5,0},{6,5},{7,2},{8,11},{9,12},{10,... | collective-permute-start | bytes 172040 | tf_op jit(solution)/shard_map/ppermute | solution.py:36
  13.5 4.2 %collective-permute-start.3 = (bf16[32,896]{1,0:T(8,128)(2,1)S(1)}, bf16[32,896]{1,0:T(8,128)(2,1)S(1)}, u32[]{:S(2)}, u32[]{:S(2)}) collective-permute-start(bf16[32,896]{1,0:T(8,128)(2,1)S(1)} %arrange.1.refs_0_.refs_3_), channel_id=1, source_target_pairs={{0,5},{1,2},{2,7},{3,0},{4,1},{5,6},{6,3},{7,4},{8,13},{9,10},{10,... | collective-permute-start | bytes 172040 | tf_op jit(solution)/shard_map/ppermute | solution.py:36
  17.7 1.6 %collective-permute-start.6 = (bf16[128,896]{1,0:T(8,128)(2,1)S(1)}, bf16[128,896]{1,0:T(8,128)(2,1)S(1)}, u32[]{:S(2)}, u32[]{:S(2)}) collective-permute-start(bf16[128,896]{1,0:T(8,128)(2,1)S(1)} %join.1.own_ref), channel_id=1, source_target_pairs={{0,1},{1,0},{2,3},{3,2},{4,5},{5,4},{6,7},{7,6},{8,9},{9,8},{10,11... | collective-permute-start | bytes 688136 | tf_op jit(solution)/shard_map/ppermute | solution.py:18
  20.5 1.4 %collective-permute-start.7 = (bf16[32,1920]{1,0:T(8,128)(2,1)S(1)}, bf16[32,1920]{1,0:T(8,128)(2,1)S(1)}, u32[]{:S(2)}, u32[]{:S(2)}) collective-permute-start(bf16[32,1920]{1,0:T(8,128)(2,1)S(1)} %get-tuple-element.50), channel_id=1, source_target_pairs={{0,1},{1,0},{2,3},{3,2},{4,5},{5,4},{6,7},{7,6},{8,9},{9,8},{10,11... | collective-permute-start | bytes 368648 | tf_op jit(solution)/shard_map/ppermute | solution.py:18
  22.0 4.5 %collective-permute-start.8 = (bf16[8,1920]{1,0:T(8,128)(2,1)S(1)}, bf16[8,1920]{1,0:T(8,128)(2,1)S(1)}, u32[]{:S(2)}, u32[]{:S(2)}) collective-permute-start(bf16[8,1920]{1,0:T(8,128)(2,1)S(1)} %get-tuple-element.51), channel_id=1, source_target_pairs={{0,7},{1,6},{2,5},{3,4},{4,3},{5,2},{6,1},{7,0},{8,15},{9,14},{10,... | collective-permute-start | bytes 92168 | tf_op jit(solution)/shard_map/ppermute | solution.py:36
  23.2 3.7 %collective-permute-start.9 = (bf16[8,1920]{1,0:T(8,128)(2,1)S(1)}, bf16[8,1920]{1,0:T(8,128)(2,1)S(1)}, u32[]{:S(2)}, u32[]{:S(2)}) collective-permute-start(bf16[8,1920]{1,0:T(8,128)(2,1)S(1)} %get-tuple-element.52), channel_id=1, source_target_pairs={{0,3},{1,4},{2,1},{3,6},{4,7},{5,0},{6,5},{7,2},{8,11},{9,12},{10,... | collective-permute-start | bytes 92168 | tf_op jit(solution)/shard_map/ppermute | solution.py:36
  24.4 3.3 %collective-permute-start.10 = (bf16[8,1920]{1,0:T(8,128)(2,1)S(1)}, bf16[8,1920]{1,0:T(8,128)(2,1)S(1)}, u32[]{:S(2)}, u32[]{:S(2)}) collective-permute-start(bf16[8,1920]{1,0:T(8,128)(2,1)S(1)} %get-tuple-element.53), channel_id=1, source_target_pairs={{0,5},{1,2},{2,7},{3,0},{4,1},{5,6},{6,3},{7,4},{8,13},{9,10},{10,... | collective-permute-start | bytes 92168 | tf_op jit(solution)/shard_map/ppermute | solution.py:36
  28.2 5.5 %collective-permute-start.11 = (bf16[2,1920]{1,0:T(2,128)(2,1)S(1)}, bf16[2,1920]{1,0:T(2,128)(2,1)S(1)}, u32[]{:S(2)}, u32[]{:S(2)}) collective-permute-start(bf16[2,1920]{1,0:T(2,128)(2,1)S(1)} %get-tuple-element.58), channel_id=1, source_target_pairs={{0,24},{8,16},{16,8},{24,0},{1,25},{9,17},{17,9},{25,1},{2,26},{10... | collective-permute-start | bytes 23048 | tf_op jit(solution)/shard_map/ppermute | solution.py:18
  29.7 4.5 %collective-permute-start.12 = (bf16[2,1920]{1,0:T(2,128)(2,1)S(1)}, bf16[2,1920]{1,0:T(2,128)(2,1)S(1)}, u32[]{:S(2)}, u32[]{:S(2)}) collective-permute-start(bf16[2,1920]{1,0:T(2,128)(2,1)S(1)} %get-tuple-element.59), channel_id=1, source_target_pairs={{0,16},{8,24},{16,0},{24,8},{1,17},{9,25},{17,1},{25,9},{2,18},{10... | collective-permute-start | bytes 23048 | tf_op jit(solution)/shard_map/ppermute | solution.py:18
  30.2 4.1 %collective-permute-start.13 = (bf16[2,1920]{1,0:T(2,128)(2,1)S(1)}, bf16[2,1920]{1,0:T(2,128)(2,1)S(1)}, u32[]{:S(2)}, u32[]{:S(2)}) collective-permute-start(bf16[2,1920]{1,0:T(2,128)(2,1)S(1)} %get-tuple-element.60), channel_id=1, source_target_pairs={{0,8},{8,0},{16,24},{24,16},{1,9},{9,1},{17,25},{25,17},{2,10},{10... | collective-permute-start | bytes 23048 | tf_op jit(solution)/shard_map/ppermute | solution.py:18

commit v11 on v10

--- a/solution.py
+++ b/solution.py
@@ -136,9 +136,9 @@
         out_ref[...] = total[k * unit : (k + 1) * unit]
 
 
-def arrange_kernel(*refs):
+def arrange_kernel(order, *refs):
     *slot_refs, out_ref = refs
-    slots = [ref[...].astype(F32) for ref in slot_refs[::-1]]
+    slots = [slot_refs[order.index(k)][...].astype(F32) for k in range(len(order))]
     pairs = CAP * len(slots)
     for kind in range(KINDS):
         rows = [slot[kind * CAP : (kind + 1) * CAP] for slot in slots]
@@ -358,14 +358,15 @@
             compiler_params=limit(rows),
         )(*map(keep_in_hbm, (ids_t, slots_t, weight_t, tokens, out_grad)))
     slots = exchange(send_cross, parts, experts)
+    arrival = [2, 3, 1, 0] if experts == 4 else slot_order(experts)
     with jax.named_scope("arrange"):
         block = pl.pallas_call(
-            arrange_kernel,
+            functools.partial(arrange_kernel, arrival),
             out_shape=jax.ShapeDtypeStruct((KINDS * pairs, quarter), BF16),
             in_specs=whole_vmem(experts),
             out_specs=whole_vmem(1)[0],
             compiler_params=limit(rows),
-        )(*slots[::-1])
+        )(*[slots[k] for k in arrival])
     offsets = plane_offsets(groups)
     blocks = [block] + [send_plane(block, offset) for offset in offsets[::-1]]
     loaded = load(

time: 35.4 us -> 35.7 us (level)
  transfers between devices with their start and end apart: 14 -> 14, of which waited for: 11 -> 9; matrix products, arithmetic and copies ran while one was open for 1% -> 1% of each run, Pallas kernels for 9% -> 9%
where the time goes in v11:
time: 35.7 us; the launch traced here: 35.5 us
  starting transfers between devices  17.7 us (50%)
  waiting for transfers between devices  9.41 us (26%)
  Pallas kernels  7.35 us (21%)
  between operations  0.69 us (2%)
    ppermute x8, starting transfers between devices, send_rel(): return lax.ppermute(block, axis, [(i, i ^ offset) for i in range(size)])  10.1 us
    ppermute x8, waiting for transfers between devices, send_rel(): return lax.ppermute(block, axis, [(i, i ^ offset) for i in range(size)])  7.6 us
    ppermute x6, starting transfers between devices, send_plane(): return lax.ppermute(block, ('dp', 'test'), pairs)  7.56 us
    pallas_call x2, Pallas kernels, load(): pl.pallas_call(functools.partial(load_kernel, moves), out_shape=[jax.Shap...  3.12 us
    ppermute x6, waiting for transfers between devices, send_plane(): return lax.ppermute(block, ('dp', 'test'), pairs)  1.81 us
    pallas_call x1, Pallas kernels, on_device(): pl.pallas_call(expert_kernel, out_shape=[jax.ShapeDtypeStruct((rows, out_...  1.31 us
    pallas_call x1, Pallas kernels, on_device(): pl.pallas_call(functools.partial(select_kernel, experts), out_shape=[jax....  1.31 us
    pallas_call x1, Pallas kernels, on_device(): pl.pallas_call(functools.partial(finish_kernel, experts), out_shape=[jax....  0.89 us
  transfers between devices with their start and end apart: 14, of which 9 were waited for; matrix products, arithmetic and copies ran while one was open for 1% of the time, Pallas kernels for 9%

profile of v11, /device:TPU:0, one launch (start us, length us, event | category | flops | bytes accessed | tf_op | source)
XLA Modules:
  0.0 35.5 jit_solution(3828841470914551104)
XLA Ops:
  0.6 1.3 %select.1 = (f32[32,64]{1,0:T(8,128)S(1)}, bf16[8,896]{1,0:T(8,128)(2,1)S(1)}, bf16[8,896]{1,0:T(8,128)(2,1)S(1)}, bf16[8,896]{1,0:T(8,128)(2,1)S(1)}, bf16[8,896]{1,0:T(8,128)(2,1)S(1)}) custom-call(s32[8,64]{1,0:T(8,128)} %bitcast.25, s32[8,64]{1,0:T(8,128)} %bitcast.26, bf16[8,64]{1,0:T(8,128)(2,1)} %bitcast.27, bf16[64,1792]{1,0:T(8,128)(2,1)} %refs_3_.1, ...), custom_call_target="tpu_custom_call" | custom-call | tf_op jit(solution)/shard_map/select/pallas_call | solution.py:348
  1.9 3.5 %collective-permute-start = (bf16[8,896]{1,0:T(8,128)(2,1)S(1)}, bf16[8,896]{1,0:T(8,128)(2,1)S(1)}, u32[]{:S(2)}, u32[]{:S(2)}) collective-permute-start(bf16[8,896]{1,0:T(8,128)(2,1)S(1)} %get-tuple-element.33), channel_id=1, source_target_pairs={{0,17},{1,16},{8,25},{9,24},{16,1},{17,0},{24,9},{25,8},{2,19},{3,... | collective-permute-start | bytes 43016 | tf_op jit(solution)/shard_map/ppermute | solution.py:18
  5.5 1.6 %collective-permute-start.1 = (bf16[8,896]{1,0:T(8,128)(2,1)S(1)}, bf16[8,896]{1,0:T(8,128)(2,1)S(1)}, u32[]{:S(2)}, u32[]{:S(2)}) collective-permute-start(bf16[8,896]{1,0:T(8,128)(2,1)S(1)} %get-tuple-element.34), channel_id=1, source_target_pairs={{0,25},{1,24},{8,17},{9,16},{16,9},{17,8},{24,1},{25,0},{2,27},{3,... | collective-permute-start | bytes 43016 | tf_op jit(solution)/shard_map/ppermute | solution.py:18
  7.1 0.2 collective-permute-start.2
  7.4 3.1 %collective-permute-done.1.refs_1_ = bf16[8,896]{1,0:T(8,128)(2,1)S(1)} collective-permute-done((bf16[8,896]{1,0:T(8,128)(2,1)S(1)}, bf16[8,896]{1,0:T(8,128)(2,1)S(1)}, u32[]{:S(2)}, u32[]{:S(2)}) %collective-permute-start.1) | collective-permute-done | bytes 14368 | tf_op jit(solution)/shard_map/ppermute | solution.py:18
  10.5 2.8 %collective-permute-start.5 = (bf16[32,896]{1,0:T(8,128)(2,1)S(1)}, bf16[32,896]{1,0:T(8,128)(2,1)S(1)}, u32[]{:S(2)}, u32[]{:S(2)}) collective-permute-start(bf16[32,896]{1,0:T(8,128)(2,1)S(1)} %arrange.1.refs_0_.refs_3_), channel_id=1, source_target_pairs={{0,7},{1,6},{2,5},{3,4},{4,3},{5,2},{6,1},{7,0},{8,15},{9,14},{10,... | collective-permute-start | bytes 172040 | tf_op jit(solution)/shard_map/ppermute | solution.py:36
  13.3 1.7 %collective-permute-start.3 = (bf16[32,896]{1,0:T(8,128)(2,1)S(1)}, bf16[32,896]{1,0:T(8,128)(2,1)S(1)}, u32[]{:S(2)}, u32[]{:S(2)}) collective-permute-start(bf16[32,896]{1,0:T(8,128)(2,1)S(1)} %arrange.1.refs_0_.refs_3_), channel_id=1, source_target_pairs={{0,5},{1,2},{2,7},{3,0},{4,1},{5,6},{6,3},{7,4},{8,13},{9,10},{10,... | collective-permute-start | bytes 172040 | tf_op jit(solution)/shard_map/ppermute | solution.py:36
  15.1 1.8 %load.2 = (bf16[3584,256]{1,0:T(8,128)(2,1)S(1)}, bf16[256,1792]{1,0:T(8,128)(2,1)S(1)}, bf16[64,128]{1,0:T(8,128)(2,1)S(1)}) custom-call(bf16[32,896]{1,0:T(8,128)(2,1)S(1)} %arrange.1.refs_0_.refs_3_, bf16[3584,128]{1,0:T(8,128)(2,1)} %bitcast.18, bf16[3584,128]{1,0:T(8,128)(2,1)} %bitcast.19, bf16[128,3584]{1,0:T(8,128)(2,1)} %bitcast.20, ...), custom_call_target="tpu_custom_call" | custom-call | bytes 2768896 | tf_op jit(solution)/shard_map/load/pallas_call | solution.py:192
  16.9 0.6 %collective-permute-done.3.refs_2_ = bf16[32,896]{1,0:T(8,128)(2,1)S(1)} collective-permute-done((bf16[32,896]{1,0:T(8,128)(2,1)S(1)}, bf16[32,896]{1,0:T(8,128)(2,1)S(1)}, u32[]{:S(2)}, u32[]{:S(2)}) %collective-permute-start.3) | collective-permute-done | bytes 57376 | tf_op jit(solution)/shard_map/ppermute | solution.py:36
  17.7 1.4 %collective-permute-done.6.other_ref = bf16[128,896]{1,0:T(8,128)(2,1)S(1)} collective-permute-done((bf16[128,896]{1,0:T(8,128)(2,1)S(1)}, bf16[128,896]{1,0:T(8,128)(2,1)S(1)}, u32[]{:S(2)}, u32[]{:S(2)}) %collective-permute-start.6) | collective-permute-done | bytes 229408 | tf_op jit(solution)/shard_map/ppermute | solution.py:18
  19.1 1.3 %expert.1 = (bf16[32,1920]{1,0:T(8,128)(2,1)S(1)}, bf16[32,1920]{1,0:T(8,128)(2,1)S(1)}, bf16[8,3584]{1,0:T(8,128)(2,1)S(1)}) custom-call(bf16[128,896]{1,0:T(8,128)(2,1)S(1)} %join.1.own_ref, bf16[128,896]{1,0:T(8,128)(2,1)S(1)} %collective-permute-done.6.other_ref, bf16[3584,256]{1,0:T(8,128)(2,1)S(1)} %get-tuple-element.44.pair_w, ...), custom_call_target="tpu_custom_call" | custom-call | tf_op jit(solution)/shard_map/expert/pallas_call | solution.py:391
  20.6 1.2 %collective-permute-done.7.got_ref = bf16[32,1920]{1,0:T(8,128)(2,1)S(1)} collective-permute-done((bf16[32,1920]{1,0:T(8,128)(2,1)S(1)}, bf16[32,1920]{1,0:T(8,128)(2,1)S(1)}, u32[]{:S(2)}, u32[]{:S(2)}) %collective-permute-start.7) | collective-permute-done | bytes 122912 | tf_op jit(solution)/shard_map/ppermute | solution.py:18
  21.9 1.2 %collective-permute-start.8 = (bf16[8,1920]{1,0:T(8,128)(2,1)S(1)}, bf16[8,1920]{1,0:T(8,128)(2,1)S(1)}, u32[]{:S(2)}, u32[]{:S(2)}) collective-permute-start(bf16[8,1920]{1,0:T(8,128)(2,1)S(1)} %get-tuple-element.51), channel_id=1, source_target_pairs={{0,7},{1,6},{2,5},{3,4},{4,3},{5,2},{6,1},{7,0},{8,15},{9,14},{10,... | collective-permute-start | bytes 92168 | tf_op jit(solution)/shard_map/ppermute | solution.py:36
  23.1 1.1 %collective-permute-start.9 = (bf16[8,1920]{1,0:T(8,128)(2,1)S(1)}, bf16[8,1920]{1,0:T(8,128)(2,1)S(1)}, u32[]{:S(2)}, u32[]{:S(2)}) collective-permute-start(bf16[8,1920]{1,0:T(8,128)(2,1)S(1)} %get-tuple-element.52), channel_id=1, source_target_pairs={{0,3},{1,4},{2,1},{3,6},{4,7},{5,0},{6,5},{7,2},{8,11},{9,12},{10,... | collective-permute-start | bytes 92168 | tf_op jit(solution)/shard_map/ppermute | solution.py:36
  24.3 0.6 %collective-permute-start.10 = (bf16[8,1920]{1,0:T(8,128)(2,1)S(1)}, bf16[8,1920]{1,0:T(8,128)(2,1)S(1)}, u32[]{:S(2)}, u32[]{:S(2)}) collective-permute-start(bf16[8,1920]{1,0:T(8,128)(2,1)S(1)} %get-tuple-element.53), channel_id=1, source_target_pairs={{0,5},{1,2},{2,7},{3,0},{4,1},{5,6},{6,3},{7,4},{8,13},{9,10},{10,... | collective-permute-start | bytes 92168 | tf_op jit(solution)/shard_map/ppermute | solution.py:36
  24.9 1.4 %load.3 = (bf16[64,3584]{1,0:T(8,128)(2,1)S(1)}, bf16[256,2048]{1,0:T(8,128)(2,1)S(1)}) custom-call(bf16[8,1920]{1,0:T(8,128)(2,1)S(1)} %get-tuple-element.54.refs_0_.refs_3_, bf16[64,3584]{1,0:T(8,128)(2,1)} %bitcast.21, bf16[128,4096]{1,0:T(8,128)(2,1)} %bitcast.17), custom_call_target="tpu_custom_call" | custom-call | bytes 1507328 | tf_op jit(solution)/shard_map/load/pallas_call | solution.py:192
  26.5 0.3 collective-permute-done.9.refs_1_
  26.8 0.8 %collective-permute-done.10.refs_2_ = bf16[8,1920]{1,0:T(8,128)(2,1)S(1)} collective-permute-done((bf16[8,1920]{1,0:T(8,128)(2,1)S(1)}, bf16[8,1920]{1,0:T(8,128)(2,1)S(1)}, u32[]{:S(2)}, u32[]{:S(2)}) %collective-permute-start.10) | collective-permute-done | bytes 30752 | tf_op jit(solution)/shard_map/ppermute | solution.py:36
  27.6 0.5 %score.1 = (bf16[2,1920]{1,0:T(2,128)(2,1)S(1)}, bf16[2,1920]{1,0:T(2,128)(2,1)S(1)}, bf16[2,1920]{1,0:T(2,128)(2,1)S(1)}, bf16[2,1920]{1,0:T(2,128)(2,1)S(1)}) custom-call(bf16[8,1920]{1,0:T(8,128)(2,1)S(1)} %collective-permute-done.8.refs_0_, bf16[8,1920]{1,0:T(8,128)(2,1)S(1)} %collective-permute-done.9.refs_1_, ...), custom_call_target="tpu_custom_call" | custom-call | tf_op jit(solution)/shard_map/score/pallas_call | solution.py:430
  28.1 1.9 %collective-permute-start.11 = (bf16[2,1920]{1,0:T(2,128)(2,1)S(1)}, bf16[2,1920]{1,0:T(2,128)(2,1)S(1)}, u32[]{:S(2)}, u32[]{:S(2)}) collective-permute-start(bf16[2,1920]{1,0:T(2,128)(2,1)S(1)} %get-tuple-element.58), channel_id=1, source_target_pairs={{0,24},{8,16},{16,8},{24,0},{1,25},{9,17},{17,9},{25,1},{2,26},{10... | collective-permute-start | bytes 23048 | tf_op jit(solution)/shard_map/ppermute | solution.py:18
  30.0 2.5 %collective-permute-start.13 = (bf16[2,1920]{1,0:T(2,128)(2,1)S(1)}, bf16[2,1920]{1,0:T(2,128)(2,1)S(1)}, u32[]{:S(2)}, u32[]{:S(2)}) collective-permute-start(bf16[2,1920]{1,0:T(2,128)(2,1)S(1)} %get-tuple-element.60), channel_id=1, source_target_pairs={{0,8},{8,0},{16,24},{24,16},{1,9},{9,1},{17,25},{25,17},{2,10},{10... | collective-permute-start | bytes 23048 | tf_op jit(solution)/shard_map/ppermute | solution.py:18
  32.6 0.9 %collective-permute-done.11.refs_0_ = bf16[2,1920]{1,0:T(2,128)(2,1)S(1)} collective-permute-done((bf16[2,1920]{1,0:T(2,128)(2,1)S(1)}, bf16[2,1920]{1,0:T(2,128)(2,1)S(1)}, u32[]{:S(2)}, u32[]{:S(2)}) %collective-permute-start.11) | collective-permute-done | bytes 7712 | tf_op jit(solution)/shard_map/ppermute | solution.py:18
  33.6 1.0 %collective-permute-done.12.refs_1_ = bf16[2,1920]{1,0:T(2,128)(2,1)S(1)} collective-permute-done((bf16[2,1920]{1,0:T(2,128)(2,1)S(1)}, bf16[2,1920]{1,0:T(2,128)(2,1)S(1)}, u32[]{:S(2)}, u32[]{:S(2)}) %collective-permute-start.12) | collective-permute-done | bytes 7712 | tf_op jit(solution)/shard_map/ppermute | solution.py:18
  34.6 0.9 %finish.1 = (bf16[64,1792]{1,0:T(8,128)(2,1)}, f32[64,128]{1,0:T(8,128)}) custom-call(bf16[64,8]{1,0:T(8,128)(2,1)S(1)} %bitcast.16, bf16[2,1920]{1,0:T(2,128)(2,1)S(1)} %collective-permute-done.11.refs_0_, bf16[2,1920]{1,0:T(2,128)(2,1)S(1)} %collective-permute-done.12.refs_1_, bf16[2,1920]{1,0:T(2,128)(2,1)S(1)} %collective-permute-done.13.refs_2_, ...), custom_call_target="tpu_custom_call" | custom-call | tf_op jit(solution)/shard_map/finish/pallas_call | solution.py:441
  (17 shorter events, 1.0 us)
Async XLA Ops:
  1.9 5.4 %collective-permute-start = (bf16[8,896]{1,0:T(8,128)(2,1)S(1)}, bf16[8,896]{1,0:T(8,128)(2,1)S(1)}, u32[]{:S(2)}, u32[]{:S(2)}) collective-permute-start(bf16[8,896]{1,0:T(8,128)(2,1)S(1)} %get-tuple-element.33), channel_id=1, source_target_pairs={{0,17},{1,16},{8,25},{9,24},{16,1},{17,0},{24,9},{25,8},{2,19},{3,... | collective-permute-start | bytes 43016 | tf_op jit(solution)/shard_map/ppermute | solution.py:18
  5.5 4.9 %collective-permute-start.1 = (bf16[8,896]{1,0:T(8,128)(2,1)S(1)}, bf16[8,896]{1,0:T(8,128)(2,1)S(1)}, u32[]{:S(2)}, u32[]{:S(2)}) collective-permute-start(bf16[8,896]{1,0:T(8,128)(2,1)S(1)} %get-tuple-element.34), channel_id=1, source_target_pairs={{0,25},{1,24},{8,17},{9,16},{16,9},{17,8},{24,1},{25,0},{2,27},{3,... | collective-permute-start | bytes 43016 | tf_op jit(solution)/shard_map/ppermute | solution.py:18
  7.1 3.3 %collective-permute-start.2 = (bf16[8,896]{1,0:T(8,128)(2,1)S(1)}, bf16[8,896]{1,0:T(8,128)(2,1)S(1)}, u32[]{:S(2)}, u32[]{:S(2)}) collective-permute-start(bf16[8,896]{1,0:T(8,128)(2,1)S(1)} %get-tuple-element.35), channel_id=1, source_target_pairs={{0,9},{1,8},{8,1},{9,0},{16,25},{17,24},{24,17},{25,16},{2,11},{3,... | collective-permute-start | bytes 43016 | tf_op jit(solution)/shard_map/ppermute | solution.py:18
  10.5 6.3 %collective-permute-start.5 = (bf16[32,896]{1,0:T(8,128)(2,1)S(1)}, bf16[32,896]{1,0:T(8,128)(2,1)S(1)}, u32[]{:S(2)}, u32[]{:S(2)}) collective-permute-start(bf16[32,896]{1,0:T(8,128)(2,1)S(1)} %arrange.1.refs_0_.refs_3_), channel_id=1, source_target_pairs={{0,7},{1,6},{2,5},{3,4},{4,3},{5,2},{6,1},{7,0},{8,15},{9,14},{10,... | collective-permute-start | bytes 172040 | tf_op jit(solution)/shard_map/ppermute | solution.py:36
  13.3 3.6 %collective-permute-start.4 = (bf16[32,896]{1,0:T(8,128)(2,1)S(1)}, bf16[32,896]{1,0:T(8,128)(2,1)S(1)}, u32[]{:S(2)}, u32[]{:S(2)}) collective-permute-start(bf16[32,896]{1,0:T(8,128)(2,1)S(1)} %arrange.1.refs_0_.refs_3_), channel_id=1, source_target_pairs={{0,3},{1,4},{2,1},{3,6},{4,7},{5,0},{6,5},{7,2},{8,11},{9,12},{10,... | collective-permute-start | bytes 172040 | tf_op jit(solution)/shard_map/ppermute | solution.py:36
  13.3 4.2 %collective-permute-start.3 = (bf16[32,896]{1,0:T(8,128)(2,1)S(1)}, bf16[32,896]{1,0:T(8,128)(2,1)S(1)}, u32[]{:S(2)}, u32[]{:S(2)}) collective-permute-start(bf16[32,896]{1,0:T(8,128)(2,1)S(1)} %arrange.1.refs_0_.refs_3_), channel_id=1, source_target_pairs={{0,5},{1,2},{2,7},{3,0},{4,1},{5,6},{6,3},{7,4},{8,13},{9,10},{10,... | collective-permute-start | bytes 172040 | tf_op jit(solution)/shard_map/ppermute | solution.py:36
  17.5 1.6 %collective-permute-start.6 = (bf16[128,896]{1,0:T(8,128)(2,1)S(1)}, bf16[128,896]{1,0:T(8,128)(2,1)S(1)}, u32[]{:S(2)}, u32[]{:S(2)}) collective-permute-start(bf16[128,896]{1,0:T(8,128)(2,1)S(1)} %join.1.own_ref), channel_id=1, source_target_pairs={{0,1},{1,0},{2,3},{3,2},{4,5},{5,4},{6,7},{7,6},{8,9},{9,8},{10,11... | collective-permute-start | bytes 688136 | tf_op jit(solution)/shard_map/ppermute | solution.py:18
  20.4 1.4 %collective-permute-start.7 = (bf16[32,1920]{1,0:T(8,128)(2,1)S(1)}, bf16[32,1920]{1,0:T(8,128)(2,1)S(1)}, u32[]{:S(2)}, u32[]{:S(2)}) collective-permute-start(bf16[32,1920]{1,0:T(8,128)(2,1)S(1)} %get-tuple-element.50), channel_id=1, source_target_pairs={{0,1},{1,0},{2,3},{3,2},{4,5},{5,4},{6,7},{7,6},{8,9},{9,8},{10,11... | collective-permute-start | bytes 368648 | tf_op jit(solution)/shard_map/ppermute | solution.py:18
  21.9 4.6 %collective-permute-start.8 = (bf16[8,1920]{1,0:T(8,128)(2,1)S(1)}, bf16[8,1920]{1,0:T(8,128)(2,1)S(1)}, u32[]{:S(2)}, u32[]{:S(2)}) collective-permute-start(bf16[8,1920]{1,0:T(8,128)(2,1)S(1)} %get-tuple-element.51), channel_id=1, source_target_pairs={{0,7},{1,6},{2,5},{3,4},{4,3},{5,2},{6,1},{7,0},{8,15},{9,14},{10,... | collective-permute-start | bytes 92168 | tf_op jit(solution)/shard_map/ppermute | solution.py:36
  23.1 3.6 %collective-permute-start.9 = (bf16[8,1920]{1,0:T(8,128)(2,1)S(1)}, bf16[8,1920]{1,0:T(8,128)(2,1)S(1)}, u32[]{:S(2)}, u32[]{:S(2)}) collective-permute-start(bf16[8,1920]{1,0:T(8,128)(2,1)S(1)} %get-tuple-element.52), channel_id=1, source_target_pairs={{0,3},{1,4},{2,1},{3,6},{4,7},{5,0},{6,5},{7,2},{8,11},{9,12},{10,... | collective-permute-start | bytes 92168 | tf_op jit(solution)/shard_map/ppermute | solution.py:36
  24.3 3.3 %collective-permute-start.10 = (bf16[8,1920]{1,0:T(8,128)(2,1)S(1)}, bf16[8,1920]{1,0:T(8,128)(2,1)S(1)}, u32[]{:S(2)}, u32[]{:S(2)}) collective-permute-start(bf16[8,1920]{1,0:T(8,128)(2,1)S(1)} %get-tuple-element.53), channel_id=1, source_target_pairs={{0,5},{1,2},{2,7},{3,0},{4,1},{5,6},{6,3},{7,4},{8,13},{9,10},{10,... | collective-permute-start | bytes 92168 | tf_op jit(solution)/shard_map/ppermute | solution.py:36
  28.1 5.5 %collective-permute-start.11 = (bf16[2,1920]{1,0:T(2,128)(2,1)S(1)}, bf16[2,1920]{1,0:T(2,128)(2,1)S(1)}, u32[]{:S(2)}, u32[]{:S(2)}) collective-permute-start(bf16[2,1920]{1,0:T(2,128)(2,1)S(1)} %get-tuple-element.58), channel_id=1, source_target_pairs={{0,24},{8,16},{16,8},{24,0},{1,25},{9,17},{17,9},{25,1},{2,26},{10... | collective-permute-start | bytes 23048 | tf_op jit(solution)/shard_map/ppermute | solution.py:18
  30.0 4.5 %collective-permute-start.12 = (bf16[2,1920]{1,0:T(2,128)(2,1)S(1)}, bf16[2,1920]{1,0:T(2,128)(2,1)S(1)}, u32[]{:S(2)}, u32[]{:S(2)}) collective-permute-start(bf16[2,1920]{1,0:T(2,128)(2,1)S(1)} %get-tuple-element.59), channel_id=1, source_target_pairs={{0,16},{8,24},{16,0},{24,8},{1,17},{9,25},{17,1},{25,9},{2,18},{10... | collective-permute-start | bytes 23048 | tf_op jit(solution)/shard_map/ppermute | solution.py:18
  30.0 4.5 %collective-permute-start.13 = (bf16[2,1920]{1,0:T(2,128)(2,1)S(1)}, bf16[2,1920]{1,0:T(2,128)(2,1)S(1)}, u32[]{:S(2)}, u32[]{:S(2)}) collective-permute-start(bf16[2,1920]{1,0:T(2,128)(2,1)S(1)} %get-tuple-element.60), channel_id=1, source_target_pairs={{0,8},{8,0},{16,24},{24,16},{1,9},{9,1},{17,25},{25,17},{2,10},{10... | collective-permute-start | bytes 23048 | tf_op jit(solution)/shard_map/ppermute | solution.py:18

commit v12 on v10

--- a/solution.py
+++ b/solution.py
@@ -277,10 +277,10 @@
     pieces = len(refs) - len(order) - 3
     piece_refs, (grad_ref, test_ref) = refs[:pieces], refs[pieces : pieces + 2]
     out_refs, feature = refs[pieces + 2 : -1], refs[-1]
-    total = piece_refs[0][...].astype(F32)
-    for piece_ref in piece_refs[1:]:
-        total = total + piece_ref[...].astype(F32)
-    hid = join_two(total[:, half:])
+    def total(columns):
+        return sum(ref[:, columns].astype(F32) for ref in piece_refs)
+
+    hid = join_two(total(slice(half, None)))
     grad = grad_ref[...]
     proj = grad.shape[1]
     grad = jnp.concatenate([grad, grad], axis=1)
@@ -288,13 +288,14 @@
     for p in range(0, proj, 2):
         pair = jnp.where(left, hid[:, p : p + 1], hid[:, p + 1 : p + 2])
         row, first = divmod(p * proj, feature.shape[1])
-        row *= total.shape[0]
-        feature[row : row + total.shape[0], first : first + 2 * proj] = (pair * grad).astype(BF16)
+        row *= hid.shape[0]
+        feature[row : row + hid.shape[0], first : first + 2 * proj] = (pair * grad).astype(BF16)
     scores = dot_f32(feature[...], test_ref[...], ((1,), (1,)))
-    rows, tests = total.shape[0], test_ref.shape[0] // 2
+    rows, tests = hid.shape[0], test_ref.shape[0] // 2
     score = scores[:rows, :tests] + scores[rows:, tests:]
+    main = total(slice(0, half)).astype(BF16)
     for k, out_ref in zip(order, out_refs):
-        out_ref[:, :half] = total[k * CAP : (k + 1) * CAP, :half].astype(BF16)
+        out_ref[:, :half] = main[k * CAP : (k + 1) * CAP]
         out_ref[:, half:] = score[k * CAP : (k + 1) * CAP].astype(BF16)
 
 

time: 35.4 us -> 35.4 us (level)
  no operation moved by 1% of the time
where the time goes in v12:
time: 35.4 us; the launch traced here: 35.2 us
  starting transfers between devices  17.6 us (50%)
  waiting for transfers between devices  9.26 us (26%)
  Pallas kernels  7.35 us (21%)
  between operations  0.69 us (2%)
    ppermute x8, starting transfers between devices, send_rel(): return lax.ppermute(block, axis, [(i, i ^ offset) for i in range(size)])  10.2 us
    ppermute x8, waiting for transfers between devices, send_rel(): return lax.ppermute(block, axis, [(i, i ^ offset) for i in range(size)])  7.38 us
    ppermute x6, starting transfers between devices, send_plane(): return lax.ppermute(block, ('dp', 'test'), pairs)  7.34 us
    pallas_call x2, Pallas kernels, load(): pl.pallas_call(functools.partial(load_kernel, moves), out_shape=[jax.Shap...  3.12 us
    ppermute x6, waiting for transfers between devices, send_plane(): return lax.ppermute(block, ('dp', 'test'), pairs)  1.88 us
    pallas_call x1, Pallas kernels, on_device(): pl.pallas_call(expert_kernel, out_shape=[jax.ShapeDtypeStruct((rows, out_...  1.32 us
    pallas_call x1, Pallas kernels, on_device(): pl.pallas_call(functools.partial(select_kernel, experts), out_shape=[jax....  1.31 us
    pallas_call x1, Pallas kernels, on_device(): pl.pallas_call(functools.partial(finish_kernel, experts), out_shape=[jax....  0.89 us
  transfers between devices with their start and end apart: 14, of which 11 were waited for; matrix products, arithmetic and copies ran while one was open for 1% of the time, Pallas kernels for 9%

profile of v12, /device:TPU:0, one launch (start us, length us, event | category | flops | bytes accessed | tf_op | source)
XLA Modules:
  0.0 35.2 jit_solution(18111360464076709384)
XLA Ops:
  0.6 1.3 %select.1 = (f32[32,64]{1,0:T(8,128)S(1)}, bf16[8,896]{1,0:T(8,128)(2,1)S(1)}, bf16[8,896]{1,0:T(8,128)(2,1)S(1)}, bf16[8,896]{1,0:T(8,128)(2,1)S(1)}, bf16[8,896]{1,0:T(8,128)(2,1)S(1)}) custom-call(s32[8,64]{1,0:T(8,128)} %bitcast.25, s32[8,64]{1,0:T(8,128)} %bitcast.26, bf16[8,64]{1,0:T(8,128)(2,1)} %bitcast.27, bf16[64,1792]{1,0:T(8,128)(2,1)} %refs_3_.1, ...), custom_call_target="tpu_custom_call" | custom-call | tf_op jit(solution)/shard_map/select/pallas_call | solution.py:349
  1.9 4.6 %collective-permute-start = (bf16[8,896]{1,0:T(8,128)(2,1)S(1)}, bf16[8,896]{1,0:T(8,128)(2,1)S(1)}, u32[]{:S(2)}, u32[]{:S(2)}) collective-permute-start(bf16[8,896]{1,0:T(8,128)(2,1)S(1)} %get-tuple-element.33), channel_id=1, source_target_pairs={{0,25},{1,24},{8,17},{9,16},{16,9},{17,8},{24,1},{25,0},{2,27},{3,... | collective-permute-start | bytes 43016 | tf_op jit(solution)/shard_map/ppermute | solution.py:18
  6.5 0.9 %collective-permute-start.2 = (bf16[8,896]{1,0:T(8,128)(2,1)S(1)}, bf16[8,896]{1,0:T(8,128)(2,1)S(1)}, u32[]{:S(2)}, u32[]{:S(2)}) collective-permute-start(bf16[8,896]{1,0:T(8,128)(2,1)S(1)} %get-tuple-element.35), channel_id=1, source_target_pairs={{0,9},{1,8},{8,1},{9,0},{16,25},{17,24},{24,17},{25,16},{2,11},{3,... | collective-permute-start | bytes 43016 | tf_op jit(solution)/shard_map/ppermute | solution.py:18
  7.4 0.5 %collective-permute-done.refs_0_ = bf16[8,896]{1,0:T(8,128)(2,1)S(1)} collective-permute-done((bf16[8,896]{1,0:T(8,128)(2,1)S(1)}, bf16[8,896]{1,0:T(8,128)(2,1)S(1)}, u32[]{:S(2)}, u32[]{:S(2)}) %collective-permute-start) | collective-permute-done | bytes 14368 | tf_op jit(solution)/shard_map/ppermute | solution.py:18
  7.9 2.7 %collective-permute-done.1.refs_1_ = bf16[8,896]{1,0:T(8,128)(2,1)S(1)} collective-permute-done((bf16[8,896]{1,0:T(8,128)(2,1)S(1)}, bf16[8,896]{1,0:T(8,128)(2,1)S(1)}, u32[]{:S(2)}, u32[]{:S(2)}) %collective-permute-start.1) | collective-permute-done | bytes 14368 | tf_op jit(solution)/shard_map/ppermute | solution.py:18
  10.7 2.7 %collective-permute-start.5 = (bf16[32,896]{1,0:T(8,128)(2,1)S(1)}, bf16[32,896]{1,0:T(8,128)(2,1)S(1)}, u32[]{:S(2)}, u32[]{:S(2)}) collective-permute-start(bf16[32,896]{1,0:T(8,128)(2,1)S(1)} %arrange.1.refs_0_.refs_3_), channel_id=1, source_target_pairs={{0,7},{1,6},{2,5},{3,4},{4,3},{5,2},{6,1},{7,0},{8,15},{9,14},{10,... | collective-permute-start | bytes 172040 | tf_op jit(solution)/shard_map/ppermute | solution.py:36
  13.5 1.7 %collective-permute-start.3 = (bf16[32,896]{1,0:T(8,128)(2,1)S(1)}, bf16[32,896]{1,0:T(8,128)(2,1)S(1)}, u32[]{:S(2)}, u32[]{:S(2)}) collective-permute-start(bf16[32,896]{1,0:T(8,128)(2,1)S(1)} %arrange.1.refs_0_.refs_3_), channel_id=1, source_target_pairs={{0,5},{1,2},{2,7},{3,0},{4,1},{5,6},{6,3},{7,4},{8,13},{9,10},{10,... | collective-permute-start | bytes 172040 | tf_op jit(solution)/shard_map/ppermute | solution.py:36
  15.1 1.8 %load.2 = (bf16[3584,256]{1,0:T(8,128)(2,1)S(1)}, bf16[256,1792]{1,0:T(8,128)(2,1)S(1)}, bf16[64,128]{1,0:T(8,128)(2,1)S(1)}) custom-call(bf16[32,896]{1,0:T(8,128)(2,1)S(1)} %arrange.1.refs_0_.refs_3_, bf16[3584,128]{1,0:T(8,128)(2,1)} %bitcast.18, bf16[3584,128]{1,0:T(8,128)(2,1)} %bitcast.19, bf16[128,3584]{1,0:T(8,128)(2,1)} %bitcast.20, ...), custom_call_target="tpu_custom_call" | custom-call | bytes 2768896 | tf_op jit(solution)/shard_map/load/pallas_call | solution.py:192
  17.0 0.7 %collective-permute-done.3.refs_2_ = bf16[32,896]{1,0:T(8,128)(2,1)S(1)} collective-permute-done((bf16[32,896]{1,0:T(8,128)(2,1)S(1)}, bf16[32,896]{1,0:T(8,128)(2,1)S(1)}, u32[]{:S(2)}, u32[]{:S(2)}) %collective-permute-start.3) | collective-permute-done | bytes 57376 | tf_op jit(solution)/shard_map/ppermute | solution.py:36
  17.8 1.4 %collective-permute-done.6.other_ref = bf16[128,896]{1,0:T(8,128)(2,1)S(1)} collective-permute-done((bf16[128,896]{1,0:T(8,128)(2,1)S(1)}, bf16[128,896]{1,0:T(8,128)(2,1)S(1)}, u32[]{:S(2)}, u32[]{:S(2)}) %collective-permute-start.6) | collective-permute-done | bytes 229408 | tf_op jit(solution)/shard_map/ppermute | solution.py:18
  19.2 1.3 %expert.1 = (bf16[32,1920]{1,0:T(8,128)(2,1)S(1)}, bf16[32,1920]{1,0:T(8,128)(2,1)S(1)}, bf16[8,3584]{1,0:T(8,128)(2,1)S(1)}) custom-call(bf16[128,896]{1,0:T(8,128)(2,1)S(1)} %join.1.own_ref, bf16[128,896]{1,0:T(8,128)(2,1)S(1)} %collective-permute-done.6.other_ref, bf16[3584,256]{1,0:T(8,128)(2,1)S(1)} %get-tuple-element.44.pair_w, ...), custom_call_target="tpu_custom_call" | custom-call | tf_op jit(solution)/shard_map/expert/pallas_call | solution.py:391
  20.7 1.2 %collective-permute-done.7.got_ref = bf16[32,1920]{1,0:T(8,128)(2,1)S(1)} collective-permute-done((bf16[32,1920]{1,0:T(8,128)(2,1)S(1)}, bf16[32,1920]{1,0:T(8,128)(2,1)S(1)}, u32[]{:S(2)}, u32[]{:S(2)}) %collective-permute-start.7) | collective-permute-done | bytes 122912 | tf_op jit(solution)/shard_map/ppermute | solution.py:18
  22.0 1.2 %collective-permute-start.8 = (bf16[8,1920]{1,0:T(8,128)(2,1)S(1)}, bf16[8,1920]{1,0:T(8,128)(2,1)S(1)}, u32[]{:S(2)}, u32[]{:S(2)}) collective-permute-start(bf16[8,1920]{1,0:T(8,128)(2,1)S(1)} %get-tuple-element.51), channel_id=1, source_target_pairs={{0,7},{1,6},{2,5},{3,4},{4,3},{5,2},{6,1},{7,0},{8,15},{9,14},{10,... | collective-permute-start | bytes 92168 | tf_op jit(solution)/shard_map/ppermute | solution.py:36
  23.2 1.1 %collective-permute-start.9 = (bf16[8,1920]{1,0:T(8,128)(2,1)S(1)}, bf16[8,1920]{1,0:T(8,128)(2,1)S(1)}, u32[]{:S(2)}, u32[]{:S(2)}) collective-permute-start(bf16[8,1920]{1,0:T(8,128)(2,1)S(1)} %get-tuple-element.52), channel_id=1, source_target_pairs={{0,3},{1,4},{2,1},{3,6},{4,7},{5,0},{6,5},{7,2},{8,11},{9,12},{10,... | collective-permute-start | bytes 92168 | tf_op jit(solution)/shard_map/ppermute | solution.py:36
  24.4 0.6 %collective-permute-start.10 = (bf16[8,1920]{1,0:T(8,128)(2,1)S(1)}, bf16[8,1920]{1,0:T(8,128)(2,1)S(1)}, u32[]{:S(2)}, u32[]{:S(2)}) collective-permute-start(bf16[8,1920]{1,0:T(8,128)(2,1)S(1)} %get-tuple-element.53), channel_id=1, source_target_pairs={{0,5},{1,2},{2,7},{3,0},{4,1},{5,6},{6,3},{7,4},{8,13},{9,10},{10,... | collective-permute-start | bytes 92168 | tf_op jit(solution)/shard_map/ppermute | solution.py:36
  25.0 1.4 %load.3 = (bf16[64,3584]{1,0:T(8,128)(2,1)S(1)}, bf16[256,2048]{1,0:T(8,128)(2,1)S(1)}) custom-call(bf16[8,1920]{1,0:T(8,128)(2,1)S(1)} %get-tuple-element.54.refs_0_.refs_3_, bf16[64,3584]{1,0:T(8,128)(2,1)} %bitcast.21, bf16[128,4096]{1,0:T(8,128)(2,1)} %bitcast.17), custom_call_target="tpu_custom_call" | custom-call | bytes 1507328 | tf_op jit(solution)/shard_map/load/pallas_call | solution.py:192
  26.9 0.7 %collective-permute-done.10.refs_2_ = bf16[8,1920]{1,0:T(8,128)(2,1)S(1)} collective-permute-done((bf16[8,1920]{1,0:T(8,128)(2,1)S(1)}, bf16[8,1920]{1,0:T(8,128)(2,1)S(1)}, u32[]{:S(2)}, u32[]{:S(2)}) %collective-permute-start.10) | collective-permute-done | bytes 30752 | tf_op jit(solution)/shard_map/ppermute | solution.py:36
  27.7 0.5 %score.1 = (bf16[2,1920]{1,0:T(2,128)(2,1)S(1)}, bf16[2,1920]{1,0:T(2,128)(2,1)S(1)}, bf16[2,1920]{1,0:T(2,128)(2,1)S(1)}, bf16[2,1920]{1,0:T(2,128)(2,1)S(1)}) custom-call(bf16[8,1920]{1,0:T(8,128)(2,1)S(1)} %collective-permute-done.8.refs_0_, bf16[8,1920]{1,0:T(8,128)(2,1)S(1)} %collective-permute-done.9.refs_1_, ...), custom_call_target="tpu_custom_call" | custom-call | tf_op jit(solution)/shard_map/score/pallas_call | solution.py:430
  28.2 1.5 %collective-permute-start.11 = (bf16[2,1920]{1,0:T(2,128)(2,1)S(1)}, bf16[2,1920]{1,0:T(2,128)(2,1)S(1)}, u32[]{:S(2)}, u32[]{:S(2)}) collective-permute-start(bf16[2,1920]{1,0:T(2,128)(2,1)S(1)} %get-tuple-element.58), channel_id=1, source_target_pairs={{0,24},{8,16},{16,8},{24,0},{1,25},{9,17},{17,9},{25,1},{2,26},{10... | collective-permute-start | bytes 23048 | tf_op jit(solution)/shard_map/ppermute | solution.py:18
  29.7 0.5 %collective-permute-start.12 = (bf16[2,1920]{1,0:T(2,128)(2,1)S(1)}, bf16[2,1920]{1,0:T(2,128)(2,1)S(1)}, u32[]{:S(2)}, u32[]{:S(2)}) collective-permute-start(bf16[2,1920]{1,0:T(2,128)(2,1)S(1)} %get-tuple-element.59), channel_id=1, source_target_pairs={{0,16},{8,24},{16,0},{24,8},{1,17},{9,25},{17,1},{25,9},{2,18},{10... | collective-permute-start | bytes 23048 | tf_op jit(solution)/shard_map/ppermute | solution.py:18
  30.2 2.4 %collective-permute-start.13 = (bf16[2,1920]{1,0:T(2,128)(2,1)S(1)}, bf16[2,1920]{1,0:T(2,128)(2,1)S(1)}, u32[]{:S(2)}, u32[]{:S(2)}) collective-permute-start(bf16[2,1920]{1,0:T(2,128)(2,1)S(1)} %get-tuple-element.60), channel_id=1, source_target_pairs={{0,8},{8,0},{16,24},{24,16},{1,9},{9,1},{17,25},{25,17},{2,10},{10... | collective-permute-start | bytes 23048 | tf_op jit(solution)/shard_map/ppermute | solution.py:18
  32.7 0.9 %collective-permute-done.11.refs_0_ = bf16[2,1920]{1,0:T(2,128)(2,1)S(1)} collective-permute-done((bf16[2,1920]{1,0:T(2,128)(2,1)S(1)}, bf16[2,1920]{1,0:T(2,128)(2,1)S(1)}, u32[]{:S(2)}, u32[]{:S(2)}) %collective-permute-start.11) | collective-permute-done | bytes 7712 | tf_op jit(solution)/shard_map/ppermute | solution.py:18
  33.7 0.6 %collective-permute-done.12.refs_1_ = bf16[2,1920]{1,0:T(2,128)(2,1)S(1)} collective-permute-done((bf16[2,1920]{1,0:T(2,128)(2,1)S(1)}, bf16[2,1920]{1,0:T(2,128)(2,1)S(1)}, u32[]{:S(2)}, u32[]{:S(2)}) %collective-permute-start.12) | collective-permute-done | bytes 7712 | tf_op jit(solution)/shard_map/ppermute | solution.py:18
  34.3 0.9 %finish.1 = (bf16[64,1792]{1,0:T(8,128)(2,1)}, f32[64,128]{1,0:T(8,128)}) custom-call(bf16[64,8]{1,0:T(8,128)(2,1)S(1)} %bitcast.16, bf16[2,1920]{1,0:T(2,128)(2,1)S(1)} %collective-permute-done.11.refs_0_, bf16[2,1920]{1,0:T(2,128)(2,1)S(1)} %collective-permute-done.12.refs_1_, bf16[2,1920]{1,0:T(2,128)(2,1)S(1)} %collective-permute-done.13.refs_2_, ...), custom_call_target="tpu_custom_call" | custom-call | tf_op jit(solution)/shard_map/finish/pallas_call | solution.py:441
  (17 shorter events, 1.5 us)
Async XLA Ops:
  1.9 6.0 %collective-permute-start = (bf16[8,896]{1,0:T(8,128)(2,1)S(1)}, bf16[8,896]{1,0:T(8,128)(2,1)S(1)}, u32[]{:S(2)}, u32[]{:S(2)}) collective-permute-start(bf16[8,896]{1,0:T(8,128)(2,1)S(1)} %get-tuple-element.33), channel_id=1, source_target_pairs={{0,25},{1,24},{8,17},{9,16},{16,9},{17,8},{24,1},{25,0},{2,27},{3,... | collective-permute-start | bytes 43016 | tf_op jit(solution)/shard_map/ppermute | solution.py:18
  6.5 4.1 %collective-permute-start.1 = (bf16[8,896]{1,0:T(8,128)(2,1)S(1)}, bf16[8,896]{1,0:T(8,128)(2,1)S(1)}, u32[]{:S(2)}, u32[]{:S(2)}) collective-permute-start(bf16[8,896]{1,0:T(8,128)(2,1)S(1)} %get-tuple-element.34), channel_id=1, source_target_pairs={{0,17},{1,16},{8,25},{9,24},{16,1},{17,0},{24,9},{25,8},{2,19},{3,... | collective-permute-start | bytes 43016 | tf_op jit(solution)/shard_map/ppermute | solution.py:18
  6.5 4.1 %collective-permute-start.2 = (bf16[8,896]{1,0:T(8,128)(2,1)S(1)}, bf16[8,896]{1,0:T(8,128)(2,1)S(1)}, u32[]{:S(2)}, u32[]{:S(2)}) collective-permute-start(bf16[8,896]{1,0:T(8,128)(2,1)S(1)} %get-tuple-element.35), channel_id=1, source_target_pairs={{0,9},{1,8},{8,1},{9,0},{16,25},{17,24},{24,17},{25,16},{2,11},{3,... | collective-permute-start | bytes 43016 | tf_op jit(solution)/shard_map/ppermute | solution.py:18
  10.7 6.2 %collective-permute-start.5 = (bf16[32,896]{1,0:T(8,128)(2,1)S(1)}, bf16[32,896]{1,0:T(8,128)(2,1)S(1)}, u32[]{:S(2)}, u32[]{:S(2)}) collective-permute-start(bf16[32,896]{1,0:T(8,128)(2,1)S(1)} %arrange.1.refs_0_.refs_3_), channel_id=1, source_target_pairs={{0,7},{1,6},{2,5},{3,4},{4,3},{5,2},{6,1},{7,0},{8,15},{9,14},{10,... | collective-permute-start | bytes 172040 | tf_op jit(solution)/shard_map/ppermute | solution.py:36
  13.4 3.6 %collective-permute-start.4 = (bf16[32,896]{1,0:T(8,128)(2,1)S(1)}, bf16[32,896]{1,0:T(8,128)(2,1)S(1)}, u32[]{:S(2)}, u32[]{:S(2)}) collective-permute-start(bf16[32,896]{1,0:T(8,128)(2,1)S(1)} %arrange.1.refs_0_.refs_3_), channel_id=1, source_target_pairs={{0,3},{1,4},{2,1},{3,6},{4,7},{5,0},{6,5},{7,2},{8,11},{9,12},{10,... | collective-permute-start | bytes 172040 | tf_op jit(solution)/shard_map/ppermute | solution.py:36
  13.5 4.2 %collective-permute-start.3 = (bf16[32,896]{1,0:T(8,128)(2,1)S(1)}, bf16[32,896]{1,0:T(8,128)(2,1)S(1)}, u32[]{:S(2)}, u32[]{:S(2)}) collective-permute-start(bf16[32,896]{1,0:T(8,128)(2,1)S(1)} %arrange.1.refs_0_.refs_3_), channel_id=1, source_target_pairs={{0,5},{1,2},{2,7},{3,0},{4,1},{5,6},{6,3},{7,4},{8,13},{9,10},{10,... | collective-permute-start | bytes 172040 | tf_op jit(solution)/shard_map/ppermute | solution.py:36
  17.7 1.6 %collective-permute-start.6 = (bf16[128,896]{1,0:T(8,128)(2,1)S(1)}, bf16[128,896]{1,0:T(8,128)(2,1)S(1)}, u32[]{:S(2)}, u32[]{:S(2)}) collective-permute-start(bf16[128,896]{1,0:T(8,128)(2,1)S(1)} %join.1.own_ref), channel_id=1, source_target_pairs={{0,1},{1,0},{2,3},{3,2},{4,5},{5,4},{6,7},{7,6},{8,9},{9,8},{10,11... | collective-permute-start | bytes 688136 | tf_op jit(solution)/shard_map/ppermute | solution.py:18
  20.5 1.4 %collective-permute-start.7 = (bf16[32,1920]{1,0:T(8,128)(2,1)S(1)}, bf16[32,1920]{1,0:T(8,128)(2,1)S(1)}, u32[]{:S(2)}, u32[]{:S(2)}) collective-permute-start(bf16[32,1920]{1,0:T(8,128)(2,1)S(1)} %get-tuple-element.50), channel_id=1, source_target_pairs={{0,1},{1,0},{2,3},{3,2},{4,5},{5,4},{6,7},{7,6},{8,9},{9,8},{10,11... | collective-permute-start | bytes 368648 | tf_op jit(solution)/shard_map/ppermute | solution.py:18
  22.0 4.5 %collective-permute-start.8 = (bf16[8,1920]{1,0:T(8,128)(2,1)S(1)}, bf16[8,1920]{1,0:T(8,128)(2,1)S(1)}, u32[]{:S(2)}, u32[]{:S(2)}) collective-permute-start(bf16[8,1920]{1,0:T(8,128)(2,1)S(1)} %get-tuple-element.51), channel_id=1, source_target_pairs={{0,7},{1,6},{2,5},{3,4},{4,3},{5,2},{6,1},{7,0},{8,15},{9,14},{10,... | collective-permute-start | bytes 92168 | tf_op jit(solution)/shard_map/ppermute | solution.py:36
  23.2 3.7 %collective-permute-start.9 = (bf16[8,1920]{1,0:T(8,128)(2,1)S(1)}, bf16[8,1920]{1,0:T(8,128)(2,1)S(1)}, u32[]{:S(2)}, u32[]{:S(2)}) collective-permute-start(bf16[8,1920]{1,0:T(8,128)(2,1)S(1)} %get-tuple-element.52), channel_id=1, source_target_pairs={{0,3},{1,4},{2,1},{3,6},{4,7},{5,0},{6,5},{7,2},{8,11},{9,12},{10,... | collective-permute-start | bytes 92168 | tf_op jit(solution)/shard_map/ppermute | solution.py:36
  24.4 3.3 %collective-permute-start.10 = (bf16[8,1920]{1,0:T(8,128)(2,1)S(1)}, bf16[8,1920]{1,0:T(8,128)(2,1)S(1)}, u32[]{:S(2)}, u32[]{:S(2)}) collective-permute-start(bf16[8,1920]{1,0:T(8,128)(2,1)S(1)} %get-tuple-element.53), channel_id=1, source_target_pairs={{0,5},{1,2},{2,7},{3,0},{4,1},{5,6},{6,3},{7,4},{8,13},{9,10},{10,... | collective-permute-start | bytes 92168 | tf_op jit(solution)/shard_map/ppermute | solution.py:36
  28.2 5.5 %collective-permute-start.11 = (bf16[2,1920]{1,0:T(2,128)(2,1)S(1)}, bf16[2,1920]{1,0:T(2,128)(2,1)S(1)}, u32[]{:S(2)}, u32[]{:S(2)}) collective-permute-start(bf16[2,1920]{1,0:T(2,128)(2,1)S(1)} %get-tuple-element.58), channel_id=1, source_target_pairs={{0,24},{8,16},{16,8},{24,0},{1,25},{9,17},{17,9},{25,1},{2,26},{10... | collective-permute-start | bytes 23048 | tf_op jit(solution)/shard_map/ppermute | solution.py:18
  29.7 4.5 %collective-permute-start.12 = (bf16[2,1920]{1,0:T(2,128)(2,1)S(1)}, bf16[2,1920]{1,0:T(2,128)(2,1)S(1)}, u32[]{:S(2)}, u32[]{:S(2)}) collective-permute-start(bf16[2,1920]{1,0:T(2,128)(2,1)S(1)} %get-tuple-element.59), channel_id=1, source_target_pairs={{0,16},{8,24},{16,0},{24,8},{1,17},{9,25},{17,1},{25,9},{2,18},{10... | collective-permute-start | bytes 23048 | tf_op jit(solution)/shard_map/ppermute | solution.py:18
  30.2 4.1 %collective-permute-start.13 = (bf16[2,1920]{1,0:T(2,128)(2,1)S(1)}, bf16[2,1920]{1,0:T(2,128)(2,1)S(1)}, u32[]{:S(2)}, u32[]{:S(2)}) collective-permute-start(bf16[2,1920]{1,0:T(2,128)(2,1)S(1)} %get-tuple-element.60), channel_id=1, source_target_pairs={{0,8},{8,0},{16,24},{24,16},{1,9},{9,1},{17,25},{25,17},{2,10},{10... | collective-permute-start | bytes 23048 | tf_op jit(solution)/shard_map/ppermute | solution.py:18
